TPU v7x, 32 devices: a whole 2x2x4 slice. The times are simulated.
32 devices in a mesh: rows: 8 (over z, x), filt: 4 (over y, core).
Axes of the slice: x: 2, y: 2, z: 4, core: 2. Of those that a mesh axis runs over, the one named last changes fastest.
Arguments:
- features: bfloat16 [96, 48, 2048], P('rows'), may hold values from -6 to 6
- point_weight: bfloat16 [2048, 256], P(None, 'filt'), may hold values from -0.125 to 0.125
- dilated_weight: bfloat16 [3, 3, 3, 2048, 256], P(None, None, None, None, 'filt'), may hold values from -0.046875 to 0.046875
- branch_bias: float32 [4, 256], P(None, 'filt'), may hold values from -3 to 3
- project_weight: bfloat16 [4, 256, 256], replicated, may hold values from -0.1875 to 0.1875
- project_bias: float32 [256], replicated, may hold values from -3 to 3
- cotangent: bfloat16 [96, 48, 256], P('rows'), may hold values from -6 to 6
Outputs:
- head_output: bfloat16 [96, 48, 256], P('rows', None, 'filt')
- feature_grad: bfloat16 [96, 48, 2048], P('rows', None, 'filt')
All inputs are finite; a program needn't handle non-finite values.
Results may differ from a plain program's by a relative error of at most 0.035.
The roundings to bfloat16 on the way count: a program that leaves them out, or rounds other values in their place, can miss the bound.
Values may be sent and summed in bfloat16 or wider, within the bound.
No kernel may reach another device: no remote copies, remote signals or barrier semaphores. Data moves between devices by JAX's collectives and lax.ppermute only.
A program may use at most 128 MiB of HBM per device.

v0:
```python
import functools

import jax
import jax.numpy as jnp
from jax import lax
from jax.experimental import pallas as pl
from jax.experimental.pallas import tpu as pltpu
from jax.sharding import PartitionSpec as P

FIRST_DILATION = 12
SECOND_DILATION = 24
THIRD_DILATION = 36


def passed_along(x, axis, by):
    devices = lax.axis_size(axis)
    pairs = [(i, i + by) for i in range(devices) if 0 <= i + by < devices]
    return lax.ppermute(x, axis, pairs)


def shift_columns(field, amount):
    breadth = field.shape[1]
    if amount == 0:
        return field
    padding = [(0, 0)] * field.ndim
    if amount > 0:
        kept = field[:, amount:]
        padding[1] = (0, amount)
    else:
        kept = field[:, : breadth + amount]
        padding[1] = (-amount, 0)
    return jnp.pad(kept, padding)


def fetch_sums(field, offset):
    return passed_along(field, "rows", offset)


def fetch_grads(field, offset):
    return passed_along(field, "rows", offset)


def shift_rows(field, amount, fetcher):
    height = field.shape[0]
    quotient = amount // height

    def extract_block(offset):
        if offset == 0:
            return field
        return fetcher(field, offset)

    return extract_block(quotient)


def make_kernel_taps(variants, dilation_rates):
    stacked = [variants[:, :, 0]]
    for branch, dilation in enumerate(dilation_rates):
        for row_tap in range(3):
            source = variants[:, :, 1 + 3 * branch + row_tap]
            for col_tap in range(3):
                stacked.append(shift_columns(source, -(col_tap - 1) * dilation))
    return jnp.stack(stacked, 2)


def on_device_general(
    features, point_weight, dilated_weight, branch_bias, project_weight, project_bias, cotangent
):
    height, breadth, channels = features.shape
    pixels = height * breadth
    own_width = point_weight.shape[1]
    filters = lax.axis_size("filt")
    member = lax.axis_index("filt")
    branch_outputs = project_weight.shape[2]
    own_out = branch_outputs // filters
    own_channels = channels // filters
    dilation_rates = (FIRST_DILATION, SECOND_DILATION, THIRD_DILATION)
    all_weights = jnp.concatenate(
        [point_weight[None], dilated_weight.reshape(27, channels, own_width)], 0
    )
    flattened = features.reshape(pixels, channels)
    tap_terms = jnp.einsum(
        "pc,tco->pto", flattened, all_weights, preferred_element_type=jnp.float32
    )
    tap_terms = tap_terms.reshape(height, breadth, 28, own_width)
    pre_list = [tap_terms[:, :, 0, :] + branch_bias[0]]
    for branch, dilation in enumerate(dilation_rates):
        summed_result = jnp.zeros((height, breadth, own_width), jnp.float32)
        for row_tap in range(3):
            row_sum = jnp.zeros((height, breadth, own_width), jnp.float32)
            for col_tap in range(3):
                row_sum = row_sum + shift_columns(
                    tap_terms[:, :, 1 + 9 * branch + 3 * row_tap + col_tap, :],
                    (col_tap - 1) * dilation,
                )
            summed_result = summed_result + shift_rows(
                row_sum, -(row_tap - 1) * dilation, fetch_sums
            )
        pre_list.append(summed_result + branch_bias[branch + 1])
    branch_pre = jnp.stack(pre_list, 2)
    activations = jnp.maximum(branch_pre, 0.0).astype(jnp.bfloat16).reshape(pixels, 4 * own_width)
    grouped = project_weight.reshape(4, filters, own_width, branch_outputs)
    own_rows = lax.dynamic_index_in_dim(grouped, member, 1, keepdims=False).reshape(
        4 * own_width, branch_outputs
    )
    flat_cotangent = cotangent.reshape(pixels, branch_outputs)
    ordered = jnp.transpose(grouped, (1, 0, 2, 3)).reshape(filters * 4 * own_width, branch_outputs)
    project_pre = jnp.dot(
        lax.all_gather(activations, "filt", axis=1, tiled=True),
        ordered,
        preferred_element_type=jnp.float32,
    )
    project_pre = project_pre + project_bias
    head_grad = jnp.where(project_pre > 0, flat_cotangent.astype(jnp.float32), 0.0).astype(
        jnp.bfloat16
    )
    own_pre = lax.dynamic_slice_in_dim(project_pre, member * own_out, own_out, 1)
    act_grad = jnp.dot(head_grad, own_rows.T, preferred_element_type=jnp.float32)
    head_output = jnp.maximum(own_pre, 0.0).astype(jnp.bfloat16).reshape(height, breadth, own_out)
    branch_grad = jnp.where(
        branch_pre > 0, act_grad.reshape(height, breadth, 4, own_width), 0.0
    ).astype(jnp.bfloat16)
    variant_list = [branch_grad[:, :, 0, :]]
    for branch, dilation in enumerate(dilation_rates):
        for row_tap in range(3):
            variant_list.append(
                shift_rows(branch_grad[:, :, branch + 1, :], (row_tap - 1) * dilation, fetch_grads)
            )
    variants = jnp.stack(variant_list, 2)
    stacked = make_kernel_taps(variants, dilation_rates).reshape(pixels, 28, own_width)
    input_grad = lax.psum_scatter(
        jnp.einsum("pto,tco->cp", stacked, all_weights, preferred_element_type=jnp.float32),
        "filt",
        scatter_dimension=0,
        tiled=True,
    ).T
    feature_grad = input_grad.astype(jnp.bfloat16).reshape(height, breadth, own_channels)
    return (head_output, feature_grad)


W = 64
BLOCK = 144
PIXELS = 576
HALF = 288
SENT = 304
CHANNELS = 2048
F32 = jnp.float32
BF16 = jnp.bfloat16

OUT_PAIRS = ((3, 1), (1, 1), (3, 0), (1, 0), (3, 2), (1, 2), (2, 1), (2, 0), (2, 2))
TAPS = (
    [(k, 1, 1) for k in (2, 1, 3)]
    + [(k, i, j) for k, j in OUT_PAIRS for i in (0, 2)]
    + [(k, 1, j) for j in (0, 2) for k in (2, 1, 3)]
)
OUT_AT, LEFT_AT, RIGHT_AT = 4 * W, 22 * W, 25 * W
PARTS = ((0, 2), (1, 3))
SWAPS = (6, 2, 1, 3, 7, 5)
GRAD_SWAPS = (1, 5, 7, 3, 6, 2)


def fits(mesh):
    return mesh.shape["rows"] == 8 and mesh.shape["filt"] == 4


def order_matrix(turned=False):
    to = lax.broadcasted_iota(jnp.int32, (192, 192), 1 if turned else 0)
    source = lax.broadcasted_iota(jnp.int32, (192, 192), 0 if turned else 1)

    def parts(value, width):
        return sum((value >= n * width).astype(jnp.int32) for n in (1, 2, 3))

    block = parts(to, 48)
    within = to - 48 * block
    line = parts(within, 12)
    wanted = line * 48 + block * 12 + within - 12 * line
    return (source == wanted).astype(F32).astype(BF16)


def tap_index(tap):
    k, i, j = tap
    return (k - 1) * 9 + i * 3 + j


def nt(a, b):
    return lax.dot_general(a, b, (((1,), (1,)), ((), ())), preferred_element_type=F32)


def nn(a, b):
    return lax.dot_general(a, b, (((1,), (0,)), ((), ())), preferred_element_type=F32)


def from_blocks(order_t, value, write):
    for g in range(3):
        parts = [value[m * BLOCK + g * 48 : m * BLOCK + g * 48 + 48] for m in range(4)]
        write(g * 192, nn(order_t, jnp.concatenate(parts, 0)).astype(BF16))


def low_lanes(shape):
    return lax.broadcasted_iota(jnp.int32, shape, 1) % 128 < W


def scaled(value):
    most = jnp.maximum(jnp.max(jnp.abs(value), axis=0, keepdims=True), 1e-30)
    power = jnp.floor(jnp.log(most) * 1.4426950408889634)
    return value * jnp.exp2(13.0 - power), power


def unscaled(sent):
    return sent[:HALF, :] * jnp.exp2(sent[HALF : HALF + 1, :] - 13.0)


def outward_slot(row, x):
    other = row ^ x
    apart = jnp.abs(other - row)
    slot = apart - 1 + jnp.where(other < row, 3, 0)
    return jnp.where(apart <= 3, slot, 0)


def fetch_tap(dilated, weights, sem, place):
    return pltpu.make_async_copy(
        dilated.at[tap_index(TAPS[place - 1])], weights.at[pl.ds(place * W, W)], sem
    )


def outward_kernel(features, dilated, point, *refs):
    row = lax.axis_index("rows")
    out, ordered, weights = refs[0:6], refs[6], refs[7]
    raw, sums, packed, feature_sems, weight_sems = refs[8:]
    loads = []
    for g in range(3):
        rows = pl.ds(g * 192, 192)
        loads.append(pltpu.make_async_copy(features.at[rows], raw.at[rows], feature_sems.at[g]))
        loads[-1].start()
    queue = [
        fetch_tap(dilated, weights, weight_sems.at[q], place)
        for q, place in enumerate((*range(4, 28), 1, 2, 3))
    ]
    queue.append(pltpu.make_async_copy(point, weights.at[pl.ds(0, W)], weight_sems.at[27]))

    def start_loads(first, last):
        for fetch in queue[first:last]:
            fetch.start()

    start_loads(0, 4)
    order = order_matrix()
    for g in range(3):
        loads[g].wait()
        start_loads((4, 12, 18)[g], (12, 18, 28)[g])
        moved = nn(order, raw[g * 192 : (g + 1) * 192, :]).astype(BF16)
        for m in range(4):
            at = m * BLOCK + g * 48
            ordered[at : at + 48, :] = moved[m * 48 : (m + 1) * 48]

    def product(pair, pairs, first, last):
        for fetch in queue[2 * pair : 2 * (pair + pairs)]:
            fetch.wait()
        at = OUT_AT + pair * 128
        return nt(ordered[first * BLOCK : last * BLOCK, :], weights[at : at + pairs * 128, :])

    d = product(0, 2, 0, 4)
    sums[2] = d[:, :128]
    sums[0] = d[:, 128:]
    d = product(2, 2, 0, 3)
    sums[2, 3 * BLOCK :, :] = sums[2, 3 * BLOCK :, :] + d[:BLOCK, :128]
    sums[0, BLOCK:, :] = sums[0, BLOCK:, :] + d[:, 128:]
    d = product(4, 2, 1, 4)
    sums[2, :BLOCK, :] = sums[2, :BLOCK, :] + d[2 * BLOCK :, :128]
    sums[0, : 3 * BLOCK, :] = sums[0, : 3 * BLOCK, :] + d[:, 128:]
    low = low_lanes((HALF, 128))

    def pack(k):
        top, bottom = sums[k, :HALF, :], sums[k, HALF:, :]
        halves = (
            jnp.where(low, top, pltpu.roll(bottom, W, 1)),
            jnp.where(low, pltpu.roll(top, W, 1), bottom),
        )
        for way, value in enumerate(halves):
            value, power = scaled(value)
            packed[k + 3 * way, :HALF, :] = value
            packed[k + 3 * way, HALF:, :] = jnp.broadcast_to(power, (SENT - HALF, 128))

    pack(2)
    pack(0)
    d = product(6, 3, 0, 4)
    sums[1] = d[:, :128]
    sums[1, 2 * BLOCK :, :] = sums[1, 2 * BLOCK :, :] + d[: 2 * BLOCK, 128:256]
    sums[1, : 2 * BLOCK, :] = sums[1, : 2 * BLOCK, :] + d[2 * BLOCK :, 256:]
    pack(1)
    for n, x in enumerate(SWAPS):
        out[n][...] = packed[outward_slot(row, x)]
    for fetch in queue[18:]:
        fetch.wait()


def outward_sums(features, dilated, point):
    return pl.pallas_call(
        outward_kernel,
        out_shape=[jax.ShapeDtypeStruct((SENT, 128), F32)] * 6
        + [pltpu.VMEM((PIXELS, CHANNELS), BF16), pltpu.VMEM((28 * W, CHANNELS), BF16)],
        in_specs=[pl.BlockSpec(memory_space=pltpu.HBM)] * 3,
        out_specs=[pl.BlockSpec(memory_space=pltpu.VMEM)] * 8,
        scratch_shapes=[
            pltpu.VMEM((PIXELS, CHANNELS), BF16),
            pltpu.VMEM((3, PIXELS, 128), F32),
            pltpu.VMEM((6, SENT, 128), F32),
            pltpu.SemaphoreType.DMA((3,)),
            pltpu.SemaphoreType.DMA((28,)),
        ],
        compiler_params=pltpu.CompilerParams(vmem_limit_bytes=28 * 2**20),
        name="outward_sums",
    )(features, dilated, point)


def own_kernel(ordered, weights, bias, *outs):
    d = nt(ordered[...], weights[:256, :])
    for part, out in enumerate(outs):
        line = jnp.concatenate([bias[k : k + 1, :] for k in PARTS[part]], 1)
        out[...] = d[:, part * 128 : part * 128 + 128] + line
    low = low_lanes((PIXELS, 128))

    def add(first, value, k):
        part = k % 2
        rows = slice(first * BLOCK, first * BLOCK + value.shape[0])
        mask, value = low[: value.shape[0]], value[:, part * 128 : part * 128 + 128]
        kept = jnp.where(mask, value, 0.0) if k == 1 else jnp.where(mask, 0.0, value)
        outs[part][rows, :] = outs[part][rows, :] + kept

    d = nt(ordered[: 3 * BLOCK, :], weights[LEFT_AT - W : LEFT_AT + 3 * W, :])
    for k in (1, 2, 3):
        add(k, d[: (4 - k) * BLOCK], k)
    d = nt(ordered[BLOCK:, :], weights[RIGHT_AT - W : RIGHT_AT + 3 * W, :])
    for k in (1, 2, 3):
        add(0, d[(k - 1) * BLOCK :], k)


def own_sums(ordered, weights, bias):
    return pl.pallas_call(
        own_kernel,
        out_shape=[jax.ShapeDtypeStruct((PIXELS, 128), F32)] * 2,
        in_specs=[pl.BlockSpec(memory_space=pltpu.VMEM)] * 3,
        out_specs=[pl.BlockSpec(memory_space=pltpu.VMEM)] * 2,
        compiler_params=pltpu.CompilerParams(vmem_limit_bytes=18 * 2**20),
        cost_estimate=pl.CostEstimate(flops=10**6, bytes_accessed=10**4, transcendentals=0),
        name="own_sums",
    )(ordered, weights, bias)


def arrival_slot(row, other):
    return jnp.where((other >= 0) & (other < 8), row ^ other, 0)


def gather_arrivals(recv, arrivals, swaps):
    arrivals[0] = jnp.zeros((HALF, 128), arrivals.dtype)
    for n, x in enumerate(swaps):
        arrivals[x] = recv[n][...] if recv[n].shape[0] == HALF else unscaled(recv[n][...])


def activation_kernel(part, swaps, own, *refs):
    recv, acts, arrivals = refs[: len(swaps)], refs[-2], refs[-1]
    row = lax.axis_index("rows")
    gather_arrivals(recv, arrivals, swaps)
    low = low_lanes((HALF, 128))

    def total(k):
        return arrivals[arrival_slot(row, row - k)] + arrivals[arrival_slot(row, row + k)]

    high = total(PARTS[part][1])
    top, bottom = jnp.where(low, 0.0, pltpu.roll(high, W, 1)), jnp.where(low, 0.0, high)
    if part:
        left = total(PARTS[part][0])
        top = jnp.where(low, left, top)
        bottom = jnp.where(low, pltpu.roll(left, W, 1), bottom)
    acts[:HALF, :] = jnp.maximum(own[:HALF, :] + top, 0.0).astype(BF16)
    acts[HALF:, :] = jnp.maximum(own[HALF:, :] + bottom, 0.0).astype(BF16)


def activations_of(part, swaps, own, received):
    return pl.pallas_call(
        functools.partial(activation_kernel, part, swaps),
        out_shape=jax.ShapeDtypeStruct((PIXELS, 128), BF16),
        in_specs=[pl.BlockSpec(memory_space=pltpu.VMEM)] * (1 + len(swaps)),
        out_specs=pl.BlockSpec(memory_space=pltpu.VMEM),
        scratch_shapes=[pltpu.VMEM((8, HALF, 128), F32)],
        compiler_params=pltpu.CompilerParams(vmem_limit_bytes=8 * 2**20),
        name="activations",
    )(own, *received)


def project_rows(project, who):
    at = pl.multiple_of(who * W, W)
    return jnp.concatenate([project[k, pl.ds(at, W), :] for part in PARTS for k in part], 0)


def both(a, b):
    return jnp.concatenate([a[...], b[...]], 1)


def near_head_kernel(a0, b0, a1, b1, project, bias, cotangent, pre, ordered):
    member = lax.axis_index("filt")
    pre[...] = nn(both(a0, b0), project_rows(project, member)) + bias[...]
    pre[...] = pre[...] + nn(both(a1, b1), project_rows(project, member ^ 1))
    order = order_matrix()
    for g in range(3):
        moved = nn(order, cotangent[g * 192 : (g + 1) * 192, :])
        for m in range(4):
            at = m * BLOCK + g * 48
            ordered[at : at + 48, :] = moved[m * 48 : (m + 1) * 48]


def near_head(own, beside, project, bias, cotangent):
    return pl.pallas_call(
        near_head_kernel,
        out_shape=[jax.ShapeDtypeStruct((PIXELS, 256), F32)] * 2,
        in_specs=[pl.BlockSpec(memory_space=pltpu.VMEM)] * 7,
        out_specs=[pl.BlockSpec(memory_space=pltpu.VMEM)] * 2,
        compiler_params=pltpu.CompilerParams(vmem_limit_bytes=10 * 2**20),
        name="near_head",
    )(*own, *beside, project, bias, cotangent)


def far_head_kernel(a0, b0, a2, b2, a3, b3, project, near, cotangent, *refs):
    output, grads, sends, packed = refs[0], refs[1], refs[2:8], refs[8]
    row, member = lax.axis_index("rows"), lax.axis_index("filt")
    pre = near[...] + nn(both(a2, b2), project_rows(project, member ^ 2))
    pre = pre + nn(both(a3, b3), project_rows(project, member ^ 3))
    output[...] = jnp.maximum(pre, 0.0).astype(BF16)
    head_grad = jnp.where(pre > 0, cotangent[...], 0.0).astype(BF16)
    act_grad = nt(head_grad, project_rows(project, member))
    a = jnp.where(a0[...].astype(F32) > 0, act_grad[:, :128], 0.0)
    b = jnp.where(b0[...].astype(F32) > 0, act_grad[:, 128:], 0.0)
    grads[:, :128] = a.astype(BF16)
    grads[:, 128:] = b.astype(BF16)
    low = low_lanes((HALF, 128))
    packed[0] = jnp.where(low, b[:HALF], pltpu.roll(b[HALF:], W, 1)).astype(BF16)
    packed[1] = jnp.where(low, pltpu.roll(a[:HALF], W, 1), a[HALF:]).astype(BF16)
    packed[2] = jnp.where(low, pltpu.roll(b[:HALF], W, 1), b[HALF:]).astype(BF16)
    for n, x in enumerate(GRAD_SWAPS):
        apart = jnp.abs((row ^ x) - row)
        sends[n][...] = packed[jnp.where(apart <= 3, apart - 1, 0)]


def far_head(own, across, corner, project, near, cotangent):
    return pl.pallas_call(
        far_head_kernel,
        out_shape=[jax.ShapeDtypeStruct((PIXELS, 256), BF16)] * 2
        + [jax.ShapeDtypeStruct((HALF, 128), BF16)] * 6,
        in_specs=[pl.BlockSpec(memory_space=pltpu.VMEM)] * 9,
        out_specs=[pl.BlockSpec(memory_space=pltpu.VMEM)] * 8,
        scratch_shapes=[pltpu.VMEM((3, HALF, 128), BF16)],
        compiler_params=pltpu.CompilerParams(vmem_limit_bytes=12 * 2**20),
        name="far_head",
    )(*own, *across, *corner, project, near, cotangent)


def own_output_kernel(output, out):
    member = lax.axis_index("filt")
    mine = jnp.zeros((PIXELS, W), F32)
    for q in range(4):
        mine = jnp.where(member == q, output[:, q * W : (q + 1) * W].astype(F32), mine)

    def put(at, value):
        out[at : at + 192, :] = value

    from_blocks(order_matrix(True), mine.astype(BF16), put)


def own_output(output):
    return pl.pallas_call(
        own_output_kernel,
        out_shape=jax.ShapeDtypeStruct((PIXELS, W), BF16),
        in_specs=[pl.BlockSpec(memory_space=pltpu.VMEM)],
        out_specs=pl.BlockSpec(memory_space=pltpu.VMEM),
        compiler_params=pltpu.CompilerParams(vmem_limit_bytes=6 * 2**20),
        name="own_output",
    )(output)


def spread_kernel(own, *refs):
    recv, stack, arrivals, pairs, twice = refs[:6], refs[6], refs[7], refs[8], refs[9]
    row = lax.axis_index("rows")
    gather_arrivals(recv, arrivals, GRAD_SWAPS)
    low = low_lanes((HALF, 128))
    low_all = low_lanes((PIXELS, 128))
    for k in (1, 2, 3):
        p = arrivals[arrival_slot(row, row + k)].astype(F32)
        m = arrivals[arrival_slot(row, row - k)].astype(F32)
        pairs[k - 1, :HALF, :] = jnp.where(low, p, pltpu.roll(m, W, 1)).astype(BF16)
        pairs[k - 1, HALF:, :] = jnp.where(low, pltpu.roll(p, W, 1), m).astype(BF16)
        g = own[:, :128].astype(F32) if k == 2 else own[:, 128:].astype(F32)
        other = pltpu.roll(g, W, 1)
        two = jnp.where(low_all, g, other) if k == 1 else jnp.where(low_all, other, g)
        twice[k - 1] = two.astype(BF16)
    stack[:, : 4 * W] = own[...]
    nothing = jnp.zeros((BLOCK, 128), BF16)

    def block_of(ref, k, source):
        if 0 <= source < 4:
            return ref[k - 1, source * BLOCK : (source + 1) * BLOCK, :]
        return nothing

    for q, (k, j) in enumerate(OUT_PAIRS):
        lanes = slice(OUT_AT + q * 128, OUT_AT + q * 128 + 128)
        for m in range(4):
            stack[m * BLOCK : (m + 1) * BLOCK, lanes] = block_of(pairs, k, m - (j - 1) * k)
    low_block = low_lanes((BLOCK, 128))
    for q, (a, b) in enumerate(((2, 1), (3, -2), (-1, -3))):
        lanes = slice(LEFT_AT + q * 128, LEFT_AT + q * 128 + 128)
        for m in range(4):
            stack[m * BLOCK : (m + 1) * BLOCK, lanes] = jnp.where(
                low_block, block_of(twice, abs(a), m + a), block_of(twice, abs(b), m + b)
            )


def spread(own, received):
    return pl.pallas_call(
        spread_kernel,
        out_shape=pltpu.VMEM((PIXELS, 28 * W), BF16),
        in_specs=[pl.BlockSpec(memory_space=pltpu.VMEM)] * 7,
        out_specs=pl.BlockSpec(memory_space=pltpu.VMEM),
        scratch_shapes=[
            pltpu.VMEM((8, HALF, 128), BF16),
            pltpu.VMEM((3, PIXELS, 128), BF16),
            pltpu.VMEM((3, PIXELS, 128), BF16),
        ],
        compiler_params=pltpu.CompilerParams(vmem_limit_bytes=12 * 2**20),
        name="spread",
    )(own, *received)


def grad_kernel(flips, stack, weights, *outs):
    member = lax.axis_index("filt")
    for out, flip in zip(outs, flips):
        columns = pl.ds(pl.multiple_of((member ^ flip) * 512, 512), 512)
        out[...] = nn(stack[...], weights[:, columns]).astype(BF16)


def grads_for(flips, stack, weights, scale=1):
    return pl.pallas_call(
        functools.partial(grad_kernel, flips),
        out_shape=[jax.ShapeDtypeStruct((PIXELS, 512), BF16)] * len(flips),
        in_specs=[pl.BlockSpec(memory_space=pltpu.VMEM)] * 2,
        out_specs=[pl.BlockSpec(memory_space=pltpu.VMEM)] * len(flips),
        compiler_params=pltpu.CompilerParams(vmem_limit_bytes=18 * 2**20),
        cost_estimate=pl.CostEstimate(
            flops=2 * PIXELS * 28 * W * 512 * scale, bytes_accessed=10**6, transcendentals=0
        ),
        name="grads_for",
    )(stack, weights)


def last_kernel(a, b, c, out):
    total = a[...].astype(F32) + b[...].astype(F32) + c[...].astype(F32)

    def put(at, value):
        out[at : at + 192, :] = value

    from_blocks(order_matrix(True), total.astype(BF16), put)


def last_sum(a, b, c):
    return pl.pallas_call(
        last_kernel,
        out_shape=jax.ShapeDtypeStruct((PIXELS, 512), BF16),
        in_specs=[pl.BlockSpec(memory_space=pltpu.VMEM)] * 3,
        out_specs=pl.BlockSpec(memory_space=pltpu.VMEM),
        compiler_params=pltpu.CompilerParams(vmem_limit_bytes=10 * 2**20),
        name="last_sum",
    )(a, b, c)


def flipped(x, bit):
    return lax.ppermute(x, "filt", [(i, i ^ bit) for i in range(lax.axis_size("filt"))])


def swapped(x, bits):
    pairs = [(r, r ^ bits) for r in range(8) if abs((r ^ bits) - r) <= 3]
    return lax.ppermute(x, "rows", pairs)


def on_device(
    features, point_weight, dilated_weight, branch_bias, project_weight, project_bias, cotangent
):
    flat = features.reshape(PIXELS, CHANNELS)
    dilated = jnp.transpose(dilated_weight, (0, 1, 2, 4, 3)).reshape(27, W, CHANNELS)
    point = point_weight.T
    flat, dilated, point = (
        pltpu.with_memory_space_constraint(x, pltpu.HBM) for x in (flat, dilated, point)
    )
    *sums, ordered, weights = outward_sums(flat, dilated, point)
    received = {
        x: swapped(sums[n].astype(jnp.float16), x).astype(F32) for n, x in enumerate(SWAPS)
    }
    own = own_sums(ordered, weights, branch_bias)
    acts = [
        activations_of(part, swaps, own[part], [received[x] for x in swaps])
        for part, swaps in ((0, SWAPS[:2]), (1, SWAPS[2:]))
    ]
    across = [flipped(x, 2) for x in acts]
    beside = [flipped(x, 1) for x in acts]
    corner = [flipped(x, 1) for x in across]
    near, ordered_cotangent = near_head(
        acts,
        beside,
        project_weight,
        project_bias.reshape(1, 256),
        cotangent.reshape(PIXELS, 256),
    )
    output, grads, *sends = far_head(
        acts, across, corner, project_weight, near, ordered_cotangent
    )
    arrived = [swapped(sends[n], x) for n, x in enumerate(GRAD_SWAPS)]
    stack = spread(grads, arrived)
    (far,) = grads_for((3,), stack, weights)
    far = flipped(far, 1)
    (kept,) = grads_for((2,), stack, weights)
    crossing = (far.astype(F32) + kept.astype(F32)).astype(BF16)
    crossed = flipped(crossing, 2)
    later, output, crossing = lax.optimization_barrier((stack, output, crossing))
    head_output = own_output(output)
    (near,) = grads_for((1,), later, weights)
    near = flipped(near, 1)
    (kept,) = grads_for((0,), later, weights, 8)
    feature_grad = last_sum(kept, near, crossed)
    return head_output.reshape(12, 48, W), feature_grad.reshape(12, 48, 512)


def solution(mesh):
    body = on_device if fits(mesh) else on_device_general
    in_specs = (
        P("rows", None, None),
        P(None, "filt"),
        P(None, None, None, None, "filt"),
        P(None, "filt"),
        P(),
        P(),
        P("rows", None, None),
    )
    out_specs = (P("rows", None, "filt"), P("rows", None, "filt"))
    return jax.shard_map(
        body, mesh=mesh, in_specs=in_specs, out_specs=out_specs, check_vma=False
    )
```

profile of v0, /device:TPU:0, one launch (start us, length us, event | category | flops | bytes accessed | tf_op | source)
XLA Modules:
  0.0 71.5 jit_solution(10507466126250515795)
XLA Ops:
  0.6 8.2 %outward_sums.1 = (f32[304,128]{1,0:T(8,128)S(1)}, f32[304,128]{1,0:T(8,128)S(1)}, f32[304,128]{1,0:T(8,128)S(1)}, f32[304,128]{1,0:T(8,128)S(1)}, f32[304,128]{...) custom-call(bf16[576,2048]{1,0:T(8,128)(2,1)} %bitcast.12, ...), custom_call_target="tpu_custom_call" | custom-call | tf_op jit(solution)/shard_map/outward_sums/pallas_call | solution.py:296
  8.9 3.1 %collective-permute-start.1 = (f16[304,128]{1,0:T(8,128)(2,1)S(1)}, f16[304,128]{1,0:T(8,128)(2,1)S(1)}, u32[]{:S(2)}, u32[]{:S(2)}) collective-permute-start(f16[304,128]{1,0:T(8,128)(2,1)S(1)} %convert_element_type.47), channel_id=1, source_target_pairs={{0,8},{4,12},{8,0},{12,4},{16,24},{20,28},{24,16},{28,20},{1,9},{5... | collective-permute-start | bytes 233480 | tf_op jit(solution)/shard_map/ppermute | solution.py:577
  12.0 0.7 collective-permute-start
  12.7 0.7 collective-permute-start.5
  13.4 0.7 collective-permute-start.4
  14.1 7.9 %collective-permute-start.3 = (f16[304,128]{1,0:T(8,128)(2,1)S(1)}, f16[304,128]{1,0:T(8,128)(2,1)S(1)}, u32[]{:S(2)}, u32[]{:S(2)}) collective-permute-start(f16[304,128]{1,0:T(8,128)(2,1)S(1)} %convert_element_type.51), channel_id=1, source_target_pairs={{0,12},{4,8},{8,4},{12,0},{16,28},{20,24},{24,20},{28,16},{1,13},{... | collective-permute-start | bytes 233480 | tf_op jit(solution)/shard_map/ppermute | solution.py:577
  22.3 1.7 %own_sums.1 = (f32[576,128]{1,0:T(8,128)S(1)}, f32[576,128]{1,0:T(8,128)S(1)}) custom-call(bf16[576,2048]{1,0:T(8,128)(2,1)S(1)} %get-tuple-element.24.ordered, bf16[1792,2048]{1,0:T(8,128)(2,1)S(1)} %get-tuple-element.25.weights, f32[4,64]{1,0:T(4,128)S(1)} %copy-done.2), custom_call_target="tpu_custom_call" | custom-call | flops 1000000 | bytes 10000 | tf_op jit(solution)/shard_map/own_sums/pallas_call | solution.py:337
  24.3 1.6 %collective-permute-start.6 = (bf16[576,128]{1,0:T(8,128)(2,1)S(1)}, bf16[576,128]{1,0:T(8,128)(2,1)S(1)}, u32[]{:S(2)}, u32[]{:S(2)}) collective-permute-start(bf16[576,128]{1,0:T(8,128)(2,1)S(1)} %activations.2.a0), channel_id=1, source_target_pairs={{0,2},{1,3},{2,0},{3,1},{4,6},{5,7},{6,4},{7,5},{8,10},{9,11},{10,... | collective-permute-start | bytes 442376 | tf_op jit(solution)/shard_map/ppermute | solution.py:572
  25.9 0.5 collective-permute-done.2
  26.7 1.6 %collective-permute-start.7 = (bf16[576,128]{1,0:T(8,128)(2,1)S(1)}, bf16[576,128]{1,0:T(8,128)(2,1)S(1)}, u32[]{:S(2)}, u32[]{:S(2)}) collective-permute-start(bf16[576,128]{1,0:T(8,128)(2,1)S(1)} %activations.3.b0), channel_id=1, source_target_pairs={{0,2},{1,3},{2,0},{3,1},{4,6},{5,7},{6,4},{7,5},{8,10},{9,11},{10,... | collective-permute-start | bytes 442376 | tf_op jit(solution)/shard_map/ppermute | solution.py:572
  28.8 2.2 %collective-permute-done.6.a2 = bf16[576,128]{1,0:T(8,128)(2,1)S(1)} collective-permute-done((bf16[576,128]{1,0:T(8,128)(2,1)S(1)}, bf16[576,128]{1,0:T(8,128)(2,1)S(1)}, u32[]{:S(2)}, u32[]{:S(2)}) %collective-permute-start.6) | collective-permute-done | bytes 147488 | tf_op jit(solution)/shard_map/ppermute | solution.py:572
  31.0 1.6 %collective-permute-done.7.b2 = bf16[576,128]{1,0:T(8,128)(2,1)S(1)} collective-permute-done((bf16[576,128]{1,0:T(8,128)(2,1)S(1)}, bf16[576,128]{1,0:T(8,128)(2,1)S(1)}, u32[]{:S(2)}, u32[]{:S(2)}) %collective-permute-start.7) | collective-permute-done | bytes 147488 | tf_op jit(solution)/shard_map/ppermute | solution.py:572
  33.1 0.9 %collective-permute-done.9.b3 = bf16[576,128]{1,0:T(8,128)(2,1)S(1)} collective-permute-done((bf16[576,128]{1,0:T(8,128)(2,1)S(1)}, bf16[576,128]{1,0:T(8,128)(2,1)S(1)}, u32[]{:S(2)}, u32[]{:S(2)}) %collective-permute-start.9) | collective-permute-done | bytes 147488 | tf_op jit(solution)/shard_map/ppermute | solution.py:572
  34.0 0.6 far_head.1
  34.6 1.2 %collective-permute-start.12 = (bf16[288,128]{1,0:T(8,128)(2,1)S(1)}, bf16[288,128]{1,0:T(8,128)(2,1)S(1)}, u32[]{:S(2)}, u32[]{:S(2)}) collective-permute-start(bf16[288,128]{1,0:T(8,128)(2,1)S(1)} %get-tuple-element.37), channel_id=1, source_target_pairs={{0,4},{4,0},{8,12},{12,8},{16,20},{20,16},{24,28},{28,24},{1,5},{5... | collective-permute-start | bytes 221192 | tf_op jit(solution)/shard_map/ppermute | solution.py:577
  35.9 0.7 collective-permute-start.13
  36.5 0.7 collective-permute-start.14
  37.2 7.2 %collective-permute-start.15 = (bf16[288,128]{1,0:T(8,128)(2,1)S(1)}, bf16[288,128]{1,0:T(8,128)(2,1)S(1)}, u32[]{:S(2)}, u32[]{:S(2)}) collective-permute-start(bf16[288,128]{1,0:T(8,128)(2,1)S(1)} %get-tuple-element.40), channel_id=1, source_target_pairs={{0,12},{4,8},{8,4},{12,0},{16,28},{20,24},{24,20},{28,16},{1,13},{... | collective-permute-start | bytes 221192 | tf_op jit(solution)/shard_map/ppermute | solution.py:577
  44.4 0.8 %collective-permute-start.16 = (bf16[288,128]{1,0:T(8,128)(2,1)S(1)}, bf16[288,128]{1,0:T(8,128)(2,1)S(1)}, u32[]{:S(2)}, u32[]{:S(2)}) collective-permute-start(bf16[288,128]{1,0:T(8,128)(2,1)S(1)} %get-tuple-element.41), channel_id=1, source_target_pairs={{8,16},{12,20},{16,8},{20,12},{9,17},{13,21},{17,9},{21,13},{10,18... | collective-permute-start | bytes 221192 | tf_op jit(solution)/shard_map/ppermute | solution.py:577
  45.3 3.2 %collective-permute-start.17 = (bf16[288,128]{1,0:T(8,128)(2,1)S(1)}, bf16[288,128]{1,0:T(8,128)(2,1)S(1)}, u32[]{:S(2)}, u32[]{:S(2)}) collective-permute-start(bf16[288,128]{1,0:T(8,128)(2,1)S(1)} %get-tuple-element.42), channel_id=1, source_target_pairs={{0,8},{4,12},{8,0},{12,4},{16,24},{20,28},{24,16},{28,20},{1,9},{5... | collective-permute-start | bytes 221192 | tf_op jit(solution)/shard_map/ppermute | solution.py:577
  48.5 2.3 %collective-permute-done.17.refs_5_ = bf16[288,128]{1,0:T(8,128)(2,1)S(1)} collective-permute-done((bf16[288,128]{1,0:T(8,128)(2,1)S(1)}, bf16[288,128]{1,0:T(8,128)(2,1)S(1)}, u32[]{:S(2)}, u32[]{:S(2)}) %collective-permute-start.17) | collective-permute-done | bytes 73760 | tf_op jit(solution)/shard_map/ppermute | solution.py:577
  50.8 0.6 spread.1.stack
  51.4 1.2 %grads_for.4 = bf16[576,512]{1,0:T(8,128)(2,1)S(1)} custom-call(bf16[576,1792]{1,0:T(8,128)(2,1)S(1)} %spread.1.stack, bf16[1792,2048]{1,0:T(8,128)(2,1)S(1)} %get-tuple-element.25.weights), custom_call_target="tpu_custom_call" | custom-call | flops 1056964608 | bytes 1000000 | tf_op jit(solution)/shard_map/grads_for/pallas_call | solution.py:538
  52.7 1.2 %grads_for.5 = bf16[576,512]{1,0:T(8,128)(2,1)S(1)} custom-call(bf16[576,1792]{1,0:T(8,128)(2,1)S(1)} %spread.1.stack, bf16[1792,2048]{1,0:T(8,128)(2,1)S(1)} %get-tuple-element.25.weights), custom_call_target="tpu_custom_call" | custom-call | flops 1056964608 | bytes 1000000 | tf_op jit(solution)/shard_map/grads_for/pallas_call | solution.py:538
  53.9 0.7 %collective-permute-done.18 = bf16[576,512]{1,0:T(8,128)(2,1)S(1)} collective-permute-done((bf16[576,512]{1,0:T(8,128)(2,1)S(1)}, bf16[576,512]{1,0:T(8,128)(2,1)S(1)}, u32[]{:S(2)}, u32[]{:S(2)}) %collective-permute-start.18) | collective-permute-done | bytes 589856 | tf_op jit(solution)/shard_map/ppermute | solution.py:572
  54.8 1.6 %collective-permute-start.20 = (bf16[576,512]{1,0:T(8,128)(2,1)S(1)}, bf16[576,512]{1,0:T(8,128)(2,1)S(1)}, u32[]{:S(2)}, u32[]{:S(2)}) collective-permute-start(bf16[576,512]{1,0:T(8,128)(2,1)S(1)} %add_convert_fusion), channel_id=1, source_target_pairs={{0,2},{1,3},{2,0},{3,1},{4,6},{5,7},{6,4},{7,5},{8,10},{9,11},{10,... | collective-permute-start | bytes 1769480 | tf_op jit(solution)/shard_map/ppermute | solution.py:572
  56.4 1.2 %own_output.1 = bf16[576,64]{1,0:T(8,128)(2,1)} custom-call(bf16[576,256]{1,0:T(8,128)(2,1)S(1)} %get-tuple-element.44.output), custom_call_target="tpu_custom_call" | custom-call | tf_op jit(solution)/shard_map/own_output/pallas_call | solution.py:468
  57.6 1.2 %grads_for.7 = bf16[576,512]{1,0:T(8,128)(2,1)S(1)} custom-call(bf16[576,1792]{1,0:T(8,128)(2,1)S(1)} %spread.1.stack, bf16[1792,2048]{1,0:T(8,128)(2,1)S(1)} %get-tuple-element.25.weights), custom_call_target="tpu_custom_call" | custom-call | flops 1056964608 | bytes 1000000 | tf_op jit(solution)/shard_map/grads_for/pallas_call | solution.py:538
  59.0 1.2 %grads_for.6.a = bf16[576,512]{1,0:T(8,128)(2,1)S(1)} custom-call(bf16[576,1792]{1,0:T(8,128)(2,1)S(1)} %spread.1.stack, bf16[1792,2048]{1,0:T(8,128)(2,1)S(1)} %get-tuple-element.25.weights), custom_call_target="tpu_custom_call" | custom-call | flops 8455716864 | bytes 1000000 | tf_op jit(solution)/shard_map/grads_for/pallas_call | solution.py:538
  60.2 0.7 %collective-permute-done.19.b = bf16[576,512]{1,0:T(8,128)(2,1)S(1)} collective-permute-done((bf16[576,512]{1,0:T(8,128)(2,1)S(1)}, bf16[576,512]{1,0:T(8,128)(2,1)S(1)}, u32[]{:S(2)}, u32[]{:S(2)}) %collective-permute-start.19) | collective-permute-done | bytes 589856 | tf_op jit(solution)/shard_map/ppermute | solution.py:572
  60.9 9.3 %collective-permute-done.20.c = bf16[576,512]{1,0:T(8,128)(2,1)S(1)} collective-permute-done((bf16[576,512]{1,0:T(8,128)(2,1)S(1)}, bf16[576,512]{1,0:T(8,128)(2,1)S(1)}, u32[]{:S(2)}, u32[]{:S(2)}) %collective-permute-start.20) | collective-permute-done | bytes 589856 | tf_op jit(solution)/shard_map/ppermute | solution.py:572
  70.3 1.3 %last_sum.1 = bf16[576,512]{1,0:T(8,128)(2,1)} custom-call(bf16[576,512]{1,0:T(8,128)(2,1)S(1)} %grads_for.6.a, bf16[576,512]{1,0:T(8,128)(2,1)S(1)} %collective-permute-done.19.b, bf16[576,512]{1,0:T(8,128)(2,1)S(1)} %collective-permute-done.20.c), custom_call_target="tpu_custom_call" | custom-call | tf_op jit(solution)/shard_map/last_sum/pallas_call | solution.py:561
  (44 shorter events, 2.0 us)
Async XLA Ops:
  0.6 21.7 %copy-start.2 = (f32[4,64]{1,0:T(4,128)S(1)}, f32[4,64]{1,0:T(4,128)}, u32[]{:S(2)}) copy-start(f32[4,64]{1,0:T(4,128)} %bias.1) | copy-start | bytes 3076
  8.9 13.1 %collective-permute-start.1 = (f16[304,128]{1,0:T(8,128)(2,1)S(1)}, f16[304,128]{1,0:T(8,128)(2,1)S(1)}, u32[]{:S(2)}, u32[]{:S(2)}) collective-permute-start(f16[304,128]{1,0:T(8,128)(2,1)S(1)} %convert_element_type.47), channel_id=1, source_target_pairs={{0,8},{4,12},{8,0},{12,4},{16,24},{20,28},{24,16},{28,20},{1,9},{5... | collective-permute-start | bytes 233480 | tf_op jit(solution)/shard_map/ppermute | solution.py:577
  12.0 12.1 %collective-permute-start = (f16[304,128]{1,0:T(8,128)(2,1)S(1)}, f16[304,128]{1,0:T(8,128)(2,1)S(1)}, u32[]{:S(2)}, u32[]{:S(2)}) collective-permute-start(f16[304,128]{1,0:T(8,128)(2,1)S(1)} %convert_element_type.45), channel_id=1, source_target_pairs={{8,16},{12,20},{16,8},{20,12},{9,17},{13,21},{17,9},{21,13},{10,18... | collective-permute-start | bytes 233480 | tf_op jit(solution)/shard_map/ppermute | solution.py:577
  12.7 13.2 %collective-permute-start.5 = (f16[304,128]{1,0:T(8,128)(2,1)S(1)}, f16[304,128]{1,0:T(8,128)(2,1)S(1)}, u32[]{:S(2)}, u32[]{:S(2)}) collective-permute-start(f16[304,128]{1,0:T(8,128)(2,1)S(1)} %convert_element_type.55), channel_id=1, source_target_pairs={{4,16},{12,24},{16,4},{24,12},{5,17},{13,25},{17,5},{25,13},{6,18}... | collective-permute-start | bytes 233480 | tf_op jit(solution)/shard_map/ppermute | solution.py:577
  13.4 12.5 %collective-permute-start.4 = (f16[304,128]{1,0:T(8,128)(2,1)S(1)}, f16[304,128]{1,0:T(8,128)(2,1)S(1)}, u32[]{:S(2)}, u32[]{:S(2)}) collective-permute-start(f16[304,128]{1,0:T(8,128)(2,1)S(1)} %convert_element_type.53), channel_id=1, source_target_pairs={{8,20},{12,16},{16,12},{20,8},{9,21},{13,17},{17,13},{21,9},{10,22... | collective-permute-start | bytes 233480 | tf_op jit(solution)/shard_map/ppermute | solution.py:577
  14.1 11.8 %collective-permute-start.3 = (f16[304,128]{1,0:T(8,128)(2,1)S(1)}, f16[304,128]{1,0:T(8,128)(2,1)S(1)}, u32[]{:S(2)}, u32[]{:S(2)}) collective-permute-start(f16[304,128]{1,0:T(8,128)(2,1)S(1)} %convert_element_type.51), channel_id=1, source_target_pairs={{0,12},{4,8},{8,4},{12,0},{16,28},{20,24},{24,20},{28,16},{1,13},{... | collective-permute-start | bytes 233480 | tf_op jit(solution)/shard_map/ppermute | solution.py:577
  22.0 4.5 %collective-permute-start.2 = (f16[304,128]{1,0:T(8,128)(2,1)S(1)}, f16[304,128]{1,0:T(8,128)(2,1)S(1)}, u32[]{:S(2)}, u32[]{:S(2)}) collective-permute-start(f16[304,128]{1,0:T(8,128)(2,1)S(1)} %convert_element_type.49), channel_id=1, source_target_pairs={{0,4},{4,0},{8,12},{12,8},{16,20},{20,16},{24,28},{28,24},{1,5},{5... | collective-permute-start | bytes 233480 | tf_op jit(solution)/shard_map/ppermute | solution.py:577
  24.0 8.6 %copy-start = (bf16[4,256,256]{2,1,0:T(8,128)(2,1)S(1)}, bf16[4,256,256]{2,1,0:T(8,128)(2,1)}, u32[]{:S(2)}) copy-start(bf16[4,256,256]{2,1,0:T(8,128)(2,1)} %project.3) | copy-start | bytes 1572868
  24.0 8.6 %copy-start.1 = (bf16[12,48,256]{2,1,0:T(8,128)(2,1)S(1)}, bf16[12,48,256]{2,1,0:T(8,128)(2,1)}, u32[]{:S(2)}) copy-start(bf16[12,48,256]{2,1,0:T(8,128)(2,1)} %param.13) | copy-start | bytes 884740
  24.0 8.6 %copy-start.3 = (f32[256]{0:T(256)S(1)}, f32[256]{0:T(256)}, u32[]{:S(2)}) copy-start(f32[256]{0:T(256)} %param.12) | copy-start | bytes 3076
  24.3 6.8 %collective-permute-start.6 = (bf16[576,128]{1,0:T(8,128)(2,1)S(1)}, bf16[576,128]{1,0:T(8,128)(2,1)S(1)}, u32[]{:S(2)}, u32[]{:S(2)}) collective-permute-start(bf16[576,128]{1,0:T(8,128)(2,1)S(1)} %activations.2.a0), channel_id=1, source_target_pairs={{0,2},{1,3},{2,0},{3,1},{4,6},{5,7},{6,4},{7,5},{8,10},{9,11},{10,... | collective-permute-start | bytes 442376 | tf_op jit(solution)/shard_map/ppermute | solution.py:572
  26.7 5.9 %collective-permute-start.7 = (bf16[576,128]{1,0:T(8,128)(2,1)S(1)}, bf16[576,128]{1,0:T(8,128)(2,1)S(1)}, u32[]{:S(2)}, u32[]{:S(2)}) collective-permute-start(bf16[576,128]{1,0:T(8,128)(2,1)S(1)} %activations.3.b0), channel_id=1, source_target_pairs={{0,2},{1,3},{2,0},{3,1},{4,6},{5,7},{6,4},{7,5},{8,10},{9,11},{10,... | collective-permute-start | bytes 442376 | tf_op jit(solution)/shard_map/ppermute | solution.py:572
  28.3 4.4 %collective-permute-start.10 = (bf16[576,128]{1,0:T(8,128)(2,1)S(1)}, bf16[576,128]{1,0:T(8,128)(2,1)S(1)}, u32[]{:S(2)}, u32[]{:S(2)}) collective-permute-start(bf16[576,128]{1,0:T(8,128)(2,1)S(1)} %activations.2.a0), channel_id=1, source_target_pairs={{0,1},{1,0},{2,3},{3,2},{4,5},{5,4},{6,7},{7,6},{8,9},{9,8},{10,11... | collective-permute-start | bytes 442376 | tf_op jit(solution)/shard_map/ppermute | solution.py:572
  28.3 4.4 %collective-permute-start.11 = (bf16[576,128]{1,0:T(8,128)(2,1)S(1)}, bf16[576,128]{1,0:T(8,128)(2,1)S(1)}, u32[]{:S(2)}, u32[]{:S(2)}) collective-permute-start(bf16[576,128]{1,0:T(8,128)(2,1)S(1)} %activations.3.b0), channel_id=1, source_target_pairs={{0,1},{1,0},{2,3},{3,2},{4,5},{5,4},{6,7},{7,6},{8,9},{9,8},{10,11... | collective-permute-start | bytes 442376 | tf_op jit(solution)/shard_map/ppermute | solution.py:572
  31.0 2.0 %collective-permute-start.8 = (bf16[576,128]{1,0:T(8,128)(2,1)S(1)}, bf16[576,128]{1,0:T(8,128)(2,1)S(1)}, u32[]{:S(2)}, u32[]{:S(2)}) collective-permute-start(bf16[576,128]{1,0:T(8,128)(2,1)S(1)} %collective-permute-done.6.a2), channel_id=1, source_target_pairs={{0,1},{1,0},{2,3},{3,2},{4,5},{5,4},{6,7},{7,6},{8,9},{9,8},{10,11... | collective-permute-start | bytes 442376 | tf_op jit(solution)/shard_map/ppermute | solution.py:572
  32.6 1.4 %collective-permute-start.9 = (bf16[576,128]{1,0:T(8,128)(2,1)S(1)}, bf16[576,128]{1,0:T(8,128)(2,1)S(1)}, u32[]{:S(2)}, u32[]{:S(2)}) collective-permute-start(bf16[576,128]{1,0:T(8,128)(2,1)S(1)} %collective-permute-done.7.b2), channel_id=1, source_target_pairs={{0,1},{1,0},{2,3},{3,2},{4,5},{5,4},{6,7},{7,6},{8,9},{9,8},{10,11... | collective-permute-start | bytes 442376 | tf_op jit(solution)/shard_map/ppermute | solution.py:572
  34.6 10.6 %collective-permute-start.12 = (bf16[288,128]{1,0:T(8,128)(2,1)S(1)}, bf16[288,128]{1,0:T(8,128)(2,1)S(1)}, u32[]{:S(2)}, u32[]{:S(2)}) collective-permute-start(bf16[288,128]{1,0:T(8,128)(2,1)S(1)} %get-tuple-element.37), channel_id=1, source_target_pairs={{0,4},{4,0},{8,12},{12,8},{16,20},{20,16},{24,28},{28,24},{1,5},{5... | collective-permute-start | bytes 221192 | tf_op jit(solution)/shard_map/ppermute | solution.py:577
  35.9 12.6 %collective-permute-start.13 = (bf16[288,128]{1,0:T(8,128)(2,1)S(1)}, bf16[288,128]{1,0:T(8,128)(2,1)S(1)}, u32[]{:S(2)}, u32[]{:S(2)}) collective-permute-start(bf16[288,128]{1,0:T(8,128)(2,1)S(1)} %get-tuple-element.38), channel_id=1, source_target_pairs={{4,16},{12,24},{16,4},{24,12},{5,17},{13,25},{17,5},{25,13},{6,18}... | collective-permute-start | bytes 221192 | tf_op jit(solution)/shard_map/ppermute | solution.py:577
  36.5 11.9 %collective-permute-start.14 = (bf16[288,128]{1,0:T(8,128)(2,1)S(1)}, bf16[288,128]{1,0:T(8,128)(2,1)S(1)}, u32[]{:S(2)}, u32[]{:S(2)}) collective-permute-start(bf16[288,128]{1,0:T(8,128)(2,1)S(1)} %get-tuple-element.39), channel_id=1, source_target_pairs={{8,20},{12,16},{16,12},{20,8},{9,21},{13,17},{17,13},{21,9},{10,22... | collective-permute-start | bytes 221192 | tf_op jit(solution)/shard_map/ppermute | solution.py:577
  37.2 11.3 %collective-permute-start.15 = (bf16[288,128]{1,0:T(8,128)(2,1)S(1)}, bf16[288,128]{1,0:T(8,128)(2,1)S(1)}, u32[]{:S(2)}, u32[]{:S(2)}) collective-permute-start(bf16[288,128]{1,0:T(8,128)(2,1)S(1)} %get-tuple-element.40), channel_id=1, source_target_pairs={{0,12},{4,8},{8,4},{12,0},{16,28},{20,24},{24,20},{28,16},{1,13},{... | collective-permute-start | bytes 221192 | tf_op jit(solution)/shard_map/ppermute | solution.py:577
  44.4 4.0 %collective-permute-start.16 = (bf16[288,128]{1,0:T(8,128)(2,1)S(1)}, bf16[288,128]{1,0:T(8,128)(2,1)S(1)}, u32[]{:S(2)}, u32[]{:S(2)}) collective-permute-start(bf16[288,128]{1,0:T(8,128)(2,1)S(1)} %get-tuple-element.41), channel_id=1, source_target_pairs={{8,16},{12,20},{16,8},{20,12},{9,17},{13,21},{17,9},{21,13},{10,18... | collective-permute-start | bytes 221192 | tf_op jit(solution)/shard_map/ppermute | solution.py:577
  45.3 5.5 %collective-permute-start.17 = (bf16[288,128]{1,0:T(8,128)(2,1)S(1)}, bf16[288,128]{1,0:T(8,128)(2,1)S(1)}, u32[]{:S(2)}, u32[]{:S(2)}) collective-permute-start(bf16[288,128]{1,0:T(8,128)(2,1)S(1)} %get-tuple-element.42), channel_id=1, source_target_pairs={{0,8},{4,12},{8,0},{12,4},{16,24},{20,28},{24,16},{28,20},{1,9},{5... | collective-permute-start | bytes 221192 | tf_op jit(solution)/shard_map/ppermute | solution.py:577
  52.6 2.1 %collective-permute-start.18 = (bf16[576,512]{1,0:T(8,128)(2,1)S(1)}, bf16[576,512]{1,0:T(8,128)(2,1)S(1)}, u32[]{:S(2)}, u32[]{:S(2)}) collective-permute-start(bf16[576,512]{1,0:T(8,128)(2,1)S(1)} %grads_for.4), channel_id=1, source_target_pairs={{0,1},{1,0},{2,3},{3,2},{4,5},{5,4},{6,7},{7,6},{8,9},{9,8},{10,11... | collective-permute-start | bytes 1769480 | tf_op jit(solution)/shard_map/ppermute | solution.py:572
  54.8 15.4 %collective-permute-start.20 = (bf16[576,512]{1,0:T(8,128)(2,1)S(1)}, bf16[576,512]{1,0:T(8,128)(2,1)S(1)}, u32[]{:S(2)}, u32[]{:S(2)}) collective-permute-start(bf16[576,512]{1,0:T(8,128)(2,1)S(1)} %add_convert_fusion), channel_id=1, source_target_pairs={{0,2},{1,3},{2,0},{3,1},{4,6},{5,7},{6,4},{7,5},{8,10},{9,11},{10,... | collective-permute-start | bytes 1769480 | tf_op jit(solution)/shard_map/ppermute | solution.py:572
  58.9 2.1 %collective-permute-start.19 = (bf16[576,512]{1,0:T(8,128)(2,1)S(1)}, bf16[576,512]{1,0:T(8,128)(2,1)S(1)}, u32[]{:S(2)}, u32[]{:S(2)}) collective-permute-start(bf16[576,512]{1,0:T(8,128)(2,1)S(1)} %grads_for.7), channel_id=1, source_target_pairs={{0,1},{1,0},{2,3},{3,2},{4,5},{5,4},{6,7},{7,6},{8,9},{9,8},{10,11... | collective-permute-start | bytes 1769480 | tf_op jit(solution)/shard_map/ppermute | solution.py:572
where the time goes:
time: 71.8 us; the launch traced here: 71.5 us
  starting transfers between devices  32.5 us (45%)
  Pallas kernels  19.3 us (27%)
  waiting for transfers between devices  18.4 us (26%)
  between operations  0.98 us (1%)
    ppermute x12, starting transfers between devices, swapped(): return lax.ppermute(x, 'rows', pairs)  27 us
    ppermute x9, waiting for transfers between devices, flipped(): lax.ppermute(x, 'filt', [(i, i ^ bit) for i in range(lax.axis_size('filt'...  15.6 us
    pallas_call x1, Pallas kernels, outward_sums(): pl.pallas_call(outward_kernel, out_shape=[jax.ShapeDtypeStruct((SENT, 128...  8.23 us
    ppermute x9, starting transfers between devices, flipped(): lax.ppermute(x, 'filt', [(i, i ^ bit) for i in range(lax.axis_size('filt'...  5.43 us
    pallas_call x4, Pallas kernels, grads_for(): pl.pallas_call(functools.partial(grad_kernel, flips), out_shape=[jax.Shap...  4.96 us
    ppermute x12, waiting for transfers between devices, swapped(): return lax.ppermute(x, 'rows', pairs)  2.88 us
    pallas_call x1, Pallas kernels, own_sums(): pl.pallas_call(own_kernel, out_shape=[jax.ShapeDtypeStruct((PIXELS, 128),...  1.72 us
  transfers between devices with their start and end apart: 21, of which 8 were waited for; matrix products, arithmetic and copies ran while one was open for 0% of the time, Pallas kernels for 10%

commit v1 on v0

--- a/solution.py
+++ b/solution.py
@@ -155,7 +155,8 @@
 OUT_AT, LEFT_AT, RIGHT_AT = 4 * W, 22 * W, 25 * W
 PARTS = ((0, 2), (1, 3))
 SWAPS = (6, 2, 1, 3, 7, 5)
-GRAD_SWAPS = (1, 5, 7, 3, 6, 2)
+GRAD_SWAPS = (6, 7, 5)
+QUARTETS = ((0, 1, 2, 3), (4, 5, 6, 7))
 
 
 def fits(mesh):
@@ -419,7 +420,7 @@
 
 
 def far_head_kernel(a0, b0, a2, b2, a3, b3, project, near, cotangent, *refs):
-    output, grads, sends, packed = refs[0], refs[1], refs[2:8], refs[8]
+    output, grads, sends, quartet, packed = refs[0], refs[1], refs[2:5], refs[5], refs[6]
     row, member = lax.axis_index("rows"), lax.axis_index("filt")
     pre = near[...] + nn(both(a2, b2), project_rows(project, member ^ 2))
     pre = pre + nn(both(a3, b3), project_rows(project, member ^ 3))
@@ -437,15 +438,19 @@
     for n, x in enumerate(GRAD_SWAPS):
         apart = jnp.abs((row ^ x) - row)
         sends[n][...] = packed[jnp.where(apart <= 3, apart - 1, 0)]
+    for q in range(4):
+        apart = jnp.abs(q - (row & 3))
+        quartet[q] = packed[jnp.where(apart > 0, apart - 1, 0)]
 
 
 def far_head(own, across, corner, project, near, cotangent):
     return pl.pallas_call(
         far_head_kernel,
         out_shape=[jax.ShapeDtypeStruct((PIXELS, 256), BF16)] * 2
-        + [jax.ShapeDtypeStruct((HALF, 128), BF16)] * 6,
+        + [jax.ShapeDtypeStruct((HALF, 128), BF16)] * 3
+        + [jax.ShapeDtypeStruct((4, HALF, 128), BF16)],
         in_specs=[pl.BlockSpec(memory_space=pltpu.VMEM)] * 9,
-        out_specs=[pl.BlockSpec(memory_space=pltpu.VMEM)] * 8,
+        out_specs=[pl.BlockSpec(memory_space=pltpu.VMEM)] * 6,
         scratch_shapes=[pltpu.VMEM((3, HALF, 128), BF16)],
         compiler_params=pltpu.CompilerParams(vmem_limit_bytes=12 * 2**20),
         name="far_head",
@@ -476,9 +481,11 @@
 
 
 def spread_kernel(own, *refs):
-    recv, stack, arrivals, pairs, twice = refs[:6], refs[6], refs[7], refs[8], refs[9]
+    recv, quartet, stack, arrivals, pairs, twice = refs[:3], *refs[3:]
     row = lax.axis_index("rows")
     gather_arrivals(recv, arrivals, GRAD_SWAPS)
+    for x in (1, 2, 3):
+        arrivals[x] = quartet[(row & 3) ^ x]
     low = low_lanes((HALF, 128))
     low_all = low_lanes((PIXELS, 128))
     for k in (1, 2, 3):
@@ -511,11 +518,11 @@
             )
 
 
-def spread(own, received):
+def spread(own, received, quartet):
     return pl.pallas_call(
         spread_kernel,
         out_shape=pltpu.VMEM((PIXELS, 28 * W), BF16),
-        in_specs=[pl.BlockSpec(memory_space=pltpu.VMEM)] * 7,
+        in_specs=[pl.BlockSpec(memory_space=pltpu.VMEM)] * 5,
         out_specs=pl.BlockSpec(memory_space=pltpu.VMEM),
         scratch_shapes=[
             pltpu.VMEM((8, HALF, 128), BF16),
@@ -524,7 +531,7 @@
         ],
         compiler_params=pltpu.CompilerParams(vmem_limit_bytes=12 * 2**20),
         name="spread",
-    )(own, *received)
+    )(own, *received, quartet)
 
 
 def grad_kernel(flips, stack, weights, *outs):
@@ -605,11 +612,12 @@
         project_bias.reshape(1, 256),
         cotangent.reshape(PIXELS, 256),
     )
-    output, grads, *sends = far_head(
+    output, grads, *sends, quartet = far_head(
         acts, across, corner, project_weight, near, ordered_cotangent
     )
     arrived = [swapped(sends[n], x) for n, x in enumerate(GRAD_SWAPS)]
-    stack = spread(grads, arrived)
+    quartet = lax.all_to_all(quartet, "rows", 0, 0, axis_index_groups=QUARTETS)
+    stack = spread(grads, arrived, quartet)
     (far,) = grads_for((3,), stack, weights)
     far = flipped(far, 1)
     (kept,) = grads_for((2,), stack, weights)

time: 71.8 us -> 77.2 us (1.075)
  the two profiles are of different devices: /device:TPU:0 before, /device:TPU:10 now
where the time goes in v1:
time: 77.2 us; the launch traced here: 76.9 us
  starting transfers between devices  28.2 us (37%)
  waiting for transfers between devices  24.2 us (31%)
  Pallas kernels  20 us (26%)
  local copies, waits for them, and re-layouts  3.1 us (4%)
  between operations  0.99 us (1%)
    ppermute x9, starting transfers between devices, swapped(): return lax.ppermute(x, 'rows', pairs)  18.7 us
    ppermute x9, waiting for transfers between devices, flipped(): lax.ppermute(x, 'filt', [(i, i ^ bit) for i in range(lax.axis_size('filt'...  15.4 us
    ppermute x9, waiting for transfers between devices, swapped(): return lax.ppermute(x, 'rows', pairs)  8.82 us
    pallas_call x1, Pallas kernels, outward_sums(): pl.pallas_call(outward_kernel, out_shape=[jax.ShapeDtypeStruct((SENT, 128...  8.23 us
    ppermute x9, starting transfers between devices, flipped(): lax.ppermute(x, 'filt', [(i, i ^ bit) for i in range(lax.axis_size('filt'...  5.39 us
    pallas_call x4, Pallas kernels, grads_for(): pl.pallas_call(functools.partial(grad_kernel, flips), out_shape=[jax.Shap...  4.94 us
    all_to_all x1, starting transfers between devices, on_device(): quartet = lax.all_to_all(quartet, 'rows', 0, 0, axis_index_groups=QUARTETS)  4.19 us
    unnamed x12, local copies, waits for them, and re-layouts  3.1 us
  transfers between devices with their start and end apart: 19, of which 9 were waited for; matrix products, arithmetic and copies ran while one was open for 0% of the time, Pallas kernels for 10%

profile of v1, /device:TPU:10, one launch (start us, length us, event | category | flops | bytes accessed | tf_op | source)
XLA Modules:
  0.0 76.9 jit_solution(17711386726881514707)
XLA Ops:
  0.6 8.2 %outward_sums.1 = (f32[304,128]{1,0:T(8,128)S(1)}, f32[304,128]{1,0:T(8,128)S(1)}, f32[304,128]{1,0:T(8,128)S(1)}, f32[304,128]{1,0:T(8,128)S(1)}, f32[304,128]{...) custom-call(bf16[576,2048]{1,0:T(8,128)(2,1)} %bitcast.12, ...), custom_call_target="tpu_custom_call" | custom-call | tf_op jit(solution)/shard_map/outward_sums/pallas_call | solution.py:297
  9.4 4.6 %collective-permute-start = (f16[304,128]{1,0:T(8,128)(2,1)S(1)}, f16[304,128]{1,0:T(8,128)(2,1)S(1)}, u32[]{:S(2)}, u32[]{:S(2)}) collective-permute-start(f16[304,128]{1,0:T(8,128)(2,1)S(1)} %convert_element_type.45), channel_id=1, source_target_pairs={{8,16},{12,20},{16,8},{20,12},{9,17},{13,21},{17,9},{21,13},{10,18... | collective-permute-start | bytes 233480 | tf_op jit(solution)/shard_map/ppermute | solution.py:584
  14.1 1.9 %collective-permute-start.5 = (f16[304,128]{1,0:T(8,128)(2,1)S(1)}, f16[304,128]{1,0:T(8,128)(2,1)S(1)}, u32[]{:S(2)}, u32[]{:S(2)}) collective-permute-start(f16[304,128]{1,0:T(8,128)(2,1)S(1)} %convert_element_type.55), channel_id=1, source_target_pairs={{4,16},{12,24},{16,4},{24,12},{5,17},{13,25},{17,5},{25,13},{6,18}... | collective-permute-start | bytes 233480 | tf_op jit(solution)/shard_map/ppermute | solution.py:584
  16.0 1.9 %collective-permute-start.4 = (f16[304,128]{1,0:T(8,128)(2,1)S(1)}, f16[304,128]{1,0:T(8,128)(2,1)S(1)}, u32[]{:S(2)}, u32[]{:S(2)}) collective-permute-start(f16[304,128]{1,0:T(8,128)(2,1)S(1)} %convert_element_type.53), channel_id=1, source_target_pairs={{8,20},{12,16},{16,12},{20,8},{9,21},{13,17},{17,13},{21,9},{10,22... | collective-permute-start | bytes 233480 | tf_op jit(solution)/shard_map/ppermute | solution.py:584
  18.1 1.7 %collective-permute-start.2 = (f16[304,128]{1,0:T(8,128)(2,1)S(1)}, f16[304,128]{1,0:T(8,128)(2,1)S(1)}, u32[]{:S(2)}, u32[]{:S(2)}) collective-permute-start(f16[304,128]{1,0:T(8,128)(2,1)S(1)} %convert_element_type.49), channel_id=1, source_target_pairs={{0,4},{4,0},{8,12},{12,8},{16,20},{20,16},{24,28},{28,24},{1,5},{5... | collective-permute-start | bytes 233480 | tf_op jit(solution)/shard_map/ppermute | solution.py:584
  19.8 1.7 %own_sums.1 = (f32[576,128]{1,0:T(8,128)S(1)}, f32[576,128]{1,0:T(8,128)S(1)}) custom-call(bf16[576,2048]{1,0:T(8,128)(2,1)S(1)} %get-tuple-element.22.ordered, bf16[1792,2048]{1,0:T(8,128)(2,1)S(1)} %get-tuple-element.23.weights, f32[4,64]{1,0:T(4,128)S(1)} %copy-done.4), custom_call_target="tpu_custom_call" | custom-call | flops 1000000 | bytes 10000 | tf_op jit(solution)/shard_map/own_sums/pallas_call | solution.py:338
  21.8 1.6 %collective-permute-start.6 = (bf16[576,128]{1,0:T(8,128)(2,1)S(1)}, bf16[576,128]{1,0:T(8,128)(2,1)S(1)}, u32[]{:S(2)}, u32[]{:S(2)}) collective-permute-start(bf16[576,128]{1,0:T(8,128)(2,1)S(1)} %activations.2.a0), channel_id=1, source_target_pairs={{0,2},{1,3},{2,0},{3,1},{4,6},{5,7},{6,4},{7,5},{8,10},{9,11},{10,... | collective-permute-start | bytes 442376 | tf_op jit(solution)/shard_map/ppermute | solution.py:579
  23.4 1.5 %collective-permute-done.4 = f16[304,128]{1,0:T(8,128)(2,1)S(1)} collective-permute-done((f16[304,128]{1,0:T(8,128)(2,1)S(1)}, f16[304,128]{1,0:T(8,128)(2,1)S(1)}, u32[]{:S(2)}, u32[]{:S(2)}) %collective-permute-start.4) | collective-permute-done | bytes 77856 | tf_op jit(solution)/shard_map/ppermute | solution.py:584
  24.9 1.4 %collective-permute-done.2 = f16[304,128]{1,0:T(8,128)(2,1)S(1)} collective-permute-done((f16[304,128]{1,0:T(8,128)(2,1)S(1)}, f16[304,128]{1,0:T(8,128)(2,1)S(1)}, u32[]{:S(2)}, u32[]{:S(2)}) %collective-permute-start.2) | collective-permute-done | bytes 77856 | tf_op jit(solution)/shard_map/ppermute | solution.py:584
  26.5 1.6 %collective-permute-start.7 = (bf16[576,128]{1,0:T(8,128)(2,1)S(1)}, bf16[576,128]{1,0:T(8,128)(2,1)S(1)}, u32[]{:S(2)}, u32[]{:S(2)}) collective-permute-start(bf16[576,128]{1,0:T(8,128)(2,1)S(1)} %activations.3.b0), channel_id=1, source_target_pairs={{0,2},{1,3},{2,0},{3,1},{4,6},{5,7},{6,4},{7,5},{8,10},{9,11},{10,... | collective-permute-start | bytes 442376 | tf_op jit(solution)/shard_map/ppermute | solution.py:579
  28.1 0.5 collective-permute-start.11
  28.6 3.6 %collective-permute-done.7.b2 = bf16[576,128]{1,0:T(8,128)(2,1)S(1)} collective-permute-done((bf16[576,128]{1,0:T(8,128)(2,1)S(1)}, bf16[576,128]{1,0:T(8,128)(2,1)S(1)}, u32[]{:S(2)}, u32[]{:S(2)}) %collective-permute-start.7) | collective-permute-done | bytes 147488 | tf_op jit(solution)/shard_map/ppermute | solution.py:579
  32.7 0.9 %collective-permute-done.9.b3 = bf16[576,128]{1,0:T(8,128)(2,1)S(1)} collective-permute-done((bf16[576,128]{1,0:T(8,128)(2,1)S(1)}, bf16[576,128]{1,0:T(8,128)(2,1)S(1)}, u32[]{:S(2)}, u32[]{:S(2)}) %collective-permute-start.9) | collective-permute-done | bytes 147488 | tf_op jit(solution)/shard_map/ppermute | solution.py:579
  33.6 1.3 %far_head.1 = (bf16[576,256]{1,0:T(8,128)(2,1)S(1)}, bf16[576,256]{1,0:T(8,128)(2,1)S(1)}, bf16[288,128]{1,0:T(8,128)(2,1)S(1)}, bf16[288,128]{1,0:T(8,128)(2,1)...) custom-call(bf16[576,128]{1,0:T(8,128)(2,1)S(1)} %activations.2.a0, ...), custom_call_target="tpu_custom_call" | custom-call | tf_op jit(solution)/shard_map/far_head/pallas_call | solution.py:447
  34.9 4.2 %all-to-all-start = ((bf16[4,288,128]{2,1,0:T(8,128)(2,1)}), bf16[4,288,128]{2,1,0:T(8,128)(2,1)S(1)}, u32[]{:S(2)}, u32[]{:S(2)}) async-start(bf16[4,288,128]{2,1,0:T(8,128)(2,1)} %get-tuple-element.38), calls=%async_computation | async-start | bytes 589824 | tf_op jit(solution)/shard_map/all_to_all | solution.py:619
  39.1 2.5 %collective-permute-start.12 = (bf16[288,128]{1,0:T(8,128)(2,1)S(1)}, bf16[288,128]{1,0:T(8,128)(2,1)S(1)}, u32[]{:S(2)}, u32[]{:S(2)}) collective-permute-start(bf16[288,128]{1,0:T(8,128)(2,1)S(1)} %get-tuple-element.35), channel_id=1, source_target_pairs={{8,16},{12,20},{16,8},{20,12},{9,17},{13,21},{17,9},{21,13},{10,18... | collective-permute-start | bytes 221192 | tf_op jit(solution)/shard_map/ppermute | solution.py:584
  41.7 3.3 %collective-permute-start.13 = (bf16[288,128]{1,0:T(8,128)(2,1)S(1)}, bf16[288,128]{1,0:T(8,128)(2,1)S(1)}, u32[]{:S(2)}, u32[]{:S(2)}) collective-permute-start(bf16[288,128]{1,0:T(8,128)(2,1)S(1)} %get-tuple-element.36), channel_id=1, source_target_pairs={{8,20},{12,16},{16,12},{20,8},{9,21},{13,17},{17,13},{21,9},{10,22... | collective-permute-start | bytes 221192 | tf_op jit(solution)/shard_map/ppermute | solution.py:584
  45.0 2.1 %collective-permute-start.14 = (bf16[288,128]{1,0:T(8,128)(2,1)S(1)}, bf16[288,128]{1,0:T(8,128)(2,1)S(1)}, u32[]{:S(2)}, u32[]{:S(2)}) collective-permute-start(bf16[288,128]{1,0:T(8,128)(2,1)S(1)} %get-tuple-element.37), channel_id=1, source_target_pairs={{4,16},{12,24},{16,4},{24,12},{5,17},{13,25},{17,5},{25,13},{6,18}... | collective-permute-start | bytes 221192 | tf_op jit(solution)/shard_map/ppermute | solution.py:584
  47.1 2.0 %collective-permute-done.13.refs_1_ = bf16[288,128]{1,0:T(8,128)(2,1)S(1)} collective-permute-done((bf16[288,128]{1,0:T(8,128)(2,1)S(1)}, bf16[288,128]{1,0:T(8,128)(2,1)S(1)}, u32[]{:S(2)}, u32[]{:S(2)}) %collective-permute-start.13) | collective-permute-done | bytes 73760 | tf_op jit(solution)/shard_map/ppermute | solution.py:584
  49.1 3.9 %collective-permute-done.14.refs_2_ = bf16[288,128]{1,0:T(8,128)(2,1)S(1)} collective-permute-done((bf16[288,128]{1,0:T(8,128)(2,1)S(1)}, bf16[288,128]{1,0:T(8,128)(2,1)S(1)}, u32[]{:S(2)}, u32[]{:S(2)}) %collective-permute-start.14) | collective-permute-done | bytes 73760 | tf_op jit(solution)/shard_map/ppermute | solution.py:584
  53.0 0.6 spread.1.stack
  53.6 3.1 %copy-done.1 = bf16[1792,2048]{1,0:T(8,128)(2,1)S(1)} copy-done((bf16[1792,2048]{1,0:T(8,128)(2,1)S(1)}, bf16[1792,2048]{1,0:T(8,128)(2,1)}, u32[]{:S(2)}) %copy-start.1) | copy-done | bytes 7340056
  56.7 1.2 %grads_for.4 = bf16[576,512]{1,0:T(8,128)(2,1)S(1)} custom-call(bf16[576,1792]{1,0:T(8,128)(2,1)S(1)} %spread.1.stack, bf16[1792,2048]{1,0:T(8,128)(2,1)S(1)} %copy-done.1), custom_call_target="tpu_custom_call" | custom-call | flops 1056964608 | bytes 1000000 | tf_op jit(solution)/shard_map/grads_for/pallas_call | solution.py:545
  58.0 1.2 %grads_for.5 = bf16[576,512]{1,0:T(8,128)(2,1)S(1)} custom-call(bf16[576,1792]{1,0:T(8,128)(2,1)S(1)} %spread.1.stack, bf16[1792,2048]{1,0:T(8,128)(2,1)S(1)} %copy-done.1), custom_call_target="tpu_custom_call" | custom-call | flops 1056964608 | bytes 1000000 | tf_op jit(solution)/shard_map/grads_for/pallas_call | solution.py:545
  59.3 0.7 collective-permute-done.15
  60.2 1.6 %collective-permute-start.17 = (bf16[576,512]{1,0:T(8,128)(2,1)S(1)}, bf16[576,512]{1,0:T(8,128)(2,1)S(1)}, u32[]{:S(2)}, u32[]{:S(2)}) collective-permute-start(bf16[576,512]{1,0:T(8,128)(2,1)S(1)} %add_convert_fusion), channel_id=1, source_target_pairs={{0,2},{1,3},{2,0},{3,1},{4,6},{5,7},{6,4},{7,5},{8,10},{9,11},{10,... | collective-permute-start | bytes 1769480 | tf_op jit(solution)/shard_map/ppermute | solution.py:579
  61.7 1.2 %own_output.1 = bf16[576,64]{1,0:T(8,128)(2,1)} custom-call(bf16[576,256]{1,0:T(8,128)(2,1)S(1)} %get-tuple-element.40.output), custom_call_target="tpu_custom_call" | custom-call | tf_op jit(solution)/shard_map/own_output/pallas_call | solution.py:473
  62.9 1.2 %grads_for.7 = bf16[576,512]{1,0:T(8,128)(2,1)S(1)} custom-call(bf16[576,1792]{1,0:T(8,128)(2,1)S(1)} %spread.1.stack, bf16[1792,2048]{1,0:T(8,128)(2,1)S(1)} %copy-done.1), custom_call_target="tpu_custom_call" | custom-call | flops 1056964608 | bytes 1000000 | tf_op jit(solution)/shard_map/grads_for/pallas_call | solution.py:545
  64.3 1.2 %grads_for.6.a = bf16[576,512]{1,0:T(8,128)(2,1)S(1)} custom-call(bf16[576,1792]{1,0:T(8,128)(2,1)S(1)} %spread.1.stack, bf16[1792,2048]{1,0:T(8,128)(2,1)S(1)} %copy-done.1), custom_call_target="tpu_custom_call" | custom-call | flops 8455716864 | bytes 1000000 | tf_op jit(solution)/shard_map/grads_for/pallas_call | solution.py:545
  65.5 0.7 collective-permute-done.16.b
  66.3 9.3 %collective-permute-done.17.c = bf16[576,512]{1,0:T(8,128)(2,1)S(1)} collective-permute-done((bf16[576,512]{1,0:T(8,128)(2,1)S(1)}, bf16[576,512]{1,0:T(8,128)(2,1)S(1)}, u32[]{:S(2)}, u32[]{:S(2)}) %collective-permute-start.17) | collective-permute-done | bytes 589856 | tf_op jit(solution)/shard_map/ppermute | solution.py:579
  75.6 1.3 %last_sum.1 = bf16[576,512]{1,0:T(8,128)(2,1)} custom-call(bf16[576,512]{1,0:T(8,128)(2,1)S(1)} %grads_for.6.a, bf16[576,512]{1,0:T(8,128)(2,1)S(1)} %collective-permute-done.16.b, bf16[576,512]{1,0:T(8,128)(2,1)S(1)} %collective-permute-done.17.c), custom_call_target="tpu_custom_call" | custom-call | tf_op jit(solution)/shard_map/last_sum/pallas_call | solution.py:568
  (44 shorter events, 1.8 us)
Async XLA Ops:
  0.6 19.2 %copy-start.4 = (f32[4,64]{1,0:T(4,128)S(1)}, f32[4,64]{1,0:T(4,128)}, u32[]{:S(2)}) copy-start(f32[4,64]{1,0:T(4,128)} %bias.1) | copy-start | bytes 3076
  8.9 12.6 %copy-start = (bf16[1792,2048]{1,0:T(8,128)(2,1)}, bf16[1792,2048]{1,0:T(8,128)(2,1)S(1)}, u32[]{:S(2)}) copy-start(bf16[1792,2048]{1,0:T(8,128)(2,1)S(1)} %get-tuple-element.23.weights) | copy-start | bytes 22020100
  8.9 9.2 %collective-permute-start.1 = (f16[304,128]{1,0:T(8,128)(2,1)S(1)}, f16[304,128]{1,0:T(8,128)(2,1)S(1)}, u32[]{:S(2)}, u32[]{:S(2)}) collective-permute-start(f16[304,128]{1,0:T(8,128)(2,1)S(1)} %convert_element_type.47), channel_id=1, source_target_pairs={{0,8},{4,12},{8,0},{12,4},{16,24},{20,28},{24,16},{28,20},{1,9},{5... | collective-permute-start | bytes 233480 | tf_op jit(solution)/shard_map/ppermute | solution.py:584
  9.4 12.2 %collective-permute-start = (f16[304,128]{1,0:T(8,128)(2,1)S(1)}, f16[304,128]{1,0:T(8,128)(2,1)S(1)}, u32[]{:S(2)}, u32[]{:S(2)}) collective-permute-start(f16[304,128]{1,0:T(8,128)(2,1)S(1)} %convert_element_type.45), channel_id=1, source_target_pairs={{8,16},{12,20},{16,8},{20,12},{9,17},{13,21},{17,9},{21,13},{10,18... | collective-permute-start | bytes 233480 | tf_op jit(solution)/shard_map/ppermute | solution.py:584
  14.1 9.3 %collective-permute-start.5 = (f16[304,128]{1,0:T(8,128)(2,1)S(1)}, f16[304,128]{1,0:T(8,128)(2,1)S(1)}, u32[]{:S(2)}, u32[]{:S(2)}) collective-permute-start(f16[304,128]{1,0:T(8,128)(2,1)S(1)} %convert_element_type.55), channel_id=1, source_target_pairs={{4,16},{12,24},{16,4},{24,12},{5,17},{13,25},{17,5},{25,13},{6,18}... | collective-permute-start | bytes 233480 | tf_op jit(solution)/shard_map/ppermute | solution.py:584
  16.0 8.9 %collective-permute-start.4 = (f16[304,128]{1,0:T(8,128)(2,1)S(1)}, f16[304,128]{1,0:T(8,128)(2,1)S(1)}, u32[]{:S(2)}, u32[]{:S(2)}) collective-permute-start(f16[304,128]{1,0:T(8,128)(2,1)S(1)} %convert_element_type.53), channel_id=1, source_target_pairs={{8,20},{12,16},{16,12},{20,8},{9,21},{13,17},{17,13},{21,9},{10,22... | collective-permute-start | bytes 233480 | tf_op jit(solution)/shard_map/ppermute | solution.py:584
  18.0 6.9 %collective-permute-start.3 = (f16[304,128]{1,0:T(8,128)(2,1)S(1)}, f16[304,128]{1,0:T(8,128)(2,1)S(1)}, u32[]{:S(2)}, u32[]{:S(2)}) collective-permute-start(f16[304,128]{1,0:T(8,128)(2,1)S(1)} %convert_element_type.51), channel_id=1, source_target_pairs={{0,12},{4,8},{8,4},{12,0},{16,28},{20,24},{24,20},{28,16},{1,13},{... | collective-permute-start | bytes 233480 | tf_op jit(solution)/shard_map/ppermute | solution.py:584
  18.1 8.2 %collective-permute-start.2 = (f16[304,128]{1,0:T(8,128)(2,1)S(1)}, f16[304,128]{1,0:T(8,128)(2,1)S(1)}, u32[]{:S(2)}, u32[]{:S(2)}) collective-permute-start(f16[304,128]{1,0:T(8,128)(2,1)S(1)} %convert_element_type.49), channel_id=1, source_target_pairs={{0,4},{4,0},{8,12},{12,8},{16,20},{20,16},{24,28},{28,24},{1,5},{5... | collective-permute-start | bytes 233480 | tf_op jit(solution)/shard_map/ppermute | solution.py:584
  21.5 10.7 %copy-start.2 = (bf16[4,256,256]{2,1,0:T(8,128)(2,1)S(1)}, bf16[4,256,256]{2,1,0:T(8,128)(2,1)}, u32[]{:S(2)}) copy-start(bf16[4,256,256]{2,1,0:T(8,128)(2,1)} %project.3) | copy-start | bytes 1572868
  21.5 10.7 %copy-start.3 = (bf16[12,48,256]{2,1,0:T(8,128)(2,1)S(1)}, bf16[12,48,256]{2,1,0:T(8,128)(2,1)}, u32[]{:S(2)}) copy-start(bf16[12,48,256]{2,1,0:T(8,128)(2,1)} %param.13) | copy-start | bytes 884740
  21.6 10.7 %copy-start.5 = (f32[256]{0:T(256)S(1)}, f32[256]{0:T(256)}, u32[]{:S(2)}) copy-start(f32[256]{0:T(256)} %param.12) | copy-start | bytes 3076
  21.8 6.8 %collective-permute-start.6 = (bf16[576,128]{1,0:T(8,128)(2,1)S(1)}, bf16[576,128]{1,0:T(8,128)(2,1)S(1)}, u32[]{:S(2)}, u32[]{:S(2)}) collective-permute-start(bf16[576,128]{1,0:T(8,128)(2,1)S(1)} %activations.2.a0), channel_id=1, source_target_pairs={{0,2},{1,3},{2,0},{3,1},{4,6},{5,7},{6,4},{7,5},{8,10},{9,11},{10,... | collective-permute-start | bytes 442376 | tf_op jit(solution)/shard_map/ppermute | solution.py:579
  26.5 5.7 %collective-permute-start.7 = (bf16[576,128]{1,0:T(8,128)(2,1)S(1)}, bf16[576,128]{1,0:T(8,128)(2,1)S(1)}, u32[]{:S(2)}, u32[]{:S(2)}) collective-permute-start(bf16[576,128]{1,0:T(8,128)(2,1)S(1)} %activations.3.b0), channel_id=1, source_target_pairs={{0,2},{1,3},{2,0},{3,1},{4,6},{5,7},{6,4},{7,5},{8,10},{9,11},{10,... | collective-permute-start | bytes 442376 | tf_op jit(solution)/shard_map/ppermute | solution.py:579
  28.1 4.1 %collective-permute-start.10 = (bf16[576,128]{1,0:T(8,128)(2,1)S(1)}, bf16[576,128]{1,0:T(8,128)(2,1)S(1)}, u32[]{:S(2)}, u32[]{:S(2)}) collective-permute-start(bf16[576,128]{1,0:T(8,128)(2,1)S(1)} %activations.2.a0), channel_id=1, source_target_pairs={{0,1},{1,0},{2,3},{3,2},{4,5},{5,4},{6,7},{7,6},{8,9},{9,8},{10,11... | collective-permute-start | bytes 442376 | tf_op jit(solution)/shard_map/ppermute | solution.py:579
  28.1 4.1 %collective-permute-start.11 = (bf16[576,128]{1,0:T(8,128)(2,1)S(1)}, bf16[576,128]{1,0:T(8,128)(2,1)S(1)}, u32[]{:S(2)}, u32[]{:S(2)}) collective-permute-start(bf16[576,128]{1,0:T(8,128)(2,1)S(1)} %activations.3.b0), channel_id=1, source_target_pairs={{0,1},{1,0},{2,3},{3,2},{4,5},{5,4},{6,7},{7,6},{8,9},{9,8},{10,11... | collective-permute-start | bytes 442376 | tf_op jit(solution)/shard_map/ppermute | solution.py:579
  28.6 4.1 %collective-permute-start.8 = (bf16[576,128]{1,0:T(8,128)(2,1)S(1)}, bf16[576,128]{1,0:T(8,128)(2,1)S(1)}, u32[]{:S(2)}, u32[]{:S(2)}) collective-permute-start(bf16[576,128]{1,0:T(8,128)(2,1)S(1)} %collective-permute-done.6.a2), channel_id=1, source_target_pairs={{0,1},{1,0},{2,3},{3,2},{4,5},{5,4},{6,7},{7,6},{8,9},{9,8},{10,11... | collective-permute-start | bytes 442376 | tf_op jit(solution)/shard_map/ppermute | solution.py:579
  32.2 1.4 %collective-permute-start.9 = (bf16[576,128]{1,0:T(8,128)(2,1)S(1)}, bf16[576,128]{1,0:T(8,128)(2,1)S(1)}, u32[]{:S(2)}, u32[]{:S(2)}) collective-permute-start(bf16[576,128]{1,0:T(8,128)(2,1)S(1)} %collective-permute-done.7.b2), channel_id=1, source_target_pairs={{0,1},{1,0},{2,3},{3,2},{4,5},{5,4},{6,7},{7,6},{8,9},{9,8},{10,11... | collective-permute-start | bytes 442376 | tf_op jit(solution)/shard_map/ppermute | solution.py:579
  34.9 18.1 %all-to-all-start = ((bf16[4,288,128]{2,1,0:T(8,128)(2,1)}), bf16[4,288,128]{2,1,0:T(8,128)(2,1)S(1)}, u32[]{:S(2)}, u32[]{:S(2)}) async-start(bf16[4,288,128]{2,1,0:T(8,128)(2,1)} %get-tuple-element.38), calls=%async_computation | async-start | bytes 589824 | tf_op jit(solution)/shard_map/all_to_all | solution.py:619
  39.1 8.0 %collective-permute-start.12 = (bf16[288,128]{1,0:T(8,128)(2,1)S(1)}, bf16[288,128]{1,0:T(8,128)(2,1)S(1)}, u32[]{:S(2)}, u32[]{:S(2)}) collective-permute-start(bf16[288,128]{1,0:T(8,128)(2,1)S(1)} %get-tuple-element.35), channel_id=1, source_target_pairs={{8,16},{12,20},{16,8},{20,12},{9,17},{13,21},{17,9},{21,13},{10,18... | collective-permute-start | bytes 221192 | tf_op jit(solution)/shard_map/ppermute | solution.py:584
  41.7 7.5 %collective-permute-start.13 = (bf16[288,128]{1,0:T(8,128)(2,1)S(1)}, bf16[288,128]{1,0:T(8,128)(2,1)S(1)}, u32[]{:S(2)}, u32[]{:S(2)}) collective-permute-start(bf16[288,128]{1,0:T(8,128)(2,1)S(1)} %get-tuple-element.36), channel_id=1, source_target_pairs={{8,20},{12,16},{16,12},{20,8},{9,21},{13,17},{17,13},{21,9},{10,22... | collective-permute-start | bytes 221192 | tf_op jit(solution)/shard_map/ppermute | solution.py:584
  45.0 8.0 %collective-permute-start.14 = (bf16[288,128]{1,0:T(8,128)(2,1)S(1)}, bf16[288,128]{1,0:T(8,128)(2,1)S(1)}, u32[]{:S(2)}, u32[]{:S(2)}) collective-permute-start(bf16[288,128]{1,0:T(8,128)(2,1)S(1)} %get-tuple-element.37), channel_id=1, source_target_pairs={{4,16},{12,24},{16,4},{24,12},{5,17},{13,25},{17,5},{25,13},{6,18}... | collective-permute-start | bytes 221192 | tf_op jit(solution)/shard_map/ppermute | solution.py:584
  53.6 3.1 %copy-start.1 = (bf16[1792,2048]{1,0:T(8,128)(2,1)S(1)}, bf16[1792,2048]{1,0:T(8,128)(2,1)}, u32[]{:S(2)}) copy-start(bf16[1792,2048]{1,0:T(8,128)(2,1)} %copy-done) | copy-start | bytes 22020100
  57.9 2.1 %collective-permute-start.15 = (bf16[576,512]{1,0:T(8,128)(2,1)S(1)}, bf16[576,512]{1,0:T(8,128)(2,1)S(1)}, u32[]{:S(2)}, u32[]{:S(2)}) collective-permute-start(bf16[576,512]{1,0:T(8,128)(2,1)S(1)} %grads_for.4), channel_id=1, source_target_pairs={{0,1},{1,0},{2,3},{3,2},{4,5},{5,4},{6,7},{7,6},{8,9},{9,8},{10,11... | collective-permute-start | bytes 1769480 | tf_op jit(solution)/shard_map/ppermute | solution.py:579
  60.2 15.4 %collective-permute-start.17 = (bf16[576,512]{1,0:T(8,128)(2,1)S(1)}, bf16[576,512]{1,0:T(8,128)(2,1)S(1)}, u32[]{:S(2)}, u32[]{:S(2)}) collective-permute-start(bf16[576,512]{1,0:T(8,128)(2,1)S(1)} %add_convert_fusion), channel_id=1, source_target_pairs={{0,2},{1,3},{2,0},{3,1},{4,6},{5,7},{6,4},{7,5},{8,10},{9,11},{10,... | collective-permute-start | bytes 1769480 | tf_op jit(solution)/shard_map/ppermute | solution.py:579
  64.2 2.1 %collective-permute-start.16 = (bf16[576,512]{1,0:T(8,128)(2,1)S(1)}, bf16[576,512]{1,0:T(8,128)(2,1)S(1)}, u32[]{:S(2)}, u32[]{:S(2)}) collective-permute-start(bf16[576,512]{1,0:T(8,128)(2,1)S(1)} %grads_for.7), channel_id=1, source_target_pairs={{0,1},{1,0},{2,3},{3,2},{4,5},{5,4},{6,7},{7,6},{8,9},{9,8},{10,11... | collective-permute-start | bytes 1769480 | tf_op jit(solution)/shard_map/ppermute | solution.py:579

commit v2 on v0

--- a/solution.py
+++ b/solution.py
@@ -155,7 +155,7 @@
 OUT_AT, LEFT_AT, RIGHT_AT = 4 * W, 22 * W, 25 * W
 PARTS = ((0, 2), (1, 3))
 SWAPS = (6, 2, 1, 3, 7, 5)
-GRAD_SWAPS = (1, 5, 7, 3, 6, 2)
+GRAD_SWAPS = ((5, 7), (2, 6), (1, 3))
 
 
 def fits(mesh):
@@ -352,7 +352,7 @@
 def gather_arrivals(recv, arrivals, swaps):
     arrivals[0] = jnp.zeros((HALF, 128), arrivals.dtype)
     for n, x in enumerate(swaps):
-        arrivals[x] = recv[n][...] if recv[n].shape[0] == HALF else unscaled(recv[n][...])
+        arrivals[x] = unscaled(recv[n][...])
 
 
 def activation_kernel(part, swaps, own, *refs):
@@ -418,38 +418,40 @@
     )(*own, *beside, project, bias, cotangent)
 
 
-def far_head_kernel(a0, b0, a2, b2, a3, b3, project, near, cotangent, *refs):
-    output, grads, sends, packed = refs[0], refs[1], refs[2:8], refs[8]
+def far_head_kernel(a0, b0, a1, b1, a2, b2, a3, b3, project, near, cotangent, *refs):
+    output, grads, sends, packed = refs[0], refs[1], refs[2:5], refs[5]
     row, member = lax.axis_index("rows"), lax.axis_index("filt")
     pre = near[...] + nn(both(a2, b2), project_rows(project, member ^ 2))
     pre = pre + nn(both(a3, b3), project_rows(project, member ^ 3))
     output[...] = jnp.maximum(pre, 0.0).astype(BF16)
     head_grad = jnp.where(pre > 0, cotangent[...], 0.0).astype(BF16)
-    act_grad = nt(head_grad, project_rows(project, member))
-    a = jnp.where(a0[...].astype(F32) > 0, act_grad[:, :128], 0.0)
-    b = jnp.where(b0[...].astype(F32) > 0, act_grad[:, 128:], 0.0)
-    grads[:, :128] = a.astype(BF16)
-    grads[:, 128:] = b.astype(BF16)
     low = low_lanes((HALF, 128))
-    packed[0] = jnp.where(low, b[:HALF], pltpu.roll(b[HALF:], W, 1)).astype(BF16)
-    packed[1] = jnp.where(low, pltpu.roll(a[:HALF], W, 1), a[HALF:]).astype(BF16)
-    packed[2] = jnp.where(low, pltpu.roll(b[:HALF], W, 1), b[HALF:]).astype(BF16)
-    for n, x in enumerate(GRAD_SWAPS):
-        apart = jnp.abs((row ^ x) - row)
+    for who, (acts_a, acts_b) in enumerate(((a0, b0), (a1, b1))):
+        act_grad = nt(head_grad, project_rows(project, member ^ who))
+        a = jnp.where(acts_a[...].astype(F32) > 0, act_grad[:, :128], 0.0)
+        b = jnp.where(acts_b[...].astype(F32) > 0, act_grad[:, 128:], 0.0)
+        if who == 0:
+            grads[:, :128] = a.astype(BF16)
+            grads[:, 128:] = b.astype(BF16)
+        packed[0, who] = jnp.where(low, b[:HALF], pltpu.roll(b[HALF:], W, 1)).astype(BF16)
+        packed[1, who] = jnp.where(low, pltpu.roll(a[:HALF], W, 1), a[HALF:]).astype(BF16)
+        packed[2, who] = jnp.where(low, pltpu.roll(b[:HALF], W, 1), b[HALF:]).astype(BF16)
+    for n, swaps in enumerate(GRAD_SWAPS):
+        apart = jnp.abs((row ^ jnp.where((member & 1) == 0, *swaps)) - row)
         sends[n][...] = packed[jnp.where(apart <= 3, apart - 1, 0)]
 
 
-def far_head(own, across, corner, project, near, cotangent):
+def far_head(own, beside, across, corner, project, near, cotangent):
     return pl.pallas_call(
         far_head_kernel,
         out_shape=[jax.ShapeDtypeStruct((PIXELS, 256), BF16)] * 2
-        + [jax.ShapeDtypeStruct((HALF, 128), BF16)] * 6,
-        in_specs=[pl.BlockSpec(memory_space=pltpu.VMEM)] * 9,
-        out_specs=[pl.BlockSpec(memory_space=pltpu.VMEM)] * 8,
-        scratch_shapes=[pltpu.VMEM((3, HALF, 128), BF16)],
+        + [jax.ShapeDtypeStruct((2, HALF, 128), BF16)] * 3,
+        in_specs=[pl.BlockSpec(memory_space=pltpu.VMEM)] * 11,
+        out_specs=[pl.BlockSpec(memory_space=pltpu.VMEM)] * 5,
+        scratch_shapes=[pltpu.VMEM((3, 2, HALF, 128), BF16)],
         compiler_params=pltpu.CompilerParams(vmem_limit_bytes=12 * 2**20),
         name="far_head",
-    )(*own, *across, *corner, project, near, cotangent)
+    )(*own, *beside, *across, *corner, project, near, cotangent)
 
 
 def own_output_kernel(output, out):
@@ -476,9 +478,13 @@
 
 
 def spread_kernel(own, *refs):
-    recv, stack, arrivals, pairs, twice = refs[:6], refs[6], refs[7], refs[8], refs[9]
-    row = lax.axis_index("rows")
-    gather_arrivals(recv, arrivals, GRAD_SWAPS)
+    recv, handed, stack, arrivals, pairs, twice = refs[:3], refs[3:6], *refs[6:]
+    row, member = lax.axis_index("rows"), lax.axis_index("filt")
+    arrivals[0] = jnp.zeros((HALF, 128), BF16)
+    for n, (even, odd) in enumerate(GRAD_SWAPS):
+        first = (member & 1) == 0
+        arrivals[jnp.where(first, even, odd)] = recv[n][0]
+        arrivals[jnp.where(first, odd, even)] = handed[n][1]
     low = low_lanes((HALF, 128))
     low_all = low_lanes((PIXELS, 128))
     for k in (1, 2, 3):
@@ -511,7 +517,7 @@
             )
 
 
-def spread(own, received):
+def spread(own, received, handed):
     return pl.pallas_call(
         spread_kernel,
         out_shape=pltpu.VMEM((PIXELS, 28 * W), BF16),
@@ -524,7 +530,7 @@
         ],
         compiler_params=pltpu.CompilerParams(vmem_limit_bytes=12 * 2**20),
         name="spread",
-    )(own, *received)
+    )(own, *received, *handed)
 
 
 def grad_kernel(flips, stack, weights, *outs):
@@ -575,6 +581,16 @@
 def swapped(x, bits):
     pairs = [(r, r ^ bits) for r in range(8) if abs((r ^ bits) - r) <= 3]
     return lax.ppermute(x, "rows", pairs)
+
+
+def swapped_by_core(x, bits):
+    pairs = [
+        (4 * r + member, 4 * (r ^ bits[member % 2]) + member)
+        for r in range(8)
+        for member in range(4)
+        if abs((r ^ bits[member % 2]) - r) <= 3
+    ]
+    return lax.ppermute(x, ("rows", "filt"), pairs)
 
 
 def on_device(
@@ -606,10 +622,11 @@
         cotangent.reshape(PIXELS, 256),
     )
     output, grads, *sends = far_head(
-        acts, across, corner, project_weight, near, ordered_cotangent
-    )
-    arrived = [swapped(sends[n], x) for n, x in enumerate(GRAD_SWAPS)]
-    stack = spread(grads, arrived)
+        acts, beside, across, corner, project_weight, near, ordered_cotangent
+    )
+    arrived = [swapped_by_core(sends[n], swaps) for n, swaps in enumerate(GRAD_SWAPS)]
+    handed = [flipped(x, 1) for x in arrived]
+    stack = spread(grads, arrived, handed)
     (far,) = grads_for((3,), stack, weights)
     far = flipped(far, 1)
     (kept,) = grads_for((2,), stack, weights)

time: 71.8 us -> 70.2 us (0.978)
  starting transfers between devices: 32.5 us -> 29.2 us
  waiting for transfers between devices: 18.4 us -> 20 us
    ppermute x12 -> x6, starting transfers between devices: 27 us -> 13.2 us  [swapped(): return lax.ppermute(x, 'rows', pairs)]
    ppermute x0 -> x3, starting transfers between devices: none -> 9.88 us  [swapped_by_core(): return lax.ppermute(x, ('rows', 'filt'), pairs)]
    ppermute x0 -> x3, waiting for transfers between devices: none -> 2.61 us  [swapped_by_core(): return lax.ppermute(x, ('rows', 'filt'), pairs)]
    ppermute x12 -> x6, waiting for transfers between devices: 2.88 us -> 0.55 us  [swapped(): return lax.ppermute(x, 'rows', pairs)]
    ppermute x9 -> x12, waiting for transfers between devices: 15.6 us -> 16.8 us  [flipped(): lax.ppermute(x, 'filt', [(i, i ^ bit) for i in range(lax.axis_size('filt'...]
    ppermute x9 -> x12, starting transfers between devices: 5.43 us -> 6.04 us  [flipped(): lax.ppermute(x, 'filt', [(i, i ^ bit) for i in range(lax.axis_size('filt'...]
  transfers between devices with their start and end apart: 21 -> 21, of which waited for: 8 -> 9; matrix products, arithmetic and copies ran while one was open for 0% -> 0% of each run, Pallas kernels for 10% -> 11%
where the time goes in v2:
time: 70.2 us; the launch traced here: 70 us
  starting transfers between devices  29.2 us (42%)
  waiting for transfers between devices  20 us (28%)
  Pallas kernels  19.5 us (28%)
  between operations  0.96 us (1%)
    ppermute x12, waiting for transfers between devices, flipped(): lax.ppermute(x, 'filt', [(i, i ^ bit) for i in range(lax.axis_size('filt'...  16.8 us
    ppermute x6, starting transfers between devices, swapped(): return lax.ppermute(x, 'rows', pairs)  13.2 us
    ppermute x3, starting transfers between devices, swapped_by_core(): return lax.ppermute(x, ('rows', 'filt'), pairs)  9.88 us
    pallas_call x1, Pallas kernels, outward_sums(): pl.pallas_call(outward_kernel, out_shape=[jax.ShapeDtypeStruct((SENT, 128...  8.23 us
    ppermute x12, starting transfers between devices, flipped(): lax.ppermute(x, 'filt', [(i, i ^ bit) for i in range(lax.axis_size('filt'...  6.04 us
    pallas_call x4, Pallas kernels, grads_for(): pl.pallas_call(functools.partial(grad_kernel, flips), out_shape=[jax.Shap...  4.94 us
    ppermute x3, waiting for transfers between devices, swapped_by_core(): return lax.ppermute(x, ('rows', 'filt'), pairs)  2.61 us
    pallas_call x1, Pallas kernels, own_sums(): pl.pallas_call(own_kernel, out_shape=[jax.ShapeDtypeStruct((PIXELS, 128),...  1.72 us
  transfers between devices with their start and end apart: 21, of which 9 were waited for; matrix products, arithmetic and copies ran while one was open for 0% of the time, Pallas kernels for 11%

profile of v2, /device:TPU:0, one launch (start us, length us, event | category | flops | bytes accessed | tf_op | source)
XLA Modules:
  0.0 70.0 jit_solution(13860685548785806010)
XLA Ops:
  0.6 8.2 %outward_sums.1 = (f32[304,128]{1,0:T(8,128)S(1)}, f32[304,128]{1,0:T(8,128)S(1)}, f32[304,128]{1,0:T(8,128)S(1)}, f32[304,128]{1,0:T(8,128)S(1)}, f32[304,128]{...) custom-call(bf16[576,2048]{1,0:T(8,128)(2,1)} %bitcast.12, ...), custom_call_target="tpu_custom_call" | custom-call | tf_op jit(solution)/shard_map/outward_sums/pallas_call | solution.py:296
  8.9 3.1 %collective-permute-start.1 = (f16[304,128]{1,0:T(8,128)(2,1)S(1)}, f16[304,128]{1,0:T(8,128)(2,1)S(1)}, u32[]{:S(2)}, u32[]{:S(2)}) collective-permute-start(f16[304,128]{1,0:T(8,128)(2,1)S(1)} %convert_element_type.47), channel_id=1, source_target_pairs={{0,8},{4,12},{8,0},{12,4},{16,24},{20,28},{24,16},{28,20},{1,9},{5... | collective-permute-start | bytes 233480 | tf_op jit(solution)/shard_map/ppermute | solution.py:583
  12.0 0.7 collective-permute-start
  12.7 0.7 collective-permute-start.5
  13.4 0.7 collective-permute-start.4
  14.1 7.9 %collective-permute-start.3 = (f16[304,128]{1,0:T(8,128)(2,1)S(1)}, f16[304,128]{1,0:T(8,128)(2,1)S(1)}, u32[]{:S(2)}, u32[]{:S(2)}) collective-permute-start(f16[304,128]{1,0:T(8,128)(2,1)S(1)} %convert_element_type.51), channel_id=1, source_target_pairs={{0,12},{4,8},{8,4},{12,0},{16,28},{20,24},{24,20},{28,16},{1,13},{... | collective-permute-start | bytes 233480 | tf_op jit(solution)/shard_map/ppermute | solution.py:583
  22.3 1.7 %own_sums.1 = (f32[576,128]{1,0:T(8,128)S(1)}, f32[576,128]{1,0:T(8,128)S(1)}) custom-call(bf16[576,2048]{1,0:T(8,128)(2,1)S(1)} %get-tuple-element.21.ordered, bf16[1792,2048]{1,0:T(8,128)(2,1)S(1)} %get-tuple-element.22.weights, f32[4,64]{1,0:T(4,128)S(1)} %copy-done.2), custom_call_target="tpu_custom_call" | custom-call | flops 1000000 | bytes 10000 | tf_op jit(solution)/shard_map/own_sums/pallas_call | solution.py:337
  24.3 1.6 %collective-permute-start.8 = (bf16[576,128]{1,0:T(8,128)(2,1)S(1)}, bf16[576,128]{1,0:T(8,128)(2,1)S(1)}, u32[]{:S(2)}, u32[]{:S(2)}) collective-permute-start(bf16[576,128]{1,0:T(8,128)(2,1)S(1)} %activations.2.a0), channel_id=1, source_target_pairs={{0,2},{1,3},{2,0},{3,1},{4,6},{5,7},{6,4},{7,5},{8,10},{9,11},{10,... | collective-permute-start | bytes 442376 | tf_op jit(solution)/shard_map/ppermute | solution.py:578
  25.9 0.5 collective-permute-done.2
  26.7 1.6 %collective-permute-start.9 = (bf16[576,128]{1,0:T(8,128)(2,1)S(1)}, bf16[576,128]{1,0:T(8,128)(2,1)S(1)}, u32[]{:S(2)}, u32[]{:S(2)}) collective-permute-start(bf16[576,128]{1,0:T(8,128)(2,1)S(1)} %activations.3.b0), channel_id=1, source_target_pairs={{0,2},{1,3},{2,0},{3,1},{4,6},{5,7},{6,4},{7,5},{8,10},{9,11},{10,... | collective-permute-start | bytes 442376 | tf_op jit(solution)/shard_map/ppermute | solution.py:578
  28.3 0.5 collective-permute-start.7
  28.8 2.2 %collective-permute-done.8.a2 = bf16[576,128]{1,0:T(8,128)(2,1)S(1)} collective-permute-done((bf16[576,128]{1,0:T(8,128)(2,1)S(1)}, bf16[576,128]{1,0:T(8,128)(2,1)S(1)}, u32[]{:S(2)}, u32[]{:S(2)}) %collective-permute-start.8) | collective-permute-done | bytes 147488 | tf_op jit(solution)/shard_map/ppermute | solution.py:578
  31.0 1.6 %collective-permute-done.9.b2 = bf16[576,128]{1,0:T(8,128)(2,1)S(1)} collective-permute-done((bf16[576,128]{1,0:T(8,128)(2,1)S(1)}, bf16[576,128]{1,0:T(8,128)(2,1)S(1)}, u32[]{:S(2)}, u32[]{:S(2)}) %collective-permute-start.9) | collective-permute-done | bytes 147488 | tf_op jit(solution)/shard_map/ppermute | solution.py:578
  33.1 0.9 %collective-permute-done.11.b3 = bf16[576,128]{1,0:T(8,128)(2,1)S(1)} collective-permute-done((bf16[576,128]{1,0:T(8,128)(2,1)S(1)}, bf16[576,128]{1,0:T(8,128)(2,1)S(1)}, u32[]{:S(2)}, u32[]{:S(2)}) %collective-permute-start.11) | collective-permute-done | bytes 147488 | tf_op jit(solution)/shard_map/ppermute | solution.py:578
  34.0 0.8 %far_head.1 = (bf16[576,256]{1,0:T(8,128)(2,1)S(1)}, bf16[576,256]{1,0:T(8,128)(2,1)S(1)}, bf16[2,288,128]{2,1,0:T(8,128)(2,1)S(1)}, bf16[2,288,128]{2,1,0:T(8,128)(2,1)S(1)}, bf16[2,288,128]{2,1,0:T(8,128)(2,1)S(1)}) custom-call(bf16[576,128]{1,0:T(8,128)(2,1)S(1)} %activations.2.a0, bf16[576,128]{1,0:T(8,128)(2,1)S(1)} %activations.3.b0, ...), custom_call_target="tpu_custom_call" | custom-call | tf_op jit(solution)/shard_map/far_head/pallas_call | solution.py:445
  34.8 0.7 collective-permute-start.12
  35.5 3.7 %collective-permute-start.13 = (bf16[2,288,128]{2,1,0:T(8,128)(2,1)S(1)}, bf16[2,288,128]{2,1,0:T(8,128)(2,1)S(1)}, u32[]{:S(2)}, u32[]{:S(2)}) collective-permute-start(bf16[2,288,128]{2,1,0:T(8,128)(2,1)S(1)} %get-tuple-element.35), channel_id=1, source_target_pairs={{0,8},{2,10},{4,12},{6,14},{8,0},{9,17},{10,2},{11,19},{12,4},{13,... | collective-permute-start | bytes 442376 | tf_op jit(solution)/shard_map/ppermute | solution.py:593
  39.2 5.5 %collective-permute-start.14 = (bf16[2,288,128]{2,1,0:T(8,128)(2,1)S(1)}, bf16[2,288,128]{2,1,0:T(8,128)(2,1)S(1)}, u32[]{:S(2)}, u32[]{:S(2)}) collective-permute-start(bf16[2,288,128]{2,1,0:T(8,128)(2,1)S(1)} %get-tuple-element.36), channel_id=1, source_target_pairs={{0,4},{1,13},{2,6},{3,15},{4,0},{5,9},{6,2},{7,11},{8,12},{9,5},{1... | collective-permute-start | bytes 442376 | tf_op jit(solution)/shard_map/ppermute | solution.py:593
  44.7 0.5 collective-permute-start.16
  45.3 2.6 %collective-permute-done.14.refs_2_ = bf16[2,288,128]{2,1,0:T(8,128)(2,1)S(1)} collective-permute-done((bf16[2,288,128]{2,1,0:T(8,128)(2,1)S(1)}, bf16[2,288,128]{2,1,0:T(8,128)(2,1)S(1)}, u32[]{:S(2)}, u32[]{:S(2)}) %collective-permute-start.14) | collective-permute-done | bytes 147488 | tf_op jit(solution)/shard_map/ppermute | solution.py:593
  47.9 1.4 %collective-permute-done.17.refs_5_ = bf16[2,288,128]{2,1,0:T(8,128)(2,1)S(1)} collective-permute-done((bf16[2,288,128]{2,1,0:T(8,128)(2,1)S(1)}, bf16[2,288,128]{2,1,0:T(8,128)(2,1)S(1)}, u32[]{:S(2)}, u32[]{:S(2)}) %collective-permute-start.17) | collective-permute-done | bytes 147488 | tf_op jit(solution)/shard_map/ppermute | solution.py:578
  49.2 0.6 spread.1.stack
  49.8 1.2 %grads_for.4 = bf16[576,512]{1,0:T(8,128)(2,1)S(1)} custom-call(bf16[576,1792]{1,0:T(8,128)(2,1)S(1)} %spread.1.stack, bf16[1792,2048]{1,0:T(8,128)(2,1)S(1)} %get-tuple-element.22.weights), custom_call_target="tpu_custom_call" | custom-call | flops 1056964608 | bytes 1000000 | tf_op jit(solution)/shard_map/grads_for/pallas_call | solution.py:544
  51.3 1.2 %grads_for.5 = bf16[576,512]{1,0:T(8,128)(2,1)S(1)} custom-call(bf16[576,1792]{1,0:T(8,128)(2,1)S(1)} %spread.1.stack, bf16[1792,2048]{1,0:T(8,128)(2,1)S(1)} %get-tuple-element.22.weights), custom_call_target="tpu_custom_call" | custom-call | flops 1056964608 | bytes 1000000 | tf_op jit(solution)/shard_map/grads_for/pallas_call | solution.py:544
  52.5 0.6 collective-permute-done.18
  53.3 1.6 %collective-permute-start.20 = (bf16[576,512]{1,0:T(8,128)(2,1)S(1)}, bf16[576,512]{1,0:T(8,128)(2,1)S(1)}, u32[]{:S(2)}, u32[]{:S(2)}) collective-permute-start(bf16[576,512]{1,0:T(8,128)(2,1)S(1)} %add_convert_fusion), channel_id=1, source_target_pairs={{0,2},{1,3},{2,0},{3,1},{4,6},{5,7},{6,4},{7,5},{8,10},{9,11},{10,... | collective-permute-start | bytes 1769480 | tf_op jit(solution)/shard_map/ppermute | solution.py:578
  54.8 1.2 %own_output.1 = bf16[576,64]{1,0:T(8,128)(2,1)} custom-call(bf16[576,256]{1,0:T(8,128)(2,1)S(1)} %get-tuple-element.38.output), custom_call_target="tpu_custom_call" | custom-call | tf_op jit(solution)/shard_map/own_output/pallas_call | solution.py:470
  56.0 1.2 %grads_for.7 = bf16[576,512]{1,0:T(8,128)(2,1)S(1)} custom-call(bf16[576,1792]{1,0:T(8,128)(2,1)S(1)} %spread.1.stack, bf16[1792,2048]{1,0:T(8,128)(2,1)S(1)} %get-tuple-element.22.weights), custom_call_target="tpu_custom_call" | custom-call | flops 1056964608 | bytes 1000000 | tf_op jit(solution)/shard_map/grads_for/pallas_call | solution.py:544
  57.4 1.2 %grads_for.6.a = bf16[576,512]{1,0:T(8,128)(2,1)S(1)} custom-call(bf16[576,1792]{1,0:T(8,128)(2,1)S(1)} %spread.1.stack, bf16[1792,2048]{1,0:T(8,128)(2,1)S(1)} %get-tuple-element.22.weights), custom_call_target="tpu_custom_call" | custom-call | flops 8455716864 | bytes 1000000 | tf_op jit(solution)/shard_map/grads_for/pallas_call | solution.py:544
  58.6 0.7 %collective-permute-done.19.b = bf16[576,512]{1,0:T(8,128)(2,1)S(1)} collective-permute-done((bf16[576,512]{1,0:T(8,128)(2,1)S(1)}, bf16[576,512]{1,0:T(8,128)(2,1)S(1)}, u32[]{:S(2)}, u32[]{:S(2)}) %collective-permute-start.19) | collective-permute-done | bytes 589856 | tf_op jit(solution)/shard_map/ppermute | solution.py:578
  59.4 9.4 %collective-permute-done.20.c = bf16[576,512]{1,0:T(8,128)(2,1)S(1)} collective-permute-done((bf16[576,512]{1,0:T(8,128)(2,1)S(1)}, bf16[576,512]{1,0:T(8,128)(2,1)S(1)}, u32[]{:S(2)}, u32[]{:S(2)}) %collective-permute-start.20) | collective-permute-done | bytes 589856 | tf_op jit(solution)/shard_map/ppermute | solution.py:578
  68.7 1.3 %last_sum.1 = bf16[576,512]{1,0:T(8,128)(2,1)} custom-call(bf16[576,512]{1,0:T(8,128)(2,1)S(1)} %grads_for.6.a, bf16[576,512]{1,0:T(8,128)(2,1)S(1)} %collective-permute-done.19.b, bf16[576,512]{1,0:T(8,128)(2,1)S(1)} %collective-permute-done.20.c), custom_call_target="tpu_custom_call" | custom-call | tf_op jit(solution)/shard_map/last_sum/pallas_call | solution.py:567
  (44 shorter events, 1.7 us)
Async XLA Ops:
  0.6 21.7 %copy-start.2 = (f32[4,64]{1,0:T(4,128)S(1)}, f32[4,64]{1,0:T(4,128)}, u32[]{:S(2)}) copy-start(f32[4,64]{1,0:T(4,128)} %bias.1) | copy-start | bytes 3076
  8.9 13.1 %collective-permute-start.1 = (f16[304,128]{1,0:T(8,128)(2,1)S(1)}, f16[304,128]{1,0:T(8,128)(2,1)S(1)}, u32[]{:S(2)}, u32[]{:S(2)}) collective-permute-start(f16[304,128]{1,0:T(8,128)(2,1)S(1)} %convert_element_type.47), channel_id=1, source_target_pairs={{0,8},{4,12},{8,0},{12,4},{16,24},{20,28},{24,16},{28,20},{1,9},{5... | collective-permute-start | bytes 233480 | tf_op jit(solution)/shard_map/ppermute | solution.py:583
  12.0 12.1 %collective-permute-start = (f16[304,128]{1,0:T(8,128)(2,1)S(1)}, f16[304,128]{1,0:T(8,128)(2,1)S(1)}, u32[]{:S(2)}, u32[]{:S(2)}) collective-permute-start(f16[304,128]{1,0:T(8,128)(2,1)S(1)} %convert_element_type.45), channel_id=1, source_target_pairs={{8,16},{12,20},{16,8},{20,12},{9,17},{13,21},{17,9},{21,13},{10,18... | collective-permute-start | bytes 233480 | tf_op jit(solution)/shard_map/ppermute | solution.py:583
  12.7 13.2 %collective-permute-start.5 = (f16[304,128]{1,0:T(8,128)(2,1)S(1)}, f16[304,128]{1,0:T(8,128)(2,1)S(1)}, u32[]{:S(2)}, u32[]{:S(2)}) collective-permute-start(f16[304,128]{1,0:T(8,128)(2,1)S(1)} %convert_element_type.55), channel_id=1, source_target_pairs={{4,16},{12,24},{16,4},{24,12},{5,17},{13,25},{17,5},{25,13},{6,18}... | collective-permute-start | bytes 233480 | tf_op jit(solution)/shard_map/ppermute | solution.py:583
  13.4 12.5 %collective-permute-start.4 = (f16[304,128]{1,0:T(8,128)(2,1)S(1)}, f16[304,128]{1,0:T(8,128)(2,1)S(1)}, u32[]{:S(2)}, u32[]{:S(2)}) collective-permute-start(f16[304,128]{1,0:T(8,128)(2,1)S(1)} %convert_element_type.53), channel_id=1, source_target_pairs={{8,20},{12,16},{16,12},{20,8},{9,21},{13,17},{17,13},{21,9},{10,22... | collective-permute-start | bytes 233480 | tf_op jit(solution)/shard_map/ppermute | solution.py:583
  14.1 11.8 %collective-permute-start.3 = (f16[304,128]{1,0:T(8,128)(2,1)S(1)}, f16[304,128]{1,0:T(8,128)(2,1)S(1)}, u32[]{:S(2)}, u32[]{:S(2)}) collective-permute-start(f16[304,128]{1,0:T(8,128)(2,1)S(1)} %convert_element_type.51), channel_id=1, source_target_pairs={{0,12},{4,8},{8,4},{12,0},{16,28},{20,24},{24,20},{28,16},{1,13},{... | collective-permute-start | bytes 233480 | tf_op jit(solution)/shard_map/ppermute | solution.py:583
  22.0 4.5 %collective-permute-start.2 = (f16[304,128]{1,0:T(8,128)(2,1)S(1)}, f16[304,128]{1,0:T(8,128)(2,1)S(1)}, u32[]{:S(2)}, u32[]{:S(2)}) collective-permute-start(f16[304,128]{1,0:T(8,128)(2,1)S(1)} %convert_element_type.49), channel_id=1, source_target_pairs={{0,4},{4,0},{8,12},{12,8},{16,20},{20,16},{24,28},{28,24},{1,5},{5... | collective-permute-start | bytes 233480 | tf_op jit(solution)/shard_map/ppermute | solution.py:583
  24.0 8.6 %copy-start = (bf16[4,256,256]{2,1,0:T(8,128)(2,1)S(1)}, bf16[4,256,256]{2,1,0:T(8,128)(2,1)}, u32[]{:S(2)}) copy-start(bf16[4,256,256]{2,1,0:T(8,128)(2,1)} %project.3) | copy-start | bytes 1572868
  24.0 8.6 %copy-start.1 = (bf16[12,48,256]{2,1,0:T(8,128)(2,1)S(1)}, bf16[12,48,256]{2,1,0:T(8,128)(2,1)}, u32[]{:S(2)}) copy-start(bf16[12,48,256]{2,1,0:T(8,128)(2,1)} %param.13) | copy-start | bytes 884740
  24.0 8.6 %copy-start.3 = (f32[256]{0:T(256)S(1)}, f32[256]{0:T(256)}, u32[]{:S(2)}) copy-start(f32[256]{0:T(256)} %param.12) | copy-start | bytes 3076
  24.3 6.8 %collective-permute-start.8 = (bf16[576,128]{1,0:T(8,128)(2,1)S(1)}, bf16[576,128]{1,0:T(8,128)(2,1)S(1)}, u32[]{:S(2)}, u32[]{:S(2)}) collective-permute-start(bf16[576,128]{1,0:T(8,128)(2,1)S(1)} %activations.2.a0), channel_id=1, source_target_pairs={{0,2},{1,3},{2,0},{3,1},{4,6},{5,7},{6,4},{7,5},{8,10},{9,11},{10,... | collective-permute-start | bytes 442376 | tf_op jit(solution)/shard_map/ppermute | solution.py:578
  26.7 5.9 %collective-permute-start.9 = (bf16[576,128]{1,0:T(8,128)(2,1)S(1)}, bf16[576,128]{1,0:T(8,128)(2,1)S(1)}, u32[]{:S(2)}, u32[]{:S(2)}) collective-permute-start(bf16[576,128]{1,0:T(8,128)(2,1)S(1)} %activations.3.b0), channel_id=1, source_target_pairs={{0,2},{1,3},{2,0},{3,1},{4,6},{5,7},{6,4},{7,5},{8,10},{9,11},{10,... | collective-permute-start | bytes 442376 | tf_op jit(solution)/shard_map/ppermute | solution.py:578
  28.3 4.4 %collective-permute-start.6 = (bf16[576,128]{1,0:T(8,128)(2,1)S(1)}, bf16[576,128]{1,0:T(8,128)(2,1)S(1)}, u32[]{:S(2)}, u32[]{:S(2)}) collective-permute-start(bf16[576,128]{1,0:T(8,128)(2,1)S(1)} %activations.2.a0), channel_id=1, source_target_pairs={{0,1},{1,0},{2,3},{3,2},{4,5},{5,4},{6,7},{7,6},{8,9},{9,8},{10,11... | collective-permute-start | bytes 442376 | tf_op jit(solution)/shard_map/ppermute | solution.py:578
  28.3 4.4 %collective-permute-start.7 = (bf16[576,128]{1,0:T(8,128)(2,1)S(1)}, bf16[576,128]{1,0:T(8,128)(2,1)S(1)}, u32[]{:S(2)}, u32[]{:S(2)}) collective-permute-start(bf16[576,128]{1,0:T(8,128)(2,1)S(1)} %activations.3.b0), channel_id=1, source_target_pairs={{0,1},{1,0},{2,3},{3,2},{4,5},{5,4},{6,7},{7,6},{8,9},{9,8},{10,11... | collective-permute-start | bytes 442376 | tf_op jit(solution)/shard_map/ppermute | solution.py:578
  31.0 2.0 %collective-permute-start.10 = (bf16[576,128]{1,0:T(8,128)(2,1)S(1)}, bf16[576,128]{1,0:T(8,128)(2,1)S(1)}, u32[]{:S(2)}, u32[]{:S(2)}) collective-permute-start(bf16[576,128]{1,0:T(8,128)(2,1)S(1)} %collective-permute-done.8.a2), channel_id=1, source_target_pairs={{0,1},{1,0},{2,3},{3,2},{4,5},{5,4},{6,7},{7,6},{8,9},{9,8},{10,11... | collective-permute-start | bytes 442376 | tf_op jit(solution)/shard_map/ppermute | solution.py:578
  32.6 1.4 %collective-permute-start.11 = (bf16[576,128]{1,0:T(8,128)(2,1)S(1)}, bf16[576,128]{1,0:T(8,128)(2,1)S(1)}, u32[]{:S(2)}, u32[]{:S(2)}) collective-permute-start(bf16[576,128]{1,0:T(8,128)(2,1)S(1)} %collective-permute-done.9.b2), channel_id=1, source_target_pairs={{0,1},{1,0},{2,3},{3,2},{4,5},{5,4},{6,7},{7,6},{8,9},{9,8},{10,11... | collective-permute-start | bytes 442376 | tf_op jit(solution)/shard_map/ppermute | solution.py:578
  34.8 9.9 %collective-permute-start.12 = (bf16[2,288,128]{2,1,0:T(8,128)(2,1)S(1)}, bf16[2,288,128]{2,1,0:T(8,128)(2,1)S(1)}, u32[]{:S(2)}, u32[]{:S(2)}) collective-permute-start(bf16[2,288,128]{2,1,0:T(8,128)(2,1)S(1)} %get-tuple-element.34), channel_id=1, source_target_pairs={{4,16},{6,18},{9,21},{11,23},{12,24},{13,17},{14,26},{15,19},{16,4... | collective-permute-start | bytes 442376 | tf_op jit(solution)/shard_map/ppermute | solution.py:593
  35.5 9.2 %collective-permute-start.13 = (bf16[2,288,128]{2,1,0:T(8,128)(2,1)S(1)}, bf16[2,288,128]{2,1,0:T(8,128)(2,1)S(1)}, u32[]{:S(2)}, u32[]{:S(2)}) collective-permute-start(bf16[2,288,128]{2,1,0:T(8,128)(2,1)S(1)} %get-tuple-element.35), channel_id=1, source_target_pairs={{0,8},{2,10},{4,12},{6,14},{8,0},{9,17},{10,2},{11,19},{12,4},{13,... | collective-permute-start | bytes 442376 | tf_op jit(solution)/shard_map/ppermute | solution.py:593
  39.2 8.6 %collective-permute-start.14 = (bf16[2,288,128]{2,1,0:T(8,128)(2,1)S(1)}, bf16[2,288,128]{2,1,0:T(8,128)(2,1)S(1)}, u32[]{:S(2)}, u32[]{:S(2)}) collective-permute-start(bf16[2,288,128]{2,1,0:T(8,128)(2,1)S(1)} %get-tuple-element.36), channel_id=1, source_target_pairs={{0,4},{1,13},{2,6},{3,15},{4,0},{5,9},{6,2},{7,11},{8,12},{9,5},{1... | collective-permute-start | bytes 442376 | tf_op jit(solution)/shard_map/ppermute | solution.py:593
  44.7 3.1 %collective-permute-start.15 = (bf16[2,288,128]{2,1,0:T(8,128)(2,1)S(1)}, bf16[2,288,128]{2,1,0:T(8,128)(2,1)S(1)}, u32[]{:S(2)}, u32[]{:S(2)}) collective-permute-start(bf16[2,288,128]{2,1,0:T(8,128)(2,1)S(1)} %collective-permute-done.12.refs_0_), channel_id=1, source_target_pairs={{0,1},{1,0},{2,3},{3,2},{4,5},{5,4},{6,7},{7,6},{8,9},{9,8},{10,11... | collective-permute-start | bytes 442376 | tf_op jit(solution)/shard_map/ppermute | solution.py:578
  44.7 3.1 %collective-permute-start.16 = (bf16[2,288,128]{2,1,0:T(8,128)(2,1)S(1)}, bf16[2,288,128]{2,1,0:T(8,128)(2,1)S(1)}, u32[]{:S(2)}, u32[]{:S(2)}) collective-permute-start(bf16[2,288,128]{2,1,0:T(8,128)(2,1)S(1)} %collective-permute-done.13.refs_1_), channel_id=1, source_target_pairs={{0,1},{1,0},{2,3},{3,2},{4,5},{5,4},{6,7},{7,6},{8,9},{9,8},{10,11... | collective-permute-start | bytes 442376 | tf_op jit(solution)/shard_map/ppermute | solution.py:578
  47.9 1.4 %collective-permute-start.17 = (bf16[2,288,128]{2,1,0:T(8,128)(2,1)S(1)}, bf16[2,288,128]{2,1,0:T(8,128)(2,1)S(1)}, u32[]{:S(2)}, u32[]{:S(2)}) collective-permute-start(bf16[2,288,128]{2,1,0:T(8,128)(2,1)S(1)} %collective-permute-done.14.refs_2_), channel_id=1, source_target_pairs={{0,1},{1,0},{2,3},{3,2},{4,5},{5,4},{6,7},{7,6},{8,9},{9,8},{10,11... | collective-permute-start | bytes 442376 | tf_op jit(solution)/shard_map/ppermute | solution.py:578
  51.1 2.1 %collective-permute-start.18 = (bf16[576,512]{1,0:T(8,128)(2,1)S(1)}, bf16[576,512]{1,0:T(8,128)(2,1)S(1)}, u32[]{:S(2)}, u32[]{:S(2)}) collective-permute-start(bf16[576,512]{1,0:T(8,128)(2,1)S(1)} %grads_for.4), channel_id=1, source_target_pairs={{0,1},{1,0},{2,3},{3,2},{4,5},{5,4},{6,7},{7,6},{8,9},{9,8},{10,11... | collective-permute-start | bytes 1769480 | tf_op jit(solution)/shard_map/ppermute | solution.py:578
  53.3 15.4 %collective-permute-start.20 = (bf16[576,512]{1,0:T(8,128)(2,1)S(1)}, bf16[576,512]{1,0:T(8,128)(2,1)S(1)}, u32[]{:S(2)}, u32[]{:S(2)}) collective-permute-start(bf16[576,512]{1,0:T(8,128)(2,1)S(1)} %add_convert_fusion), channel_id=1, source_target_pairs={{0,2},{1,3},{2,0},{3,1},{4,6},{5,7},{6,4},{7,5},{8,10},{9,11},{10,... | collective-permute-start | bytes 1769480 | tf_op jit(solution)/shard_map/ppermute | solution.py:578
  57.3 2.1 %collective-permute-start.19 = (bf16[576,512]{1,0:T(8,128)(2,1)S(1)}, bf16[576,512]{1,0:T(8,128)(2,1)S(1)}, u32[]{:S(2)}, u32[]{:S(2)}) collective-permute-start(bf16[576,512]{1,0:T(8,128)(2,1)S(1)} %grads_for.7), channel_id=1, source_target_pairs={{0,1},{1,0},{2,3},{3,2},{4,5},{5,4},{6,7},{7,6},{8,9},{9,8},{10,11... | collective-permute-start | bytes 1769480 | tf_op jit(solution)/shard_map/ppermute | solution.py:578

commit v3 on v2

--- a/solution.py
+++ b/solution.py
@@ -148,14 +148,15 @@
 
 OUT_PAIRS = ((3, 1), (1, 1), (3, 0), (1, 0), (3, 2), (1, 2), (2, 1), (2, 0), (2, 2))
 TAPS = (
-    [(k, 1, 1) for k in (2, 1, 3)]
+    [(k, 1, 1) for k in (1, 2, 3)]
     + [(k, i, j) for k, j in OUT_PAIRS for i in (0, 2)]
-    + [(k, 1, j) for j in (0, 2) for k in (2, 1, 3)]
+    + [(k, 1, j) for j in (0, 2) for k in (1, 2, 3)]
 )
 OUT_AT, LEFT_AT, RIGHT_AT = 4 * W, 22 * W, 25 * W
-PARTS = ((0, 2), (1, 3))
-SWAPS = (6, 2, 1, 3, 7, 5)
-GRAD_SWAPS = ((5, 7), (2, 6), (1, 3))
+PARTS = ((0, 1), (2, 3))
+PART_SWAPS = ((7, 3, 1), (6, 2, 5, 7, 3))
+SWAPS = (1, 3, 7, 5, 2, 6)
+GRAD_SWAPS = ((1, 3), (5, 7), (2, 6))
 
 
 def fits(mesh):
@@ -319,10 +320,10 @@
     low = low_lanes((PIXELS, 128))
 
     def add(first, value, k):
-        part = k % 2
+        part = k // 2
         rows = slice(first * BLOCK, first * BLOCK + value.shape[0])
         mask, value = low[: value.shape[0]], value[:, part * 128 : part * 128 + 128]
-        kept = jnp.where(mask, value, 0.0) if k == 1 else jnp.where(mask, 0.0, value)
+        kept = jnp.where(mask, value, 0.0) if k == 2 else jnp.where(mask, 0.0, value)
         outs[part][rows, :] = outs[part][rows, :] + kept
 
     d = nt(ordered[: 3 * BLOCK, :], weights[LEFT_AT - W : LEFT_AT + 3 * W, :])
@@ -433,8 +434,8 @@
         if who == 0:
             grads[:, :128] = a.astype(BF16)
             grads[:, 128:] = b.astype(BF16)
-        packed[0, who] = jnp.where(low, b[:HALF], pltpu.roll(b[HALF:], W, 1)).astype(BF16)
-        packed[1, who] = jnp.where(low, pltpu.roll(a[:HALF], W, 1), a[HALF:]).astype(BF16)
+        packed[0, who] = jnp.where(low, pltpu.roll(a[:HALF], W, 1), a[HALF:]).astype(BF16)
+        packed[1, who] = jnp.where(low, b[:HALF], pltpu.roll(b[HALF:], W, 1)).astype(BF16)
         packed[2, who] = jnp.where(low, pltpu.roll(b[:HALF], W, 1), b[HALF:]).astype(BF16)
     for n, swaps in enumerate(GRAD_SWAPS):
         apart = jnp.abs((row ^ jnp.where((member & 1) == 0, *swaps)) - row)
@@ -492,9 +493,9 @@
         m = arrivals[arrival_slot(row, row - k)].astype(F32)
         pairs[k - 1, :HALF, :] = jnp.where(low, p, pltpu.roll(m, W, 1)).astype(BF16)
         pairs[k - 1, HALF:, :] = jnp.where(low, pltpu.roll(p, W, 1), m).astype(BF16)
-        g = own[:, :128].astype(F32) if k == 2 else own[:, 128:].astype(F32)
+        g = own[:, :128].astype(F32) if k == 1 else own[:, 128:].astype(F32)
         other = pltpu.roll(g, W, 1)
-        two = jnp.where(low_all, g, other) if k == 1 else jnp.where(low_all, other, g)
+        two = jnp.where(low_all, g, other) if k == 2 else jnp.where(low_all, other, g)
         twice[k - 1] = two.astype(BF16)
     stack[:, : 4 * W] = own[...]
     nothing = jnp.zeros((BLOCK, 128), BF16)
@@ -509,7 +510,7 @@
         for m in range(4):
             stack[m * BLOCK : (m + 1) * BLOCK, lanes] = block_of(pairs, k, m - (j - 1) * k)
     low_block = low_lanes((BLOCK, 128))
-    for q, (a, b) in enumerate(((2, 1), (3, -2), (-1, -3))):
+    for q, (a, b) in enumerate(((1, 2), (3, -1), (-2, -3))):
         lanes = slice(LEFT_AT + q * 128, LEFT_AT + q * 128 + 128)
         for m in range(4):
             stack[m * BLOCK : (m + 1) * BLOCK, lanes] = jnp.where(
@@ -609,7 +610,7 @@
     own = own_sums(ordered, weights, branch_bias)
     acts = [
         activations_of(part, swaps, own[part], [received[x] for x in swaps])
-        for part, swaps in ((0, SWAPS[:2]), (1, SWAPS[2:]))
+        for part, swaps in enumerate(PART_SWAPS)
     ]
     across = [flipped(x, 2) for x in acts]
     beside = [flipped(x, 1) for x in acts]

time: 70.2 us -> 68.5 us (0.976)
  starting transfers between devices: 29.2 us -> 25.3 us
  waiting for transfers between devices: 20 us -> 21.5 us
    ppermute x3, starting transfers between devices: 9.88 us -> 8.24 us  [swapped_by_core(): return lax.ppermute(x, ('rows', 'filt'), pairs)]
    ppermute x6, starting transfers between devices: 13.2 us -> 12 us  [swapped(): return lax.ppermute(x, 'rows', pairs)]
    ppermute x3, waiting for transfers between devices: 2.61 us -> 3.69 us  [swapped_by_core(): return lax.ppermute(x, ('rows', 'filt'), pairs)]
    ppermute x12, starting transfers between devices: 6.04 us -> 5.08 us  [flipped(): lax.ppermute(x, 'filt', [(i, i ^ bit) for i in range(lax.axis_size('filt'...]
    ppermute x12, waiting for transfers between devices: 16.8 us -> 17.7 us  [flipped(): lax.ppermute(x, 'filt', [(i, i ^ bit) for i in range(lax.axis_size('filt'...]
  transfers between devices with their start and end apart: 21 -> 21, of which waited for: 9 -> 8; matrix products, arithmetic and copies ran while one was open for 0% -> 0% of each run, Pallas kernels for 11% -> 11%
where the time goes in v3:
time: 68.5 us; the launch traced here: 67.6 us
  starting transfers between devices  25.3 us (37%)
  waiting for transfers between devices  21.5 us (31%)
  Pallas kernels  19.5 us (28%)
  between operations  0.99 us (1%)
    ppermute x12, waiting for transfers between devices, flipped(): lax.ppermute(x, 'filt', [(i, i ^ bit) for i in range(lax.axis_size('filt'...  17.7 us
    ppermute x6, starting transfers between devices, swapped(): return lax.ppermute(x, 'rows', pairs)  12 us
    ppermute x3, starting transfers between devices, swapped_by_core(): return lax.ppermute(x, ('rows', 'filt'), pairs)  8.24 us
    pallas_call x1, Pallas kernels, outward_sums(): pl.pallas_call(outward_kernel, out_shape=[jax.ShapeDtypeStruct((SENT, 128...  8.23 us
    ppermute x12, starting transfers between devices, flipped(): lax.ppermute(x, 'filt', [(i, i ^ bit) for i in range(lax.axis_size('filt'...  5.08 us
    pallas_call x4, Pallas kernels, grads_for(): pl.pallas_call(functools.partial(grad_kernel, flips), out_shape=[jax.Shap...  4.94 us
    ppermute x3, waiting for transfers between devices, swapped_by_core(): return lax.ppermute(x, ('rows', 'filt'), pairs)  3.69 us
    pallas_call x1, Pallas kernels, own_sums(): pl.pallas_call(own_kernel, out_shape=[jax.ShapeDtypeStruct((PIXELS, 128),...  1.73 us
  transfers between devices with their start and end apart: 21, of which 8 were waited for; matrix products, arithmetic and copies ran while one was open for 0% of the time, Pallas kernels for 11%

profile of v3, /device:TPU:0, one launch (start us, length us, event | category | flops | bytes accessed | tf_op | source)
XLA Modules:
  0.0 67.6 jit_solution(4172202949521655764)
XLA Ops:
  0.6 8.2 %outward_sums.1 = (f32[304,128]{1,0:T(8,128)S(1)}, f32[304,128]{1,0:T(8,128)S(1)}, f32[304,128]{1,0:T(8,128)S(1)}, f32[304,128]{1,0:T(8,128)S(1)}, f32[304,128]{...) custom-call(bf16[576,2048]{1,0:T(8,128)(2,1)} %bitcast.12, ...), custom_call_target="tpu_custom_call" | custom-call | tf_op jit(solution)/shard_map/outward_sums/pallas_call | solution.py:297
  8.9 3.0 %collective-permute-start.2 = (f16[304,128]{1,0:T(8,128)(2,1)S(1)}, f16[304,128]{1,0:T(8,128)(2,1)S(1)}, u32[]{:S(2)}, u32[]{:S(2)}) collective-permute-start(f16[304,128]{1,0:T(8,128)(2,1)S(1)} %convert_element_type.49), channel_id=1, source_target_pairs={{0,4},{4,0},{8,12},{12,8},{16,20},{20,16},{24,28},{28,24},{1,5},{5... | collective-permute-start | bytes 233480 | tf_op jit(solution)/shard_map/ppermute | solution.py:584
  11.9 1.6 %collective-permute-start.1 = (f16[304,128]{1,0:T(8,128)(2,1)S(1)}, f16[304,128]{1,0:T(8,128)(2,1)S(1)}, u32[]{:S(2)}, u32[]{:S(2)}) collective-permute-start(f16[304,128]{1,0:T(8,128)(2,1)S(1)} %convert_element_type.47), channel_id=1, source_target_pairs={{0,12},{4,8},{8,4},{12,0},{16,28},{20,24},{24,20},{28,16},{1,13},{... | collective-permute-start | bytes 233480 | tf_op jit(solution)/shard_map/ppermute | solution.py:584
  13.5 0.7 collective-permute-start
  14.2 0.7 collective-permute-start.5
  14.9 5.4 %collective-permute-start.4 = (f16[304,128]{1,0:T(8,128)(2,1)S(1)}, f16[304,128]{1,0:T(8,128)(2,1)S(1)}, u32[]{:S(2)}, u32[]{:S(2)}) collective-permute-start(f16[304,128]{1,0:T(8,128)(2,1)S(1)} %convert_element_type.53), channel_id=1, source_target_pairs={{0,8},{4,12},{8,0},{12,4},{16,24},{20,28},{24,16},{28,20},{1,9},{5... | collective-permute-start | bytes 233480 | tf_op jit(solution)/shard_map/ppermute | solution.py:584
  20.3 0.7 collective-permute-start.3
  21.0 1.7 %own_sums.1 = (f32[576,128]{1,0:T(8,128)S(1)}, f32[576,128]{1,0:T(8,128)S(1)}) custom-call(bf16[576,2048]{1,0:T(8,128)(2,1)S(1)} %get-tuple-element.21.ordered, bf16[1792,2048]{1,0:T(8,128)(2,1)S(1)} %get-tuple-element.22.weights, f32[4,64]{1,0:T(4,128)S(1)} %copy-done.2), custom_call_target="tpu_custom_call" | custom-call | flops 1000000 | bytes 10000 | tf_op jit(solution)/shard_map/own_sums/pallas_call | solution.py:338
  23.1 1.6 %collective-permute-start.8 = (bf16[576,128]{1,0:T(8,128)(2,1)S(1)}, bf16[576,128]{1,0:T(8,128)(2,1)S(1)}, u32[]{:S(2)}, u32[]{:S(2)}) collective-permute-start(bf16[576,128]{1,0:T(8,128)(2,1)S(1)} %activations.2.a0), channel_id=1, source_target_pairs={{0,2},{1,3},{2,0},{3,1},{4,6},{5,7},{6,4},{7,5},{8,10},{9,11},{10,... | collective-permute-start | bytes 442376 | tf_op jit(solution)/shard_map/ppermute | solution.py:579
  24.9 0.6 collective-permute-start.9
  25.5 0.5 collective-permute-start.7
  26.0 3.2 %collective-permute-done.8.a2 = bf16[576,128]{1,0:T(8,128)(2,1)S(1)} collective-permute-done((bf16[576,128]{1,0:T(8,128)(2,1)S(1)}, bf16[576,128]{1,0:T(8,128)(2,1)S(1)}, u32[]{:S(2)}, u32[]{:S(2)}) %collective-permute-start.8) | collective-permute-done | bytes 147488 | tf_op jit(solution)/shard_map/ppermute | solution.py:579
  29.2 1.6 %collective-permute-done.9.b2 = bf16[576,128]{1,0:T(8,128)(2,1)S(1)} collective-permute-done((bf16[576,128]{1,0:T(8,128)(2,1)S(1)}, bf16[576,128]{1,0:T(8,128)(2,1)S(1)}, u32[]{:S(2)}, u32[]{:S(2)}) %collective-permute-start.9) | collective-permute-done | bytes 147488 | tf_op jit(solution)/shard_map/ppermute | solution.py:579
  31.2 0.9 %collective-permute-done.11.b3 = bf16[576,128]{1,0:T(8,128)(2,1)S(1)} collective-permute-done((bf16[576,128]{1,0:T(8,128)(2,1)S(1)}, bf16[576,128]{1,0:T(8,128)(2,1)S(1)}, u32[]{:S(2)}, u32[]{:S(2)}) %collective-permute-start.11) | collective-permute-done | bytes 147488 | tf_op jit(solution)/shard_map/ppermute | solution.py:579
  32.1 0.8 %far_head.1 = (bf16[576,256]{1,0:T(8,128)(2,1)S(1)}, bf16[576,256]{1,0:T(8,128)(2,1)S(1)}, bf16[2,288,128]{2,1,0:T(8,128)(2,1)S(1)}, bf16[2,288,128]{2,1,0:T(8,128)(2,1)S(1)}, bf16[2,288,128]{2,1,0:T(8,128)(2,1)S(1)}) custom-call(bf16[576,128]{1,0:T(8,128)(2,1)S(1)} %activations.2.a0, bf16[576,128]{1,0:T(8,128)(2,1)S(1)} %activations.3.b0, ...), custom_call_target="tpu_custom_call" | custom-call | tf_op jit(solution)/shard_map/far_head/pallas_call | solution.py:446
  33.0 1.9 %collective-permute-start.12 = (bf16[2,288,128]{2,1,0:T(8,128)(2,1)S(1)}, bf16[2,288,128]{2,1,0:T(8,128)(2,1)S(1)}, u32[]{:S(2)}, u32[]{:S(2)}) collective-permute-start(bf16[2,288,128]{2,1,0:T(8,128)(2,1)S(1)} %get-tuple-element.34), channel_id=1, source_target_pairs={{0,4},{1,13},{2,6},{3,15},{4,0},{5,9},{6,2},{7,11},{8,12},{9,5},{1... | collective-permute-start | bytes 442376 | tf_op jit(solution)/shard_map/ppermute | solution.py:594
  34.8 0.7 collective-permute-start.13
  35.5 5.7 %collective-permute-start.14 = (bf16[2,288,128]{2,1,0:T(8,128)(2,1)S(1)}, bf16[2,288,128]{2,1,0:T(8,128)(2,1)S(1)}, u32[]{:S(2)}, u32[]{:S(2)}) collective-permute-start(bf16[2,288,128]{2,1,0:T(8,128)(2,1)S(1)} %get-tuple-element.36), channel_id=1, source_target_pairs={{0,8},{2,10},{4,12},{6,14},{8,0},{9,17},{10,2},{11,19},{12,4},{13,... | collective-permute-start | bytes 442376 | tf_op jit(solution)/shard_map/ppermute | solution.py:594
  41.3 0.5 collective-permute-start.16
  41.8 3.7 %collective-permute-done.14.refs_2_ = bf16[2,288,128]{2,1,0:T(8,128)(2,1)S(1)} collective-permute-done((bf16[2,288,128]{2,1,0:T(8,128)(2,1)S(1)}, bf16[2,288,128]{2,1,0:T(8,128)(2,1)S(1)}, u32[]{:S(2)}, u32[]{:S(2)}) %collective-permute-start.14) | collective-permute-done | bytes 147488 | tf_op jit(solution)/shard_map/ppermute | solution.py:594
  45.5 1.4 %collective-permute-done.17.refs_5_ = bf16[2,288,128]{2,1,0:T(8,128)(2,1)S(1)} collective-permute-done((bf16[2,288,128]{2,1,0:T(8,128)(2,1)S(1)}, bf16[2,288,128]{2,1,0:T(8,128)(2,1)S(1)}, u32[]{:S(2)}, u32[]{:S(2)}) %collective-permute-start.17) | collective-permute-done | bytes 147488 | tf_op jit(solution)/shard_map/ppermute | solution.py:579
  46.9 0.6 spread.1.stack
  47.5 1.2 %grads_for.4 = bf16[576,512]{1,0:T(8,128)(2,1)S(1)} custom-call(bf16[576,1792]{1,0:T(8,128)(2,1)S(1)} %spread.1.stack, bf16[1792,2048]{1,0:T(8,128)(2,1)S(1)} %get-tuple-element.22.weights), custom_call_target="tpu_custom_call" | custom-call | flops 1056964608 | bytes 1000000 | tf_op jit(solution)/shard_map/grads_for/pallas_call | solution.py:545
  48.9 1.2 %grads_for.5 = bf16[576,512]{1,0:T(8,128)(2,1)S(1)} custom-call(bf16[576,1792]{1,0:T(8,128)(2,1)S(1)} %spread.1.stack, bf16[1792,2048]{1,0:T(8,128)(2,1)S(1)} %get-tuple-element.22.weights), custom_call_target="tpu_custom_call" | custom-call | flops 1056964608 | bytes 1000000 | tf_op jit(solution)/shard_map/grads_for/pallas_call | solution.py:545
  50.2 0.6 collective-permute-done.18
  50.9 1.6 %collective-permute-start.20 = (bf16[576,512]{1,0:T(8,128)(2,1)S(1)}, bf16[576,512]{1,0:T(8,128)(2,1)S(1)}, u32[]{:S(2)}, u32[]{:S(2)}) collective-permute-start(bf16[576,512]{1,0:T(8,128)(2,1)S(1)} %add_convert_fusion), channel_id=1, source_target_pairs={{0,2},{1,3},{2,0},{3,1},{4,6},{5,7},{6,4},{7,5},{8,10},{9,11},{10,... | collective-permute-start | bytes 1769480 | tf_op jit(solution)/shard_map/ppermute | solution.py:579
  52.5 1.2 %own_output.1 = bf16[576,64]{1,0:T(8,128)(2,1)} custom-call(bf16[576,256]{1,0:T(8,128)(2,1)S(1)} %get-tuple-element.38.output), custom_call_target="tpu_custom_call" | custom-call | tf_op jit(solution)/shard_map/own_output/pallas_call | solution.py:471
  53.7 1.2 %grads_for.7 = bf16[576,512]{1,0:T(8,128)(2,1)S(1)} custom-call(bf16[576,1792]{1,0:T(8,128)(2,1)S(1)} %spread.1.stack, bf16[1792,2048]{1,0:T(8,128)(2,1)S(1)} %get-tuple-element.22.weights), custom_call_target="tpu_custom_call" | custom-call | flops 1056964608 | bytes 1000000 | tf_op jit(solution)/shard_map/grads_for/pallas_call | solution.py:545
  55.0 1.2 %grads_for.6.a = bf16[576,512]{1,0:T(8,128)(2,1)S(1)} custom-call(bf16[576,1792]{1,0:T(8,128)(2,1)S(1)} %spread.1.stack, bf16[1792,2048]{1,0:T(8,128)(2,1)S(1)} %get-tuple-element.22.weights), custom_call_target="tpu_custom_call" | custom-call | flops 8455716864 | bytes 1000000 | tf_op jit(solution)/shard_map/grads_for/pallas_call | solution.py:545
  56.3 0.7 %collective-permute-done.19.b = bf16[576,512]{1,0:T(8,128)(2,1)S(1)} collective-permute-done((bf16[576,512]{1,0:T(8,128)(2,1)S(1)}, bf16[576,512]{1,0:T(8,128)(2,1)S(1)}, u32[]{:S(2)}, u32[]{:S(2)}) %collective-permute-start.19) | collective-permute-done | bytes 589856 | tf_op jit(solution)/shard_map/ppermute | solution.py:579
  57.0 9.4 %collective-permute-done.20.c = bf16[576,512]{1,0:T(8,128)(2,1)S(1)} collective-permute-done((bf16[576,512]{1,0:T(8,128)(2,1)S(1)}, bf16[576,512]{1,0:T(8,128)(2,1)S(1)}, u32[]{:S(2)}, u32[]{:S(2)}) %collective-permute-start.20) | collective-permute-done | bytes 589856 | tf_op jit(solution)/shard_map/ppermute | solution.py:579
  66.4 1.3 %last_sum.1 = bf16[576,512]{1,0:T(8,128)(2,1)} custom-call(bf16[576,512]{1,0:T(8,128)(2,1)S(1)} %grads_for.6.a, bf16[576,512]{1,0:T(8,128)(2,1)S(1)} %collective-permute-done.19.b, bf16[576,512]{1,0:T(8,128)(2,1)S(1)} %collective-permute-done.20.c), custom_call_target="tpu_custom_call" | custom-call | tf_op jit(solution)/shard_map/last_sum/pallas_call | solution.py:568
  (44 shorter events, 1.5 us)
Async XLA Ops:
  0.6 20.4 %copy-start.2 = (f32[4,64]{1,0:T(4,128)S(1)}, f32[4,64]{1,0:T(4,128)}, u32[]{:S(2)}) copy-start(f32[4,64]{1,0:T(4,128)} %bias.1) | copy-start | bytes 3076
  8.9 11.4 %collective-permute-start.2 = (f16[304,128]{1,0:T(8,128)(2,1)S(1)}, f16[304,128]{1,0:T(8,128)(2,1)S(1)}, u32[]{:S(2)}, u32[]{:S(2)}) collective-permute-start(f16[304,128]{1,0:T(8,128)(2,1)S(1)} %convert_element_type.49), channel_id=1, source_target_pairs={{0,4},{4,0},{8,12},{12,8},{16,20},{20,16},{24,28},{28,24},{1,5},{5... | collective-permute-start | bytes 233480 | tf_op jit(solution)/shard_map/ppermute | solution.py:584
  11.9 10.9 %collective-permute-start.1 = (f16[304,128]{1,0:T(8,128)(2,1)S(1)}, f16[304,128]{1,0:T(8,128)(2,1)S(1)}, u32[]{:S(2)}, u32[]{:S(2)}) collective-permute-start(f16[304,128]{1,0:T(8,128)(2,1)S(1)} %convert_element_type.47), channel_id=1, source_target_pairs={{0,12},{4,8},{8,4},{12,0},{16,28},{20,24},{24,20},{28,16},{1,13},{... | collective-permute-start | bytes 233480 | tf_op jit(solution)/shard_map/ppermute | solution.py:584
  13.5 9.3 %collective-permute-start = (f16[304,128]{1,0:T(8,128)(2,1)S(1)}, f16[304,128]{1,0:T(8,128)(2,1)S(1)}, u32[]{:S(2)}, u32[]{:S(2)}) collective-permute-start(f16[304,128]{1,0:T(8,128)(2,1)S(1)} %convert_element_type.45), channel_id=1, source_target_pairs={{8,20},{12,16},{16,12},{20,8},{9,21},{13,17},{17,13},{21,9},{10,22... | collective-permute-start | bytes 233480 | tf_op jit(solution)/shard_map/ppermute | solution.py:584
  14.2 10.4 %collective-permute-start.5 = (f16[304,128]{1,0:T(8,128)(2,1)S(1)}, f16[304,128]{1,0:T(8,128)(2,1)S(1)}, u32[]{:S(2)}, u32[]{:S(2)}) collective-permute-start(f16[304,128]{1,0:T(8,128)(2,1)S(1)} %convert_element_type.55), channel_id=1, source_target_pairs={{4,16},{12,24},{16,4},{24,12},{5,17},{13,25},{17,5},{25,13},{6,18}... | collective-permute-start | bytes 233480 | tf_op jit(solution)/shard_map/ppermute | solution.py:584
  14.9 9.7 %collective-permute-start.4 = (f16[304,128]{1,0:T(8,128)(2,1)S(1)}, f16[304,128]{1,0:T(8,128)(2,1)S(1)}, u32[]{:S(2)}, u32[]{:S(2)}) collective-permute-start(f16[304,128]{1,0:T(8,128)(2,1)S(1)} %convert_element_type.53), channel_id=1, source_target_pairs={{0,8},{4,12},{8,0},{12,4},{16,24},{20,28},{24,16},{28,20},{1,9},{5... | collective-permute-start | bytes 233480 | tf_op jit(solution)/shard_map/ppermute | solution.py:584
  20.3 4.3 %collective-permute-start.3 = (f16[304,128]{1,0:T(8,128)(2,1)S(1)}, f16[304,128]{1,0:T(8,128)(2,1)S(1)}, u32[]{:S(2)}, u32[]{:S(2)}) collective-permute-start(f16[304,128]{1,0:T(8,128)(2,1)S(1)} %convert_element_type.51), channel_id=1, source_target_pairs={{8,16},{12,20},{16,8},{20,12},{9,17},{13,21},{17,9},{21,13},{10,18... | collective-permute-start | bytes 233480 | tf_op jit(solution)/shard_map/ppermute | solution.py:584
  22.8 8.0 %copy-start = (bf16[4,256,256]{2,1,0:T(8,128)(2,1)S(1)}, bf16[4,256,256]{2,1,0:T(8,128)(2,1)}, u32[]{:S(2)}) copy-start(bf16[4,256,256]{2,1,0:T(8,128)(2,1)} %project.3) | copy-start | bytes 1572868
  22.8 8.0 %copy-start.1 = (bf16[12,48,256]{2,1,0:T(8,128)(2,1)S(1)}, bf16[12,48,256]{2,1,0:T(8,128)(2,1)}, u32[]{:S(2)}) copy-start(bf16[12,48,256]{2,1,0:T(8,128)(2,1)} %param.13) | copy-start | bytes 884740
  22.8 8.0 %copy-start.3 = (f32[256]{0:T(256)S(1)}, f32[256]{0:T(256)}, u32[]{:S(2)}) copy-start(f32[256]{0:T(256)} %param.12) | copy-start | bytes 3076
  23.1 6.1 %collective-permute-start.8 = (bf16[576,128]{1,0:T(8,128)(2,1)S(1)}, bf16[576,128]{1,0:T(8,128)(2,1)S(1)}, u32[]{:S(2)}, u32[]{:S(2)}) collective-permute-start(bf16[576,128]{1,0:T(8,128)(2,1)S(1)} %activations.2.a0), channel_id=1, source_target_pairs={{0,2},{1,3},{2,0},{3,1},{4,6},{5,7},{6,4},{7,5},{8,10},{9,11},{10,... | collective-permute-start | bytes 442376 | tf_op jit(solution)/shard_map/ppermute | solution.py:579
  24.9 5.8 %collective-permute-start.9 = (bf16[576,128]{1,0:T(8,128)(2,1)S(1)}, bf16[576,128]{1,0:T(8,128)(2,1)S(1)}, u32[]{:S(2)}, u32[]{:S(2)}) collective-permute-start(bf16[576,128]{1,0:T(8,128)(2,1)S(1)} %activations.3.b0), channel_id=1, source_target_pairs={{0,2},{1,3},{2,0},{3,1},{4,6},{5,7},{6,4},{7,5},{8,10},{9,11},{10,... | collective-permute-start | bytes 442376 | tf_op jit(solution)/shard_map/ppermute | solution.py:579
  25.5 5.3 %collective-permute-start.6 = (bf16[576,128]{1,0:T(8,128)(2,1)S(1)}, bf16[576,128]{1,0:T(8,128)(2,1)S(1)}, u32[]{:S(2)}, u32[]{:S(2)}) collective-permute-start(bf16[576,128]{1,0:T(8,128)(2,1)S(1)} %activations.2.a0), channel_id=1, source_target_pairs={{0,1},{1,0},{2,3},{3,2},{4,5},{5,4},{6,7},{7,6},{8,9},{9,8},{10,11... | collective-permute-start | bytes 442376 | tf_op jit(solution)/shard_map/ppermute | solution.py:579
  25.5 5.3 %collective-permute-start.7 = (bf16[576,128]{1,0:T(8,128)(2,1)S(1)}, bf16[576,128]{1,0:T(8,128)(2,1)S(1)}, u32[]{:S(2)}, u32[]{:S(2)}) collective-permute-start(bf16[576,128]{1,0:T(8,128)(2,1)S(1)} %activations.3.b0), channel_id=1, source_target_pairs={{0,1},{1,0},{2,3},{3,2},{4,5},{5,4},{6,7},{7,6},{8,9},{9,8},{10,11... | collective-permute-start | bytes 442376 | tf_op jit(solution)/shard_map/ppermute | solution.py:579
  29.2 2.0 %collective-permute-start.10 = (bf16[576,128]{1,0:T(8,128)(2,1)S(1)}, bf16[576,128]{1,0:T(8,128)(2,1)S(1)}, u32[]{:S(2)}, u32[]{:S(2)}) collective-permute-start(bf16[576,128]{1,0:T(8,128)(2,1)S(1)} %collective-permute-done.8.a2), channel_id=1, source_target_pairs={{0,1},{1,0},{2,3},{3,2},{4,5},{5,4},{6,7},{7,6},{8,9},{9,8},{10,11... | collective-permute-start | bytes 442376 | tf_op jit(solution)/shard_map/ppermute | solution.py:579
  30.8 1.4 %collective-permute-start.11 = (bf16[576,128]{1,0:T(8,128)(2,1)S(1)}, bf16[576,128]{1,0:T(8,128)(2,1)S(1)}, u32[]{:S(2)}, u32[]{:S(2)}) collective-permute-start(bf16[576,128]{1,0:T(8,128)(2,1)S(1)} %collective-permute-done.9.b2), channel_id=1, source_target_pairs={{0,1},{1,0},{2,3},{3,2},{4,5},{5,4},{6,7},{7,6},{8,9},{9,8},{10,11... | collective-permute-start | bytes 442376 | tf_op jit(solution)/shard_map/ppermute | solution.py:579
  33.0 8.3 %collective-permute-start.12 = (bf16[2,288,128]{2,1,0:T(8,128)(2,1)S(1)}, bf16[2,288,128]{2,1,0:T(8,128)(2,1)S(1)}, u32[]{:S(2)}, u32[]{:S(2)}) collective-permute-start(bf16[2,288,128]{2,1,0:T(8,128)(2,1)S(1)} %get-tuple-element.34), channel_id=1, source_target_pairs={{0,4},{1,13},{2,6},{3,15},{4,0},{5,9},{6,2},{7,11},{8,12},{9,5},{1... | collective-permute-start | bytes 442376 | tf_op jit(solution)/shard_map/ppermute | solution.py:594
  34.8 6.5 %collective-permute-start.13 = (bf16[2,288,128]{2,1,0:T(8,128)(2,1)S(1)}, bf16[2,288,128]{2,1,0:T(8,128)(2,1)S(1)}, u32[]{:S(2)}, u32[]{:S(2)}) collective-permute-start(bf16[2,288,128]{2,1,0:T(8,128)(2,1)S(1)} %get-tuple-element.35), channel_id=1, source_target_pairs={{4,16},{6,18},{9,21},{11,23},{12,24},{13,17},{14,26},{15,19},{16,4... | collective-permute-start | bytes 442376 | tf_op jit(solution)/shard_map/ppermute | solution.py:594
  35.5 10.0 %collective-permute-start.14 = (bf16[2,288,128]{2,1,0:T(8,128)(2,1)S(1)}, bf16[2,288,128]{2,1,0:T(8,128)(2,1)S(1)}, u32[]{:S(2)}, u32[]{:S(2)}) collective-permute-start(bf16[2,288,128]{2,1,0:T(8,128)(2,1)S(1)} %get-tuple-element.36), channel_id=1, source_target_pairs={{0,8},{2,10},{4,12},{6,14},{8,0},{9,17},{10,2},{11,19},{12,4},{13,... | collective-permute-start | bytes 442376 | tf_op jit(solution)/shard_map/ppermute | solution.py:594
  41.2 4.3 %collective-permute-start.15 = (bf16[2,288,128]{2,1,0:T(8,128)(2,1)S(1)}, bf16[2,288,128]{2,1,0:T(8,128)(2,1)S(1)}, u32[]{:S(2)}, u32[]{:S(2)}) collective-permute-start(bf16[2,288,128]{2,1,0:T(8,128)(2,1)S(1)} %collective-permute-done.12.refs_0_), channel_id=1, source_target_pairs={{0,1},{1,0},{2,3},{3,2},{4,5},{5,4},{6,7},{7,6},{8,9},{9,8},{10,11... | collective-permute-start | bytes 442376 | tf_op jit(solution)/shard_map/ppermute | solution.py:579
  41.3 4.2 %collective-permute-start.16 = (bf16[2,288,128]{2,1,0:T(8,128)(2,1)S(1)}, bf16[2,288,128]{2,1,0:T(8,128)(2,1)S(1)}, u32[]{:S(2)}, u32[]{:S(2)}) collective-permute-start(bf16[2,288,128]{2,1,0:T(8,128)(2,1)S(1)} %collective-permute-done.13.refs_1_), channel_id=1, source_target_pairs={{0,1},{1,0},{2,3},{3,2},{4,5},{5,4},{6,7},{7,6},{8,9},{9,8},{10,11... | collective-permute-start | bytes 442376 | tf_op jit(solution)/shard_map/ppermute | solution.py:579
  45.5 1.4 %collective-permute-start.17 = (bf16[2,288,128]{2,1,0:T(8,128)(2,1)S(1)}, bf16[2,288,128]{2,1,0:T(8,128)(2,1)S(1)}, u32[]{:S(2)}, u32[]{:S(2)}) collective-permute-start(bf16[2,288,128]{2,1,0:T(8,128)(2,1)S(1)} %collective-permute-done.14.refs_2_), channel_id=1, source_target_pairs={{0,1},{1,0},{2,3},{3,2},{4,5},{5,4},{6,7},{7,6},{8,9},{9,8},{10,11... | collective-permute-start | bytes 442376 | tf_op jit(solution)/shard_map/ppermute | solution.py:579
  48.7 2.1 %collective-permute-start.18 = (bf16[576,512]{1,0:T(8,128)(2,1)S(1)}, bf16[576,512]{1,0:T(8,128)(2,1)S(1)}, u32[]{:S(2)}, u32[]{:S(2)}) collective-permute-start(bf16[576,512]{1,0:T(8,128)(2,1)S(1)} %grads_for.4), channel_id=1, source_target_pairs={{0,1},{1,0},{2,3},{3,2},{4,5},{5,4},{6,7},{7,6},{8,9},{9,8},{10,11... | collective-permute-start | bytes 1769480 | tf_op jit(solution)/shard_map/ppermute | solution.py:579
  50.9 15.4 %collective-permute-start.20 = (bf16[576,512]{1,0:T(8,128)(2,1)S(1)}, bf16[576,512]{1,0:T(8,128)(2,1)S(1)}, u32[]{:S(2)}, u32[]{:S(2)}) collective-permute-start(bf16[576,512]{1,0:T(8,128)(2,1)S(1)} %add_convert_fusion), channel_id=1, source_target_pairs={{0,2},{1,3},{2,0},{3,1},{4,6},{5,7},{6,4},{7,5},{8,10},{9,11},{10,... | collective-permute-start | bytes 1769480 | tf_op jit(solution)/shard_map/ppermute | solution.py:579
  55.0 2.1 %collective-permute-start.19 = (bf16[576,512]{1,0:T(8,128)(2,1)S(1)}, bf16[576,512]{1,0:T(8,128)(2,1)S(1)}, u32[]{:S(2)}, u32[]{:S(2)}) collective-permute-start(bf16[576,512]{1,0:T(8,128)(2,1)S(1)} %grads_for.7), channel_id=1, source_target_pairs={{0,1},{1,0},{2,3},{3,2},{4,5},{5,4},{6,7},{7,6},{8,9},{9,8},{10,11... | collective-permute-start | bytes 1769480 | tf_op jit(solution)/shard_map/ppermute | solution.py:579

commit v4 on v3

--- a/solution.py
+++ b/solution.py
@@ -579,17 +579,19 @@
     return lax.ppermute(x, "filt", [(i, i ^ bit) for i in range(lax.axis_size("filt"))])
 
 
+def partner(r, bits):
+    return r ^ bits if abs((r ^ bits) - r) <= 3 else r
+
+
 def swapped(x, bits):
-    pairs = [(r, r ^ bits) for r in range(8) if abs((r ^ bits) - r) <= 3]
-    return lax.ppermute(x, "rows", pairs)
+    return lax.ppermute(x, "rows", [(r, partner(r, bits)) for r in range(8)])
 
 
 def swapped_by_core(x, bits):
     pairs = [
-        (4 * r + member, 4 * (r ^ bits[member % 2]) + member)
+        (4 * r + member, 4 * partner(r, bits[member % 2]) + member)
         for r in range(8)
         for member in range(4)
-        if abs((r ^ bits[member % 2]) - r) <= 3
     ]
     return lax.ppermute(x, ("rows", "filt"), pairs)
 

time: 68.5 us -> 68.5 us (level)
  no operation moved by 1% of the time
where the time goes in v4:
time: 68.5 us; the launch traced here: 67.6 us
  starting transfers between devices  25.3 us (37%)
  waiting for transfers between devices  21.5 us (31%)
  Pallas kernels  19.5 us (28%)
  between operations  0.99 us (1%)
    ppermute x12, waiting for transfers between devices, flipped(): lax.ppermute(x, 'filt', [(i, i ^ bit) for i in range(lax.axis_size('filt'...  17.7 us
    ppermute x6, starting transfers between devices, swapped(): return lax.ppermute(x, 'rows', [(r, partner(r, bits)) for r in range(8)])  12 us
    ppermute x3, starting transfers between devices, swapped_by_core(): return lax.ppermute(x, ('rows', 'filt'), pairs)  8.24 us
    pallas_call x1, Pallas kernels, outward_sums(): pl.pallas_call(outward_kernel, out_shape=[jax.ShapeDtypeStruct((SENT, 128...  8.23 us
    ppermute x12, starting transfers between devices, flipped(): lax.ppermute(x, 'filt', [(i, i ^ bit) for i in range(lax.axis_size('filt'...  5.08 us
    pallas_call x4, Pallas kernels, grads_for(): pl.pallas_call(functools.partial(grad_kernel, flips), out_shape=[jax.Shap...  4.94 us
    ppermute x3, waiting for transfers between devices, swapped_by_core(): return lax.ppermute(x, ('rows', 'filt'), pairs)  3.69 us
    pallas_call x1, Pallas kernels, own_sums(): pl.pallas_call(own_kernel, out_shape=[jax.ShapeDtypeStruct((PIXELS, 128),...  1.73 us
  transfers between devices with their start and end apart: 21, of which 8 were waited for; matrix products, arithmetic and copies ran while one was open for 0% of the time, Pallas kernels for 11%

profile of v4, /device:TPU:0, one launch (start us, length us, event | category | flops | bytes accessed | tf_op | source)
XLA Modules:
  0.0 67.6 jit_solution(3993987183850137966)
XLA Ops:
  0.6 8.2 %outward_sums.1 = (f32[304,128]{1,0:T(8,128)S(1)}, f32[304,128]{1,0:T(8,128)S(1)}, f32[304,128]{1,0:T(8,128)S(1)}, f32[304,128]{1,0:T(8,128)S(1)}, f32[304,128]{...) custom-call(bf16[576,2048]{1,0:T(8,128)(2,1)} %bitcast.12, ...), custom_call_target="tpu_custom_call" | custom-call | tf_op jit(solution)/shard_map/outward_sums/pallas_call | solution.py:297
  8.9 3.0 %collective-permute-start.2 = (f16[304,128]{1,0:T(8,128)(2,1)S(1)}, f16[304,128]{1,0:T(8,128)(2,1)S(1)}, u32[]{:S(2)}, u32[]{:S(2)}) collective-permute-start(f16[304,128]{1,0:T(8,128)(2,1)S(1)} %convert_element_type.49), channel_id=1, source_target_pairs={{0,4},{4,0},{8,12},{12,8},{16,20},{20,16},{24,28},{28,24},{1,5},{5... | collective-permute-start | bytes 233480 | tf_op jit(solution)/shard_map/ppermute | solution.py:587
  11.9 1.6 %collective-permute-start.1 = (f16[304,128]{1,0:T(8,128)(2,1)S(1)}, f16[304,128]{1,0:T(8,128)(2,1)S(1)}, u32[]{:S(2)}, u32[]{:S(2)}) collective-permute-start(f16[304,128]{1,0:T(8,128)(2,1)S(1)} %convert_element_type.47), channel_id=1, source_target_pairs={{0,12},{4,8},{8,4},{12,0},{16,28},{20,24},{24,20},{28,16},{1,13},{... | collective-permute-start | bytes 233480 | tf_op jit(solution)/shard_map/ppermute | solution.py:587
  13.5 0.7 collective-permute-start
  14.2 0.7 collective-permute-start.5
  14.9 5.4 %collective-permute-start.4 = (f16[304,128]{1,0:T(8,128)(2,1)S(1)}, f16[304,128]{1,0:T(8,128)(2,1)S(1)}, u32[]{:S(2)}, u32[]{:S(2)}) collective-permute-start(f16[304,128]{1,0:T(8,128)(2,1)S(1)} %convert_element_type.53), channel_id=1, source_target_pairs={{0,8},{4,12},{8,0},{12,4},{16,24},{20,28},{24,16},{28,20},{1,9},{5... | collective-permute-start | bytes 233480 | tf_op jit(solution)/shard_map/ppermute | solution.py:587
  20.3 0.7 collective-permute-start.3
  21.0 1.7 %own_sums.1 = (f32[576,128]{1,0:T(8,128)S(1)}, f32[576,128]{1,0:T(8,128)S(1)}) custom-call(bf16[576,2048]{1,0:T(8,128)(2,1)S(1)} %get-tuple-element.21.ordered, bf16[1792,2048]{1,0:T(8,128)(2,1)S(1)} %get-tuple-element.22.weights, f32[4,64]{1,0:T(4,128)S(1)} %copy-done.2), custom_call_target="tpu_custom_call" | custom-call | flops 1000000 | bytes 10000 | tf_op jit(solution)/shard_map/own_sums/pallas_call | solution.py:338
  23.1 1.6 %collective-permute-start.8 = (bf16[576,128]{1,0:T(8,128)(2,1)S(1)}, bf16[576,128]{1,0:T(8,128)(2,1)S(1)}, u32[]{:S(2)}, u32[]{:S(2)}) collective-permute-start(bf16[576,128]{1,0:T(8,128)(2,1)S(1)} %activations.2.a0), channel_id=1, source_target_pairs={{0,2},{1,3},{2,0},{3,1},{4,6},{5,7},{6,4},{7,5},{8,10},{9,11},{10,... | collective-permute-start | bytes 442376 | tf_op jit(solution)/shard_map/ppermute | solution.py:579
  24.9 0.6 collective-permute-start.9
  25.5 0.5 collective-permute-start.7
  26.0 3.2 %collective-permute-done.8.a2 = bf16[576,128]{1,0:T(8,128)(2,1)S(1)} collective-permute-done((bf16[576,128]{1,0:T(8,128)(2,1)S(1)}, bf16[576,128]{1,0:T(8,128)(2,1)S(1)}, u32[]{:S(2)}, u32[]{:S(2)}) %collective-permute-start.8) | collective-permute-done | bytes 147488 | tf_op jit(solution)/shard_map/ppermute | solution.py:579
  29.2 1.6 %collective-permute-done.9.b2 = bf16[576,128]{1,0:T(8,128)(2,1)S(1)} collective-permute-done((bf16[576,128]{1,0:T(8,128)(2,1)S(1)}, bf16[576,128]{1,0:T(8,128)(2,1)S(1)}, u32[]{:S(2)}, u32[]{:S(2)}) %collective-permute-start.9) | collective-permute-done | bytes 147488 | tf_op jit(solution)/shard_map/ppermute | solution.py:579
  31.2 0.9 %collective-permute-done.11.b3 = bf16[576,128]{1,0:T(8,128)(2,1)S(1)} collective-permute-done((bf16[576,128]{1,0:T(8,128)(2,1)S(1)}, bf16[576,128]{1,0:T(8,128)(2,1)S(1)}, u32[]{:S(2)}, u32[]{:S(2)}) %collective-permute-start.11) | collective-permute-done | bytes 147488 | tf_op jit(solution)/shard_map/ppermute | solution.py:579
  32.1 0.8 %far_head.1 = (bf16[576,256]{1,0:T(8,128)(2,1)S(1)}, bf16[576,256]{1,0:T(8,128)(2,1)S(1)}, bf16[2,288,128]{2,1,0:T(8,128)(2,1)S(1)}, bf16[2,288,128]{2,1,0:T(8,128)(2,1)S(1)}, bf16[2,288,128]{2,1,0:T(8,128)(2,1)S(1)}) custom-call(bf16[576,128]{1,0:T(8,128)(2,1)S(1)} %activations.2.a0, bf16[576,128]{1,0:T(8,128)(2,1)S(1)} %activations.3.b0, ...), custom_call_target="tpu_custom_call" | custom-call | tf_op jit(solution)/shard_map/far_head/pallas_call | solution.py:446
  33.0 1.9 %collective-permute-start.12 = (bf16[2,288,128]{2,1,0:T(8,128)(2,1)S(1)}, bf16[2,288,128]{2,1,0:T(8,128)(2,1)S(1)}, u32[]{:S(2)}, u32[]{:S(2)}) collective-permute-start(bf16[2,288,128]{2,1,0:T(8,128)(2,1)S(1)} %get-tuple-element.34), channel_id=1, source_target_pairs={{0,4},{1,13},{2,6},{3,15},{4,0},{5,9},{6,2},{7,11},{8,12},{9,5},{1... | collective-permute-start | bytes 442376 | tf_op jit(solution)/shard_map/ppermute | solution.py:596
  34.8 0.7 collective-permute-start.13
  35.5 5.7 %collective-permute-start.14 = (bf16[2,288,128]{2,1,0:T(8,128)(2,1)S(1)}, bf16[2,288,128]{2,1,0:T(8,128)(2,1)S(1)}, u32[]{:S(2)}, u32[]{:S(2)}) collective-permute-start(bf16[2,288,128]{2,1,0:T(8,128)(2,1)S(1)} %get-tuple-element.36), channel_id=1, source_target_pairs={{0,8},{1,1},{2,10},{3,3},{4,12},{5,5},{6,14},{7,7},{8,0},{9,17},{1... | collective-permute-start | bytes 442376 | tf_op jit(solution)/shard_map/ppermute | solution.py:596
  41.3 0.5 collective-permute-start.16
  41.8 3.7 %collective-permute-done.14.refs_2_ = bf16[2,288,128]{2,1,0:T(8,128)(2,1)S(1)} collective-permute-done((bf16[2,288,128]{2,1,0:T(8,128)(2,1)S(1)}, bf16[2,288,128]{2,1,0:T(8,128)(2,1)S(1)}, u32[]{:S(2)}, u32[]{:S(2)}) %collective-permute-start.14) | collective-permute-done | bytes 147488 | tf_op jit(solution)/shard_map/ppermute | solution.py:596
  45.5 1.4 %collective-permute-done.17.refs_5_ = bf16[2,288,128]{2,1,0:T(8,128)(2,1)S(1)} collective-permute-done((bf16[2,288,128]{2,1,0:T(8,128)(2,1)S(1)}, bf16[2,288,128]{2,1,0:T(8,128)(2,1)S(1)}, u32[]{:S(2)}, u32[]{:S(2)}) %collective-permute-start.17) | collective-permute-done | bytes 147488 | tf_op jit(solution)/shard_map/ppermute | solution.py:579
  46.9 0.6 spread.1.stack
  47.5 1.2 %grads_for.4 = bf16[576,512]{1,0:T(8,128)(2,1)S(1)} custom-call(bf16[576,1792]{1,0:T(8,128)(2,1)S(1)} %spread.1.stack, bf16[1792,2048]{1,0:T(8,128)(2,1)S(1)} %get-tuple-element.22.weights), custom_call_target="tpu_custom_call" | custom-call | flops 1056964608 | bytes 1000000 | tf_op jit(solution)/shard_map/grads_for/pallas_call | solution.py:545
  48.9 1.2 %grads_for.5 = bf16[576,512]{1,0:T(8,128)(2,1)S(1)} custom-call(bf16[576,1792]{1,0:T(8,128)(2,1)S(1)} %spread.1.stack, bf16[1792,2048]{1,0:T(8,128)(2,1)S(1)} %get-tuple-element.22.weights), custom_call_target="tpu_custom_call" | custom-call | flops 1056964608 | bytes 1000000 | tf_op jit(solution)/shard_map/grads_for/pallas_call | solution.py:545
  50.2 0.6 collective-permute-done.18
  50.9 1.6 %collective-permute-start.20 = (bf16[576,512]{1,0:T(8,128)(2,1)S(1)}, bf16[576,512]{1,0:T(8,128)(2,1)S(1)}, u32[]{:S(2)}, u32[]{:S(2)}) collective-permute-start(bf16[576,512]{1,0:T(8,128)(2,1)S(1)} %add_convert_fusion), channel_id=1, source_target_pairs={{0,2},{1,3},{2,0},{3,1},{4,6},{5,7},{6,4},{7,5},{8,10},{9,11},{10,... | collective-permute-start | bytes 1769480 | tf_op jit(solution)/shard_map/ppermute | solution.py:579
  52.5 1.2 %own_output.1 = bf16[576,64]{1,0:T(8,128)(2,1)} custom-call(bf16[576,256]{1,0:T(8,128)(2,1)S(1)} %get-tuple-element.38.output), custom_call_target="tpu_custom_call" | custom-call | tf_op jit(solution)/shard_map/own_output/pallas_call | solution.py:471
  53.7 1.2 %grads_for.7 = bf16[576,512]{1,0:T(8,128)(2,1)S(1)} custom-call(bf16[576,1792]{1,0:T(8,128)(2,1)S(1)} %spread.1.stack, bf16[1792,2048]{1,0:T(8,128)(2,1)S(1)} %get-tuple-element.22.weights), custom_call_target="tpu_custom_call" | custom-call | flops 1056964608 | bytes 1000000 | tf_op jit(solution)/shard_map/grads_for/pallas_call | solution.py:545
  55.0 1.2 %grads_for.6.a = bf16[576,512]{1,0:T(8,128)(2,1)S(1)} custom-call(bf16[576,1792]{1,0:T(8,128)(2,1)S(1)} %spread.1.stack, bf16[1792,2048]{1,0:T(8,128)(2,1)S(1)} %get-tuple-element.22.weights), custom_call_target="tpu_custom_call" | custom-call | flops 8455716864 | bytes 1000000 | tf_op jit(solution)/shard_map/grads_for/pallas_call | solution.py:545
  56.3 0.7 %collective-permute-done.19.b = bf16[576,512]{1,0:T(8,128)(2,1)S(1)} collective-permute-done((bf16[576,512]{1,0:T(8,128)(2,1)S(1)}, bf16[576,512]{1,0:T(8,128)(2,1)S(1)}, u32[]{:S(2)}, u32[]{:S(2)}) %collective-permute-start.19) | collective-permute-done | bytes 589856 | tf_op jit(solution)/shard_map/ppermute | solution.py:579
  57.0 9.4 %collective-permute-done.20.c = bf16[576,512]{1,0:T(8,128)(2,1)S(1)} collective-permute-done((bf16[576,512]{1,0:T(8,128)(2,1)S(1)}, bf16[576,512]{1,0:T(8,128)(2,1)S(1)}, u32[]{:S(2)}, u32[]{:S(2)}) %collective-permute-start.20) | collective-permute-done | bytes 589856 | tf_op jit(solution)/shard_map/ppermute | solution.py:579
  66.4 1.3 %last_sum.1 = bf16[576,512]{1,0:T(8,128)(2,1)} custom-call(bf16[576,512]{1,0:T(8,128)(2,1)S(1)} %grads_for.6.a, bf16[576,512]{1,0:T(8,128)(2,1)S(1)} %collective-permute-done.19.b, bf16[576,512]{1,0:T(8,128)(2,1)S(1)} %collective-permute-done.20.c), custom_call_target="tpu_custom_call" | custom-call | tf_op jit(solution)/shard_map/last_sum/pallas_call | solution.py:568
  (44 shorter events, 1.5 us)
Async XLA Ops:
  0.6 20.4 %copy-start.2 = (f32[4,64]{1,0:T(4,128)S(1)}, f32[4,64]{1,0:T(4,128)}, u32[]{:S(2)}) copy-start(f32[4,64]{1,0:T(4,128)} %bias.1) | copy-start | bytes 3076
  8.9 11.4 %collective-permute-start.2 = (f16[304,128]{1,0:T(8,128)(2,1)S(1)}, f16[304,128]{1,0:T(8,128)(2,1)S(1)}, u32[]{:S(2)}, u32[]{:S(2)}) collective-permute-start(f16[304,128]{1,0:T(8,128)(2,1)S(1)} %convert_element_type.49), channel_id=1, source_target_pairs={{0,4},{4,0},{8,12},{12,8},{16,20},{20,16},{24,28},{28,24},{1,5},{5... | collective-permute-start | bytes 233480 | tf_op jit(solution)/shard_map/ppermute | solution.py:587
  11.9 10.9 %collective-permute-start.1 = (f16[304,128]{1,0:T(8,128)(2,1)S(1)}, f16[304,128]{1,0:T(8,128)(2,1)S(1)}, u32[]{:S(2)}, u32[]{:S(2)}) collective-permute-start(f16[304,128]{1,0:T(8,128)(2,1)S(1)} %convert_element_type.47), channel_id=1, source_target_pairs={{0,12},{4,8},{8,4},{12,0},{16,28},{20,24},{24,20},{28,16},{1,13},{... | collective-permute-start | bytes 233480 | tf_op jit(solution)/shard_map/ppermute | solution.py:587
  13.5 9.3 %collective-permute-start = (f16[304,128]{1,0:T(8,128)(2,1)S(1)}, f16[304,128]{1,0:T(8,128)(2,1)S(1)}, u32[]{:S(2)}, u32[]{:S(2)}) collective-permute-start(f16[304,128]{1,0:T(8,128)(2,1)S(1)} %convert_element_type.45), channel_id=1, source_target_pairs={{0,0},{4,4},{8,20},{12,16},{16,12},{20,8},{24,24},{28,28},{1,1},{5... | collective-permute-start | bytes 233480 | tf_op jit(solution)/shard_map/ppermute | solution.py:587
  14.2 10.4 %collective-permute-start.5 = (f16[304,128]{1,0:T(8,128)(2,1)S(1)}, f16[304,128]{1,0:T(8,128)(2,1)S(1)}, u32[]{:S(2)}, u32[]{:S(2)}) collective-permute-start(f16[304,128]{1,0:T(8,128)(2,1)S(1)} %convert_element_type.55), channel_id=1, source_target_pairs={{0,0},{4,16},{8,8},{12,24},{16,4},{20,20},{24,12},{28,28},{1,1},{5... | collective-permute-start | bytes 233480 | tf_op jit(solution)/shard_map/ppermute | solution.py:587
  14.9 9.7 %collective-permute-start.4 = (f16[304,128]{1,0:T(8,128)(2,1)S(1)}, f16[304,128]{1,0:T(8,128)(2,1)S(1)}, u32[]{:S(2)}, u32[]{:S(2)}) collective-permute-start(f16[304,128]{1,0:T(8,128)(2,1)S(1)} %convert_element_type.53), channel_id=1, source_target_pairs={{0,8},{4,12},{8,0},{12,4},{16,24},{20,28},{24,16},{28,20},{1,9},{5... | collective-permute-start | bytes 233480 | tf_op jit(solution)/shard_map/ppermute | solution.py:587
  20.3 4.3 %collective-permute-start.3 = (f16[304,128]{1,0:T(8,128)(2,1)S(1)}, f16[304,128]{1,0:T(8,128)(2,1)S(1)}, u32[]{:S(2)}, u32[]{:S(2)}) collective-permute-start(f16[304,128]{1,0:T(8,128)(2,1)S(1)} %convert_element_type.51), channel_id=1, source_target_pairs={{0,0},{4,4},{8,16},{12,20},{16,8},{20,12},{24,24},{28,28},{1,1},{5... | collective-permute-start | bytes 233480 | tf_op jit(solution)/shard_map/ppermute | solution.py:587
  22.8 8.0 %copy-start = (bf16[4,256,256]{2,1,0:T(8,128)(2,1)S(1)}, bf16[4,256,256]{2,1,0:T(8,128)(2,1)}, u32[]{:S(2)}) copy-start(bf16[4,256,256]{2,1,0:T(8,128)(2,1)} %project.3) | copy-start | bytes 1572868
  22.8 8.0 %copy-start.1 = (bf16[12,48,256]{2,1,0:T(8,128)(2,1)S(1)}, bf16[12,48,256]{2,1,0:T(8,128)(2,1)}, u32[]{:S(2)}) copy-start(bf16[12,48,256]{2,1,0:T(8,128)(2,1)} %param.13) | copy-start | bytes 884740
  22.8 8.0 %copy-start.3 = (f32[256]{0:T(256)S(1)}, f32[256]{0:T(256)}, u32[]{:S(2)}) copy-start(f32[256]{0:T(256)} %param.12) | copy-start | bytes 3076
  23.1 6.1 %collective-permute-start.8 = (bf16[576,128]{1,0:T(8,128)(2,1)S(1)}, bf16[576,128]{1,0:T(8,128)(2,1)S(1)}, u32[]{:S(2)}, u32[]{:S(2)}) collective-permute-start(bf16[576,128]{1,0:T(8,128)(2,1)S(1)} %activations.2.a0), channel_id=1, source_target_pairs={{0,2},{1,3},{2,0},{3,1},{4,6},{5,7},{6,4},{7,5},{8,10},{9,11},{10,... | collective-permute-start | bytes 442376 | tf_op jit(solution)/shard_map/ppermute | solution.py:579
  24.9 5.8 %collective-permute-start.9 = (bf16[576,128]{1,0:T(8,128)(2,1)S(1)}, bf16[576,128]{1,0:T(8,128)(2,1)S(1)}, u32[]{:S(2)}, u32[]{:S(2)}) collective-permute-start(bf16[576,128]{1,0:T(8,128)(2,1)S(1)} %activations.3.b0), channel_id=1, source_target_pairs={{0,2},{1,3},{2,0},{3,1},{4,6},{5,7},{6,4},{7,5},{8,10},{9,11},{10,... | collective-permute-start | bytes 442376 | tf_op jit(solution)/shard_map/ppermute | solution.py:579
  25.5 5.3 %collective-permute-start.6 = (bf16[576,128]{1,0:T(8,128)(2,1)S(1)}, bf16[576,128]{1,0:T(8,128)(2,1)S(1)}, u32[]{:S(2)}, u32[]{:S(2)}) collective-permute-start(bf16[576,128]{1,0:T(8,128)(2,1)S(1)} %activations.2.a0), channel_id=1, source_target_pairs={{0,1},{1,0},{2,3},{3,2},{4,5},{5,4},{6,7},{7,6},{8,9},{9,8},{10,11... | collective-permute-start | bytes 442376 | tf_op jit(solution)/shard_map/ppermute | solution.py:579
  25.5 5.3 %collective-permute-start.7 = (bf16[576,128]{1,0:T(8,128)(2,1)S(1)}, bf16[576,128]{1,0:T(8,128)(2,1)S(1)}, u32[]{:S(2)}, u32[]{:S(2)}) collective-permute-start(bf16[576,128]{1,0:T(8,128)(2,1)S(1)} %activations.3.b0), channel_id=1, source_target_pairs={{0,1},{1,0},{2,3},{3,2},{4,5},{5,4},{6,7},{7,6},{8,9},{9,8},{10,11... | collective-permute-start | bytes 442376 | tf_op jit(solution)/shard_map/ppermute | solution.py:579
  29.2 2.0 %collective-permute-start.10 = (bf16[576,128]{1,0:T(8,128)(2,1)S(1)}, bf16[576,128]{1,0:T(8,128)(2,1)S(1)}, u32[]{:S(2)}, u32[]{:S(2)}) collective-permute-start(bf16[576,128]{1,0:T(8,128)(2,1)S(1)} %collective-permute-done.8.a2), channel_id=1, source_target_pairs={{0,1},{1,0},{2,3},{3,2},{4,5},{5,4},{6,7},{7,6},{8,9},{9,8},{10,11... | collective-permute-start | bytes 442376 | tf_op jit(solution)/shard_map/ppermute | solution.py:579
  30.8 1.4 %collective-permute-start.11 = (bf16[576,128]{1,0:T(8,128)(2,1)S(1)}, bf16[576,128]{1,0:T(8,128)(2,1)S(1)}, u32[]{:S(2)}, u32[]{:S(2)}) collective-permute-start(bf16[576,128]{1,0:T(8,128)(2,1)S(1)} %collective-permute-done.9.b2), channel_id=1, source_target_pairs={{0,1},{1,0},{2,3},{3,2},{4,5},{5,4},{6,7},{7,6},{8,9},{9,8},{10,11... | collective-permute-start | bytes 442376 | tf_op jit(solution)/shard_map/ppermute | solution.py:579
  33.0 8.3 %collective-permute-start.12 = (bf16[2,288,128]{2,1,0:T(8,128)(2,1)S(1)}, bf16[2,288,128]{2,1,0:T(8,128)(2,1)S(1)}, u32[]{:S(2)}, u32[]{:S(2)}) collective-permute-start(bf16[2,288,128]{2,1,0:T(8,128)(2,1)S(1)} %get-tuple-element.34), channel_id=1, source_target_pairs={{0,4},{1,13},{2,6},{3,15},{4,0},{5,9},{6,2},{7,11},{8,12},{9,5},{1... | collective-permute-start | bytes 442376 | tf_op jit(solution)/shard_map/ppermute | solution.py:596
  34.8 6.5 %collective-permute-start.13 = (bf16[2,288,128]{2,1,0:T(8,128)(2,1)S(1)}, bf16[2,288,128]{2,1,0:T(8,128)(2,1)S(1)}, u32[]{:S(2)}, u32[]{:S(2)}) collective-permute-start(bf16[2,288,128]{2,1,0:T(8,128)(2,1)S(1)} %get-tuple-element.35), channel_id=1, source_target_pairs={{0,0},{1,1},{2,2},{3,3},{4,16},{5,5},{6,18},{7,7},{8,8},{9,21},{10... | collective-permute-start | bytes 442376 | tf_op jit(solution)/shard_map/ppermute | solution.py:596
  35.5 10.0 %collective-permute-start.14 = (bf16[2,288,128]{2,1,0:T(8,128)(2,1)S(1)}, bf16[2,288,128]{2,1,0:T(8,128)(2,1)S(1)}, u32[]{:S(2)}, u32[]{:S(2)}) collective-permute-start(bf16[2,288,128]{2,1,0:T(8,128)(2,1)S(1)} %get-tuple-element.36), channel_id=1, source_target_pairs={{0,8},{1,1},{2,10},{3,3},{4,12},{5,5},{6,14},{7,7},{8,0},{9,17},{1... | collective-permute-start | bytes 442376 | tf_op jit(solution)/shard_map/ppermute | solution.py:596
  41.2 4.3 %collective-permute-start.15 = (bf16[2,288,128]{2,1,0:T(8,128)(2,1)S(1)}, bf16[2,288,128]{2,1,0:T(8,128)(2,1)S(1)}, u32[]{:S(2)}, u32[]{:S(2)}) collective-permute-start(bf16[2,288,128]{2,1,0:T(8,128)(2,1)S(1)} %collective-permute-done.12.refs_0_), channel_id=1, source_target_pairs={{0,1},{1,0},{2,3},{3,2},{4,5},{5,4},{6,7},{7,6},{8,9},{9,8},{10,11... | collective-permute-start | bytes 442376 | tf_op jit(solution)/shard_map/ppermute | solution.py:579
  41.3 4.2 %collective-permute-start.16 = (bf16[2,288,128]{2,1,0:T(8,128)(2,1)S(1)}, bf16[2,288,128]{2,1,0:T(8,128)(2,1)S(1)}, u32[]{:S(2)}, u32[]{:S(2)}) collective-permute-start(bf16[2,288,128]{2,1,0:T(8,128)(2,1)S(1)} %collective-permute-done.13.refs_1_), channel_id=1, source_target_pairs={{0,1},{1,0},{2,3},{3,2},{4,5},{5,4},{6,7},{7,6},{8,9},{9,8},{10,11... | collective-permute-start | bytes 442376 | tf_op jit(solution)/shard_map/ppermute | solution.py:579
  45.5 1.4 %collective-permute-start.17 = (bf16[2,288,128]{2,1,0:T(8,128)(2,1)S(1)}, bf16[2,288,128]{2,1,0:T(8,128)(2,1)S(1)}, u32[]{:S(2)}, u32[]{:S(2)}) collective-permute-start(bf16[2,288,128]{2,1,0:T(8,128)(2,1)S(1)} %collective-permute-done.14.refs_2_), channel_id=1, source_target_pairs={{0,1},{1,0},{2,3},{3,2},{4,5},{5,4},{6,7},{7,6},{8,9},{9,8},{10,11... | collective-permute-start | bytes 442376 | tf_op jit(solution)/shard_map/ppermute | solution.py:579
  48.7 2.1 %collective-permute-start.18 = (bf16[576,512]{1,0:T(8,128)(2,1)S(1)}, bf16[576,512]{1,0:T(8,128)(2,1)S(1)}, u32[]{:S(2)}, u32[]{:S(2)}) collective-permute-start(bf16[576,512]{1,0:T(8,128)(2,1)S(1)} %grads_for.4), channel_id=1, source_target_pairs={{0,1},{1,0},{2,3},{3,2},{4,5},{5,4},{6,7},{7,6},{8,9},{9,8},{10,11... | collective-permute-start | bytes 1769480 | tf_op jit(solution)/shard_map/ppermute | solution.py:579
  50.9 15.4 %collective-permute-start.20 = (bf16[576,512]{1,0:T(8,128)(2,1)S(1)}, bf16[576,512]{1,0:T(8,128)(2,1)S(1)}, u32[]{:S(2)}, u32[]{:S(2)}) collective-permute-start(bf16[576,512]{1,0:T(8,128)(2,1)S(1)} %add_convert_fusion), channel_id=1, source_target_pairs={{0,2},{1,3},{2,0},{3,1},{4,6},{5,7},{6,4},{7,5},{8,10},{9,11},{10,... | collective-permute-start | bytes 1769480 | tf_op jit(solution)/shard_map/ppermute | solution.py:579
  55.0 2.1 %collective-permute-start.19 = (bf16[576,512]{1,0:T(8,128)(2,1)S(1)}, bf16[576,512]{1,0:T(8,128)(2,1)S(1)}, u32[]{:S(2)}, u32[]{:S(2)}) collective-permute-start(bf16[576,512]{1,0:T(8,128)(2,1)S(1)} %grads_for.7), channel_id=1, source_target_pairs={{0,1},{1,0},{2,3},{3,2},{4,5},{5,4},{6,7},{7,6},{8,9},{9,8},{10,11... | collective-permute-start | bytes 1769480 | tf_op jit(solution)/shard_map/ppermute | solution.py:579

commit v5 on v4

--- a/solution.py
+++ b/solution.py
@@ -580,7 +580,7 @@
 
 
 def partner(r, bits):
-    return r ^ bits if abs((r ^ bits) - r) <= 3 else r
+    return r ^ bits if abs((r ^ bits) - r) <= 3 else r ^ {5: 2, 6: 1, 7: 1}[bits]
 
 
 def swapped(x, bits):

time: 68.5 us -> 63.3 us (0.924); the launches traced: 67.6 us -> 63.2 us
  starting transfers between devices: 25.3 us -> 20 us
  waiting for transfers between devices: 21.5 us -> 22.4 us
    ppermute x3, starting transfers between devices: 8.24 us -> 2.7 us  [swapped_by_core(): return lax.ppermute(x, ('rows', 'filt'), pairs)]
    ppermute x3, waiting for transfers between devices: 3.69 us -> 5.5 us  [swapped_by_core(): return lax.ppermute(x, ('rows', 'filt'), pairs)]
    ppermute x12, starting transfers between devices: 5.08 us -> 6.39 us  [flipped(): lax.ppermute(x, 'filt', [(i, i ^ bit) for i in range(lax.axis_size('filt'...]
    ppermute x6, starting transfers between devices: 12 us -> 10.9 us  [swapped(): return lax.ppermute(x, 'rows', [(r, partner(r, bits)) for r in range(8)])]
    ppermute x12, waiting for transfers between devices: 17.7 us -> 16.9 us  [flipped(): lax.ppermute(x, 'filt', [(i, i ^ bit) for i in range(lax.axis_size('filt'...]
  transfers between devices with their start and end apart: 21 -> 21, of which waited for: 8 -> 8; matrix products, arithmetic and copies ran while one was open for 0% -> 0% of each run, Pallas kernels for 11% -> 12%
where the time goes in v5:
time: 63.3 us; the launch traced here: 63.2 us
  waiting for transfers between devices  22.4 us (35%)
  starting transfers between devices  20 us (32%)
  Pallas kernels  19.5 us (31%)
  between operations  0.9 us (1%)
    ppermute x12, waiting for transfers between devices, flipped(): lax.ppermute(x, 'filt', [(i, i ^ bit) for i in range(lax.axis_size('filt'...  16.9 us
    ppermute x6, starting transfers between devices, swapped(): return lax.ppermute(x, 'rows', [(r, partner(r, bits)) for r in range(8)])  10.9 us
    pallas_call x1, Pallas kernels, outward_sums(): pl.pallas_call(outward_kernel, out_shape=[jax.ShapeDtypeStruct((SENT, 128...  8.22 us
    ppermute x12, starting transfers between devices, flipped(): lax.ppermute(x, 'filt', [(i, i ^ bit) for i in range(lax.axis_size('filt'...  6.39 us
    ppermute x3, waiting for transfers between devices, swapped_by_core(): return lax.ppermute(x, ('rows', 'filt'), pairs)  5.5 us
    pallas_call x4, Pallas kernels, grads_for(): pl.pallas_call(functools.partial(grad_kernel, flips), out_shape=[jax.Shap...  4.94 us
    ppermute x3, starting transfers between devices, swapped_by_core(): return lax.ppermute(x, ('rows', 'filt'), pairs)  2.7 us
    pallas_call x1, Pallas kernels, own_sums(): pl.pallas_call(own_kernel, out_shape=[jax.ShapeDtypeStruct((PIXELS, 128),...  1.72 us
  transfers between devices with their start and end apart: 21, of which 8 were waited for; matrix products, arithmetic and copies ran while one was open for 0% of the time, Pallas kernels for 12%

profile of v5, /device:TPU:0, one launch (start us, length us, event | category | flops | bytes accessed | tf_op | source)
XLA Modules:
  0.0 63.2 jit_solution(13645110331636706349)
XLA Ops:
  0.6 8.2 %outward_sums.1 = (f32[304,128]{1,0:T(8,128)S(1)}, f32[304,128]{1,0:T(8,128)S(1)}, f32[304,128]{1,0:T(8,128)S(1)}, f32[304,128]{1,0:T(8,128)S(1)}, f32[304,128]{...) custom-call(bf16[576,2048]{1,0:T(8,128)(2,1)} %bitcast.12, ...), custom_call_target="tpu_custom_call" | custom-call | tf_op jit(solution)/shard_map/outward_sums/pallas_call | solution.py:297
  8.9 3.0 %collective-permute-start.2 = (f16[304,128]{1,0:T(8,128)(2,1)S(1)}, f16[304,128]{1,0:T(8,128)(2,1)S(1)}, u32[]{:S(2)}, u32[]{:S(2)}) collective-permute-start(f16[304,128]{1,0:T(8,128)(2,1)S(1)} %convert_element_type.49), channel_id=1, source_target_pairs={{0,4},{4,0},{8,12},{12,8},{16,20},{20,16},{24,28},{28,24},{1,5},{5... | collective-permute-start | bytes 233480 | tf_op jit(solution)/shard_map/ppermute | solution.py:587
  11.9 1.6 %collective-permute-start.1 = (f16[304,128]{1,0:T(8,128)(2,1)S(1)}, f16[304,128]{1,0:T(8,128)(2,1)S(1)}, u32[]{:S(2)}, u32[]{:S(2)}) collective-permute-start(f16[304,128]{1,0:T(8,128)(2,1)S(1)} %convert_element_type.47), channel_id=1, source_target_pairs={{0,12},{4,8},{8,4},{12,0},{16,28},{20,24},{24,20},{28,16},{1,13},{... | collective-permute-start | bytes 233480 | tf_op jit(solution)/shard_map/ppermute | solution.py:587
  13.6 1.5 %collective-permute-start = (f16[304,128]{1,0:T(8,128)(2,1)S(1)}, f16[304,128]{1,0:T(8,128)(2,1)S(1)}, u32[]{:S(2)}, u32[]{:S(2)}) collective-permute-start(f16[304,128]{1,0:T(8,128)(2,1)S(1)} %convert_element_type.45), channel_id=1, source_target_pairs={{0,4},{4,0},{8,20},{12,16},{16,12},{20,8},{24,28},{28,24},{1,5},{5... | collective-permute-start | bytes 233480 | tf_op jit(solution)/shard_map/ppermute | solution.py:587
  15.1 2.7 %collective-permute-start.5 = (f16[304,128]{1,0:T(8,128)(2,1)S(1)}, f16[304,128]{1,0:T(8,128)(2,1)S(1)}, u32[]{:S(2)}, u32[]{:S(2)}) collective-permute-start(f16[304,128]{1,0:T(8,128)(2,1)S(1)} %convert_element_type.55), channel_id=1, source_target_pairs={{0,8},{4,16},{8,0},{12,24},{16,4},{20,28},{24,12},{28,20},{1,9},{5... | collective-permute-start | bytes 233480 | tf_op jit(solution)/shard_map/ppermute | solution.py:587
  17.9 2.0 %collective-permute-start.3 = (f16[304,128]{1,0:T(8,128)(2,1)S(1)}, f16[304,128]{1,0:T(8,128)(2,1)S(1)}, u32[]{:S(2)}, u32[]{:S(2)}) collective-permute-start(f16[304,128]{1,0:T(8,128)(2,1)S(1)} %convert_element_type.51), channel_id=1, source_target_pairs={{0,4},{4,0},{8,16},{12,20},{16,8},{20,12},{24,28},{28,24},{1,5},{5... | collective-permute-start | bytes 233480 | tf_op jit(solution)/shard_map/ppermute | solution.py:587
  19.9 1.7 %own_sums.1 = (f32[576,128]{1,0:T(8,128)S(1)}, f32[576,128]{1,0:T(8,128)S(1)}) custom-call(bf16[576,2048]{1,0:T(8,128)(2,1)S(1)} %get-tuple-element.21.ordered, bf16[1792,2048]{1,0:T(8,128)(2,1)S(1)} %get-tuple-element.22.weights, f32[4,64]{1,0:T(4,128)S(1)} %copy-done.2), custom_call_target="tpu_custom_call" | custom-call | flops 1000000 | bytes 10000 | tf_op jit(solution)/shard_map/own_sums/pallas_call | solution.py:338
  21.9 1.6 %collective-permute-start.8 = (bf16[576,128]{1,0:T(8,128)(2,1)S(1)}, bf16[576,128]{1,0:T(8,128)(2,1)S(1)}, u32[]{:S(2)}, u32[]{:S(2)}) collective-permute-start(bf16[576,128]{1,0:T(8,128)(2,1)S(1)} %activations.2.a0), channel_id=1, source_target_pairs={{0,2},{1,3},{2,0},{3,1},{4,6},{5,7},{6,4},{7,5},{8,10},{9,11},{10,... | collective-permute-start | bytes 442376 | tf_op jit(solution)/shard_map/ppermute | solution.py:579
  23.8 0.6 collective-permute-start.9
  24.4 0.5 collective-permute-start.7
  24.9 2.8 %collective-permute-done.8.a2 = bf16[576,128]{1,0:T(8,128)(2,1)S(1)} collective-permute-done((bf16[576,128]{1,0:T(8,128)(2,1)S(1)}, bf16[576,128]{1,0:T(8,128)(2,1)S(1)}, u32[]{:S(2)}, u32[]{:S(2)}) %collective-permute-start.8) | collective-permute-done | bytes 147488 | tf_op jit(solution)/shard_map/ppermute | solution.py:579
  27.6 1.6 %collective-permute-done.9.b2 = bf16[576,128]{1,0:T(8,128)(2,1)S(1)} collective-permute-done((bf16[576,128]{1,0:T(8,128)(2,1)S(1)}, bf16[576,128]{1,0:T(8,128)(2,1)S(1)}, u32[]{:S(2)}, u32[]{:S(2)}) %collective-permute-start.9) | collective-permute-done | bytes 147488 | tf_op jit(solution)/shard_map/ppermute | solution.py:579
  29.7 0.9 %collective-permute-done.11.b3 = bf16[576,128]{1,0:T(8,128)(2,1)S(1)} collective-permute-done((bf16[576,128]{1,0:T(8,128)(2,1)S(1)}, bf16[576,128]{1,0:T(8,128)(2,1)S(1)}, u32[]{:S(2)}, u32[]{:S(2)}) %collective-permute-start.11) | collective-permute-done | bytes 147488 | tf_op jit(solution)/shard_map/ppermute | solution.py:579
  30.6 0.8 %far_head.1 = (bf16[576,256]{1,0:T(8,128)(2,1)S(1)}, bf16[576,256]{1,0:T(8,128)(2,1)S(1)}, bf16[2,288,128]{2,1,0:T(8,128)(2,1)S(1)}, bf16[2,288,128]{2,1,0:T(8,128)(2,1)S(1)}, bf16[2,288,128]{2,1,0:T(8,128)(2,1)S(1)}) custom-call(bf16[576,128]{1,0:T(8,128)(2,1)S(1)} %activations.2.a0, bf16[576,128]{1,0:T(8,128)(2,1)S(1)} %activations.3.b0, ...), custom_call_target="tpu_custom_call" | custom-call | tf_op jit(solution)/shard_map/far_head/pallas_call | solution.py:446
  31.4 0.7 %collective-permute-start.12 = (bf16[2,288,128]{2,1,0:T(8,128)(2,1)S(1)}, bf16[2,288,128]{2,1,0:T(8,128)(2,1)S(1)}, u32[]{:S(2)}, u32[]{:S(2)}) collective-permute-start(bf16[2,288,128]{2,1,0:T(8,128)(2,1)S(1)} %get-tuple-element.34), channel_id=1, source_target_pairs={{0,4},{1,13},{2,6},{3,15},{4,0},{5,9},{6,2},{7,11},{8,12},{9,5},{1... | collective-permute-start | bytes 442376 | tf_op jit(solution)/shard_map/ppermute | solution.py:596
  32.1 1.6 %collective-permute-start.13 = (bf16[2,288,128]{2,1,0:T(8,128)(2,1)S(1)}, bf16[2,288,128]{2,1,0:T(8,128)(2,1)S(1)}, u32[]{:S(2)}, u32[]{:S(2)}) collective-permute-start(bf16[2,288,128]{2,1,0:T(8,128)(2,1)S(1)} %get-tuple-element.35), channel_id=1, source_target_pairs={{0,8},{1,5},{2,10},{3,7},{4,16},{5,1},{6,18},{7,3},{8,0},{9,21},{1... | collective-permute-start | bytes 442376 | tf_op jit(solution)/shard_map/ppermute | solution.py:596
  34.1 5.5 %collective-permute-done.12.refs_0_ = bf16[2,288,128]{2,1,0:T(8,128)(2,1)S(1)} collective-permute-done((bf16[2,288,128]{2,1,0:T(8,128)(2,1)S(1)}, bf16[2,288,128]{2,1,0:T(8,128)(2,1)S(1)}, u32[]{:S(2)}, u32[]{:S(2)}) %collective-permute-start.12) | collective-permute-done | bytes 147488 | tf_op jit(solution)/shard_map/ppermute | solution.py:596
  39.6 0.5 collective-permute-start.16
  40.1 1.1 %collective-permute-start.17 = (bf16[2,288,128]{2,1,0:T(8,128)(2,1)S(1)}, bf16[2,288,128]{2,1,0:T(8,128)(2,1)S(1)}, u32[]{:S(2)}, u32[]{:S(2)}) collective-permute-start(bf16[2,288,128]{2,1,0:T(8,128)(2,1)S(1)} %collective-permute-done.14.refs_2_), channel_id=1, source_target_pairs={{0,1},{1,0},{2,3},{3,2},{4,5},{5,4},{6,7},{7,6},{8,9},{9,8},{10,11... | collective-permute-start | bytes 442376 | tf_op jit(solution)/shard_map/ppermute | solution.py:579
  41.2 1.0 %collective-permute-done.17.refs_5_ = bf16[2,288,128]{2,1,0:T(8,128)(2,1)S(1)} collective-permute-done((bf16[2,288,128]{2,1,0:T(8,128)(2,1)S(1)}, bf16[2,288,128]{2,1,0:T(8,128)(2,1)S(1)}, u32[]{:S(2)}, u32[]{:S(2)}) %collective-permute-start.17) | collective-permute-done | bytes 147488 | tf_op jit(solution)/shard_map/ppermute | solution.py:579
  42.2 0.6 spread.1.stack
  42.8 1.2 %grads_for.4 = bf16[576,512]{1,0:T(8,128)(2,1)S(1)} custom-call(bf16[576,1792]{1,0:T(8,128)(2,1)S(1)} %spread.1.stack, bf16[1792,2048]{1,0:T(8,128)(2,1)S(1)} %get-tuple-element.22.weights), custom_call_target="tpu_custom_call" | custom-call | flops 1056964608 | bytes 1000000 | tf_op jit(solution)/shard_map/grads_for/pallas_call | solution.py:545
  44.0 0.4 collective-permute-start.18
  44.5 1.2 %grads_for.5 = bf16[576,512]{1,0:T(8,128)(2,1)S(1)} custom-call(bf16[576,1792]{1,0:T(8,128)(2,1)S(1)} %spread.1.stack, bf16[1792,2048]{1,0:T(8,128)(2,1)S(1)} %get-tuple-element.22.weights), custom_call_target="tpu_custom_call" | custom-call | flops 1056964608 | bytes 1000000 | tf_op jit(solution)/shard_map/grads_for/pallas_call | solution.py:545
  45.7 0.4 collective-permute-done.18
  46.3 1.6 %collective-permute-start.20 = (bf16[576,512]{1,0:T(8,128)(2,1)S(1)}, bf16[576,512]{1,0:T(8,128)(2,1)S(1)}, u32[]{:S(2)}, u32[]{:S(2)}) collective-permute-start(bf16[576,512]{1,0:T(8,128)(2,1)S(1)} %add_convert_fusion), channel_id=1, source_target_pairs={{0,2},{1,3},{2,0},{3,1},{4,6},{5,7},{6,4},{7,5},{8,10},{9,11},{10,... | collective-permute-start | bytes 1769480 | tf_op jit(solution)/shard_map/ppermute | solution.py:579
  47.8 1.2 %own_output.1 = bf16[576,64]{1,0:T(8,128)(2,1)} custom-call(bf16[576,256]{1,0:T(8,128)(2,1)S(1)} %get-tuple-element.38.output), custom_call_target="tpu_custom_call" | custom-call | tf_op jit(solution)/shard_map/own_output/pallas_call | solution.py:471
  49.0 1.2 %grads_for.7 = bf16[576,512]{1,0:T(8,128)(2,1)S(1)} custom-call(bf16[576,1792]{1,0:T(8,128)(2,1)S(1)} %spread.1.stack, bf16[1792,2048]{1,0:T(8,128)(2,1)S(1)} %get-tuple-element.22.weights), custom_call_target="tpu_custom_call" | custom-call | flops 1056964608 | bytes 1000000 | tf_op jit(solution)/shard_map/grads_for/pallas_call | solution.py:545
  50.4 1.2 %grads_for.6.a = bf16[576,512]{1,0:T(8,128)(2,1)S(1)} custom-call(bf16[576,1792]{1,0:T(8,128)(2,1)S(1)} %spread.1.stack, bf16[1792,2048]{1,0:T(8,128)(2,1)S(1)} %get-tuple-element.22.weights), custom_call_target="tpu_custom_call" | custom-call | flops 8455716864 | bytes 1000000 | tf_op jit(solution)/shard_map/grads_for/pallas_call | solution.py:545
  51.6 0.7 %collective-permute-done.19.b = bf16[576,512]{1,0:T(8,128)(2,1)S(1)} collective-permute-done((bf16[576,512]{1,0:T(8,128)(2,1)S(1)}, bf16[576,512]{1,0:T(8,128)(2,1)S(1)}, u32[]{:S(2)}, u32[]{:S(2)}) %collective-permute-start.19) | collective-permute-done | bytes 589856 | tf_op jit(solution)/shard_map/ppermute | solution.py:579
  52.4 9.6 %collective-permute-done.20.c = bf16[576,512]{1,0:T(8,128)(2,1)S(1)} collective-permute-done((bf16[576,512]{1,0:T(8,128)(2,1)S(1)}, bf16[576,512]{1,0:T(8,128)(2,1)S(1)}, u32[]{:S(2)}, u32[]{:S(2)}) %collective-permute-start.20) | collective-permute-done | bytes 589856 | tf_op jit(solution)/shard_map/ppermute | solution.py:579
  61.9 1.3 %last_sum.1 = bf16[576,512]{1,0:T(8,128)(2,1)} custom-call(bf16[576,512]{1,0:T(8,128)(2,1)S(1)} %grads_for.6.a, bf16[576,512]{1,0:T(8,128)(2,1)S(1)} %collective-permute-done.19.b, bf16[576,512]{1,0:T(8,128)(2,1)S(1)} %collective-permute-done.20.c), custom_call_target="tpu_custom_call" | custom-call | tf_op jit(solution)/shard_map/last_sum/pallas_call | solution.py:568
  (44 shorter events, 1.8 us)
Async XLA Ops:
  0.6 19.2 %copy-start.2 = (f32[4,64]{1,0:T(4,128)S(1)}, f32[4,64]{1,0:T(4,128)}, u32[]{:S(2)}) copy-start(f32[4,64]{1,0:T(4,128)} %bias.1) | copy-start | bytes 3076
  8.9 9.0 %collective-permute-start.2 = (f16[304,128]{1,0:T(8,128)(2,1)S(1)}, f16[304,128]{1,0:T(8,128)(2,1)S(1)}, u32[]{:S(2)}, u32[]{:S(2)}) collective-permute-start(f16[304,128]{1,0:T(8,128)(2,1)S(1)} %convert_element_type.49), channel_id=1, source_target_pairs={{0,4},{4,0},{8,12},{12,8},{16,20},{20,16},{24,28},{28,24},{1,5},{5... | collective-permute-start | bytes 233480 | tf_op jit(solution)/shard_map/ppermute | solution.py:587
  11.9 9.7 %collective-permute-start.1 = (f16[304,128]{1,0:T(8,128)(2,1)S(1)}, f16[304,128]{1,0:T(8,128)(2,1)S(1)}, u32[]{:S(2)}, u32[]{:S(2)}) collective-permute-start(f16[304,128]{1,0:T(8,128)(2,1)S(1)} %convert_element_type.47), channel_id=1, source_target_pairs={{0,12},{4,8},{8,4},{12,0},{16,28},{20,24},{24,20},{28,16},{1,13},{... | collective-permute-start | bytes 233480 | tf_op jit(solution)/shard_map/ppermute | solution.py:587
  13.6 8.1 %collective-permute-start = (f16[304,128]{1,0:T(8,128)(2,1)S(1)}, f16[304,128]{1,0:T(8,128)(2,1)S(1)}, u32[]{:S(2)}, u32[]{:S(2)}) collective-permute-start(f16[304,128]{1,0:T(8,128)(2,1)S(1)} %convert_element_type.45), channel_id=1, source_target_pairs={{0,4},{4,0},{8,20},{12,16},{16,12},{20,8},{24,28},{28,24},{1,5},{5... | collective-permute-start | bytes 233480 | tf_op jit(solution)/shard_map/ppermute | solution.py:587
  15.1 8.4 %collective-permute-start.5 = (f16[304,128]{1,0:T(8,128)(2,1)S(1)}, f16[304,128]{1,0:T(8,128)(2,1)S(1)}, u32[]{:S(2)}, u32[]{:S(2)}) collective-permute-start(f16[304,128]{1,0:T(8,128)(2,1)S(1)} %convert_element_type.55), channel_id=1, source_target_pairs={{0,8},{4,16},{8,0},{12,24},{16,4},{20,28},{24,12},{28,20},{1,9},{5... | collective-permute-start | bytes 233480 | tf_op jit(solution)/shard_map/ppermute | solution.py:587
  17.8 5.7 %collective-permute-start.4 = (f16[304,128]{1,0:T(8,128)(2,1)S(1)}, f16[304,128]{1,0:T(8,128)(2,1)S(1)}, u32[]{:S(2)}, u32[]{:S(2)}) collective-permute-start(f16[304,128]{1,0:T(8,128)(2,1)S(1)} %convert_element_type.53), channel_id=1, source_target_pairs={{0,8},{4,12},{8,0},{12,4},{16,24},{20,28},{24,16},{28,20},{1,9},{5... | collective-permute-start | bytes 233480 | tf_op jit(solution)/shard_map/ppermute | solution.py:587
  17.9 5.6 %collective-permute-start.3 = (f16[304,128]{1,0:T(8,128)(2,1)S(1)}, f16[304,128]{1,0:T(8,128)(2,1)S(1)}, u32[]{:S(2)}, u32[]{:S(2)}) collective-permute-start(f16[304,128]{1,0:T(8,128)(2,1)S(1)} %convert_element_type.51), channel_id=1, source_target_pairs={{0,4},{4,0},{8,16},{12,20},{16,8},{20,12},{24,28},{28,24},{1,5},{5... | collective-permute-start | bytes 233480 | tf_op jit(solution)/shard_map/ppermute | solution.py:587
  21.6 7.6 %copy-start = (bf16[4,256,256]{2,1,0:T(8,128)(2,1)S(1)}, bf16[4,256,256]{2,1,0:T(8,128)(2,1)}, u32[]{:S(2)}) copy-start(bf16[4,256,256]{2,1,0:T(8,128)(2,1)} %project.3) | copy-start | bytes 1572868
  21.6 7.6 %copy-start.1 = (bf16[12,48,256]{2,1,0:T(8,128)(2,1)S(1)}, bf16[12,48,256]{2,1,0:T(8,128)(2,1)}, u32[]{:S(2)}) copy-start(bf16[12,48,256]{2,1,0:T(8,128)(2,1)} %param.13) | copy-start | bytes 884740
  21.6 7.6 %copy-start.3 = (f32[256]{0:T(256)S(1)}, f32[256]{0:T(256)}, u32[]{:S(2)}) copy-start(f32[256]{0:T(256)} %param.12) | copy-start | bytes 3076
  21.9 5.7 %collective-permute-start.8 = (bf16[576,128]{1,0:T(8,128)(2,1)S(1)}, bf16[576,128]{1,0:T(8,128)(2,1)S(1)}, u32[]{:S(2)}, u32[]{:S(2)}) collective-permute-start(bf16[576,128]{1,0:T(8,128)(2,1)S(1)} %activations.2.a0), channel_id=1, source_target_pairs={{0,2},{1,3},{2,0},{3,1},{4,6},{5,7},{6,4},{7,5},{8,10},{9,11},{10,... | collective-permute-start | bytes 442376 | tf_op jit(solution)/shard_map/ppermute | solution.py:579
  23.8 5.4 %collective-permute-start.9 = (bf16[576,128]{1,0:T(8,128)(2,1)S(1)}, bf16[576,128]{1,0:T(8,128)(2,1)S(1)}, u32[]{:S(2)}, u32[]{:S(2)}) collective-permute-start(bf16[576,128]{1,0:T(8,128)(2,1)S(1)} %activations.3.b0), channel_id=1, source_target_pairs={{0,2},{1,3},{2,0},{3,1},{4,6},{5,7},{6,4},{7,5},{8,10},{9,11},{10,... | collective-permute-start | bytes 442376 | tf_op jit(solution)/shard_map/ppermute | solution.py:579
  24.4 4.9 %collective-permute-start.6 = (bf16[576,128]{1,0:T(8,128)(2,1)S(1)}, bf16[576,128]{1,0:T(8,128)(2,1)S(1)}, u32[]{:S(2)}, u32[]{:S(2)}) collective-permute-start(bf16[576,128]{1,0:T(8,128)(2,1)S(1)} %activations.2.a0), channel_id=1, source_target_pairs={{0,1},{1,0},{2,3},{3,2},{4,5},{5,4},{6,7},{7,6},{8,9},{9,8},{10,11... | collective-permute-start | bytes 442376 | tf_op jit(solution)/shard_map/ppermute | solution.py:579
  24.4 4.9 %collective-permute-start.7 = (bf16[576,128]{1,0:T(8,128)(2,1)S(1)}, bf16[576,128]{1,0:T(8,128)(2,1)S(1)}, u32[]{:S(2)}, u32[]{:S(2)}) collective-permute-start(bf16[576,128]{1,0:T(8,128)(2,1)S(1)} %activations.3.b0), channel_id=1, source_target_pairs={{0,1},{1,0},{2,3},{3,2},{4,5},{5,4},{6,7},{7,6},{8,9},{9,8},{10,11... | collective-permute-start | bytes 442376 | tf_op jit(solution)/shard_map/ppermute | solution.py:579
  27.6 2.0 %collective-permute-start.10 = (bf16[576,128]{1,0:T(8,128)(2,1)S(1)}, bf16[576,128]{1,0:T(8,128)(2,1)S(1)}, u32[]{:S(2)}, u32[]{:S(2)}) collective-permute-start(bf16[576,128]{1,0:T(8,128)(2,1)S(1)} %collective-permute-done.8.a2), channel_id=1, source_target_pairs={{0,1},{1,0},{2,3},{3,2},{4,5},{5,4},{6,7},{7,6},{8,9},{9,8},{10,11... | collective-permute-start | bytes 442376 | tf_op jit(solution)/shard_map/ppermute | solution.py:579
  29.2 1.4 %collective-permute-start.11 = (bf16[576,128]{1,0:T(8,128)(2,1)S(1)}, bf16[576,128]{1,0:T(8,128)(2,1)S(1)}, u32[]{:S(2)}, u32[]{:S(2)}) collective-permute-start(bf16[576,128]{1,0:T(8,128)(2,1)S(1)} %collective-permute-done.9.b2), channel_id=1, source_target_pairs={{0,1},{1,0},{2,3},{3,2},{4,5},{5,4},{6,7},{7,6},{8,9},{9,8},{10,11... | collective-permute-start | bytes 442376 | tf_op jit(solution)/shard_map/ppermute | solution.py:579
  31.4 8.2 %collective-permute-start.12 = (bf16[2,288,128]{2,1,0:T(8,128)(2,1)S(1)}, bf16[2,288,128]{2,1,0:T(8,128)(2,1)S(1)}, u32[]{:S(2)}, u32[]{:S(2)}) collective-permute-start(bf16[2,288,128]{2,1,0:T(8,128)(2,1)S(1)} %get-tuple-element.34), channel_id=1, source_target_pairs={{0,4},{1,13},{2,6},{3,15},{4,0},{5,9},{6,2},{7,11},{8,12},{9,5},{1... | collective-permute-start | bytes 442376 | tf_op jit(solution)/shard_map/ppermute | solution.py:596
  32.1 7.5 %collective-permute-start.13 = (bf16[2,288,128]{2,1,0:T(8,128)(2,1)S(1)}, bf16[2,288,128]{2,1,0:T(8,128)(2,1)S(1)}, u32[]{:S(2)}, u32[]{:S(2)}) collective-permute-start(bf16[2,288,128]{2,1,0:T(8,128)(2,1)S(1)} %get-tuple-element.35), channel_id=1, source_target_pairs={{0,8},{1,5},{2,10},{3,7},{4,16},{5,1},{6,18},{7,3},{8,0},{9,21},{1... | collective-permute-start | bytes 442376 | tf_op jit(solution)/shard_map/ppermute | solution.py:596
  33.7 6.4 %collective-permute-start.14 = (bf16[2,288,128]{2,1,0:T(8,128)(2,1)S(1)}, bf16[2,288,128]{2,1,0:T(8,128)(2,1)S(1)}, u32[]{:S(2)}, u32[]{:S(2)}) collective-permute-start(bf16[2,288,128]{2,1,0:T(8,128)(2,1)S(1)} %get-tuple-element.36), channel_id=1, source_target_pairs={{0,8},{1,5},{2,10},{3,7},{4,12},{5,1},{6,14},{7,3},{8,0},{9,17},{1... | collective-permute-start | bytes 442376 | tf_op jit(solution)/shard_map/ppermute | solution.py:596
  39.6 1.6 %collective-permute-start.15 = (bf16[2,288,128]{2,1,0:T(8,128)(2,1)S(1)}, bf16[2,288,128]{2,1,0:T(8,128)(2,1)S(1)}, u32[]{:S(2)}, u32[]{:S(2)}) collective-permute-start(bf16[2,288,128]{2,1,0:T(8,128)(2,1)S(1)} %collective-permute-done.12.refs_0_), channel_id=1, source_target_pairs={{0,1},{1,0},{2,3},{3,2},{4,5},{5,4},{6,7},{7,6},{8,9},{9,8},{10,11... | collective-permute-start | bytes 442376 | tf_op jit(solution)/shard_map/ppermute | solution.py:579
  39.6 1.6 %collective-permute-start.16 = (bf16[2,288,128]{2,1,0:T(8,128)(2,1)S(1)}, bf16[2,288,128]{2,1,0:T(8,128)(2,1)S(1)}, u32[]{:S(2)}, u32[]{:S(2)}) collective-permute-start(bf16[2,288,128]{2,1,0:T(8,128)(2,1)S(1)} %collective-permute-done.13.refs_1_), channel_id=1, source_target_pairs={{0,1},{1,0},{2,3},{3,2},{4,5},{5,4},{6,7},{7,6},{8,9},{9,8},{10,11... | collective-permute-start | bytes 442376 | tf_op jit(solution)/shard_map/ppermute | solution.py:579
  40.1 2.1 %collective-permute-start.17 = (bf16[2,288,128]{2,1,0:T(8,128)(2,1)S(1)}, bf16[2,288,128]{2,1,0:T(8,128)(2,1)S(1)}, u32[]{:S(2)}, u32[]{:S(2)}) collective-permute-start(bf16[2,288,128]{2,1,0:T(8,128)(2,1)S(1)} %collective-permute-done.14.refs_2_), channel_id=1, source_target_pairs={{0,1},{1,0},{2,3},{3,2},{4,5},{5,4},{6,7},{7,6},{8,9},{9,8},{10,11... | collective-permute-start | bytes 442376 | tf_op jit(solution)/shard_map/ppermute | solution.py:579
  44.0 2.1 %collective-permute-start.18 = (bf16[576,512]{1,0:T(8,128)(2,1)S(1)}, bf16[576,512]{1,0:T(8,128)(2,1)S(1)}, u32[]{:S(2)}, u32[]{:S(2)}) collective-permute-start(bf16[576,512]{1,0:T(8,128)(2,1)S(1)} %grads_for.4), channel_id=1, source_target_pairs={{0,1},{1,0},{2,3},{3,2},{4,5},{5,4},{6,7},{7,6},{8,9},{9,8},{10,11... | collective-permute-start | bytes 1769480 | tf_op jit(solution)/shard_map/ppermute | solution.py:579
  46.3 15.7 %collective-permute-start.20 = (bf16[576,512]{1,0:T(8,128)(2,1)S(1)}, bf16[576,512]{1,0:T(8,128)(2,1)S(1)}, u32[]{:S(2)}, u32[]{:S(2)}) collective-permute-start(bf16[576,512]{1,0:T(8,128)(2,1)S(1)} %add_convert_fusion), channel_id=1, source_target_pairs={{0,2},{1,3},{2,0},{3,1},{4,6},{5,7},{6,4},{7,5},{8,10},{9,11},{10,... | collective-permute-start | bytes 1769480 | tf_op jit(solution)/shard_map/ppermute | solution.py:579
  50.3 2.1 %collective-permute-start.19 = (bf16[576,512]{1,0:T(8,128)(2,1)S(1)}, bf16[576,512]{1,0:T(8,128)(2,1)S(1)}, u32[]{:S(2)}, u32[]{:S(2)}) collective-permute-start(bf16[576,512]{1,0:T(8,128)(2,1)S(1)} %grads_for.7), channel_id=1, source_target_pairs={{0,1},{1,0},{2,3},{3,2},{4,5},{5,4},{6,7},{7,6},{8,9},{9,8},{10,11... | collective-permute-start | bytes 1769480 | tf_op jit(solution)/shard_map/ppermute | solution.py:579

commit v6 on v5

--- a/solution.py
+++ b/solution.py
@@ -579,17 +579,15 @@
     return lax.ppermute(x, "filt", [(i, i ^ bit) for i in range(lax.axis_size("filt"))])
 
 
-def partner(r, bits):
-    return r ^ bits if abs((r ^ bits) - r) <= 3 else r ^ {5: 2, 6: 1, 7: 1}[bits]
-
-
-def swapped(x, bits):
-    return lax.ppermute(x, "rows", [(r, partner(r, bits)) for r in range(8)])
-
-
-def swapped_by_core(x, bits):
+def partner(r, member, bits):
+    if abs((r ^ bits) - r) <= 3:
+        return 4 * (r ^ bits) + member
+    return 4 * r + (member ^ 2)
+
+
+def swapped(x, *bits):
     pairs = [
-        (4 * r + member, 4 * partner(r, bits[member % 2]) + member)
+        (4 * r + member, partner(r, member, bits[member % len(bits)]))
         for r in range(8)
         for member in range(4)
     ]
@@ -627,7 +625,7 @@
     output, grads, *sends = far_head(
         acts, beside, across, corner, project_weight, near, ordered_cotangent
     )
-    arrived = [swapped_by_core(sends[n], swaps) for n, swaps in enumerate(GRAD_SWAPS)]
+    arrived = [swapped(sends[n], *swaps) for n, swaps in enumerate(GRAD_SWAPS)]
     handed = [flipped(x, 1) for x in arrived]
     stack = spread(grads, arrived, handed)
     (far,) = grads_for((3,), stack, weights)

time: 63.3 us -> 64.3 us (1.016)
  the two profiles are of different devices: /device:TPU:0 before, /device:TPU:2 now
where the time goes in v6:
time: 64.3 us; the launch traced here: 64.1 us
  waiting for transfers between devices  26.4 us (41%)
  Pallas kernels  19.5 us (30%)
  starting transfers between devices  16.9 us (26%)
  between operations  0.91 us (1%)
    ppermute x12, waiting for transfers between devices, flipped(): lax.ppermute(x, 'filt', [(i, i ^ bit) for i in range(lax.axis_size('filt'...  17.6 us
    ppermute x9, starting transfers between devices, swapped(): return lax.ppermute(x, ('rows', 'filt'), pairs)  12.5 us
    ppermute x9, waiting for transfers between devices, swapped(): return lax.ppermute(x, ('rows', 'filt'), pairs)  8.82 us
    pallas_call x1, Pallas kernels, outward_sums(): pl.pallas_call(outward_kernel, out_shape=[jax.ShapeDtypeStruct((SENT, 128...  8.23 us
    pallas_call x4, Pallas kernels, grads_for(): pl.pallas_call(functools.partial(grad_kernel, flips), out_shape=[jax.Shap...  4.95 us
    ppermute x12, starting transfers between devices, flipped(): lax.ppermute(x, 'filt', [(i, i ^ bit) for i in range(lax.axis_size('filt'...  4.41 us
    pallas_call x1, Pallas kernels, own_sums(): pl.pallas_call(own_kernel, out_shape=[jax.ShapeDtypeStruct((PIXELS, 128),...  1.72 us
  transfers between devices with their start and end apart: 21, of which 12 were waited for; matrix products, arithmetic and copies ran while one was open for 0% of the time, Pallas kernels for 12%

profile of v6, /device:TPU:2, one launch (start us, length us, event | category | flops | bytes accessed | tf_op | source)
XLA Modules:
  0.0 64.1 jit_solution(12942097361573376402)
XLA Ops:
  0.6 8.2 %outward_sums.1 = (f32[304,128]{1,0:T(8,128)S(1)}, f32[304,128]{1,0:T(8,128)S(1)}, f32[304,128]{1,0:T(8,128)S(1)}, f32[304,128]{1,0:T(8,128)S(1)}, f32[304,128]{...) custom-call(bf16[576,2048]{1,0:T(8,128)(2,1)} %bitcast.12, ...), custom_call_target="tpu_custom_call" | custom-call | tf_op jit(solution)/shard_map/outward_sums/pallas_call | solution.py:297
  9.0 3.1 %collective-permute-start.1 = (f16[304,128]{1,0:T(8,128)(2,1)S(1)}, f16[304,128]{1,0:T(8,128)(2,1)S(1)}, u32[]{:S(2)}, u32[]{:S(2)}) collective-permute-start(f16[304,128]{1,0:T(8,128)(2,1)S(1)} %convert_element_type.47), channel_id=1, source_target_pairs={{0,12},{1,13},{2,14},{3,15},{4,8},{5,9},{6,10},{7,11},{8,4},{9,5},... | collective-permute-start | bytes 233480 | tf_op jit(solution)/shard_map/ppermute | solution.py:594
  12.1 1.6 %collective-permute-start = (f16[304,128]{1,0:T(8,128)(2,1)S(1)}, f16[304,128]{1,0:T(8,128)(2,1)S(1)}, u32[]{:S(2)}, u32[]{:S(2)}) collective-permute-start(f16[304,128]{1,0:T(8,128)(2,1)S(1)} %convert_element_type.45), channel_id=1, source_target_pairs={{0,2},{1,3},{2,0},{3,1},{4,6},{5,7},{6,4},{7,5},{8,20},{9,21},{10,... | collective-permute-start | bytes 233480 | tf_op jit(solution)/shard_map/ppermute | solution.py:594
  13.7 1.4 %collective-permute-start.5 = (f16[304,128]{1,0:T(8,128)(2,1)S(1)}, f16[304,128]{1,0:T(8,128)(2,1)S(1)}, u32[]{:S(2)}, u32[]{:S(2)}) collective-permute-start(f16[304,128]{1,0:T(8,128)(2,1)S(1)} %convert_element_type.55), channel_id=1, source_target_pairs={{0,2},{1,3},{2,0},{3,1},{4,16},{5,17},{6,18},{7,19},{8,10},{9,11},... | collective-permute-start | bytes 233480 | tf_op jit(solution)/shard_map/ppermute | solution.py:594
  15.1 1.8 %collective-permute-start.4 = (f16[304,128]{1,0:T(8,128)(2,1)S(1)}, f16[304,128]{1,0:T(8,128)(2,1)S(1)}, u32[]{:S(2)}, u32[]{:S(2)}) collective-permute-start(f16[304,128]{1,0:T(8,128)(2,1)S(1)} %convert_element_type.53), channel_id=1, source_target_pairs={{0,8},{1,9},{2,10},{3,11},{4,12},{5,13},{6,14},{7,15},{8,0},{9,1},... | collective-permute-start | bytes 233480 | tf_op jit(solution)/shard_map/ppermute | solution.py:594
  16.9 0.6 collective-permute-start.3
  17.5 1.7 %own_sums.1 = (f32[576,128]{1,0:T(8,128)S(1)}, f32[576,128]{1,0:T(8,128)S(1)}) custom-call(bf16[576,2048]{1,0:T(8,128)(2,1)S(1)} %get-tuple-element.21.ordered, bf16[1792,2048]{1,0:T(8,128)(2,1)S(1)} %get-tuple-element.22.weights, f32[4,64]{1,0:T(4,128)S(1)} %copy-done.2), custom_call_target="tpu_custom_call" | custom-call | flops 1000000 | bytes 10000 | tf_op jit(solution)/shard_map/own_sums/pallas_call | solution.py:338
  19.5 1.6 %collective-permute-start.8 = (bf16[576,128]{1,0:T(8,128)(2,1)S(1)}, bf16[576,128]{1,0:T(8,128)(2,1)S(1)}, u32[]{:S(2)}, u32[]{:S(2)}) collective-permute-start(bf16[576,128]{1,0:T(8,128)(2,1)S(1)} %activations.2.a0), channel_id=1, source_target_pairs={{0,2},{1,3},{2,0},{3,1},{4,6},{5,7},{6,4},{7,5},{8,10},{9,11},{10,... | collective-permute-start | bytes 442376 | tf_op jit(solution)/shard_map/ppermute | solution.py:579
  21.6 0.6 collective-permute-done.3
  22.4 0.7 %collective-permute-start.9 = (bf16[576,128]{1,0:T(8,128)(2,1)S(1)}, bf16[576,128]{1,0:T(8,128)(2,1)S(1)}, u32[]{:S(2)}, u32[]{:S(2)}) collective-permute-start(bf16[576,128]{1,0:T(8,128)(2,1)S(1)} %activations.3.b0), channel_id=1, source_target_pairs={{0,2},{1,3},{2,0},{3,1},{4,6},{5,7},{6,4},{7,5},{8,10},{9,11},{10,... | collective-permute-start | bytes 442376 | tf_op jit(solution)/shard_map/ppermute | solution.py:579
  23.1 0.5 collective-permute-start.7
  23.6 2.2 %collective-permute-done.8.a2 = bf16[576,128]{1,0:T(8,128)(2,1)S(1)} collective-permute-done((bf16[576,128]{1,0:T(8,128)(2,1)S(1)}, bf16[576,128]{1,0:T(8,128)(2,1)S(1)}, u32[]{:S(2)}, u32[]{:S(2)}) %collective-permute-start.8) | collective-permute-done | bytes 147488 | tf_op jit(solution)/shard_map/ppermute | solution.py:579
  25.9 1.7 %collective-permute-done.9.b2 = bf16[576,128]{1,0:T(8,128)(2,1)S(1)} collective-permute-done((bf16[576,128]{1,0:T(8,128)(2,1)S(1)}, bf16[576,128]{1,0:T(8,128)(2,1)S(1)}, u32[]{:S(2)}, u32[]{:S(2)}) %collective-permute-start.9) | collective-permute-done | bytes 147488 | tf_op jit(solution)/shard_map/ppermute | solution.py:579
  28.1 0.9 %collective-permute-done.11.b3 = bf16[576,128]{1,0:T(8,128)(2,1)S(1)} collective-permute-done((bf16[576,128]{1,0:T(8,128)(2,1)S(1)}, bf16[576,128]{1,0:T(8,128)(2,1)S(1)}, u32[]{:S(2)}, u32[]{:S(2)}) %collective-permute-start.11) | collective-permute-done | bytes 147488 | tf_op jit(solution)/shard_map/ppermute | solution.py:579
  29.0 0.8 %far_head.1 = (bf16[576,256]{1,0:T(8,128)(2,1)S(1)}, bf16[576,256]{1,0:T(8,128)(2,1)S(1)}, bf16[2,288,128]{2,1,0:T(8,128)(2,1)S(1)}, bf16[2,288,128]{2,1,0:T(8,128)(2,1)S(1)}, bf16[2,288,128]{2,1,0:T(8,128)(2,1)S(1)}) custom-call(bf16[576,128]{1,0:T(8,128)(2,1)S(1)} %activations.2.a0, bf16[576,128]{1,0:T(8,128)(2,1)S(1)} %activations.3.b0, ...), custom_call_target="tpu_custom_call" | custom-call | tf_op jit(solution)/shard_map/far_head/pallas_call | solution.py:446
  29.8 1.7 %collective-permute-start.12 = (bf16[2,288,128]{2,1,0:T(8,128)(2,1)S(1)}, bf16[2,288,128]{2,1,0:T(8,128)(2,1)S(1)}, u32[]{:S(2)}, u32[]{:S(2)}) collective-permute-start(bf16[2,288,128]{2,1,0:T(8,128)(2,1)S(1)} %get-tuple-element.34), channel_id=1, source_target_pairs={{0,4},{1,13},{2,6},{3,15},{4,0},{5,9},{6,2},{7,11},{8,12},{9,5},{1... | collective-permute-start | bytes 442376 | tf_op jit(solution)/shard_map/ppermute | solution.py:594
  31.5 2.4 %collective-permute-start.13 = (bf16[2,288,128]{2,1,0:T(8,128)(2,1)S(1)}, bf16[2,288,128]{2,1,0:T(8,128)(2,1)S(1)}, u32[]{:S(2)}, u32[]{:S(2)}) collective-permute-start(bf16[2,288,128]{2,1,0:T(8,128)(2,1)S(1)} %get-tuple-element.35), channel_id=1, source_target_pairs={{0,2},{1,3},{2,0},{3,1},{4,16},{5,7},{6,18},{7,5},{8,10},{9,21},{1... | collective-permute-start | bytes 442376 | tf_op jit(solution)/shard_map/ppermute | solution.py:594
  33.9 2.8 %collective-permute-done.12.refs_0_ = bf16[2,288,128]{2,1,0:T(8,128)(2,1)S(1)} collective-permute-done((bf16[2,288,128]{2,1,0:T(8,128)(2,1)S(1)}, bf16[2,288,128]{2,1,0:T(8,128)(2,1)S(1)}, u32[]{:S(2)}, u32[]{:S(2)}) %collective-permute-start.12) | collective-permute-done | bytes 147488 | tf_op jit(solution)/shard_map/ppermute | solution.py:594
  36.6 5.0 %collective-permute-done.13.refs_1_ = bf16[2,288,128]{2,1,0:T(8,128)(2,1)S(1)} collective-permute-done((bf16[2,288,128]{2,1,0:T(8,128)(2,1)S(1)}, bf16[2,288,128]{2,1,0:T(8,128)(2,1)S(1)}, u32[]{:S(2)}, u32[]{:S(2)}) %collective-permute-start.13) | collective-permute-done | bytes 147488 | tf_op jit(solution)/shard_map/ppermute | solution.py:594
  41.6 0.5 collective-permute-start.17
  42.1 0.9 %collective-permute-done.16.refs_4_ = bf16[2,288,128]{2,1,0:T(8,128)(2,1)S(1)} collective-permute-done((bf16[2,288,128]{2,1,0:T(8,128)(2,1)S(1)}, bf16[2,288,128]{2,1,0:T(8,128)(2,1)S(1)}, u32[]{:S(2)}, u32[]{:S(2)}) %collective-permute-start.16) | collective-permute-done | bytes 147488 | tf_op jit(solution)/shard_map/ppermute | solution.py:579
  43.2 0.6 spread.1.stack
  43.8 1.2 %grads_for.4 = bf16[576,512]{1,0:T(8,128)(2,1)S(1)} custom-call(bf16[576,1792]{1,0:T(8,128)(2,1)S(1)} %spread.1.stack, bf16[1792,2048]{1,0:T(8,128)(2,1)S(1)} %get-tuple-element.22.weights), custom_call_target="tpu_custom_call" | custom-call | flops 1056964608 | bytes 1000000 | tf_op jit(solution)/shard_map/grads_for/pallas_call | solution.py:545
  45.4 1.2 %grads_for.5 = bf16[576,512]{1,0:T(8,128)(2,1)S(1)} custom-call(bf16[576,1792]{1,0:T(8,128)(2,1)S(1)} %spread.1.stack, bf16[1792,2048]{1,0:T(8,128)(2,1)S(1)} %get-tuple-element.22.weights), custom_call_target="tpu_custom_call" | custom-call | flops 1056964608 | bytes 1000000 | tf_op jit(solution)/shard_map/grads_for/pallas_call | solution.py:545
  46.6 0.5 collective-permute-done.18
  47.3 0.6 collective-permute-start.20
  47.9 1.2 %own_output.1 = bf16[576,64]{1,0:T(8,128)(2,1)} custom-call(bf16[576,256]{1,0:T(8,128)(2,1)S(1)} %get-tuple-element.38.output), custom_call_target="tpu_custom_call" | custom-call | tf_op jit(solution)/shard_map/own_output/pallas_call | solution.py:471
  49.1 1.2 %grads_for.7 = bf16[576,512]{1,0:T(8,128)(2,1)S(1)} custom-call(bf16[576,1792]{1,0:T(8,128)(2,1)S(1)} %spread.1.stack, bf16[1792,2048]{1,0:T(8,128)(2,1)S(1)} %get-tuple-element.22.weights), custom_call_target="tpu_custom_call" | custom-call | flops 1056964608 | bytes 1000000 | tf_op jit(solution)/shard_map/grads_for/pallas_call | solution.py:545
  50.4 1.2 %grads_for.6.a = bf16[576,512]{1,0:T(8,128)(2,1)S(1)} custom-call(bf16[576,1792]{1,0:T(8,128)(2,1)S(1)} %spread.1.stack, bf16[1792,2048]{1,0:T(8,128)(2,1)S(1)} %get-tuple-element.22.weights), custom_call_target="tpu_custom_call" | custom-call | flops 8455716864 | bytes 1000000 | tf_op jit(solution)/shard_map/grads_for/pallas_call | solution.py:545
  51.7 0.7 %collective-permute-done.19.b = bf16[576,512]{1,0:T(8,128)(2,1)S(1)} collective-permute-done((bf16[576,512]{1,0:T(8,128)(2,1)S(1)}, bf16[576,512]{1,0:T(8,128)(2,1)S(1)}, u32[]{:S(2)}, u32[]{:S(2)}) %collective-permute-start.19) | collective-permute-done | bytes 589856 | tf_op jit(solution)/shard_map/ppermute | solution.py:579
  52.4 10.4 %collective-permute-done.20.c = bf16[576,512]{1,0:T(8,128)(2,1)S(1)} collective-permute-done((bf16[576,512]{1,0:T(8,128)(2,1)S(1)}, bf16[576,512]{1,0:T(8,128)(2,1)S(1)}, u32[]{:S(2)}, u32[]{:S(2)}) %collective-permute-start.20) | collective-permute-done | bytes 589856 | tf_op jit(solution)/shard_map/ppermute | solution.py:579
  62.9 1.3 %last_sum.1 = bf16[576,512]{1,0:T(8,128)(2,1)} custom-call(bf16[576,512]{1,0:T(8,128)(2,1)S(1)} %grads_for.6.a, bf16[576,512]{1,0:T(8,128)(2,1)S(1)} %collective-permute-done.19.b, bf16[576,512]{1,0:T(8,128)(2,1)S(1)} %collective-permute-done.20.c), custom_call_target="tpu_custom_call" | custom-call | tf_op jit(solution)/shard_map/last_sum/pallas_call | solution.py:568
  (44 shorter events, 2.3 us)
Async XLA Ops:
  0.6 16.8 %copy-start.2 = (f32[4,64]{1,0:T(4,128)S(1)}, f32[4,64]{1,0:T(4,128)}, u32[]{:S(2)}) copy-start(f32[4,64]{1,0:T(4,128)} %bias.1) | copy-start | bytes 3076
  8.9 8.0 %collective-permute-start.2 = (f16[304,128]{1,0:T(8,128)(2,1)S(1)}, f16[304,128]{1,0:T(8,128)(2,1)S(1)}, u32[]{:S(2)}, u32[]{:S(2)}) collective-permute-start(f16[304,128]{1,0:T(8,128)(2,1)S(1)} %convert_element_type.49), channel_id=1, source_target_pairs={{0,4},{1,5},{2,6},{3,7},{4,0},{5,1},{6,2},{7,3},{8,12},{9,13},{10,... | collective-permute-start | bytes 233480 | tf_op jit(solution)/shard_map/ppermute | solution.py:594
  9.0 10.3 %collective-permute-start.1 = (f16[304,128]{1,0:T(8,128)(2,1)S(1)}, f16[304,128]{1,0:T(8,128)(2,1)S(1)}, u32[]{:S(2)}, u32[]{:S(2)}) collective-permute-start(f16[304,128]{1,0:T(8,128)(2,1)S(1)} %convert_element_type.47), channel_id=1, source_target_pairs={{0,12},{1,13},{2,14},{3,15},{4,8},{5,9},{6,10},{7,11},{8,4},{9,5},... | collective-permute-start | bytes 233480 | tf_op jit(solution)/shard_map/ppermute | solution.py:594
  12.1 7.2 %collective-permute-start = (f16[304,128]{1,0:T(8,128)(2,1)S(1)}, f16[304,128]{1,0:T(8,128)(2,1)S(1)}, u32[]{:S(2)}, u32[]{:S(2)}) collective-permute-start(f16[304,128]{1,0:T(8,128)(2,1)S(1)} %convert_element_type.45), channel_id=1, source_target_pairs={{0,2},{1,3},{2,0},{3,1},{4,6},{5,7},{6,4},{7,5},{8,20},{9,21},{10,... | collective-permute-start | bytes 233480 | tf_op jit(solution)/shard_map/ppermute | solution.py:594
  13.7 7.8 %collective-permute-start.5 = (f16[304,128]{1,0:T(8,128)(2,1)S(1)}, f16[304,128]{1,0:T(8,128)(2,1)S(1)}, u32[]{:S(2)}, u32[]{:S(2)}) collective-permute-start(f16[304,128]{1,0:T(8,128)(2,1)S(1)} %convert_element_type.55), channel_id=1, source_target_pairs={{0,2},{1,3},{2,0},{3,1},{4,16},{5,17},{6,18},{7,19},{8,10},{9,11},... | collective-permute-start | bytes 233480 | tf_op jit(solution)/shard_map/ppermute | solution.py:594
  15.1 6.5 %collective-permute-start.4 = (f16[304,128]{1,0:T(8,128)(2,1)S(1)}, f16[304,128]{1,0:T(8,128)(2,1)S(1)}, u32[]{:S(2)}, u32[]{:S(2)}) collective-permute-start(f16[304,128]{1,0:T(8,128)(2,1)S(1)} %convert_element_type.53), channel_id=1, source_target_pairs={{0,8},{1,9},{2,10},{3,11},{4,12},{5,13},{6,14},{7,15},{8,0},{9,1},... | collective-permute-start | bytes 233480 | tf_op jit(solution)/shard_map/ppermute | solution.py:594
  16.9 5.3 %collective-permute-start.3 = (f16[304,128]{1,0:T(8,128)(2,1)S(1)}, f16[304,128]{1,0:T(8,128)(2,1)S(1)}, u32[]{:S(2)}, u32[]{:S(2)}) collective-permute-start(f16[304,128]{1,0:T(8,128)(2,1)S(1)} %convert_element_type.51), channel_id=1, source_target_pairs={{0,2},{1,3},{2,0},{3,1},{4,6},{5,7},{6,4},{7,5},{8,16},{9,17},{10,... | collective-permute-start | bytes 233480 | tf_op jit(solution)/shard_map/ppermute | solution.py:594
  19.2 8.4 %copy-start = (bf16[4,256,256]{2,1,0:T(8,128)(2,1)S(1)}, bf16[4,256,256]{2,1,0:T(8,128)(2,1)}, u32[]{:S(2)}) copy-start(bf16[4,256,256]{2,1,0:T(8,128)(2,1)} %project.3) | copy-start | bytes 1572868
  19.2 8.4 %copy-start.1 = (bf16[12,48,256]{2,1,0:T(8,128)(2,1)S(1)}, bf16[12,48,256]{2,1,0:T(8,128)(2,1)}, u32[]{:S(2)}) copy-start(bf16[12,48,256]{2,1,0:T(8,128)(2,1)} %param.13) | copy-start | bytes 884740
  19.2 8.4 %copy-start.3 = (f32[256]{0:T(256)S(1)}, f32[256]{0:T(256)}, u32[]{:S(2)}) copy-start(f32[256]{0:T(256)} %param.12) | copy-start | bytes 3076
  19.5 6.4 %collective-permute-start.8 = (bf16[576,128]{1,0:T(8,128)(2,1)S(1)}, bf16[576,128]{1,0:T(8,128)(2,1)S(1)}, u32[]{:S(2)}, u32[]{:S(2)}) collective-permute-start(bf16[576,128]{1,0:T(8,128)(2,1)S(1)} %activations.2.a0), channel_id=1, source_target_pairs={{0,2},{1,3},{2,0},{3,1},{4,6},{5,7},{6,4},{7,5},{8,10},{9,11},{10,... | collective-permute-start | bytes 442376 | tf_op jit(solution)/shard_map/ppermute | solution.py:579
  22.4 5.2 %collective-permute-start.9 = (bf16[576,128]{1,0:T(8,128)(2,1)S(1)}, bf16[576,128]{1,0:T(8,128)(2,1)S(1)}, u32[]{:S(2)}, u32[]{:S(2)}) collective-permute-start(bf16[576,128]{1,0:T(8,128)(2,1)S(1)} %activations.3.b0), channel_id=1, source_target_pairs={{0,2},{1,3},{2,0},{3,1},{4,6},{5,7},{6,4},{7,5},{8,10},{9,11},{10,... | collective-permute-start | bytes 442376 | tf_op jit(solution)/shard_map/ppermute | solution.py:579
  23.1 4.5 %collective-permute-start.6 = (bf16[576,128]{1,0:T(8,128)(2,1)S(1)}, bf16[576,128]{1,0:T(8,128)(2,1)S(1)}, u32[]{:S(2)}, u32[]{:S(2)}) collective-permute-start(bf16[576,128]{1,0:T(8,128)(2,1)S(1)} %activations.2.a0), channel_id=1, source_target_pairs={{0,1},{1,0},{2,3},{3,2},{4,5},{5,4},{6,7},{7,6},{8,9},{9,8},{10,11... | collective-permute-start | bytes 442376 | tf_op jit(solution)/shard_map/ppermute | solution.py:579
  23.1 4.5 %collective-permute-start.7 = (bf16[576,128]{1,0:T(8,128)(2,1)S(1)}, bf16[576,128]{1,0:T(8,128)(2,1)S(1)}, u32[]{:S(2)}, u32[]{:S(2)}) collective-permute-start(bf16[576,128]{1,0:T(8,128)(2,1)S(1)} %activations.3.b0), channel_id=1, source_target_pairs={{0,1},{1,0},{2,3},{3,2},{4,5},{5,4},{6,7},{7,6},{8,9},{9,8},{10,11... | collective-permute-start | bytes 442376 | tf_op jit(solution)/shard_map/ppermute | solution.py:579
  25.9 2.2 %collective-permute-start.10 = (bf16[576,128]{1,0:T(8,128)(2,1)S(1)}, bf16[576,128]{1,0:T(8,128)(2,1)S(1)}, u32[]{:S(2)}, u32[]{:S(2)}) collective-permute-start(bf16[576,128]{1,0:T(8,128)(2,1)S(1)} %collective-permute-done.8.a2), channel_id=1, source_target_pairs={{0,1},{1,0},{2,3},{3,2},{4,5},{5,4},{6,7},{7,6},{8,9},{9,8},{10,11... | collective-permute-start | bytes 442376 | tf_op jit(solution)/shard_map/ppermute | solution.py:579
  27.6 1.4 %collective-permute-start.11 = (bf16[576,128]{1,0:T(8,128)(2,1)S(1)}, bf16[576,128]{1,0:T(8,128)(2,1)S(1)}, u32[]{:S(2)}, u32[]{:S(2)}) collective-permute-start(bf16[576,128]{1,0:T(8,128)(2,1)S(1)} %collective-permute-done.9.b2), channel_id=1, source_target_pairs={{0,1},{1,0},{2,3},{3,2},{4,5},{5,4},{6,7},{7,6},{8,9},{9,8},{10,11... | collective-permute-start | bytes 442376 | tf_op jit(solution)/shard_map/ppermute | solution.py:579
  29.8 6.8 %collective-permute-start.12 = (bf16[2,288,128]{2,1,0:T(8,128)(2,1)S(1)}, bf16[2,288,128]{2,1,0:T(8,128)(2,1)S(1)}, u32[]{:S(2)}, u32[]{:S(2)}) collective-permute-start(bf16[2,288,128]{2,1,0:T(8,128)(2,1)S(1)} %get-tuple-element.34), channel_id=1, source_target_pairs={{0,4},{1,13},{2,6},{3,15},{4,0},{5,9},{6,2},{7,11},{8,12},{9,5},{1... | collective-permute-start | bytes 442376 | tf_op jit(solution)/shard_map/ppermute | solution.py:594
  31.5 10.1 %collective-permute-start.13 = (bf16[2,288,128]{2,1,0:T(8,128)(2,1)S(1)}, bf16[2,288,128]{2,1,0:T(8,128)(2,1)S(1)}, u32[]{:S(2)}, u32[]{:S(2)}) collective-permute-start(bf16[2,288,128]{2,1,0:T(8,128)(2,1)S(1)} %get-tuple-element.35), channel_id=1, source_target_pairs={{0,2},{1,3},{2,0},{3,1},{4,16},{5,7},{6,18},{7,5},{8,10},{9,21},{1... | collective-permute-start | bytes 442376 | tf_op jit(solution)/shard_map/ppermute | solution.py:594
  33.9 7.8 %collective-permute-start.14 = (bf16[2,288,128]{2,1,0:T(8,128)(2,1)S(1)}, bf16[2,288,128]{2,1,0:T(8,128)(2,1)S(1)}, u32[]{:S(2)}, u32[]{:S(2)}) collective-permute-start(bf16[2,288,128]{2,1,0:T(8,128)(2,1)S(1)} %get-tuple-element.36), channel_id=1, source_target_pairs={{0,8},{1,3},{2,10},{3,1},{4,12},{5,7},{6,14},{7,5},{8,0},{9,17},{1... | collective-permute-start | bytes 442376 | tf_op jit(solution)/shard_map/ppermute | solution.py:594
  36.6 5.5 %collective-permute-start.15 = (bf16[2,288,128]{2,1,0:T(8,128)(2,1)S(1)}, bf16[2,288,128]{2,1,0:T(8,128)(2,1)S(1)}, u32[]{:S(2)}, u32[]{:S(2)}) collective-permute-start(bf16[2,288,128]{2,1,0:T(8,128)(2,1)S(1)} %collective-permute-done.12.refs_0_), channel_id=1, source_target_pairs={{0,1},{1,0},{2,3},{3,2},{4,5},{5,4},{6,7},{7,6},{8,9},{9,8},{10,11... | collective-permute-start | bytes 442376 | tf_op jit(solution)/shard_map/ppermute | solution.py:579
  41.6 1.4 %collective-permute-start.16 = (bf16[2,288,128]{2,1,0:T(8,128)(2,1)S(1)}, bf16[2,288,128]{2,1,0:T(8,128)(2,1)S(1)}, u32[]{:S(2)}, u32[]{:S(2)}) collective-permute-start(bf16[2,288,128]{2,1,0:T(8,128)(2,1)S(1)} %collective-permute-done.13.refs_1_), channel_id=1, source_target_pairs={{0,1},{1,0},{2,3},{3,2},{4,5},{5,4},{6,7},{7,6},{8,9},{9,8},{10,11... | collective-permute-start | bytes 442376 | tf_op jit(solution)/shard_map/ppermute | solution.py:579
  41.6 1.6 %collective-permute-start.17 = (bf16[2,288,128]{2,1,0:T(8,128)(2,1)S(1)}, bf16[2,288,128]{2,1,0:T(8,128)(2,1)S(1)}, u32[]{:S(2)}, u32[]{:S(2)}) collective-permute-start(bf16[2,288,128]{2,1,0:T(8,128)(2,1)S(1)} %collective-permute-done.14.refs_2_), channel_id=1, source_target_pairs={{0,1},{1,0},{2,3},{3,2},{4,5},{5,4},{6,7},{7,6},{8,9},{9,8},{10,11... | collective-permute-start | bytes 442376 | tf_op jit(solution)/shard_map/ppermute | solution.py:579
  45.0 2.1 %collective-permute-start.18 = (bf16[576,512]{1,0:T(8,128)(2,1)S(1)}, bf16[576,512]{1,0:T(8,128)(2,1)S(1)}, u32[]{:S(2)}, u32[]{:S(2)}) collective-permute-start(bf16[576,512]{1,0:T(8,128)(2,1)S(1)} %grads_for.4), channel_id=1, source_target_pairs={{0,1},{1,0},{2,3},{3,2},{4,5},{5,4},{6,7},{7,6},{8,9},{9,8},{10,11... | collective-permute-start | bytes 1769480 | tf_op jit(solution)/shard_map/ppermute | solution.py:579
  47.3 15.6 %collective-permute-start.20 = (bf16[576,512]{1,0:T(8,128)(2,1)S(1)}, bf16[576,512]{1,0:T(8,128)(2,1)S(1)}, u32[]{:S(2)}, u32[]{:S(2)}) collective-permute-start(bf16[576,512]{1,0:T(8,128)(2,1)S(1)} %add_convert_fusion), channel_id=1, source_target_pairs={{0,2},{1,3},{2,0},{3,1},{4,6},{5,7},{6,4},{7,5},{8,10},{9,11},{10,... | collective-permute-start | bytes 1769480 | tf_op jit(solution)/shard_map/ppermute | solution.py:579
  50.3 2.1 %collective-permute-start.19 = (bf16[576,512]{1,0:T(8,128)(2,1)S(1)}, bf16[576,512]{1,0:T(8,128)(2,1)S(1)}, u32[]{:S(2)}, u32[]{:S(2)}) collective-permute-start(bf16[576,512]{1,0:T(8,128)(2,1)S(1)} %grads_for.7), channel_id=1, source_target_pairs={{0,1},{1,0},{2,3},{3,2},{4,5},{5,4},{6,7},{7,6},{8,9},{9,8},{10,11... | collective-permute-start | bytes 1769480 | tf_op jit(solution)/shard_map/ppermute | solution.py:579

commit v7 on v5

--- a/solution.py
+++ b/solution.py
@@ -156,7 +156,7 @@
 PARTS = ((0, 1), (2, 3))
 PART_SWAPS = ((7, 3, 1), (6, 2, 5, 7, 3))
 SWAPS = (1, 3, 7, 5, 2, 6)
-GRAD_SWAPS = ((1, 3), (5, 7), (2, 6))
+GRAD_SWAPS = ((5, 7), (2, 6), (1, 3))
 
 
 def fits(mesh):

time: 63.3 us -> 64 us (1.011)
  starting transfers between devices: 20 us -> 20.8 us
    ppermute x3, starting transfers between devices: 2.7 us -> 4.68 us  [swapped_by_core(): return lax.ppermute(x, ('rows', 'filt'), pairs)]
    ppermute x12, starting transfers between devices: 6.39 us -> 5.23 us  [flipped(): lax.ppermute(x, 'filt', [(i, i ^ bit) for i in range(lax.axis_size('filt'...]
  transfers between devices with their start and end apart: 21 -> 21, of which waited for: 8 -> 10; matrix products, arithmetic and copies ran while one was open for 0% -> 0% of each run, Pallas kernels for 12% -> 12%
where the time goes in v7:
time: 64 us; the launch traced here: 63.9 us
  waiting for transfers between devices  22.3 us (35%)
  starting transfers between devices  20.8 us (32%)
  Pallas kernels  19.5 us (30%)
  between operations  0.91 us (1%)
    ppermute x12, waiting for transfers between devices, flipped(): lax.ppermute(x, 'filt', [(i, i ^ bit) for i in range(lax.axis_size('filt'...  17 us
    ppermute x6, starting transfers between devices, swapped(): return lax.ppermute(x, 'rows', [(r, partner(r, bits)) for r in range(8)])  10.9 us
    pallas_call x1, Pallas kernels, outward_sums(): pl.pallas_call(outward_kernel, out_shape=[jax.ShapeDtypeStruct((SENT, 128...  8.22 us
    ppermute x3, waiting for transfers between devices, swapped_by_core(): return lax.ppermute(x, ('rows', 'filt'), pairs)  5.27 us
    ppermute x12, starting transfers between devices, flipped(): lax.ppermute(x, 'filt', [(i, i ^ bit) for i in range(lax.axis_size('filt'...  5.23 us
    pallas_call x4, Pallas kernels, grads_for(): pl.pallas_call(functools.partial(grad_kernel, flips), out_shape=[jax.Shap...  4.94 us
    ppermute x3, starting transfers between devices, swapped_by_core(): return lax.ppermute(x, ('rows', 'filt'), pairs)  4.68 us
    pallas_call x1, Pallas kernels, own_sums(): pl.pallas_call(own_kernel, out_shape=[jax.ShapeDtypeStruct((PIXELS, 128),...  1.72 us
  transfers between devices with their start and end apart: 21, of which 10 were waited for; matrix products, arithmetic and copies ran while one was open for 0% of the time, Pallas kernels for 12%

profile of v7, /device:TPU:0, one launch (start us, length us, event | category | flops | bytes accessed | tf_op | source)
XLA Modules:
  0.0 63.9 jit_solution(16750760594688117336)
XLA Ops:
  0.6 8.2 %outward_sums.1 = (f32[304,128]{1,0:T(8,128)S(1)}, f32[304,128]{1,0:T(8,128)S(1)}, f32[304,128]{1,0:T(8,128)S(1)}, f32[304,128]{1,0:T(8,128)S(1)}, f32[304,128]{...) custom-call(bf16[576,2048]{1,0:T(8,128)(2,1)} %bitcast.12, ...), custom_call_target="tpu_custom_call" | custom-call | tf_op jit(solution)/shard_map/outward_sums/pallas_call | solution.py:297
  8.9 3.0 %collective-permute-start.2 = (f16[304,128]{1,0:T(8,128)(2,1)S(1)}, f16[304,128]{1,0:T(8,128)(2,1)S(1)}, u32[]{:S(2)}, u32[]{:S(2)}) collective-permute-start(f16[304,128]{1,0:T(8,128)(2,1)S(1)} %convert_element_type.49), channel_id=1, source_target_pairs={{0,4},{4,0},{8,12},{12,8},{16,20},{20,16},{24,28},{28,24},{1,5},{5... | collective-permute-start | bytes 233480 | tf_op jit(solution)/shard_map/ppermute | solution.py:587
  11.9 1.6 %collective-permute-start.1 = (f16[304,128]{1,0:T(8,128)(2,1)S(1)}, f16[304,128]{1,0:T(8,128)(2,1)S(1)}, u32[]{:S(2)}, u32[]{:S(2)}) collective-permute-start(f16[304,128]{1,0:T(8,128)(2,1)S(1)} %convert_element_type.47), channel_id=1, source_target_pairs={{0,12},{4,8},{8,4},{12,0},{16,28},{20,24},{24,20},{28,16},{1,13},{... | collective-permute-start | bytes 233480 | tf_op jit(solution)/shard_map/ppermute | solution.py:587
  13.6 1.5 %collective-permute-start = (f16[304,128]{1,0:T(8,128)(2,1)S(1)}, f16[304,128]{1,0:T(8,128)(2,1)S(1)}, u32[]{:S(2)}, u32[]{:S(2)}) collective-permute-start(f16[304,128]{1,0:T(8,128)(2,1)S(1)} %convert_element_type.45), channel_id=1, source_target_pairs={{0,4},{4,0},{8,20},{12,16},{16,12},{20,8},{24,28},{28,24},{1,5},{5... | collective-permute-start | bytes 233480 | tf_op jit(solution)/shard_map/ppermute | solution.py:587
  15.1 2.7 %collective-permute-start.5 = (f16[304,128]{1,0:T(8,128)(2,1)S(1)}, f16[304,128]{1,0:T(8,128)(2,1)S(1)}, u32[]{:S(2)}, u32[]{:S(2)}) collective-permute-start(f16[304,128]{1,0:T(8,128)(2,1)S(1)} %convert_element_type.55), channel_id=1, source_target_pairs={{0,8},{4,16},{8,0},{12,24},{16,4},{20,28},{24,12},{28,20},{1,9},{5... | collective-permute-start | bytes 233480 | tf_op jit(solution)/shard_map/ppermute | solution.py:587
  17.9 2.0 %collective-permute-start.3 = (f16[304,128]{1,0:T(8,128)(2,1)S(1)}, f16[304,128]{1,0:T(8,128)(2,1)S(1)}, u32[]{:S(2)}, u32[]{:S(2)}) collective-permute-start(f16[304,128]{1,0:T(8,128)(2,1)S(1)} %convert_element_type.51), channel_id=1, source_target_pairs={{0,4},{4,0},{8,16},{12,20},{16,8},{20,12},{24,28},{28,24},{1,5},{5... | collective-permute-start | bytes 233480 | tf_op jit(solution)/shard_map/ppermute | solution.py:587
  19.9 1.7 %own_sums.1 = (f32[576,128]{1,0:T(8,128)S(1)}, f32[576,128]{1,0:T(8,128)S(1)}) custom-call(bf16[576,2048]{1,0:T(8,128)(2,1)S(1)} %get-tuple-element.21.ordered, bf16[1792,2048]{1,0:T(8,128)(2,1)S(1)} %get-tuple-element.22.weights, f32[4,64]{1,0:T(4,128)S(1)} %copy-done.2), custom_call_target="tpu_custom_call" | custom-call | flops 1000000 | bytes 10000 | tf_op jit(solution)/shard_map/own_sums/pallas_call | solution.py:338
  21.9 1.6 %collective-permute-start.8 = (bf16[576,128]{1,0:T(8,128)(2,1)S(1)}, bf16[576,128]{1,0:T(8,128)(2,1)S(1)}, u32[]{:S(2)}, u32[]{:S(2)}) collective-permute-start(bf16[576,128]{1,0:T(8,128)(2,1)S(1)} %activations.2.a0), channel_id=1, source_target_pairs={{0,2},{1,3},{2,0},{3,1},{4,6},{5,7},{6,4},{7,5},{8,10},{9,11},{10,... | collective-permute-start | bytes 442376 | tf_op jit(solution)/shard_map/ppermute | solution.py:579
  23.8 0.6 collective-permute-start.9
  24.4 0.5 collective-permute-start.7
  24.9 2.8 %collective-permute-done.8.a2 = bf16[576,128]{1,0:T(8,128)(2,1)S(1)} collective-permute-done((bf16[576,128]{1,0:T(8,128)(2,1)S(1)}, bf16[576,128]{1,0:T(8,128)(2,1)S(1)}, u32[]{:S(2)}, u32[]{:S(2)}) %collective-permute-start.8) | collective-permute-done | bytes 147488 | tf_op jit(solution)/shard_map/ppermute | solution.py:579
  27.6 1.6 %collective-permute-done.9.b2 = bf16[576,128]{1,0:T(8,128)(2,1)S(1)} collective-permute-done((bf16[576,128]{1,0:T(8,128)(2,1)S(1)}, bf16[576,128]{1,0:T(8,128)(2,1)S(1)}, u32[]{:S(2)}, u32[]{:S(2)}) %collective-permute-start.9) | collective-permute-done | bytes 147488 | tf_op jit(solution)/shard_map/ppermute | solution.py:579
  29.2 0.4 near_head.1
  29.7 0.9 %collective-permute-done.11.b3 = bf16[576,128]{1,0:T(8,128)(2,1)S(1)} collective-permute-done((bf16[576,128]{1,0:T(8,128)(2,1)S(1)}, bf16[576,128]{1,0:T(8,128)(2,1)S(1)}, u32[]{:S(2)}, u32[]{:S(2)}) %collective-permute-start.11) | collective-permute-done | bytes 147488 | tf_op jit(solution)/shard_map/ppermute | solution.py:579
  30.6 0.8 %far_head.1 = (bf16[576,256]{1,0:T(8,128)(2,1)S(1)}, bf16[576,256]{1,0:T(8,128)(2,1)S(1)}, bf16[2,288,128]{2,1,0:T(8,128)(2,1)S(1)}, bf16[2,288,128]{2,1,0:T(8,128)(2,1)S(1)}, bf16[2,288,128]{2,1,0:T(8,128)(2,1)S(1)}) custom-call(bf16[576,128]{1,0:T(8,128)(2,1)S(1)} %activations.2.a0, bf16[576,128]{1,0:T(8,128)(2,1)S(1)} %activations.3.b0, ...), custom_call_target="tpu_custom_call" | custom-call | tf_op jit(solution)/shard_map/far_head/pallas_call | solution.py:446
  31.4 1.8 %collective-permute-start.12 = (bf16[2,288,128]{2,1,0:T(8,128)(2,1)S(1)}, bf16[2,288,128]{2,1,0:T(8,128)(2,1)S(1)}, u32[]{:S(2)}, u32[]{:S(2)}) collective-permute-start(bf16[2,288,128]{2,1,0:T(8,128)(2,1)S(1)} %get-tuple-element.34), channel_id=1, source_target_pairs={{0,8},{1,5},{2,10},{3,7},{4,16},{5,1},{6,18},{7,3},{8,0},{9,21},{1... | collective-permute-start | bytes 442376 | tf_op jit(solution)/shard_map/ppermute | solution.py:596
  33.5 2.6 %collective-permute-start.14 = (bf16[2,288,128]{2,1,0:T(8,128)(2,1)S(1)}, bf16[2,288,128]{2,1,0:T(8,128)(2,1)S(1)}, u32[]{:S(2)}, u32[]{:S(2)}) collective-permute-start(bf16[2,288,128]{2,1,0:T(8,128)(2,1)S(1)} %get-tuple-element.36), channel_id=1, source_target_pairs={{0,4},{1,13},{2,6},{3,15},{4,0},{5,9},{6,2},{7,11},{8,12},{9,5},{1... | collective-permute-start | bytes 442376 | tf_op jit(solution)/shard_map/ppermute | solution.py:596
  36.1 2.2 %collective-permute-done.12.refs_0_ = bf16[2,288,128]{2,1,0:T(8,128)(2,1)S(1)} collective-permute-done((bf16[2,288,128]{2,1,0:T(8,128)(2,1)S(1)}, bf16[2,288,128]{2,1,0:T(8,128)(2,1)S(1)}, u32[]{:S(2)}, u32[]{:S(2)}) %collective-permute-start.12) | collective-permute-done | bytes 147488 | tf_op jit(solution)/shard_map/ppermute | solution.py:596
  38.3 3.0 %collective-permute-done.13.refs_1_ = bf16[2,288,128]{2,1,0:T(8,128)(2,1)S(1)} collective-permute-done((bf16[2,288,128]{2,1,0:T(8,128)(2,1)S(1)}, bf16[2,288,128]{2,1,0:T(8,128)(2,1)S(1)}, u32[]{:S(2)}, u32[]{:S(2)}) %collective-permute-start.13) | collective-permute-done | bytes 147488 | tf_op jit(solution)/shard_map/ppermute | solution.py:596
  41.4 0.5 collective-permute-start.17
  41.9 0.9 %collective-permute-done.16.refs_4_ = bf16[2,288,128]{2,1,0:T(8,128)(2,1)S(1)} collective-permute-done((bf16[2,288,128]{2,1,0:T(8,128)(2,1)S(1)}, bf16[2,288,128]{2,1,0:T(8,128)(2,1)S(1)}, u32[]{:S(2)}, u32[]{:S(2)}) %collective-permute-start.16) | collective-permute-done | bytes 147488 | tf_op jit(solution)/shard_map/ppermute | solution.py:579
  43.0 0.6 spread.1.stack
  43.5 1.2 %grads_for.4 = bf16[576,512]{1,0:T(8,128)(2,1)S(1)} custom-call(bf16[576,1792]{1,0:T(8,128)(2,1)S(1)} %spread.1.stack, bf16[1792,2048]{1,0:T(8,128)(2,1)S(1)} %get-tuple-element.22.weights), custom_call_target="tpu_custom_call" | custom-call | flops 1056964608 | bytes 1000000 | tf_op jit(solution)/shard_map/grads_for/pallas_call | solution.py:545
  45.1 1.2 %grads_for.5 = bf16[576,512]{1,0:T(8,128)(2,1)S(1)} custom-call(bf16[576,1792]{1,0:T(8,128)(2,1)S(1)} %spread.1.stack, bf16[1792,2048]{1,0:T(8,128)(2,1)S(1)} %get-tuple-element.22.weights), custom_call_target="tpu_custom_call" | custom-call | flops 1056964608 | bytes 1000000 | tf_op jit(solution)/shard_map/grads_for/pallas_call | solution.py:545
  46.4 0.5 collective-permute-done.18
  47.0 1.6 %collective-permute-start.20 = (bf16[576,512]{1,0:T(8,128)(2,1)S(1)}, bf16[576,512]{1,0:T(8,128)(2,1)S(1)}, u32[]{:S(2)}, u32[]{:S(2)}) collective-permute-start(bf16[576,512]{1,0:T(8,128)(2,1)S(1)} %add_convert_fusion), channel_id=1, source_target_pairs={{0,2},{1,3},{2,0},{3,1},{4,6},{5,7},{6,4},{7,5},{8,10},{9,11},{10,... | collective-permute-start | bytes 1769480 | tf_op jit(solution)/shard_map/ppermute | solution.py:579
  48.6 1.2 %own_output.1 = bf16[576,64]{1,0:T(8,128)(2,1)} custom-call(bf16[576,256]{1,0:T(8,128)(2,1)S(1)} %get-tuple-element.38.output), custom_call_target="tpu_custom_call" | custom-call | tf_op jit(solution)/shard_map/own_output/pallas_call | solution.py:471
  49.8 1.2 %grads_for.7 = bf16[576,512]{1,0:T(8,128)(2,1)S(1)} custom-call(bf16[576,1792]{1,0:T(8,128)(2,1)S(1)} %spread.1.stack, bf16[1792,2048]{1,0:T(8,128)(2,1)S(1)} %get-tuple-element.22.weights), custom_call_target="tpu_custom_call" | custom-call | flops 1056964608 | bytes 1000000 | tf_op jit(solution)/shard_map/grads_for/pallas_call | solution.py:545
  51.1 1.2 %grads_for.6.a = bf16[576,512]{1,0:T(8,128)(2,1)S(1)} custom-call(bf16[576,1792]{1,0:T(8,128)(2,1)S(1)} %spread.1.stack, bf16[1792,2048]{1,0:T(8,128)(2,1)S(1)} %get-tuple-element.22.weights), custom_call_target="tpu_custom_call" | custom-call | flops 8455716864 | bytes 1000000 | tf_op jit(solution)/shard_map/grads_for/pallas_call | solution.py:545
  52.4 0.7 %collective-permute-done.19.b = bf16[576,512]{1,0:T(8,128)(2,1)S(1)} collective-permute-done((bf16[576,512]{1,0:T(8,128)(2,1)S(1)}, bf16[576,512]{1,0:T(8,128)(2,1)S(1)}, u32[]{:S(2)}, u32[]{:S(2)}) %collective-permute-start.19) | collective-permute-done | bytes 589856 | tf_op jit(solution)/shard_map/ppermute | solution.py:579
  53.1 9.5 %collective-permute-done.20.c = bf16[576,512]{1,0:T(8,128)(2,1)S(1)} collective-permute-done((bf16[576,512]{1,0:T(8,128)(2,1)S(1)}, bf16[576,512]{1,0:T(8,128)(2,1)S(1)}, u32[]{:S(2)}, u32[]{:S(2)}) %collective-permute-start.20) | collective-permute-done | bytes 589856 | tf_op jit(solution)/shard_map/ppermute | solution.py:579
  62.6 1.3 %last_sum.1 = bf16[576,512]{1,0:T(8,128)(2,1)} custom-call(bf16[576,512]{1,0:T(8,128)(2,1)S(1)} %grads_for.6.a, bf16[576,512]{1,0:T(8,128)(2,1)S(1)} %collective-permute-done.19.b, bf16[576,512]{1,0:T(8,128)(2,1)S(1)} %collective-permute-done.20.c), custom_call_target="tpu_custom_call" | custom-call | tf_op jit(solution)/shard_map/last_sum/pallas_call | solution.py:568
  (44 shorter events, 1.7 us)
Async XLA Ops:
  0.6 19.2 %copy-start.2 = (f32[4,64]{1,0:T(4,128)S(1)}, f32[4,64]{1,0:T(4,128)}, u32[]{:S(2)}) copy-start(f32[4,64]{1,0:T(4,128)} %bias.1) | copy-start | bytes 3076
  8.9 9.0 %collective-permute-start.2 = (f16[304,128]{1,0:T(8,128)(2,1)S(1)}, f16[304,128]{1,0:T(8,128)(2,1)S(1)}, u32[]{:S(2)}, u32[]{:S(2)}) collective-permute-start(f16[304,128]{1,0:T(8,128)(2,1)S(1)} %convert_element_type.49), channel_id=1, source_target_pairs={{0,4},{4,0},{8,12},{12,8},{16,20},{20,16},{24,28},{28,24},{1,5},{5... | collective-permute-start | bytes 233480 | tf_op jit(solution)/shard_map/ppermute | solution.py:587
  11.9 9.7 %collective-permute-start.1 = (f16[304,128]{1,0:T(8,128)(2,1)S(1)}, f16[304,128]{1,0:T(8,128)(2,1)S(1)}, u32[]{:S(2)}, u32[]{:S(2)}) collective-permute-start(f16[304,128]{1,0:T(8,128)(2,1)S(1)} %convert_element_type.47), channel_id=1, source_target_pairs={{0,12},{4,8},{8,4},{12,0},{16,28},{20,24},{24,20},{28,16},{1,13},{... | collective-permute-start | bytes 233480 | tf_op jit(solution)/shard_map/ppermute | solution.py:587
  13.6 8.1 %collective-permute-start = (f16[304,128]{1,0:T(8,128)(2,1)S(1)}, f16[304,128]{1,0:T(8,128)(2,1)S(1)}, u32[]{:S(2)}, u32[]{:S(2)}) collective-permute-start(f16[304,128]{1,0:T(8,128)(2,1)S(1)} %convert_element_type.45), channel_id=1, source_target_pairs={{0,4},{4,0},{8,20},{12,16},{16,12},{20,8},{24,28},{28,24},{1,5},{5... | collective-permute-start | bytes 233480 | tf_op jit(solution)/shard_map/ppermute | solution.py:587
  15.1 8.4 %collective-permute-start.5 = (f16[304,128]{1,0:T(8,128)(2,1)S(1)}, f16[304,128]{1,0:T(8,128)(2,1)S(1)}, u32[]{:S(2)}, u32[]{:S(2)}) collective-permute-start(f16[304,128]{1,0:T(8,128)(2,1)S(1)} %convert_element_type.55), channel_id=1, source_target_pairs={{0,8},{4,16},{8,0},{12,24},{16,4},{20,28},{24,12},{28,20},{1,9},{5... | collective-permute-start | bytes 233480 | tf_op jit(solution)/shard_map/ppermute | solution.py:587
  17.8 5.7 %collective-permute-start.4 = (f16[304,128]{1,0:T(8,128)(2,1)S(1)}, f16[304,128]{1,0:T(8,128)(2,1)S(1)}, u32[]{:S(2)}, u32[]{:S(2)}) collective-permute-start(f16[304,128]{1,0:T(8,128)(2,1)S(1)} %convert_element_type.53), channel_id=1, source_target_pairs={{0,8},{4,12},{8,0},{12,4},{16,24},{20,28},{24,16},{28,20},{1,9},{5... | collective-permute-start | bytes 233480 | tf_op jit(solution)/shard_map/ppermute | solution.py:587
  17.9 5.6 %collective-permute-start.3 = (f16[304,128]{1,0:T(8,128)(2,1)S(1)}, f16[304,128]{1,0:T(8,128)(2,1)S(1)}, u32[]{:S(2)}, u32[]{:S(2)}) collective-permute-start(f16[304,128]{1,0:T(8,128)(2,1)S(1)} %convert_element_type.51), channel_id=1, source_target_pairs={{0,4},{4,0},{8,16},{12,20},{16,8},{20,12},{24,28},{28,24},{1,5},{5... | collective-permute-start | bytes 233480 | tf_op jit(solution)/shard_map/ppermute | solution.py:587
  21.6 7.6 %copy-start = (bf16[4,256,256]{2,1,0:T(8,128)(2,1)S(1)}, bf16[4,256,256]{2,1,0:T(8,128)(2,1)}, u32[]{:S(2)}) copy-start(bf16[4,256,256]{2,1,0:T(8,128)(2,1)} %project.3) | copy-start | bytes 1572868
  21.6 7.6 %copy-start.1 = (bf16[12,48,256]{2,1,0:T(8,128)(2,1)S(1)}, bf16[12,48,256]{2,1,0:T(8,128)(2,1)}, u32[]{:S(2)}) copy-start(bf16[12,48,256]{2,1,0:T(8,128)(2,1)} %param.13) | copy-start | bytes 884740
  21.6 7.6 %copy-start.3 = (f32[256]{0:T(256)S(1)}, f32[256]{0:T(256)}, u32[]{:S(2)}) copy-start(f32[256]{0:T(256)} %param.12) | copy-start | bytes 3076
  21.9 5.7 %collective-permute-start.8 = (bf16[576,128]{1,0:T(8,128)(2,1)S(1)}, bf16[576,128]{1,0:T(8,128)(2,1)S(1)}, u32[]{:S(2)}, u32[]{:S(2)}) collective-permute-start(bf16[576,128]{1,0:T(8,128)(2,1)S(1)} %activations.2.a0), channel_id=1, source_target_pairs={{0,2},{1,3},{2,0},{3,1},{4,6},{5,7},{6,4},{7,5},{8,10},{9,11},{10,... | collective-permute-start | bytes 442376 | tf_op jit(solution)/shard_map/ppermute | solution.py:579
  23.8 5.4 %collective-permute-start.9 = (bf16[576,128]{1,0:T(8,128)(2,1)S(1)}, bf16[576,128]{1,0:T(8,128)(2,1)S(1)}, u32[]{:S(2)}, u32[]{:S(2)}) collective-permute-start(bf16[576,128]{1,0:T(8,128)(2,1)S(1)} %activations.3.b0), channel_id=1, source_target_pairs={{0,2},{1,3},{2,0},{3,1},{4,6},{5,7},{6,4},{7,5},{8,10},{9,11},{10,... | collective-permute-start | bytes 442376 | tf_op jit(solution)/shard_map/ppermute | solution.py:579
  24.4 4.9 %collective-permute-start.6 = (bf16[576,128]{1,0:T(8,128)(2,1)S(1)}, bf16[576,128]{1,0:T(8,128)(2,1)S(1)}, u32[]{:S(2)}, u32[]{:S(2)}) collective-permute-start(bf16[576,128]{1,0:T(8,128)(2,1)S(1)} %activations.2.a0), channel_id=1, source_target_pairs={{0,1},{1,0},{2,3},{3,2},{4,5},{5,4},{6,7},{7,6},{8,9},{9,8},{10,11... | collective-permute-start | bytes 442376 | tf_op jit(solution)/shard_map/ppermute | solution.py:579
  24.4 4.9 %collective-permute-start.7 = (bf16[576,128]{1,0:T(8,128)(2,1)S(1)}, bf16[576,128]{1,0:T(8,128)(2,1)S(1)}, u32[]{:S(2)}, u32[]{:S(2)}) collective-permute-start(bf16[576,128]{1,0:T(8,128)(2,1)S(1)} %activations.3.b0), channel_id=1, source_target_pairs={{0,1},{1,0},{2,3},{3,2},{4,5},{5,4},{6,7},{7,6},{8,9},{9,8},{10,11... | collective-permute-start | bytes 442376 | tf_op jit(solution)/shard_map/ppermute | solution.py:579
  27.6 2.0 %collective-permute-start.10 = (bf16[576,128]{1,0:T(8,128)(2,1)S(1)}, bf16[576,128]{1,0:T(8,128)(2,1)S(1)}, u32[]{:S(2)}, u32[]{:S(2)}) collective-permute-start(bf16[576,128]{1,0:T(8,128)(2,1)S(1)} %collective-permute-done.8.a2), channel_id=1, source_target_pairs={{0,1},{1,0},{2,3},{3,2},{4,5},{5,4},{6,7},{7,6},{8,9},{9,8},{10,11... | collective-permute-start | bytes 442376 | tf_op jit(solution)/shard_map/ppermute | solution.py:579
  29.2 1.4 %collective-permute-start.11 = (bf16[576,128]{1,0:T(8,128)(2,1)S(1)}, bf16[576,128]{1,0:T(8,128)(2,1)S(1)}, u32[]{:S(2)}, u32[]{:S(2)}) collective-permute-start(bf16[576,128]{1,0:T(8,128)(2,1)S(1)} %collective-permute-done.9.b2), channel_id=1, source_target_pairs={{0,1},{1,0},{2,3},{3,2},{4,5},{5,4},{6,7},{7,6},{8,9},{9,8},{10,11... | collective-permute-start | bytes 442376 | tf_op jit(solution)/shard_map/ppermute | solution.py:579
  31.4 6.9 %collective-permute-start.12 = (bf16[2,288,128]{2,1,0:T(8,128)(2,1)S(1)}, bf16[2,288,128]{2,1,0:T(8,128)(2,1)S(1)}, u32[]{:S(2)}, u32[]{:S(2)}) collective-permute-start(bf16[2,288,128]{2,1,0:T(8,128)(2,1)S(1)} %get-tuple-element.34), channel_id=1, source_target_pairs={{0,8},{1,5},{2,10},{3,7},{4,16},{5,1},{6,18},{7,3},{8,0},{9,21},{1... | collective-permute-start | bytes 442376 | tf_op jit(solution)/shard_map/ppermute | solution.py:596
  33.3 8.1 %collective-permute-start.13 = (bf16[2,288,128]{2,1,0:T(8,128)(2,1)S(1)}, bf16[2,288,128]{2,1,0:T(8,128)(2,1)S(1)}, u32[]{:S(2)}, u32[]{:S(2)}) collective-permute-start(bf16[2,288,128]{2,1,0:T(8,128)(2,1)S(1)} %get-tuple-element.35), channel_id=1, source_target_pairs={{0,8},{1,5},{2,10},{3,7},{4,12},{5,1},{6,14},{7,3},{8,0},{9,17},{1... | collective-permute-start | bytes 442376 | tf_op jit(solution)/shard_map/ppermute | solution.py:596
  33.5 7.9 %collective-permute-start.14 = (bf16[2,288,128]{2,1,0:T(8,128)(2,1)S(1)}, bf16[2,288,128]{2,1,0:T(8,128)(2,1)S(1)}, u32[]{:S(2)}, u32[]{:S(2)}) collective-permute-start(bf16[2,288,128]{2,1,0:T(8,128)(2,1)S(1)} %get-tuple-element.36), channel_id=1, source_target_pairs={{0,4},{1,13},{2,6},{3,15},{4,0},{5,9},{6,2},{7,11},{8,12},{9,5},{1... | collective-permute-start | bytes 442376 | tf_op jit(solution)/shard_map/ppermute | solution.py:596
  38.3 3.6 %collective-permute-start.15 = (bf16[2,288,128]{2,1,0:T(8,128)(2,1)S(1)}, bf16[2,288,128]{2,1,0:T(8,128)(2,1)S(1)}, u32[]{:S(2)}, u32[]{:S(2)}) collective-permute-start(bf16[2,288,128]{2,1,0:T(8,128)(2,1)S(1)} %collective-permute-done.12.refs_0_), channel_id=1, source_target_pairs={{0,1},{1,0},{2,3},{3,2},{4,5},{5,4},{6,7},{7,6},{8,9},{9,8},{10,11... | collective-permute-start | bytes 442376 | tf_op jit(solution)/shard_map/ppermute | solution.py:579
  41.4 1.4 %collective-permute-start.16 = (bf16[2,288,128]{2,1,0:T(8,128)(2,1)S(1)}, bf16[2,288,128]{2,1,0:T(8,128)(2,1)S(1)}, u32[]{:S(2)}, u32[]{:S(2)}) collective-permute-start(bf16[2,288,128]{2,1,0:T(8,128)(2,1)S(1)} %collective-permute-done.13.refs_1_), channel_id=1, source_target_pairs={{0,1},{1,0},{2,3},{3,2},{4,5},{5,4},{6,7},{7,6},{8,9},{9,8},{10,11... | collective-permute-start | bytes 442376 | tf_op jit(solution)/shard_map/ppermute | solution.py:579
  41.4 1.6 %collective-permute-start.17 = (bf16[2,288,128]{2,1,0:T(8,128)(2,1)S(1)}, bf16[2,288,128]{2,1,0:T(8,128)(2,1)S(1)}, u32[]{:S(2)}, u32[]{:S(2)}) collective-permute-start(bf16[2,288,128]{2,1,0:T(8,128)(2,1)S(1)} %collective-permute-done.14.refs_2_), channel_id=1, source_target_pairs={{0,1},{1,0},{2,3},{3,2},{4,5},{5,4},{6,7},{7,6},{8,9},{9,8},{10,11... | collective-permute-start | bytes 442376 | tf_op jit(solution)/shard_map/ppermute | solution.py:579
  44.8 2.1 %collective-permute-start.18 = (bf16[576,512]{1,0:T(8,128)(2,1)S(1)}, bf16[576,512]{1,0:T(8,128)(2,1)S(1)}, u32[]{:S(2)}, u32[]{:S(2)}) collective-permute-start(bf16[576,512]{1,0:T(8,128)(2,1)S(1)} %grads_for.4), channel_id=1, source_target_pairs={{0,1},{1,0},{2,3},{3,2},{4,5},{5,4},{6,7},{7,6},{8,9},{9,8},{10,11... | collective-permute-start | bytes 1769480 | tf_op jit(solution)/shard_map/ppermute | solution.py:579
  47.0 15.6 %collective-permute-start.20 = (bf16[576,512]{1,0:T(8,128)(2,1)S(1)}, bf16[576,512]{1,0:T(8,128)(2,1)S(1)}, u32[]{:S(2)}, u32[]{:S(2)}) collective-permute-start(bf16[576,512]{1,0:T(8,128)(2,1)S(1)} %add_convert_fusion), channel_id=1, source_target_pairs={{0,2},{1,3},{2,0},{3,1},{4,6},{5,7},{6,4},{7,5},{8,10},{9,11},{10,... | collective-permute-start | bytes 1769480 | tf_op jit(solution)/shard_map/ppermute | solution.py:579
  51.0 2.1 %collective-permute-start.19 = (bf16[576,512]{1,0:T(8,128)(2,1)S(1)}, bf16[576,512]{1,0:T(8,128)(2,1)S(1)}, u32[]{:S(2)}, u32[]{:S(2)}) collective-permute-start(bf16[576,512]{1,0:T(8,128)(2,1)S(1)} %grads_for.7), channel_id=1, source_target_pairs={{0,1},{1,0},{2,3},{3,2},{4,5},{5,4},{6,7},{7,6},{8,9},{9,8},{10,11... | collective-permute-start | bytes 1769480 | tf_op jit(solution)/shard_map/ppermute | solution.py:579

commit v8 on v0

--- a/solution.py
+++ b/solution.py
@@ -148,14 +148,15 @@
 
 OUT_PAIRS = ((3, 1), (1, 1), (3, 0), (1, 0), (3, 2), (1, 2), (2, 1), (2, 0), (2, 2))
 TAPS = (
-    [(k, 1, 1) for k in (2, 1, 3)]
+    [(k, 1, 1) for k in (1, 2, 3)]
     + [(k, i, j) for k, j in OUT_PAIRS for i in (0, 2)]
-    + [(k, 1, j) for j in (0, 2) for k in (2, 1, 3)]
+    + [(k, 1, j) for j in (0, 2) for k in (1, 2, 3)]
 )
 OUT_AT, LEFT_AT, RIGHT_AT = 4 * W, 22 * W, 25 * W
-PARTS = ((0, 2), (1, 3))
-SWAPS = (6, 2, 1, 3, 7, 5)
-GRAD_SWAPS = (1, 5, 7, 3, 6, 2)
+PARTS = ((0, 1), (2, 3))
+PART_SWAPS = ((7, 3, 1), (6, 2, 5, 7, 3))
+SWAPS = (1, 3, 7, 5, 2, 6)
+GRAD_SWAPS = (1, 3, 7, 5, 2, 6)
 
 
 def fits(mesh):
@@ -319,10 +320,10 @@
     low = low_lanes((PIXELS, 128))
 
     def add(first, value, k):
-        part = k % 2
+        part = k // 2
         rows = slice(first * BLOCK, first * BLOCK + value.shape[0])
         mask, value = low[: value.shape[0]], value[:, part * 128 : part * 128 + 128]
-        kept = jnp.where(mask, value, 0.0) if k == 1 else jnp.where(mask, 0.0, value)
+        kept = jnp.where(mask, value, 0.0) if k == 2 else jnp.where(mask, 0.0, value)
         outs[part][rows, :] = outs[part][rows, :] + kept
 
     d = nt(ordered[: 3 * BLOCK, :], weights[LEFT_AT - W : LEFT_AT + 3 * W, :])
@@ -352,7 +353,7 @@
 def gather_arrivals(recv, arrivals, swaps):
     arrivals[0] = jnp.zeros((HALF, 128), arrivals.dtype)
     for n, x in enumerate(swaps):
-        arrivals[x] = recv[n][...] if recv[n].shape[0] == HALF else unscaled(recv[n][...])
+        arrivals[x] = unscaled(recv[n][...])
 
 
 def activation_kernel(part, swaps, own, *refs):
@@ -431,8 +432,8 @@
     grads[:, :128] = a.astype(BF16)
     grads[:, 128:] = b.astype(BF16)
     low = low_lanes((HALF, 128))
-    packed[0] = jnp.where(low, b[:HALF], pltpu.roll(b[HALF:], W, 1)).astype(BF16)
-    packed[1] = jnp.where(low, pltpu.roll(a[:HALF], W, 1), a[HALF:]).astype(BF16)
+    packed[0] = jnp.where(low, pltpu.roll(a[:HALF], W, 1), a[HALF:]).astype(BF16)
+    packed[1] = jnp.where(low, b[:HALF], pltpu.roll(b[HALF:], W, 1)).astype(BF16)
     packed[2] = jnp.where(low, pltpu.roll(b[:HALF], W, 1), b[HALF:]).astype(BF16)
     for n, x in enumerate(GRAD_SWAPS):
         apart = jnp.abs((row ^ x) - row)
@@ -476,9 +477,11 @@
 
 
 def spread_kernel(own, *refs):
-    recv, stack, arrivals, pairs, twice = refs[:6], refs[6], refs[7], refs[8], refs[9]
+    recv, stack, arrivals, pairs, twice = refs[:6], *refs[6:]
     row = lax.axis_index("rows")
-    gather_arrivals(recv, arrivals, GRAD_SWAPS)
+    arrivals[0] = jnp.zeros((HALF, 128), BF16)
+    for n, x in enumerate(GRAD_SWAPS):
+        arrivals[x] = recv[n][...]
     low = low_lanes((HALF, 128))
     low_all = low_lanes((PIXELS, 128))
     for k in (1, 2, 3):
@@ -486,9 +489,9 @@
         m = arrivals[arrival_slot(row, row - k)].astype(F32)
         pairs[k - 1, :HALF, :] = jnp.where(low, p, pltpu.roll(m, W, 1)).astype(BF16)
         pairs[k - 1, HALF:, :] = jnp.where(low, pltpu.roll(p, W, 1), m).astype(BF16)
-        g = own[:, :128].astype(F32) if k == 2 else own[:, 128:].astype(F32)
+        g = own[:, :128].astype(F32) if k == 1 else own[:, 128:].astype(F32)
         other = pltpu.roll(g, W, 1)
-        two = jnp.where(low_all, g, other) if k == 1 else jnp.where(low_all, other, g)
+        two = jnp.where(low_all, g, other) if k == 2 else jnp.where(low_all, other, g)
         twice[k - 1] = two.astype(BF16)
     stack[:, : 4 * W] = own[...]
     nothing = jnp.zeros((BLOCK, 128), BF16)
@@ -503,7 +506,7 @@
         for m in range(4):
             stack[m * BLOCK : (m + 1) * BLOCK, lanes] = block_of(pairs, k, m - (j - 1) * k)
     low_block = low_lanes((BLOCK, 128))
-    for q, (a, b) in enumerate(((2, 1), (3, -2), (-1, -3))):
+    for q, (a, b) in enumerate(((1, 2), (3, -1), (-2, -3))):
         lanes = slice(LEFT_AT + q * 128, LEFT_AT + q * 128 + 128)
         for m in range(4):
             stack[m * BLOCK : (m + 1) * BLOCK, lanes] = jnp.where(
@@ -572,9 +575,12 @@
     return lax.ppermute(x, "filt", [(i, i ^ bit) for i in range(lax.axis_size("filt"))])
 
 
+def partner(r, bits):
+    return r ^ bits if abs((r ^ bits) - r) <= 3 else r ^ {5: 2, 6: 1, 7: 1}[bits]
+
+
 def swapped(x, bits):
-    pairs = [(r, r ^ bits) for r in range(8) if abs((r ^ bits) - r) <= 3]
-    return lax.ppermute(x, "rows", pairs)
+    return lax.ppermute(x, "rows", [(r, partner(r, bits)) for r in range(8)])
 
 
 def on_device(
@@ -593,7 +599,7 @@
     own = own_sums(ordered, weights, branch_bias)
     acts = [
         activations_of(part, swaps, own[part], [received[x] for x in swaps])
-        for part, swaps in ((0, SWAPS[:2]), (1, SWAPS[2:]))
+        for part, swaps in enumerate(PART_SWAPS)
     ]
     across = [flipped(x, 2) for x in acts]
     beside = [flipped(x, 1) for x in acts]

time: 71.8 us -> 62.8 us (0.87)
  starting transfers between devices: 32.5 us -> 23.5 us
    ppermute x12, starting transfers between devices: 27 us -> 19 us  [swapped(): return lax.ppermute(x, 'rows', [(r, partner(r, bits)) for r in range(8)])]
    ppermute x9, starting transfers between devices: 5.43 us -> 4.44 us  [flipped(): lax.ppermute(x, 'filt', [(i, i ^ bit) for i in range(lax.axis_size('filt'...]
  transfers between devices with their start and end apart: 21 -> 21, of which waited for: 8 -> 10; matrix products, arithmetic and copies ran while one was open for 0% -> 0% of each run, Pallas kernels for 10% -> 12%
where the time goes in v8:
time: 62.8 us; the launch traced here: 62.7 us
  starting transfers between devices  23.5 us (37%)
  Pallas kernels  19.3 us (31%)
  waiting for transfers between devices  18.6 us (30%)
  between operations  0.92 us (1%)
    ppermute x12, starting transfers between devices, swapped(): return lax.ppermute(x, 'rows', [(r, partner(r, bits)) for r in range(8)])  19 us
    ppermute x9, waiting for transfers between devices, flipped(): lax.ppermute(x, 'filt', [(i, i ^ bit) for i in range(lax.axis_size('filt'...  16.1 us
    pallas_call x1, Pallas kernels, outward_sums(): pl.pallas_call(outward_kernel, out_shape=[jax.ShapeDtypeStruct((SENT, 128...  8.22 us
    pallas_call x4, Pallas kernels, grads_for(): pl.pallas_call(functools.partial(grad_kernel, flips), out_shape=[jax.Shap...  4.95 us
    ppermute x9, starting transfers between devices, flipped(): lax.ppermute(x, 'filt', [(i, i ^ bit) for i in range(lax.axis_size('filt'...  4.44 us
    ppermute x12, waiting for transfers between devices, swapped(): return lax.ppermute(x, 'rows', [(r, partner(r, bits)) for r in range(8)])  2.56 us
    pallas_call x1, Pallas kernels, own_sums(): pl.pallas_call(own_kernel, out_shape=[jax.ShapeDtypeStruct((PIXELS, 128),...  1.72 us
    pallas_call x1, Pallas kernels, last_sum(): pl.pallas_call(last_kernel, out_shape=jax.ShapeDtypeStruct((PIXELS, 512),...  1.26 us
  transfers between devices with their start and end apart: 21, of which 10 were waited for; matrix products, arithmetic and copies ran while one was open for 0% of the time, Pallas kernels for 12%

profile of v8, /device:TPU:0, one launch (start us, length us, event | category | flops | bytes accessed | tf_op | source)
XLA Modules:
  0.0 62.7 jit_solution(2725726187413224939)
XLA Ops:
  0.6 8.2 %outward_sums.1 = (f32[304,128]{1,0:T(8,128)S(1)}, f32[304,128]{1,0:T(8,128)S(1)}, f32[304,128]{1,0:T(8,128)S(1)}, f32[304,128]{1,0:T(8,128)S(1)}, f32[304,128]{...) custom-call(bf16[576,2048]{1,0:T(8,128)(2,1)} %bitcast.12, ...), custom_call_target="tpu_custom_call" | custom-call | tf_op jit(solution)/shard_map/outward_sums/pallas_call | solution.py:297
  8.9 3.0 %collective-permute-start.2 = (f16[304,128]{1,0:T(8,128)(2,1)S(1)}, f16[304,128]{1,0:T(8,128)(2,1)S(1)}, u32[]{:S(2)}, u32[]{:S(2)}) collective-permute-start(f16[304,128]{1,0:T(8,128)(2,1)S(1)} %convert_element_type.49), channel_id=1, source_target_pairs={{0,4},{4,0},{8,12},{12,8},{16,20},{20,16},{24,28},{28,24},{1,5},{5... | collective-permute-start | bytes 233480 | tf_op jit(solution)/shard_map/ppermute | solution.py:583
  11.9 1.6 %collective-permute-start.1 = (f16[304,128]{1,0:T(8,128)(2,1)S(1)}, f16[304,128]{1,0:T(8,128)(2,1)S(1)}, u32[]{:S(2)}, u32[]{:S(2)}) collective-permute-start(f16[304,128]{1,0:T(8,128)(2,1)S(1)} %convert_element_type.47), channel_id=1, source_target_pairs={{0,12},{4,8},{8,4},{12,0},{16,28},{20,24},{24,20},{28,16},{1,13},{... | collective-permute-start | bytes 233480 | tf_op jit(solution)/shard_map/ppermute | solution.py:583
  13.6 1.5 %collective-permute-start = (f16[304,128]{1,0:T(8,128)(2,1)S(1)}, f16[304,128]{1,0:T(8,128)(2,1)S(1)}, u32[]{:S(2)}, u32[]{:S(2)}) collective-permute-start(f16[304,128]{1,0:T(8,128)(2,1)S(1)} %convert_element_type.45), channel_id=1, source_target_pairs={{0,4},{4,0},{8,20},{12,16},{16,12},{20,8},{24,28},{28,24},{1,5},{5... | collective-permute-start | bytes 233480 | tf_op jit(solution)/shard_map/ppermute | solution.py:583
  15.1 2.7 %collective-permute-start.5 = (f16[304,128]{1,0:T(8,128)(2,1)S(1)}, f16[304,128]{1,0:T(8,128)(2,1)S(1)}, u32[]{:S(2)}, u32[]{:S(2)}) collective-permute-start(f16[304,128]{1,0:T(8,128)(2,1)S(1)} %convert_element_type.55), channel_id=1, source_target_pairs={{0,8},{4,16},{8,0},{12,24},{16,4},{20,28},{24,12},{28,20},{1,9},{5... | collective-permute-start | bytes 233480 | tf_op jit(solution)/shard_map/ppermute | solution.py:583
  17.9 2.0 %collective-permute-start.3 = (f16[304,128]{1,0:T(8,128)(2,1)S(1)}, f16[304,128]{1,0:T(8,128)(2,1)S(1)}, u32[]{:S(2)}, u32[]{:S(2)}) collective-permute-start(f16[304,128]{1,0:T(8,128)(2,1)S(1)} %convert_element_type.51), channel_id=1, source_target_pairs={{0,4},{4,0},{8,16},{12,20},{16,8},{20,12},{24,28},{28,24},{1,5},{5... | collective-permute-start | bytes 233480 | tf_op jit(solution)/shard_map/ppermute | solution.py:583
  19.9 1.7 %own_sums.1 = (f32[576,128]{1,0:T(8,128)S(1)}, f32[576,128]{1,0:T(8,128)S(1)}) custom-call(bf16[576,2048]{1,0:T(8,128)(2,1)S(1)} %get-tuple-element.24.ordered, bf16[1792,2048]{1,0:T(8,128)(2,1)S(1)} %get-tuple-element.25.weights, f32[4,64]{1,0:T(4,128)S(1)} %copy-done.2), custom_call_target="tpu_custom_call" | custom-call | flops 1000000 | bytes 10000 | tf_op jit(solution)/shard_map/own_sums/pallas_call | solution.py:338
  21.9 1.6 %collective-permute-start.6 = (bf16[576,128]{1,0:T(8,128)(2,1)S(1)}, bf16[576,128]{1,0:T(8,128)(2,1)S(1)}, u32[]{:S(2)}, u32[]{:S(2)}) collective-permute-start(bf16[576,128]{1,0:T(8,128)(2,1)S(1)} %activations.2.a0), channel_id=1, source_target_pairs={{0,2},{1,3},{2,0},{3,1},{4,6},{5,7},{6,4},{7,5},{8,10},{9,11},{10,... | collective-permute-start | bytes 442376 | tf_op jit(solution)/shard_map/ppermute | solution.py:575
  23.8 0.6 collective-permute-start.7
  24.4 0.5 collective-permute-start.11
  24.9 2.8 %collective-permute-done.6.a2 = bf16[576,128]{1,0:T(8,128)(2,1)S(1)} collective-permute-done((bf16[576,128]{1,0:T(8,128)(2,1)S(1)}, bf16[576,128]{1,0:T(8,128)(2,1)S(1)}, u32[]{:S(2)}, u32[]{:S(2)}) %collective-permute-start.6) | collective-permute-done | bytes 147488 | tf_op jit(solution)/shard_map/ppermute | solution.py:575
  27.6 1.6 %collective-permute-done.7.b2 = bf16[576,128]{1,0:T(8,128)(2,1)S(1)} collective-permute-done((bf16[576,128]{1,0:T(8,128)(2,1)S(1)}, bf16[576,128]{1,0:T(8,128)(2,1)S(1)}, u32[]{:S(2)}, u32[]{:S(2)}) %collective-permute-start.7) | collective-permute-done | bytes 147488 | tf_op jit(solution)/shard_map/ppermute | solution.py:575
  29.7 0.9 %collective-permute-done.9.b3 = bf16[576,128]{1,0:T(8,128)(2,1)S(1)} collective-permute-done((bf16[576,128]{1,0:T(8,128)(2,1)S(1)}, bf16[576,128]{1,0:T(8,128)(2,1)S(1)}, u32[]{:S(2)}, u32[]{:S(2)}) %collective-permute-start.9) | collective-permute-done | bytes 147488 | tf_op jit(solution)/shard_map/ppermute | solution.py:575
  30.6 0.6 %far_head.1 = (bf16[576,256]{1,0:T(8,128)(2,1)S(1)}, bf16[576,256]{1,0:T(8,128)(2,1)S(1)}, bf16[288,128]{1,0:T(8,128)(2,1)S(1)}, bf16[288,128]{1,0:T(8,128)(2,1)...) custom-call(bf16[576,128]{1,0:T(8,128)(2,1)S(1)} %activations.2.a0, ...), custom_call_target="tpu_custom_call" | custom-call | tf_op jit(solution)/shard_map/far_head/pallas_call | solution.py:444
  31.2 0.7 %collective-permute-start.12 = (bf16[288,128]{1,0:T(8,128)(2,1)S(1)}, bf16[288,128]{1,0:T(8,128)(2,1)S(1)}, u32[]{:S(2)}, u32[]{:S(2)}) collective-permute-start(bf16[288,128]{1,0:T(8,128)(2,1)S(1)} %get-tuple-element.37), channel_id=1, source_target_pairs={{0,4},{4,0},{8,12},{12,8},{16,20},{20,16},{24,28},{28,24},{1,5},{5... | collective-permute-start | bytes 221192 | tf_op jit(solution)/shard_map/ppermute | solution.py:583
  31.9 2.6 %collective-permute-start.13 = (bf16[288,128]{1,0:T(8,128)(2,1)S(1)}, bf16[288,128]{1,0:T(8,128)(2,1)S(1)}, u32[]{:S(2)}, u32[]{:S(2)}) collective-permute-start(bf16[288,128]{1,0:T(8,128)(2,1)S(1)} %get-tuple-element.38), channel_id=1, source_target_pairs={{0,12},{4,8},{8,4},{12,0},{16,28},{20,24},{24,20},{28,16},{1,13},{... | collective-permute-start | bytes 221192 | tf_op jit(solution)/shard_map/ppermute | solution.py:583
  35.0 1.2 %collective-permute-start.15 = (bf16[288,128]{1,0:T(8,128)(2,1)S(1)}, bf16[288,128]{1,0:T(8,128)(2,1)S(1)}, u32[]{:S(2)}, u32[]{:S(2)}) collective-permute-start(bf16[288,128]{1,0:T(8,128)(2,1)S(1)} %get-tuple-element.40), channel_id=1, source_target_pairs={{0,8},{4,16},{8,0},{12,24},{16,4},{20,28},{24,12},{28,20},{1,9},{5... | collective-permute-start | bytes 221192 | tf_op jit(solution)/shard_map/ppermute | solution.py:583
  36.1 0.9 %collective-permute-start.16 = (bf16[288,128]{1,0:T(8,128)(2,1)S(1)}, bf16[288,128]{1,0:T(8,128)(2,1)S(1)}, u32[]{:S(2)}, u32[]{:S(2)}) collective-permute-start(bf16[288,128]{1,0:T(8,128)(2,1)S(1)} %get-tuple-element.41), channel_id=1, source_target_pairs={{0,8},{4,12},{8,0},{12,4},{16,24},{20,28},{24,16},{28,20},{1,9},{5... | collective-permute-start | bytes 221192 | tf_op jit(solution)/shard_map/ppermute | solution.py:583
  37.2 2.4 %collective-permute-start.17 = (bf16[288,128]{1,0:T(8,128)(2,1)S(1)}, bf16[288,128]{1,0:T(8,128)(2,1)S(1)}, u32[]{:S(2)}, u32[]{:S(2)}) collective-permute-start(bf16[288,128]{1,0:T(8,128)(2,1)S(1)} %get-tuple-element.42), channel_id=1, source_target_pairs={{0,4},{4,0},{8,16},{12,20},{16,8},{20,12},{24,28},{28,24},{1,5},{5... | collective-permute-start | bytes 221192 | tf_op jit(solution)/shard_map/ppermute | solution.py:583
  39.6 0.6 %collective-permute-done.15.refs_3_ = bf16[288,128]{1,0:T(8,128)(2,1)S(1)} collective-permute-done((bf16[288,128]{1,0:T(8,128)(2,1)S(1)}, bf16[288,128]{1,0:T(8,128)(2,1)S(1)}, u32[]{:S(2)}, u32[]{:S(2)}) %collective-permute-start.15) | collective-permute-done | bytes 73760 | tf_op jit(solution)/shard_map/ppermute | solution.py:583
  40.3 1.3 %collective-permute-done.16.refs_4_ = bf16[288,128]{1,0:T(8,128)(2,1)S(1)} collective-permute-done((bf16[288,128]{1,0:T(8,128)(2,1)S(1)}, bf16[288,128]{1,0:T(8,128)(2,1)S(1)}, u32[]{:S(2)}, u32[]{:S(2)}) %collective-permute-start.16) | collective-permute-done | bytes 73760 | tf_op jit(solution)/shard_map/ppermute | solution.py:583
  41.9 0.6 spread.1.stack
  42.5 1.2 %grads_for.4 = bf16[576,512]{1,0:T(8,128)(2,1)S(1)} custom-call(bf16[576,1792]{1,0:T(8,128)(2,1)S(1)} %spread.1.stack, bf16[1792,2048]{1,0:T(8,128)(2,1)S(1)} %get-tuple-element.25.weights), custom_call_target="tpu_custom_call" | custom-call | flops 1056964608 | bytes 1000000 | tf_op jit(solution)/shard_map/grads_for/pallas_call | solution.py:541
  43.8 1.2 %grads_for.5 = bf16[576,512]{1,0:T(8,128)(2,1)S(1)} custom-call(bf16[576,1792]{1,0:T(8,128)(2,1)S(1)} %spread.1.stack, bf16[1792,2048]{1,0:T(8,128)(2,1)S(1)} %get-tuple-element.25.weights), custom_call_target="tpu_custom_call" | custom-call | flops 1056964608 | bytes 1000000 | tf_op jit(solution)/shard_map/grads_for/pallas_call | solution.py:541
  45.1 0.7 %collective-permute-done.18 = bf16[576,512]{1,0:T(8,128)(2,1)S(1)} collective-permute-done((bf16[576,512]{1,0:T(8,128)(2,1)S(1)}, bf16[576,512]{1,0:T(8,128)(2,1)S(1)}, u32[]{:S(2)}, u32[]{:S(2)}) %collective-permute-start.18) | collective-permute-done | bytes 589856 | tf_op jit(solution)/shard_map/ppermute | solution.py:575
  46.0 1.6 %collective-permute-start.20 = (bf16[576,512]{1,0:T(8,128)(2,1)S(1)}, bf16[576,512]{1,0:T(8,128)(2,1)S(1)}, u32[]{:S(2)}, u32[]{:S(2)}) collective-permute-start(bf16[576,512]{1,0:T(8,128)(2,1)S(1)} %add_convert_fusion), channel_id=1, source_target_pairs={{0,2},{1,3},{2,0},{3,1},{4,6},{5,7},{6,4},{7,5},{8,10},{9,11},{10,... | collective-permute-start | bytes 1769480 | tf_op jit(solution)/shard_map/ppermute | solution.py:575
  47.6 1.2 %own_output.1 = bf16[576,64]{1,0:T(8,128)(2,1)} custom-call(bf16[576,256]{1,0:T(8,128)(2,1)S(1)} %get-tuple-element.44.output), custom_call_target="tpu_custom_call" | custom-call | tf_op jit(solution)/shard_map/own_output/pallas_call | solution.py:469
  48.8 1.2 %grads_for.7 = bf16[576,512]{1,0:T(8,128)(2,1)S(1)} custom-call(bf16[576,1792]{1,0:T(8,128)(2,1)S(1)} %spread.1.stack, bf16[1792,2048]{1,0:T(8,128)(2,1)S(1)} %get-tuple-element.25.weights), custom_call_target="tpu_custom_call" | custom-call | flops 1056964608 | bytes 1000000 | tf_op jit(solution)/shard_map/grads_for/pallas_call | solution.py:541
  50.1 1.2 %grads_for.6.a = bf16[576,512]{1,0:T(8,128)(2,1)S(1)} custom-call(bf16[576,1792]{1,0:T(8,128)(2,1)S(1)} %spread.1.stack, bf16[1792,2048]{1,0:T(8,128)(2,1)S(1)} %get-tuple-element.25.weights), custom_call_target="tpu_custom_call" | custom-call | flops 8455716864 | bytes 1000000 | tf_op jit(solution)/shard_map/grads_for/pallas_call | solution.py:541
  51.4 0.7 %collective-permute-done.19.b = bf16[576,512]{1,0:T(8,128)(2,1)S(1)} collective-permute-done((bf16[576,512]{1,0:T(8,128)(2,1)S(1)}, bf16[576,512]{1,0:T(8,128)(2,1)S(1)}, u32[]{:S(2)}, u32[]{:S(2)}) %collective-permute-start.19) | collective-permute-done | bytes 589856 | tf_op jit(solution)/shard_map/ppermute | solution.py:575
  52.1 9.3 %collective-permute-done.20.c = bf16[576,512]{1,0:T(8,128)(2,1)S(1)} collective-permute-done((bf16[576,512]{1,0:T(8,128)(2,1)S(1)}, bf16[576,512]{1,0:T(8,128)(2,1)S(1)}, u32[]{:S(2)}, u32[]{:S(2)}) %collective-permute-start.20) | collective-permute-done | bytes 589856 | tf_op jit(solution)/shard_map/ppermute | solution.py:575
  61.4 1.3 %last_sum.1 = bf16[576,512]{1,0:T(8,128)(2,1)} custom-call(bf16[576,512]{1,0:T(8,128)(2,1)S(1)} %grads_for.6.a, bf16[576,512]{1,0:T(8,128)(2,1)S(1)} %collective-permute-done.19.b, bf16[576,512]{1,0:T(8,128)(2,1)S(1)} %collective-permute-done.20.c), custom_call_target="tpu_custom_call" | custom-call | tf_op jit(solution)/shard_map/last_sum/pallas_call | solution.py:564
  (44 shorter events, 2.5 us)
Async XLA Ops:
  0.6 19.2 %copy-start.2 = (f32[4,64]{1,0:T(4,128)S(1)}, f32[4,64]{1,0:T(4,128)}, u32[]{:S(2)}) copy-start(f32[4,64]{1,0:T(4,128)} %bias.1) | copy-start | bytes 3076
  8.9 9.0 %collective-permute-start.2 = (f16[304,128]{1,0:T(8,128)(2,1)S(1)}, f16[304,128]{1,0:T(8,128)(2,1)S(1)}, u32[]{:S(2)}, u32[]{:S(2)}) collective-permute-start(f16[304,128]{1,0:T(8,128)(2,1)S(1)} %convert_element_type.49), channel_id=1, source_target_pairs={{0,4},{4,0},{8,12},{12,8},{16,20},{20,16},{24,28},{28,24},{1,5},{5... | collective-permute-start | bytes 233480 | tf_op jit(solution)/shard_map/ppermute | solution.py:583
  11.9 9.7 %collective-permute-start.1 = (f16[304,128]{1,0:T(8,128)(2,1)S(1)}, f16[304,128]{1,0:T(8,128)(2,1)S(1)}, u32[]{:S(2)}, u32[]{:S(2)}) collective-permute-start(f16[304,128]{1,0:T(8,128)(2,1)S(1)} %convert_element_type.47), channel_id=1, source_target_pairs={{0,12},{4,8},{8,4},{12,0},{16,28},{20,24},{24,20},{28,16},{1,13},{... | collective-permute-start | bytes 233480 | tf_op jit(solution)/shard_map/ppermute | solution.py:583
  13.6 8.1 %collective-permute-start = (f16[304,128]{1,0:T(8,128)(2,1)S(1)}, f16[304,128]{1,0:T(8,128)(2,1)S(1)}, u32[]{:S(2)}, u32[]{:S(2)}) collective-permute-start(f16[304,128]{1,0:T(8,128)(2,1)S(1)} %convert_element_type.45), channel_id=1, source_target_pairs={{0,4},{4,0},{8,20},{12,16},{16,12},{20,8},{24,28},{28,24},{1,5},{5... | collective-permute-start | bytes 233480 | tf_op jit(solution)/shard_map/ppermute | solution.py:583
  15.1 8.4 %collective-permute-start.5 = (f16[304,128]{1,0:T(8,128)(2,1)S(1)}, f16[304,128]{1,0:T(8,128)(2,1)S(1)}, u32[]{:S(2)}, u32[]{:S(2)}) collective-permute-start(f16[304,128]{1,0:T(8,128)(2,1)S(1)} %convert_element_type.55), channel_id=1, source_target_pairs={{0,8},{4,16},{8,0},{12,24},{16,4},{20,28},{24,12},{28,20},{1,9},{5... | collective-permute-start | bytes 233480 | tf_op jit(solution)/shard_map/ppermute | solution.py:583
  17.8 5.7 %collective-permute-start.4 = (f16[304,128]{1,0:T(8,128)(2,1)S(1)}, f16[304,128]{1,0:T(8,128)(2,1)S(1)}, u32[]{:S(2)}, u32[]{:S(2)}) collective-permute-start(f16[304,128]{1,0:T(8,128)(2,1)S(1)} %convert_element_type.53), channel_id=1, source_target_pairs={{0,8},{4,12},{8,0},{12,4},{16,24},{20,28},{24,16},{28,20},{1,9},{5... | collective-permute-start | bytes 233480 | tf_op jit(solution)/shard_map/ppermute | solution.py:583
  17.9 5.6 %collective-permute-start.3 = (f16[304,128]{1,0:T(8,128)(2,1)S(1)}, f16[304,128]{1,0:T(8,128)(2,1)S(1)}, u32[]{:S(2)}, u32[]{:S(2)}) collective-permute-start(f16[304,128]{1,0:T(8,128)(2,1)S(1)} %convert_element_type.51), channel_id=1, source_target_pairs={{0,4},{4,0},{8,16},{12,20},{16,8},{20,12},{24,28},{28,24},{1,5},{5... | collective-permute-start | bytes 233480 | tf_op jit(solution)/shard_map/ppermute | solution.py:583
  21.6 7.6 %copy-start = (bf16[4,256,256]{2,1,0:T(8,128)(2,1)S(1)}, bf16[4,256,256]{2,1,0:T(8,128)(2,1)}, u32[]{:S(2)}) copy-start(bf16[4,256,256]{2,1,0:T(8,128)(2,1)} %project.3) | copy-start | bytes 1572868
  21.6 7.6 %copy-start.1 = (bf16[12,48,256]{2,1,0:T(8,128)(2,1)S(1)}, bf16[12,48,256]{2,1,0:T(8,128)(2,1)}, u32[]{:S(2)}) copy-start(bf16[12,48,256]{2,1,0:T(8,128)(2,1)} %param.13) | copy-start | bytes 884740
  21.6 7.6 %copy-start.3 = (f32[256]{0:T(256)S(1)}, f32[256]{0:T(256)}, u32[]{:S(2)}) copy-start(f32[256]{0:T(256)} %param.12) | copy-start | bytes 3076
  21.9 5.7 %collective-permute-start.6 = (bf16[576,128]{1,0:T(8,128)(2,1)S(1)}, bf16[576,128]{1,0:T(8,128)(2,1)S(1)}, u32[]{:S(2)}, u32[]{:S(2)}) collective-permute-start(bf16[576,128]{1,0:T(8,128)(2,1)S(1)} %activations.2.a0), channel_id=1, source_target_pairs={{0,2},{1,3},{2,0},{3,1},{4,6},{5,7},{6,4},{7,5},{8,10},{9,11},{10,... | collective-permute-start | bytes 442376 | tf_op jit(solution)/shard_map/ppermute | solution.py:575
  23.8 5.4 %collective-permute-start.7 = (bf16[576,128]{1,0:T(8,128)(2,1)S(1)}, bf16[576,128]{1,0:T(8,128)(2,1)S(1)}, u32[]{:S(2)}, u32[]{:S(2)}) collective-permute-start(bf16[576,128]{1,0:T(8,128)(2,1)S(1)} %activations.3.b0), channel_id=1, source_target_pairs={{0,2},{1,3},{2,0},{3,1},{4,6},{5,7},{6,4},{7,5},{8,10},{9,11},{10,... | collective-permute-start | bytes 442376 | tf_op jit(solution)/shard_map/ppermute | solution.py:575
  24.4 4.9 %collective-permute-start.10 = (bf16[576,128]{1,0:T(8,128)(2,1)S(1)}, bf16[576,128]{1,0:T(8,128)(2,1)S(1)}, u32[]{:S(2)}, u32[]{:S(2)}) collective-permute-start(bf16[576,128]{1,0:T(8,128)(2,1)S(1)} %activations.2.a0), channel_id=1, source_target_pairs={{0,1},{1,0},{2,3},{3,2},{4,5},{5,4},{6,7},{7,6},{8,9},{9,8},{10,11... | collective-permute-start | bytes 442376 | tf_op jit(solution)/shard_map/ppermute | solution.py:575
  24.4 4.9 %collective-permute-start.11 = (bf16[576,128]{1,0:T(8,128)(2,1)S(1)}, bf16[576,128]{1,0:T(8,128)(2,1)S(1)}, u32[]{:S(2)}, u32[]{:S(2)}) collective-permute-start(bf16[576,128]{1,0:T(8,128)(2,1)S(1)} %activations.3.b0), channel_id=1, source_target_pairs={{0,1},{1,0},{2,3},{3,2},{4,5},{5,4},{6,7},{7,6},{8,9},{9,8},{10,11... | collective-permute-start | bytes 442376 | tf_op jit(solution)/shard_map/ppermute | solution.py:575
  27.6 2.0 %collective-permute-start.8 = (bf16[576,128]{1,0:T(8,128)(2,1)S(1)}, bf16[576,128]{1,0:T(8,128)(2,1)S(1)}, u32[]{:S(2)}, u32[]{:S(2)}) collective-permute-start(bf16[576,128]{1,0:T(8,128)(2,1)S(1)} %collective-permute-done.6.a2), channel_id=1, source_target_pairs={{0,1},{1,0},{2,3},{3,2},{4,5},{5,4},{6,7},{7,6},{8,9},{9,8},{10,11... | collective-permute-start | bytes 442376 | tf_op jit(solution)/shard_map/ppermute | solution.py:575
  29.2 1.4 %collective-permute-start.9 = (bf16[576,128]{1,0:T(8,128)(2,1)S(1)}, bf16[576,128]{1,0:T(8,128)(2,1)S(1)}, u32[]{:S(2)}, u32[]{:S(2)}) collective-permute-start(bf16[576,128]{1,0:T(8,128)(2,1)S(1)} %collective-permute-done.7.b2), channel_id=1, source_target_pairs={{0,1},{1,0},{2,3},{3,2},{4,5},{5,4},{6,7},{7,6},{8,9},{9,8},{10,11... | collective-permute-start | bytes 442376 | tf_op jit(solution)/shard_map/ppermute | solution.py:575
  31.2 6.0 %collective-permute-start.12 = (bf16[288,128]{1,0:T(8,128)(2,1)S(1)}, bf16[288,128]{1,0:T(8,128)(2,1)S(1)}, u32[]{:S(2)}, u32[]{:S(2)}) collective-permute-start(bf16[288,128]{1,0:T(8,128)(2,1)S(1)} %get-tuple-element.37), channel_id=1, source_target_pairs={{0,4},{4,0},{8,12},{12,8},{16,20},{20,16},{24,28},{28,24},{1,5},{5... | collective-permute-start | bytes 221192 | tf_op jit(solution)/shard_map/ppermute | solution.py:583
  31.9 7.7 %collective-permute-start.13 = (bf16[288,128]{1,0:T(8,128)(2,1)S(1)}, bf16[288,128]{1,0:T(8,128)(2,1)S(1)}, u32[]{:S(2)}, u32[]{:S(2)}) collective-permute-start(bf16[288,128]{1,0:T(8,128)(2,1)S(1)} %get-tuple-element.38), channel_id=1, source_target_pairs={{0,12},{4,8},{8,4},{12,0},{16,28},{20,24},{24,20},{28,16},{1,13},{... | collective-permute-start | bytes 221192 | tf_op jit(solution)/shard_map/ppermute | solution.py:583
  34.5 5.1 %collective-permute-start.14 = (bf16[288,128]{1,0:T(8,128)(2,1)S(1)}, bf16[288,128]{1,0:T(8,128)(2,1)S(1)}, u32[]{:S(2)}, u32[]{:S(2)}) collective-permute-start(bf16[288,128]{1,0:T(8,128)(2,1)S(1)} %get-tuple-element.39), channel_id=1, source_target_pairs={{0,4},{4,0},{8,20},{12,16},{16,12},{20,8},{24,28},{28,24},{1,5},{5... | collective-permute-start | bytes 221192 | tf_op jit(solution)/shard_map/ppermute | solution.py:583
  35.0 5.3 %collective-permute-start.15 = (bf16[288,128]{1,0:T(8,128)(2,1)S(1)}, bf16[288,128]{1,0:T(8,128)(2,1)S(1)}, u32[]{:S(2)}, u32[]{:S(2)}) collective-permute-start(bf16[288,128]{1,0:T(8,128)(2,1)S(1)} %get-tuple-element.40), channel_id=1, source_target_pairs={{0,8},{4,16},{8,0},{12,24},{16,4},{20,28},{24,12},{28,20},{1,9},{5... | collective-permute-start | bytes 221192 | tf_op jit(solution)/shard_map/ppermute | solution.py:583
  36.1 5.4 %collective-permute-start.16 = (bf16[288,128]{1,0:T(8,128)(2,1)S(1)}, bf16[288,128]{1,0:T(8,128)(2,1)S(1)}, u32[]{:S(2)}, u32[]{:S(2)}) collective-permute-start(bf16[288,128]{1,0:T(8,128)(2,1)S(1)} %get-tuple-element.41), channel_id=1, source_target_pairs={{0,8},{4,12},{8,0},{12,4},{16,24},{20,28},{24,16},{28,20},{1,9},{5... | collective-permute-start | bytes 221192 | tf_op jit(solution)/shard_map/ppermute | solution.py:583
  37.2 4.7 %collective-permute-start.17 = (bf16[288,128]{1,0:T(8,128)(2,1)S(1)}, bf16[288,128]{1,0:T(8,128)(2,1)S(1)}, u32[]{:S(2)}, u32[]{:S(2)}) collective-permute-start(bf16[288,128]{1,0:T(8,128)(2,1)S(1)} %get-tuple-element.42), channel_id=1, source_target_pairs={{0,4},{4,0},{8,16},{12,20},{16,8},{20,12},{24,28},{28,24},{1,5},{5... | collective-permute-start | bytes 221192 | tf_op jit(solution)/shard_map/ppermute | solution.py:583
  43.8 2.1 %collective-permute-start.18 = (bf16[576,512]{1,0:T(8,128)(2,1)S(1)}, bf16[576,512]{1,0:T(8,128)(2,1)S(1)}, u32[]{:S(2)}, u32[]{:S(2)}) collective-permute-start(bf16[576,512]{1,0:T(8,128)(2,1)S(1)} %grads_for.4), channel_id=1, source_target_pairs={{0,1},{1,0},{2,3},{3,2},{4,5},{5,4},{6,7},{7,6},{8,9},{9,8},{10,11... | collective-permute-start | bytes 1769480 | tf_op jit(solution)/shard_map/ppermute | solution.py:575
  46.0 15.4 %collective-permute-start.20 = (bf16[576,512]{1,0:T(8,128)(2,1)S(1)}, bf16[576,512]{1,0:T(8,128)(2,1)S(1)}, u32[]{:S(2)}, u32[]{:S(2)}) collective-permute-start(bf16[576,512]{1,0:T(8,128)(2,1)S(1)} %add_convert_fusion), channel_id=1, source_target_pairs={{0,2},{1,3},{2,0},{3,1},{4,6},{5,7},{6,4},{7,5},{8,10},{9,11},{10,... | collective-permute-start | bytes 1769480 | tf_op jit(solution)/shard_map/ppermute | solution.py:575
  50.0 2.1 %collective-permute-start.19 = (bf16[576,512]{1,0:T(8,128)(2,1)S(1)}, bf16[576,512]{1,0:T(8,128)(2,1)S(1)}, u32[]{:S(2)}, u32[]{:S(2)}) collective-permute-start(bf16[576,512]{1,0:T(8,128)(2,1)S(1)} %grads_for.7), channel_id=1, source_target_pairs={{0,1},{1,0},{2,3},{3,2},{4,5},{5,4},{6,7},{7,6},{8,9},{9,8},{10,11... | collective-permute-start | bytes 1769480 | tf_op jit(solution)/shard_map/ppermute | solution.py:575

commit v9 on v8

--- a/solution.py
+++ b/solution.py
@@ -156,7 +156,7 @@
 PARTS = ((0, 1), (2, 3))
 PART_SWAPS = ((7, 3, 1), (6, 2, 5, 7, 3))
 SWAPS = (1, 3, 7, 5, 2, 6)
-GRAD_SWAPS = (1, 3, 7, 5, 2, 6)
+GRAD_SWAPS = (7, 5, 6, 3, 1, 2)
 
 
 def fits(mesh):
@@ -530,29 +530,28 @@
     )(own, *received)
 
 
-def grad_kernel(flips, stack, weights, *outs):
+def grad_kernel(flip, first, stack, weights, out):
     member = lax.axis_index("filt")
-    for out, flip in zip(outs, flips):
-        columns = pl.ds(pl.multiple_of((member ^ flip) * 512, 512), 512)
-        out[...] = nn(stack[...], weights[:, columns]).astype(BF16)
-
-
-def grads_for(flips, stack, weights, scale=1):
-    return pl.pallas_call(
-        functools.partial(grad_kernel, flips),
-        out_shape=[jax.ShapeDtypeStruct((PIXELS, 512), BF16)] * len(flips),
+    columns = pl.ds(pl.multiple_of((member ^ flip) * 512 + first, 256), out.shape[1])
+    out[...] = nn(stack[...], weights[:, columns]).astype(BF16)
+
+
+def grads_for(flip, stack, weights, first=0, width=512, scale=1):
+    return pl.pallas_call(
+        functools.partial(grad_kernel, flip, first),
+        out_shape=jax.ShapeDtypeStruct((PIXELS, width), BF16),
         in_specs=[pl.BlockSpec(memory_space=pltpu.VMEM)] * 2,
-        out_specs=[pl.BlockSpec(memory_space=pltpu.VMEM)] * len(flips),
+        out_specs=pl.BlockSpec(memory_space=pltpu.VMEM),
         compiler_params=pltpu.CompilerParams(vmem_limit_bytes=18 * 2**20),
         cost_estimate=pl.CostEstimate(
-            flops=2 * PIXELS * 28 * W * 512 * scale, bytes_accessed=10**6, transcendentals=0
+            flops=2 * PIXELS * 28 * W * width * scale, bytes_accessed=10**6, transcendentals=0
         ),
         name="grads_for",
     )(stack, weights)
 
 
-def last_kernel(a, b, c, out):
-    total = a[...].astype(F32) + b[...].astype(F32) + c[...].astype(F32)
+def last_kernel(a, b, c, d, out):
+    total = a[...].astype(F32) + b[...].astype(F32) + both(c, d).astype(F32)
 
     def put(at, value):
         out[at : at + 192, :] = value
@@ -560,15 +559,15 @@
     from_blocks(order_matrix(True), total.astype(BF16), put)
 
 
-def last_sum(a, b, c):
+def last_sum(a, b, c, d):
     return pl.pallas_call(
         last_kernel,
         out_shape=jax.ShapeDtypeStruct((PIXELS, 512), BF16),
-        in_specs=[pl.BlockSpec(memory_space=pltpu.VMEM)] * 3,
+        in_specs=[pl.BlockSpec(memory_space=pltpu.VMEM)] * 4,
         out_specs=pl.BlockSpec(memory_space=pltpu.VMEM),
         compiler_params=pltpu.CompilerParams(vmem_limit_bytes=10 * 2**20),
         name="last_sum",
-    )(a, b, c)
+    )(a, b, c, d)
 
 
 def flipped(x, bit):
@@ -616,17 +615,19 @@
     )
     arrived = [swapped(sends[n], x) for n, x in enumerate(GRAD_SWAPS)]
     stack = spread(grads, arrived)
-    (far,) = grads_for((3,), stack, weights)
-    far = flipped(far, 1)
-    (kept,) = grads_for((2,), stack, weights)
-    crossing = (far.astype(F32) + kept.astype(F32)).astype(BF16)
-    crossed = flipped(crossing, 2)
+    far = [flipped(grads_for(3, stack, weights, at, 256), 1) for at in (0, 256)]
+    kept = grads_for(2, stack, weights, 0, 256)
+    crossing = (far[0].astype(F32) + kept.astype(F32)).astype(BF16)
+    crossed = [flipped(crossing, 2)]
+    later, crossing = lax.optimization_barrier((stack, crossing))
+    kept = grads_for(2, later, weights, 256, 256)
+    crossing = (far[1].astype(F32) + kept.astype(F32)).astype(BF16)
+    crossed.append(flipped(crossing, 2))
     later, output, crossing = lax.optimization_barrier((stack, output, crossing))
     head_output = own_output(output)
-    (near,) = grads_for((1,), later, weights)
-    near = flipped(near, 1)
-    (kept,) = grads_for((0,), later, weights, 8)
-    feature_grad = last_sum(kept, near, crossed)
+    near = flipped(grads_for(1, later, weights), 1)
+    kept = grads_for(0, later, weights, scale=8)
+    feature_grad = last_sum(kept, near, *crossed)
     return head_output.reshape(12, 48, W), feature_grad.reshape(12, 48, 512)
 
 

time: 62.8 us -> 62.5 us (level)
  waiting for transfers between devices: 18.6 us -> 16.7 us
  starting transfers between devices: 23.5 us -> 24.6 us
    ppermute x9 -> x11, waiting for transfers between devices: 16.1 us -> 13.8 us  [flipped(): lax.ppermute(x, 'filt', [(i, i ^ bit) for i in range(lax.axis_size('filt'...]
    ppermute x9 -> x11, starting transfers between devices: 4.44 us -> 5.56 us  [flipped(): lax.ppermute(x, 'filt', [(i, i ^ bit) for i in range(lax.axis_size('filt'...]
    pallas_call x4 -> x6, Pallas kernels: 4.95 us -> 5.34 us  [grads_for(): pl.pallas_call(functools.partial(grad_kernel, flip, first), out_shape=jax...]
  transfers between devices with their start and end apart: 21 -> 23, of which waited for: 10 -> 7; matrix products, arithmetic and copies ran while one was open for 0% -> 0% of each run, Pallas kernels for 12% -> 13%
where the time goes in v9:
time: 62.5 us; the launch traced here: 62.3 us
  starting transfers between devices  24.6 us (39%)
  Pallas kernels  19.7 us (32%)
  waiting for transfers between devices  16.7 us (27%)
  between operations  0.95 us (2%)
    ppermute x12, starting transfers between devices, swapped(): return lax.ppermute(x, 'rows', [(r, partner(r, bits)) for r in range(8)])  19 us
    ppermute x11, waiting for transfers between devices, flipped(): lax.ppermute(x, 'filt', [(i, i ^ bit) for i in range(lax.axis_size('filt'...  13.8 us
    pallas_call x1, Pallas kernels, outward_sums(): pl.pallas_call(outward_kernel, out_shape=[jax.ShapeDtypeStruct((SENT, 128...  8.22 us
    ppermute x11, starting transfers between devices, flipped(): lax.ppermute(x, 'filt', [(i, i ^ bit) for i in range(lax.axis_size('filt'...  5.56 us
    pallas_call x6, Pallas kernels, grads_for(): pl.pallas_call(functools.partial(grad_kernel, flip, first), out_shape=jax...  5.34 us
    ppermute x12, waiting for transfers between devices, swapped(): return lax.ppermute(x, 'rows', [(r, partner(r, bits)) for r in range(8)])  2.89 us
    pallas_call x1, Pallas kernels, own_sums(): pl.pallas_call(own_kernel, out_shape=[jax.ShapeDtypeStruct((PIXELS, 128),...  1.72 us
    pallas_call x1, Pallas kernels, last_sum(): pl.pallas_call(last_kernel, out_shape=jax.ShapeDtypeStruct((PIXELS, 512),...  1.26 us
  transfers between devices with their start and end apart: 23, of which 7 were waited for; matrix products, arithmetic and copies ran while one was open for 0% of the time, Pallas kernels for 13%

profile of v9, /device:TPU:0, one launch (start us, length us, event | category | flops | bytes accessed | tf_op | source)
XLA Modules:
  0.0 62.3 jit_solution(8116831882759581211)
XLA Ops:
  0.6 8.2 %outward_sums.1 = (f32[304,128]{1,0:T(8,128)S(1)}, f32[304,128]{1,0:T(8,128)S(1)}, f32[304,128]{1,0:T(8,128)S(1)}, f32[304,128]{1,0:T(8,128)S(1)}, f32[304,128]{...) custom-call(bf16[576,2048]{1,0:T(8,128)(2,1)} %bitcast.12, ...), custom_call_target="tpu_custom_call" | custom-call | tf_op jit(solution)/shard_map/outward_sums/pallas_call | solution.py:297
  8.9 3.0 %collective-permute-start.2 = (f16[304,128]{1,0:T(8,128)(2,1)S(1)}, f16[304,128]{1,0:T(8,128)(2,1)S(1)}, u32[]{:S(2)}, u32[]{:S(2)}) collective-permute-start(f16[304,128]{1,0:T(8,128)(2,1)S(1)} %convert_element_type.58), channel_id=1, source_target_pairs={{0,4},{4,0},{8,12},{12,8},{16,20},{20,16},{24,28},{28,24},{1,5},{5... | collective-permute-start | bytes 233480 | tf_op jit(solution)/shard_map/ppermute | solution.py:582
  11.9 1.6 %collective-permute-start.1 = (f16[304,128]{1,0:T(8,128)(2,1)S(1)}, f16[304,128]{1,0:T(8,128)(2,1)S(1)}, u32[]{:S(2)}, u32[]{:S(2)}) collective-permute-start(f16[304,128]{1,0:T(8,128)(2,1)S(1)} %convert_element_type.56), channel_id=1, source_target_pairs={{0,12},{4,8},{8,4},{12,0},{16,28},{20,24},{24,20},{28,16},{1,13},{... | collective-permute-start | bytes 233480 | tf_op jit(solution)/shard_map/ppermute | solution.py:582
  13.6 1.5 %collective-permute-start = (f16[304,128]{1,0:T(8,128)(2,1)S(1)}, f16[304,128]{1,0:T(8,128)(2,1)S(1)}, u32[]{:S(2)}, u32[]{:S(2)}) collective-permute-start(f16[304,128]{1,0:T(8,128)(2,1)S(1)} %convert_element_type.54), channel_id=1, source_target_pairs={{0,4},{4,0},{8,20},{12,16},{16,12},{20,8},{24,28},{28,24},{1,5},{5... | collective-permute-start | bytes 233480 | tf_op jit(solution)/shard_map/ppermute | solution.py:582
  15.1 2.7 %collective-permute-start.5 = (f16[304,128]{1,0:T(8,128)(2,1)S(1)}, f16[304,128]{1,0:T(8,128)(2,1)S(1)}, u32[]{:S(2)}, u32[]{:S(2)}) collective-permute-start(f16[304,128]{1,0:T(8,128)(2,1)S(1)} %convert_element_type.64), channel_id=1, source_target_pairs={{0,8},{4,16},{8,0},{12,24},{16,4},{20,28},{24,12},{28,20},{1,9},{5... | collective-permute-start | bytes 233480 | tf_op jit(solution)/shard_map/ppermute | solution.py:582
  17.9 2.0 %collective-permute-start.3 = (f16[304,128]{1,0:T(8,128)(2,1)S(1)}, f16[304,128]{1,0:T(8,128)(2,1)S(1)}, u32[]{:S(2)}, u32[]{:S(2)}) collective-permute-start(f16[304,128]{1,0:T(8,128)(2,1)S(1)} %convert_element_type.60), channel_id=1, source_target_pairs={{0,4},{4,0},{8,16},{12,20},{16,8},{20,12},{24,28},{28,24},{1,5},{5... | collective-permute-start | bytes 233480 | tf_op jit(solution)/shard_map/ppermute | solution.py:582
  19.9 1.7 %own_sums.1 = (f32[576,128]{1,0:T(8,128)S(1)}, f32[576,128]{1,0:T(8,128)S(1)}) custom-call(bf16[576,2048]{1,0:T(8,128)(2,1)S(1)} %get-tuple-element.25.ordered, bf16[1792,2048]{1,0:T(8,128)(2,1)S(1)} %get-tuple-element.26.weights, f32[4,64]{1,0:T(4,128)S(1)} %copy-done.2), custom_call_target="tpu_custom_call" | custom-call | flops 1000000 | bytes 10000 | tf_op jit(solution)/shard_map/own_sums/pallas_call | solution.py:338
  21.9 1.6 %collective-permute-start.6 = (bf16[576,128]{1,0:T(8,128)(2,1)S(1)}, bf16[576,128]{1,0:T(8,128)(2,1)S(1)}, u32[]{:S(2)}, u32[]{:S(2)}) collective-permute-start(bf16[576,128]{1,0:T(8,128)(2,1)S(1)} %activations.2.a0), channel_id=1, source_target_pairs={{0,2},{1,3},{2,0},{3,1},{4,6},{5,7},{6,4},{7,5},{8,10},{9,11},{10,... | collective-permute-start | bytes 442376 | tf_op jit(solution)/shard_map/ppermute | solution.py:574
  23.8 0.6 collective-permute-start.7
  24.9 2.8 %collective-permute-done.6.a2 = bf16[576,128]{1,0:T(8,128)(2,1)S(1)} collective-permute-done((bf16[576,128]{1,0:T(8,128)(2,1)S(1)}, bf16[576,128]{1,0:T(8,128)(2,1)S(1)}, u32[]{:S(2)}, u32[]{:S(2)}) %collective-permute-start.6) | collective-permute-done | bytes 147488 | tf_op jit(solution)/shard_map/ppermute | solution.py:574
  27.6 1.6 %collective-permute-done.7.b2 = bf16[576,128]{1,0:T(8,128)(2,1)S(1)} collective-permute-done((bf16[576,128]{1,0:T(8,128)(2,1)S(1)}, bf16[576,128]{1,0:T(8,128)(2,1)S(1)}, u32[]{:S(2)}, u32[]{:S(2)}) %collective-permute-start.7) | collective-permute-done | bytes 147488 | tf_op jit(solution)/shard_map/ppermute | solution.py:574
  29.7 0.9 %collective-permute-done.9.b3 = bf16[576,128]{1,0:T(8,128)(2,1)S(1)} collective-permute-done((bf16[576,128]{1,0:T(8,128)(2,1)S(1)}, bf16[576,128]{1,0:T(8,128)(2,1)S(1)}, u32[]{:S(2)}, u32[]{:S(2)}) %collective-permute-start.9) | collective-permute-done | bytes 147488 | tf_op jit(solution)/shard_map/ppermute | solution.py:574
  30.6 0.6 %far_head.1 = (bf16[576,256]{1,0:T(8,128)(2,1)S(1)}, bf16[576,256]{1,0:T(8,128)(2,1)S(1)}, bf16[288,128]{1,0:T(8,128)(2,1)S(1)}, bf16[288,128]{1,0:T(8,128)(2,1)...) custom-call(bf16[576,128]{1,0:T(8,128)(2,1)S(1)} %activations.2.a0, ...), custom_call_target="tpu_custom_call" | custom-call | tf_op jit(solution)/shard_map/far_head/pallas_call | solution.py:444
  31.2 0.7 %collective-permute-start.12 = (bf16[288,128]{1,0:T(8,128)(2,1)S(1)}, bf16[288,128]{1,0:T(8,128)(2,1)S(1)}, u32[]{:S(2)}, u32[]{:S(2)}) collective-permute-start(bf16[288,128]{1,0:T(8,128)(2,1)S(1)} %get-tuple-element.38), channel_id=1, source_target_pairs={{0,4},{4,0},{8,20},{12,16},{16,12},{20,8},{24,28},{28,24},{1,5},{5... | collective-permute-start | bytes 221192 | tf_op jit(solution)/shard_map/ppermute | solution.py:582
  31.9 2.8 %collective-permute-start.13 = (bf16[288,128]{1,0:T(8,128)(2,1)S(1)}, bf16[288,128]{1,0:T(8,128)(2,1)S(1)}, u32[]{:S(2)}, u32[]{:S(2)}) collective-permute-start(bf16[288,128]{1,0:T(8,128)(2,1)S(1)} %get-tuple-element.39), channel_id=1, source_target_pairs={{0,8},{4,16},{8,0},{12,24},{16,4},{20,28},{24,12},{28,20},{1,9},{5... | collective-permute-start | bytes 221192 | tf_op jit(solution)/shard_map/ppermute | solution.py:582
  34.6 1.2 %collective-permute-start.14 = (bf16[288,128]{1,0:T(8,128)(2,1)S(1)}, bf16[288,128]{1,0:T(8,128)(2,1)S(1)}, u32[]{:S(2)}, u32[]{:S(2)}) collective-permute-start(bf16[288,128]{1,0:T(8,128)(2,1)S(1)} %get-tuple-element.40), channel_id=1, source_target_pairs={{0,4},{4,0},{8,16},{12,20},{16,8},{20,12},{24,28},{28,24},{1,5},{5... | collective-permute-start | bytes 221192 | tf_op jit(solution)/shard_map/ppermute | solution.py:582
  35.9 0.6 collective-permute-start.15
  36.5 1.2 %collective-permute-start.16 = (bf16[288,128]{1,0:T(8,128)(2,1)S(1)}, bf16[288,128]{1,0:T(8,128)(2,1)S(1)}, u32[]{:S(2)}, u32[]{:S(2)}) collective-permute-start(bf16[288,128]{1,0:T(8,128)(2,1)S(1)} %get-tuple-element.42), channel_id=1, source_target_pairs={{0,4},{4,0},{8,12},{12,8},{16,20},{20,16},{24,28},{28,24},{1,5},{5... | collective-permute-start | bytes 221192 | tf_op jit(solution)/shard_map/ppermute | solution.py:582
  37.7 1.7 %collective-permute-start.17 = (bf16[288,128]{1,0:T(8,128)(2,1)S(1)}, bf16[288,128]{1,0:T(8,128)(2,1)S(1)}, u32[]{:S(2)}, u32[]{:S(2)}) collective-permute-start(bf16[288,128]{1,0:T(8,128)(2,1)S(1)} %get-tuple-element.43), channel_id=1, source_target_pairs={{0,8},{4,12},{8,0},{12,4},{16,24},{20,28},{24,16},{28,20},{1,9},{5... | collective-permute-start | bytes 221192 | tf_op jit(solution)/shard_map/ppermute | solution.py:582
  39.4 1.9 %collective-permute-done.14.refs_2_ = bf16[288,128]{1,0:T(8,128)(2,1)S(1)} collective-permute-done((bf16[288,128]{1,0:T(8,128)(2,1)S(1)}, bf16[288,128]{1,0:T(8,128)(2,1)S(1)}, u32[]{:S(2)}, u32[]{:S(2)}) %collective-permute-start.14) | collective-permute-done | bytes 73760 | tf_op jit(solution)/shard_map/ppermute | solution.py:582
  41.2 0.8 %collective-permute-done.16.refs_4_ = bf16[288,128]{1,0:T(8,128)(2,1)S(1)} collective-permute-done((bf16[288,128]{1,0:T(8,128)(2,1)S(1)}, bf16[288,128]{1,0:T(8,128)(2,1)S(1)}, u32[]{:S(2)}, u32[]{:S(2)}) %collective-permute-start.16) | collective-permute-done | bytes 73760 | tf_op jit(solution)/shard_map/ppermute | solution.py:582
  42.2 0.6 spread.1.stack
  42.8 0.7 %grads_for.7 = bf16[576,256]{1,0:T(8,128)(2,1)S(1)} custom-call(bf16[576,1792]{1,0:T(8,128)(2,1)S(1)} %spread.1.stack, bf16[1792,2048]{1,0:T(8,128)(2,1)S(1)} %get-tuple-element.26.weights), custom_call_target="tpu_custom_call" | custom-call | flops 528482304 | bytes 1000000 | tf_op jit(solution)/shard_map/grads_for/pallas_call | solution.py:540
  43.6 0.7 %grads_for.6 = bf16[576,256]{1,0:T(8,128)(2,1)S(1)} custom-call(bf16[576,1792]{1,0:T(8,128)(2,1)S(1)} %spread.1.stack, bf16[1792,2048]{1,0:T(8,128)(2,1)S(1)} %get-tuple-element.26.weights), custom_call_target="tpu_custom_call" | custom-call | flops 528482304 | bytes 1000000 | tf_op jit(solution)/shard_map/grads_for/pallas_call | solution.py:540
  44.9 0.7 %grads_for.8 = bf16[576,256]{1,0:T(8,128)(2,1)S(1)} custom-call(bf16[576,1792]{1,0:T(8,128)(2,1)S(1)} %spread.1.stack, bf16[1792,2048]{1,0:T(8,128)(2,1)S(1)} %get-tuple-element.26.weights), custom_call_target="tpu_custom_call" | custom-call | flops 528482304 | bytes 1000000 | tf_op jit(solution)/shard_map/grads_for/pallas_call | solution.py:540
  45.7 1.6 %collective-permute-start.21 = (bf16[576,256]{1,0:T(8,128)(2,1)S(1)}, bf16[576,256]{1,0:T(8,128)(2,1)S(1)}, u32[]{:S(2)}, u32[]{:S(2)}) collective-permute-start(bf16[576,256]{1,0:T(8,128)(2,1)S(1)} %add_convert_fusion.1), channel_id=1, source_target_pairs={{0,2},{1,3},{2,0},{3,1},{4,6},{5,7},{6,4},{7,5},{8,10},{9,11},{10,... | collective-permute-start | bytes 884744 | tf_op jit(solution)/shard_map/ppermute | solution.py:574
  47.3 0.7 %grads_for.9 = bf16[576,256]{1,0:T(8,128)(2,1)S(1)} custom-call(bf16[576,1792]{1,0:T(8,128)(2,1)S(1)} %spread.1.stack, bf16[1792,2048]{1,0:T(8,128)(2,1)S(1)} %get-tuple-element.26.weights), custom_call_target="tpu_custom_call" | custom-call | flops 528482304 | bytes 1000000 | tf_op jit(solution)/shard_map/grads_for/pallas_call | solution.py:540
  48.7 1.2 %grads_for.11 = bf16[576,512]{1,0:T(8,128)(2,1)S(1)} custom-call(bf16[576,1792]{1,0:T(8,128)(2,1)S(1)} %spread.1.stack, bf16[1792,2048]{1,0:T(8,128)(2,1)S(1)} %get-tuple-element.26.weights), custom_call_target="tpu_custom_call" | custom-call | flops 1056964608 | bytes 1000000 | tf_op jit(solution)/shard_map/grads_for/pallas_call | solution.py:540
  50.0 1.2 %grads_for.10.a = bf16[576,512]{1,0:T(8,128)(2,1)S(1)} custom-call(bf16[576,1792]{1,0:T(8,128)(2,1)S(1)} %spread.1.stack, bf16[1792,2048]{1,0:T(8,128)(2,1)S(1)} %get-tuple-element.26.weights), custom_call_target="tpu_custom_call" | custom-call | flops 8455716864 | bytes 1000000 | tf_op jit(solution)/shard_map/grads_for/pallas_call | solution.py:540
  51.2 1.2 %own_output.1 = bf16[576,64]{1,0:T(8,128)(2,1)} custom-call(bf16[576,256]{1,0:T(8,128)(2,1)S(1)} %get-tuple-element.46.output), custom_call_target="tpu_custom_call" | custom-call | tf_op jit(solution)/shard_map/own_output/pallas_call | solution.py:469
  52.5 8.6 %collective-permute-done.22.d = bf16[576,256]{1,0:T(8,128)(2,1)S(1)} collective-permute-done((bf16[576,256]{1,0:T(8,128)(2,1)S(1)}, bf16[576,256]{1,0:T(8,128)(2,1)S(1)}, u32[]{:S(2)}, u32[]{:S(2)}) %collective-permute-start.22) | collective-permute-done | bytes 294944 | tf_op jit(solution)/shard_map/ppermute | solution.py:574
  61.0 1.3 %last_sum.1 = bf16[576,512]{1,0:T(8,128)(2,1)} custom-call(bf16[576,512]{1,0:T(8,128)(2,1)S(1)} %grads_for.10.a, bf16[576,512]{1,0:T(8,128)(2,1)S(1)} %collective-permute-done.20.b, bf16[576,256]{1,0:T(8,128)(2,1)S(1)} %collective-permute-done.21.c, bf16[576,256]{1,0:T(8,128)(2,1)S(1)} %collective-permute-done.22.d), custom_call_target="tpu_custom_call" | custom-call | tf_op jit(solution)/shard_map/last_sum/pallas_call | solution.py:563
  (51 shorter events, 3.2 us)
Async XLA Ops:
  0.6 19.2 %copy-start.2 = (f32[4,64]{1,0:T(4,128)S(1)}, f32[4,64]{1,0:T(4,128)}, u32[]{:S(2)}) copy-start(f32[4,64]{1,0:T(4,128)} %bias.1) | copy-start | bytes 3076
  8.9 9.0 %collective-permute-start.2 = (f16[304,128]{1,0:T(8,128)(2,1)S(1)}, f16[304,128]{1,0:T(8,128)(2,1)S(1)}, u32[]{:S(2)}, u32[]{:S(2)}) collective-permute-start(f16[304,128]{1,0:T(8,128)(2,1)S(1)} %convert_element_type.58), channel_id=1, source_target_pairs={{0,4},{4,0},{8,12},{12,8},{16,20},{20,16},{24,28},{28,24},{1,5},{5... | collective-permute-start | bytes 233480 | tf_op jit(solution)/shard_map/ppermute | solution.py:582
  11.9 9.7 %collective-permute-start.1 = (f16[304,128]{1,0:T(8,128)(2,1)S(1)}, f16[304,128]{1,0:T(8,128)(2,1)S(1)}, u32[]{:S(2)}, u32[]{:S(2)}) collective-permute-start(f16[304,128]{1,0:T(8,128)(2,1)S(1)} %convert_element_type.56), channel_id=1, source_target_pairs={{0,12},{4,8},{8,4},{12,0},{16,28},{20,24},{24,20},{28,16},{1,13},{... | collective-permute-start | bytes 233480 | tf_op jit(solution)/shard_map/ppermute | solution.py:582
  13.6 8.1 %collective-permute-start = (f16[304,128]{1,0:T(8,128)(2,1)S(1)}, f16[304,128]{1,0:T(8,128)(2,1)S(1)}, u32[]{:S(2)}, u32[]{:S(2)}) collective-permute-start(f16[304,128]{1,0:T(8,128)(2,1)S(1)} %convert_element_type.54), channel_id=1, source_target_pairs={{0,4},{4,0},{8,20},{12,16},{16,12},{20,8},{24,28},{28,24},{1,5},{5... | collective-permute-start | bytes 233480 | tf_op jit(solution)/shard_map/ppermute | solution.py:582
  15.1 8.4 %collective-permute-start.5 = (f16[304,128]{1,0:T(8,128)(2,1)S(1)}, f16[304,128]{1,0:T(8,128)(2,1)S(1)}, u32[]{:S(2)}, u32[]{:S(2)}) collective-permute-start(f16[304,128]{1,0:T(8,128)(2,1)S(1)} %convert_element_type.64), channel_id=1, source_target_pairs={{0,8},{4,16},{8,0},{12,24},{16,4},{20,28},{24,12},{28,20},{1,9},{5... | collective-permute-start | bytes 233480 | tf_op jit(solution)/shard_map/ppermute | solution.py:582
  17.8 5.7 %collective-permute-start.4 = (f16[304,128]{1,0:T(8,128)(2,1)S(1)}, f16[304,128]{1,0:T(8,128)(2,1)S(1)}, u32[]{:S(2)}, u32[]{:S(2)}) collective-permute-start(f16[304,128]{1,0:T(8,128)(2,1)S(1)} %convert_element_type.62), channel_id=1, source_target_pairs={{0,8},{4,12},{8,0},{12,4},{16,24},{20,28},{24,16},{28,20},{1,9},{5... | collective-permute-start | bytes 233480 | tf_op jit(solution)/shard_map/ppermute | solution.py:582
  17.9 5.6 %collective-permute-start.3 = (f16[304,128]{1,0:T(8,128)(2,1)S(1)}, f16[304,128]{1,0:T(8,128)(2,1)S(1)}, u32[]{:S(2)}, u32[]{:S(2)}) collective-permute-start(f16[304,128]{1,0:T(8,128)(2,1)S(1)} %convert_element_type.60), channel_id=1, source_target_pairs={{0,4},{4,0},{8,16},{12,20},{16,8},{20,12},{24,28},{28,24},{1,5},{5... | collective-permute-start | bytes 233480 | tf_op jit(solution)/shard_map/ppermute | solution.py:582
  21.6 7.6 %copy-start = (bf16[4,256,256]{2,1,0:T(8,128)(2,1)S(1)}, bf16[4,256,256]{2,1,0:T(8,128)(2,1)}, u32[]{:S(2)}) copy-start(bf16[4,256,256]{2,1,0:T(8,128)(2,1)} %project.3) | copy-start | bytes 1572868
  21.6 7.6 %copy-start.1 = (bf16[12,48,256]{2,1,0:T(8,128)(2,1)S(1)}, bf16[12,48,256]{2,1,0:T(8,128)(2,1)}, u32[]{:S(2)}) copy-start(bf16[12,48,256]{2,1,0:T(8,128)(2,1)} %param.13) | copy-start | bytes 884740
  21.6 7.6 %copy-start.3 = (f32[256]{0:T(256)S(1)}, f32[256]{0:T(256)}, u32[]{:S(2)}) copy-start(f32[256]{0:T(256)} %param.12) | copy-start | bytes 3076
  21.9 5.7 %collective-permute-start.6 = (bf16[576,128]{1,0:T(8,128)(2,1)S(1)}, bf16[576,128]{1,0:T(8,128)(2,1)S(1)}, u32[]{:S(2)}, u32[]{:S(2)}) collective-permute-start(bf16[576,128]{1,0:T(8,128)(2,1)S(1)} %activations.2.a0), channel_id=1, source_target_pairs={{0,2},{1,3},{2,0},{3,1},{4,6},{5,7},{6,4},{7,5},{8,10},{9,11},{10,... | collective-permute-start | bytes 442376 | tf_op jit(solution)/shard_map/ppermute | solution.py:574
  23.8 5.4 %collective-permute-start.7 = (bf16[576,128]{1,0:T(8,128)(2,1)S(1)}, bf16[576,128]{1,0:T(8,128)(2,1)S(1)}, u32[]{:S(2)}, u32[]{:S(2)}) collective-permute-start(bf16[576,128]{1,0:T(8,128)(2,1)S(1)} %activations.3.b0), channel_id=1, source_target_pairs={{0,2},{1,3},{2,0},{3,1},{4,6},{5,7},{6,4},{7,5},{8,10},{9,11},{10,... | collective-permute-start | bytes 442376 | tf_op jit(solution)/shard_map/ppermute | solution.py:574
  24.4 4.9 %collective-permute-start.10 = (bf16[576,128]{1,0:T(8,128)(2,1)S(1)}, bf16[576,128]{1,0:T(8,128)(2,1)S(1)}, u32[]{:S(2)}, u32[]{:S(2)}) collective-permute-start(bf16[576,128]{1,0:T(8,128)(2,1)S(1)} %activations.2.a0), channel_id=1, source_target_pairs={{0,1},{1,0},{2,3},{3,2},{4,5},{5,4},{6,7},{7,6},{8,9},{9,8},{10,11... | collective-permute-start | bytes 442376 | tf_op jit(solution)/shard_map/ppermute | solution.py:574
  24.4 4.9 %collective-permute-start.11 = (bf16[576,128]{1,0:T(8,128)(2,1)S(1)}, bf16[576,128]{1,0:T(8,128)(2,1)S(1)}, u32[]{:S(2)}, u32[]{:S(2)}) collective-permute-start(bf16[576,128]{1,0:T(8,128)(2,1)S(1)} %activations.3.b0), channel_id=1, source_target_pairs={{0,1},{1,0},{2,3},{3,2},{4,5},{5,4},{6,7},{7,6},{8,9},{9,8},{10,11... | collective-permute-start | bytes 442376 | tf_op jit(solution)/shard_map/ppermute | solution.py:574
  27.6 2.0 %collective-permute-start.8 = (bf16[576,128]{1,0:T(8,128)(2,1)S(1)}, bf16[576,128]{1,0:T(8,128)(2,1)S(1)}, u32[]{:S(2)}, u32[]{:S(2)}) collective-permute-start(bf16[576,128]{1,0:T(8,128)(2,1)S(1)} %collective-permute-done.6.a2), channel_id=1, source_target_pairs={{0,1},{1,0},{2,3},{3,2},{4,5},{5,4},{6,7},{7,6},{8,9},{9,8},{10,11... | collective-permute-start | bytes 442376 | tf_op jit(solution)/shard_map/ppermute | solution.py:574
  29.2 1.4 %collective-permute-start.9 = (bf16[576,128]{1,0:T(8,128)(2,1)S(1)}, bf16[576,128]{1,0:T(8,128)(2,1)S(1)}, u32[]{:S(2)}, u32[]{:S(2)}) collective-permute-start(bf16[576,128]{1,0:T(8,128)(2,1)S(1)} %collective-permute-done.7.b2), channel_id=1, source_target_pairs={{0,1},{1,0},{2,3},{3,2},{4,5},{5,4},{6,7},{7,6},{8,9},{9,8},{10,11... | collective-permute-start | bytes 442376 | tf_op jit(solution)/shard_map/ppermute | solution.py:574
  31.2 6.5 %collective-permute-start.12 = (bf16[288,128]{1,0:T(8,128)(2,1)S(1)}, bf16[288,128]{1,0:T(8,128)(2,1)S(1)}, u32[]{:S(2)}, u32[]{:S(2)}) collective-permute-start(bf16[288,128]{1,0:T(8,128)(2,1)S(1)} %get-tuple-element.38), channel_id=1, source_target_pairs={{0,4},{4,0},{8,20},{12,16},{16,12},{20,8},{24,28},{28,24},{1,5},{5... | collective-permute-start | bytes 221192 | tf_op jit(solution)/shard_map/ppermute | solution.py:582
  31.9 7.5 %collective-permute-start.13 = (bf16[288,128]{1,0:T(8,128)(2,1)S(1)}, bf16[288,128]{1,0:T(8,128)(2,1)S(1)}, u32[]{:S(2)}, u32[]{:S(2)}) collective-permute-start(bf16[288,128]{1,0:T(8,128)(2,1)S(1)} %get-tuple-element.39), channel_id=1, source_target_pairs={{0,8},{4,16},{8,0},{12,24},{16,4},{20,28},{24,12},{28,20},{1,9},{5... | collective-permute-start | bytes 221192 | tf_op jit(solution)/shard_map/ppermute | solution.py:582
  34.6 6.6 %collective-permute-start.14 = (bf16[288,128]{1,0:T(8,128)(2,1)S(1)}, bf16[288,128]{1,0:T(8,128)(2,1)S(1)}, u32[]{:S(2)}, u32[]{:S(2)}) collective-permute-start(bf16[288,128]{1,0:T(8,128)(2,1)S(1)} %get-tuple-element.40), channel_id=1, source_target_pairs={{0,4},{4,0},{8,16},{12,20},{16,8},{20,12},{24,28},{28,24},{1,5},{5... | collective-permute-start | bytes 221192 | tf_op jit(solution)/shard_map/ppermute | solution.py:582
  35.9 5.4 %collective-permute-start.15 = (bf16[288,128]{1,0:T(8,128)(2,1)S(1)}, bf16[288,128]{1,0:T(8,128)(2,1)S(1)}, u32[]{:S(2)}, u32[]{:S(2)}) collective-permute-start(bf16[288,128]{1,0:T(8,128)(2,1)S(1)} %get-tuple-element.41), channel_id=1, source_target_pairs={{0,12},{4,8},{8,4},{12,0},{16,28},{20,24},{24,20},{28,16},{1,13},{... | collective-permute-start | bytes 221192 | tf_op jit(solution)/shard_map/ppermute | solution.py:582
  36.5 5.6 %collective-permute-start.16 = (bf16[288,128]{1,0:T(8,128)(2,1)S(1)}, bf16[288,128]{1,0:T(8,128)(2,1)S(1)}, u32[]{:S(2)}, u32[]{:S(2)}) collective-permute-start(bf16[288,128]{1,0:T(8,128)(2,1)S(1)} %get-tuple-element.42), channel_id=1, source_target_pairs={{0,4},{4,0},{8,12},{12,8},{16,20},{20,16},{24,28},{28,24},{1,5},{5... | collective-permute-start | bytes 221192 | tf_op jit(solution)/shard_map/ppermute | solution.py:582
  37.7 4.5 %collective-permute-start.17 = (bf16[288,128]{1,0:T(8,128)(2,1)S(1)}, bf16[288,128]{1,0:T(8,128)(2,1)S(1)}, u32[]{:S(2)}, u32[]{:S(2)}) collective-permute-start(bf16[288,128]{1,0:T(8,128)(2,1)S(1)} %get-tuple-element.43), channel_id=1, source_target_pairs={{0,8},{4,12},{8,0},{12,4},{16,24},{20,28},{24,16},{28,20},{1,9},{5... | collective-permute-start | bytes 221192 | tf_op jit(solution)/shard_map/ppermute | solution.py:582
  43.5 2.1 %collective-permute-start.19 = (bf16[576,256]{1,0:T(8,128)(2,1)S(1)}, bf16[576,256]{1,0:T(8,128)(2,1)S(1)}, u32[]{:S(2)}, u32[]{:S(2)}) collective-permute-start(bf16[576,256]{1,0:T(8,128)(2,1)S(1)} %grads_for.7), channel_id=1, source_target_pairs={{0,1},{1,0},{2,3},{3,2},{4,5},{5,4},{6,7},{7,6},{8,9},{9,8},{10,11... | collective-permute-start | bytes 884744 | tf_op jit(solution)/shard_map/ppermute | solution.py:574
  44.4 3.7 %collective-permute-start.18 = (bf16[576,256]{1,0:T(8,128)(2,1)S(1)}, bf16[576,256]{1,0:T(8,128)(2,1)S(1)}, u32[]{:S(2)}, u32[]{:S(2)}) collective-permute-start(bf16[576,256]{1,0:T(8,128)(2,1)S(1)} %grads_for.6), channel_id=1, source_target_pairs={{0,1},{1,0},{2,3},{3,2},{4,5},{5,4},{6,7},{7,6},{8,9},{9,8},{10,11... | collective-permute-start | bytes 884744 | tf_op jit(solution)/shard_map/ppermute | solution.py:574
  45.7 15.3 %collective-permute-start.21 = (bf16[576,256]{1,0:T(8,128)(2,1)S(1)}, bf16[576,256]{1,0:T(8,128)(2,1)S(1)}, u32[]{:S(2)}, u32[]{:S(2)}) collective-permute-start(bf16[576,256]{1,0:T(8,128)(2,1)S(1)} %add_convert_fusion.1), channel_id=1, source_target_pairs={{0,2},{1,3},{2,0},{3,1},{4,6},{5,7},{6,4},{7,5},{8,10},{9,11},{10,... | collective-permute-start | bytes 884744 | tf_op jit(solution)/shard_map/ppermute | solution.py:574
  48.1 12.9 %collective-permute-start.22 = (bf16[576,256]{1,0:T(8,128)(2,1)S(1)}, bf16[576,256]{1,0:T(8,128)(2,1)S(1)}, u32[]{:S(2)}, u32[]{:S(2)}) collective-permute-start(bf16[576,256]{1,0:T(8,128)(2,1)S(1)} %add_convert_fusion), channel_id=1, source_target_pairs={{0,2},{1,3},{2,0},{3,1},{4,6},{5,7},{6,4},{7,5},{8,10},{9,11},{10,... | collective-permute-start | bytes 884744 | tf_op jit(solution)/shard_map/ppermute | solution.py:574
  49.9 11.1 %collective-permute-start.20 = (bf16[576,512]{1,0:T(8,128)(2,1)S(1)}, bf16[576,512]{1,0:T(8,128)(2,1)S(1)}, u32[]{:S(2)}, u32[]{:S(2)}) collective-permute-start(bf16[576,512]{1,0:T(8,128)(2,1)S(1)} %grads_for.11), channel_id=1, source_target_pairs={{0,1},{1,0},{2,3},{3,2},{4,5},{5,4},{6,7},{7,6},{8,9},{9,8},{10,11... | collective-permute-start | bytes 1769480 | tf_op jit(solution)/shard_map/ppermute | solution.py:574

commit v10 on v9

--- a/solution.py
+++ b/solution.py
@@ -228,8 +228,8 @@
     out, ordered, weights = refs[0:6], refs[6], refs[7]
     raw, sums, packed, feature_sems, weight_sems = refs[8:]
     loads = []
-    for g in range(3):
-        rows = pl.ds(g * 192, 192)
+    for g in range(12):
+        rows = pl.ds(g * 48, 48)
         loads.append(pltpu.make_async_copy(features.at[rows], raw.at[rows], feature_sems.at[g]))
         loads[-1].start()
     queue = [
@@ -242,11 +242,11 @@
         for fetch in queue[first:last]:
             fetch.start()
 
-    start_loads(0, 4)
     order = order_matrix()
     for g in range(3):
-        loads[g].wait()
-        start_loads((4, 12, 18)[g], (12, 18, 28)[g])
+        for load in loads[4 * g : 4 * g + 4]:
+            load.wait()
+        start_loads((0, 8, 18)[g], (8, 18, 28)[g])
         moved = nn(order, raw[g * 192 : (g + 1) * 192, :]).astype(BF16)
         for m in range(4):
             at = m * BLOCK + g * 48
@@ -304,7 +304,7 @@
             pltpu.VMEM((PIXELS, CHANNELS), BF16),
             pltpu.VMEM((3, PIXELS, 128), F32),
             pltpu.VMEM((6, SENT, 128), F32),
-            pltpu.SemaphoreType.DMA((3,)),
+            pltpu.SemaphoreType.DMA((12,)),
             pltpu.SemaphoreType.DMA((28,)),
         ],
         compiler_params=pltpu.CompilerParams(vmem_limit_bytes=28 * 2**20),

time: 62.5 us -> 62.8 us (level)
  no operation moved by 1% of the time
where the time goes in v10:
time: 62.8 us; the launch traced here: 62.6 us
  starting transfers between devices  24.5 us (39%)
  Pallas kernels  20 us (32%)
  waiting for transfers between devices  16.8 us (27%)
  between operations  0.95 us (2%)
    ppermute x12, starting transfers between devices, swapped(): return lax.ppermute(x, 'rows', [(r, partner(r, bits)) for r in range(8)])  19 us
    ppermute x11, waiting for transfers between devices, flipped(): lax.ppermute(x, 'filt', [(i, i ^ bit) for i in range(lax.axis_size('filt'...  13.8 us
    pallas_call x1, Pallas kernels, outward_sums(): pl.pallas_call(outward_kernel, out_shape=[jax.ShapeDtypeStruct((SENT, 128...  8.52 us
    ppermute x11, starting transfers between devices, flipped(): lax.ppermute(x, 'filt', [(i, i ^ bit) for i in range(lax.axis_size('filt'...  5.54 us
    pallas_call x6, Pallas kernels, grads_for(): pl.pallas_call(functools.partial(grad_kernel, flip, first), out_shape=jax...  5.34 us
    ppermute x12, waiting for transfers between devices, swapped(): return lax.ppermute(x, 'rows', [(r, partner(r, bits)) for r in range(8)])  2.96 us
    pallas_call x1, Pallas kernels, own_sums(): pl.pallas_call(own_kernel, out_shape=[jax.ShapeDtypeStruct((PIXELS, 128),...  1.73 us
  transfers between devices with their start and end apart: 23, of which 7 were waited for; matrix products, arithmetic and copies ran while one was open for 0% of the time, Pallas kernels for 13%

profile of v10, /device:TPU:0, one launch (start us, length us, event | category | flops | bytes accessed | tf_op | source)
XLA Modules:
  0.0 62.6 jit_solution(9179241085176195467)
XLA Ops:
  0.6 8.5 %outward_sums.1 = (f32[304,128]{1,0:T(8,128)S(1)}, f32[304,128]{1,0:T(8,128)S(1)}, f32[304,128]{1,0:T(8,128)S(1)}, f32[304,128]{1,0:T(8,128)S(1)}, f32[304,128]{...) custom-call(bf16[576,2048]{1,0:T(8,128)(2,1)} %bitcast.12, ...), custom_call_target="tpu_custom_call" | custom-call | tf_op jit(solution)/shard_map/outward_sums/pallas_call | solution.py:297
  9.2 3.0 %collective-permute-start.2 = (f16[304,128]{1,0:T(8,128)(2,1)S(1)}, f16[304,128]{1,0:T(8,128)(2,1)S(1)}, u32[]{:S(2)}, u32[]{:S(2)}) collective-permute-start(f16[304,128]{1,0:T(8,128)(2,1)S(1)} %convert_element_type.58), channel_id=1, source_target_pairs={{0,4},{4,0},{8,12},{12,8},{16,20},{20,16},{24,28},{28,24},{1,5},{5... | collective-permute-start | bytes 233480 | tf_op jit(solution)/shard_map/ppermute | solution.py:582
  12.2 1.6 %collective-permute-start.1 = (f16[304,128]{1,0:T(8,128)(2,1)S(1)}, f16[304,128]{1,0:T(8,128)(2,1)S(1)}, u32[]{:S(2)}, u32[]{:S(2)}) collective-permute-start(f16[304,128]{1,0:T(8,128)(2,1)S(1)} %convert_element_type.56), channel_id=1, source_target_pairs={{0,12},{4,8},{8,4},{12,0},{16,28},{20,24},{24,20},{28,16},{1,13},{... | collective-permute-start | bytes 233480 | tf_op jit(solution)/shard_map/ppermute | solution.py:582
  13.8 1.6 %collective-permute-start = (f16[304,128]{1,0:T(8,128)(2,1)S(1)}, f16[304,128]{1,0:T(8,128)(2,1)S(1)}, u32[]{:S(2)}, u32[]{:S(2)}) collective-permute-start(f16[304,128]{1,0:T(8,128)(2,1)S(1)} %convert_element_type.54), channel_id=1, source_target_pairs={{0,4},{4,0},{8,20},{12,16},{16,12},{20,8},{24,28},{28,24},{1,5},{5... | collective-permute-start | bytes 233480 | tf_op jit(solution)/shard_map/ppermute | solution.py:582
  15.4 2.6 %collective-permute-start.5 = (f16[304,128]{1,0:T(8,128)(2,1)S(1)}, f16[304,128]{1,0:T(8,128)(2,1)S(1)}, u32[]{:S(2)}, u32[]{:S(2)}) collective-permute-start(f16[304,128]{1,0:T(8,128)(2,1)S(1)} %convert_element_type.64), channel_id=1, source_target_pairs={{0,8},{4,16},{8,0},{12,24},{16,4},{20,28},{24,12},{28,20},{1,9},{5... | collective-permute-start | bytes 233480 | tf_op jit(solution)/shard_map/ppermute | solution.py:582
  18.2 2.0 %collective-permute-start.3 = (f16[304,128]{1,0:T(8,128)(2,1)S(1)}, f16[304,128]{1,0:T(8,128)(2,1)S(1)}, u32[]{:S(2)}, u32[]{:S(2)}) collective-permute-start(f16[304,128]{1,0:T(8,128)(2,1)S(1)} %convert_element_type.60), channel_id=1, source_target_pairs={{0,4},{4,0},{8,16},{12,20},{16,8},{20,12},{24,28},{28,24},{1,5},{5... | collective-permute-start | bytes 233480 | tf_op jit(solution)/shard_map/ppermute | solution.py:582
  20.2 1.7 %own_sums.1 = (f32[576,128]{1,0:T(8,128)S(1)}, f32[576,128]{1,0:T(8,128)S(1)}) custom-call(bf16[576,2048]{1,0:T(8,128)(2,1)S(1)} %get-tuple-element.25.ordered, bf16[1792,2048]{1,0:T(8,128)(2,1)S(1)} %get-tuple-element.26.weights, f32[4,64]{1,0:T(4,128)S(1)} %copy-done.2), custom_call_target="tpu_custom_call" | custom-call | flops 1000000 | bytes 10000 | tf_op jit(solution)/shard_map/own_sums/pallas_call | solution.py:338
  22.2 1.6 %collective-permute-start.6 = (bf16[576,128]{1,0:T(8,128)(2,1)S(1)}, bf16[576,128]{1,0:T(8,128)(2,1)S(1)}, u32[]{:S(2)}, u32[]{:S(2)}) collective-permute-start(bf16[576,128]{1,0:T(8,128)(2,1)S(1)} %activations.2.a0), channel_id=1, source_target_pairs={{0,2},{1,3},{2,0},{3,1},{4,6},{5,7},{6,4},{7,5},{8,10},{9,11},{10,... | collective-permute-start | bytes 442376 | tf_op jit(solution)/shard_map/ppermute | solution.py:574
  24.1 0.6 collective-permute-start.7
  25.2 2.8 %collective-permute-done.6.a2 = bf16[576,128]{1,0:T(8,128)(2,1)S(1)} collective-permute-done((bf16[576,128]{1,0:T(8,128)(2,1)S(1)}, bf16[576,128]{1,0:T(8,128)(2,1)S(1)}, u32[]{:S(2)}, u32[]{:S(2)}) %collective-permute-start.6) | collective-permute-done | bytes 147488 | tf_op jit(solution)/shard_map/ppermute | solution.py:574
  27.9 1.6 %collective-permute-done.7.b2 = bf16[576,128]{1,0:T(8,128)(2,1)S(1)} collective-permute-done((bf16[576,128]{1,0:T(8,128)(2,1)S(1)}, bf16[576,128]{1,0:T(8,128)(2,1)S(1)}, u32[]{:S(2)}, u32[]{:S(2)}) %collective-permute-start.7) | collective-permute-done | bytes 147488 | tf_op jit(solution)/shard_map/ppermute | solution.py:574
  30.0 0.9 %collective-permute-done.9.b3 = bf16[576,128]{1,0:T(8,128)(2,1)S(1)} collective-permute-done((bf16[576,128]{1,0:T(8,128)(2,1)S(1)}, bf16[576,128]{1,0:T(8,128)(2,1)S(1)}, u32[]{:S(2)}, u32[]{:S(2)}) %collective-permute-start.9) | collective-permute-done | bytes 147488 | tf_op jit(solution)/shard_map/ppermute | solution.py:574
  30.9 0.6 %far_head.1 = (bf16[576,256]{1,0:T(8,128)(2,1)S(1)}, bf16[576,256]{1,0:T(8,128)(2,1)S(1)}, bf16[288,128]{1,0:T(8,128)(2,1)S(1)}, bf16[288,128]{1,0:T(8,128)(2,1)...) custom-call(bf16[576,128]{1,0:T(8,128)(2,1)S(1)} %activations.2.a0, ...), custom_call_target="tpu_custom_call" | custom-call | tf_op jit(solution)/shard_map/far_head/pallas_call | solution.py:444
  31.5 0.7 %collective-permute-start.12 = (bf16[288,128]{1,0:T(8,128)(2,1)S(1)}, bf16[288,128]{1,0:T(8,128)(2,1)S(1)}, u32[]{:S(2)}, u32[]{:S(2)}) collective-permute-start(bf16[288,128]{1,0:T(8,128)(2,1)S(1)} %get-tuple-element.38), channel_id=1, source_target_pairs={{0,4},{4,0},{8,20},{12,16},{16,12},{20,8},{24,28},{28,24},{1,5},{5... | collective-permute-start | bytes 221192 | tf_op jit(solution)/shard_map/ppermute | solution.py:582
  32.2 2.9 %collective-permute-start.13 = (bf16[288,128]{1,0:T(8,128)(2,1)S(1)}, bf16[288,128]{1,0:T(8,128)(2,1)S(1)}, u32[]{:S(2)}, u32[]{:S(2)}) collective-permute-start(bf16[288,128]{1,0:T(8,128)(2,1)S(1)} %get-tuple-element.39), channel_id=1, source_target_pairs={{0,8},{4,16},{8,0},{12,24},{16,4},{20,28},{24,12},{28,20},{1,9},{5... | collective-permute-start | bytes 221192 | tf_op jit(solution)/shard_map/ppermute | solution.py:582
  35.0 1.1 %collective-permute-start.14 = (bf16[288,128]{1,0:T(8,128)(2,1)S(1)}, bf16[288,128]{1,0:T(8,128)(2,1)S(1)}, u32[]{:S(2)}, u32[]{:S(2)}) collective-permute-start(bf16[288,128]{1,0:T(8,128)(2,1)S(1)} %get-tuple-element.40), channel_id=1, source_target_pairs={{0,4},{4,0},{8,16},{12,20},{16,8},{20,12},{24,28},{28,24},{1,5},{5... | collective-permute-start | bytes 221192 | tf_op jit(solution)/shard_map/ppermute | solution.py:582
  36.1 0.6 collective-permute-start.15
  36.7 1.3 %collective-permute-start.16 = (bf16[288,128]{1,0:T(8,128)(2,1)S(1)}, bf16[288,128]{1,0:T(8,128)(2,1)S(1)}, u32[]{:S(2)}, u32[]{:S(2)}) collective-permute-start(bf16[288,128]{1,0:T(8,128)(2,1)S(1)} %get-tuple-element.42), channel_id=1, source_target_pairs={{0,4},{4,0},{8,12},{12,8},{16,20},{20,16},{24,28},{28,24},{1,5},{5... | collective-permute-start | bytes 221192 | tf_op jit(solution)/shard_map/ppermute | solution.py:582
  38.0 1.6 %collective-permute-start.17 = (bf16[288,128]{1,0:T(8,128)(2,1)S(1)}, bf16[288,128]{1,0:T(8,128)(2,1)S(1)}, u32[]{:S(2)}, u32[]{:S(2)}) collective-permute-start(bf16[288,128]{1,0:T(8,128)(2,1)S(1)} %get-tuple-element.43), channel_id=1, source_target_pairs={{0,8},{4,12},{8,0},{12,4},{16,24},{20,28},{24,16},{28,20},{1,9},{5... | collective-permute-start | bytes 221192 | tf_op jit(solution)/shard_map/ppermute | solution.py:582
  39.6 1.9 %collective-permute-done.14.refs_2_ = bf16[288,128]{1,0:T(8,128)(2,1)S(1)} collective-permute-done((bf16[288,128]{1,0:T(8,128)(2,1)S(1)}, bf16[288,128]{1,0:T(8,128)(2,1)S(1)}, u32[]{:S(2)}, u32[]{:S(2)}) %collective-permute-start.14) | collective-permute-done | bytes 73760 | tf_op jit(solution)/shard_map/ppermute | solution.py:582
  41.5 0.8 %collective-permute-done.16.refs_4_ = bf16[288,128]{1,0:T(8,128)(2,1)S(1)} collective-permute-done((bf16[288,128]{1,0:T(8,128)(2,1)S(1)}, bf16[288,128]{1,0:T(8,128)(2,1)S(1)}, u32[]{:S(2)}, u32[]{:S(2)}) %collective-permute-start.16) | collective-permute-done | bytes 73760 | tf_op jit(solution)/shard_map/ppermute | solution.py:582
  43.2 0.7 %grads_for.7 = bf16[576,256]{1,0:T(8,128)(2,1)S(1)} custom-call(bf16[576,1792]{1,0:T(8,128)(2,1)S(1)} %spread.1.stack, bf16[1792,2048]{1,0:T(8,128)(2,1)S(1)} %get-tuple-element.26.weights), custom_call_target="tpu_custom_call" | custom-call | flops 528482304 | bytes 1000000 | tf_op jit(solution)/shard_map/grads_for/pallas_call | solution.py:540
  44.0 0.7 %grads_for.6 = bf16[576,256]{1,0:T(8,128)(2,1)S(1)} custom-call(bf16[576,1792]{1,0:T(8,128)(2,1)S(1)} %spread.1.stack, bf16[1792,2048]{1,0:T(8,128)(2,1)S(1)} %get-tuple-element.26.weights), custom_call_target="tpu_custom_call" | custom-call | flops 528482304 | bytes 1000000 | tf_op jit(solution)/shard_map/grads_for/pallas_call | solution.py:540
  45.3 0.7 %grads_for.8 = bf16[576,256]{1,0:T(8,128)(2,1)S(1)} custom-call(bf16[576,1792]{1,0:T(8,128)(2,1)S(1)} %spread.1.stack, bf16[1792,2048]{1,0:T(8,128)(2,1)S(1)} %get-tuple-element.26.weights), custom_call_target="tpu_custom_call" | custom-call | flops 528482304 | bytes 1000000 | tf_op jit(solution)/shard_map/grads_for/pallas_call | solution.py:540
  46.1 1.6 %collective-permute-start.21 = (bf16[576,256]{1,0:T(8,128)(2,1)S(1)}, bf16[576,256]{1,0:T(8,128)(2,1)S(1)}, u32[]{:S(2)}, u32[]{:S(2)}) collective-permute-start(bf16[576,256]{1,0:T(8,128)(2,1)S(1)} %add_convert_fusion.1), channel_id=1, source_target_pairs={{0,2},{1,3},{2,0},{3,1},{4,6},{5,7},{6,4},{7,5},{8,10},{9,11},{10,... | collective-permute-start | bytes 884744 | tf_op jit(solution)/shard_map/ppermute | solution.py:574
  47.6 0.7 %grads_for.9 = bf16[576,256]{1,0:T(8,128)(2,1)S(1)} custom-call(bf16[576,1792]{1,0:T(8,128)(2,1)S(1)} %spread.1.stack, bf16[1792,2048]{1,0:T(8,128)(2,1)S(1)} %get-tuple-element.26.weights), custom_call_target="tpu_custom_call" | custom-call | flops 528482304 | bytes 1000000 | tf_op jit(solution)/shard_map/grads_for/pallas_call | solution.py:540
  48.4 0.6 collective-permute-start.22
  49.0 1.2 %grads_for.11 = bf16[576,512]{1,0:T(8,128)(2,1)S(1)} custom-call(bf16[576,1792]{1,0:T(8,128)(2,1)S(1)} %spread.1.stack, bf16[1792,2048]{1,0:T(8,128)(2,1)S(1)} %get-tuple-element.26.weights), custom_call_target="tpu_custom_call" | custom-call | flops 1056964608 | bytes 1000000 | tf_op jit(solution)/shard_map/grads_for/pallas_call | solution.py:540
  50.3 1.2 %grads_for.10.a = bf16[576,512]{1,0:T(8,128)(2,1)S(1)} custom-call(bf16[576,1792]{1,0:T(8,128)(2,1)S(1)} %spread.1.stack, bf16[1792,2048]{1,0:T(8,128)(2,1)S(1)} %get-tuple-element.26.weights), custom_call_target="tpu_custom_call" | custom-call | flops 8455716864 | bytes 1000000 | tf_op jit(solution)/shard_map/grads_for/pallas_call | solution.py:540
  51.6 1.2 %own_output.1 = bf16[576,64]{1,0:T(8,128)(2,1)} custom-call(bf16[576,256]{1,0:T(8,128)(2,1)S(1)} %get-tuple-element.46.output), custom_call_target="tpu_custom_call" | custom-call | tf_op jit(solution)/shard_map/own_output/pallas_call | solution.py:469
  52.8 8.6 %collective-permute-done.22.d = bf16[576,256]{1,0:T(8,128)(2,1)S(1)} collective-permute-done((bf16[576,256]{1,0:T(8,128)(2,1)S(1)}, bf16[576,256]{1,0:T(8,128)(2,1)S(1)}, u32[]{:S(2)}, u32[]{:S(2)}) %collective-permute-start.22) | collective-permute-done | bytes 294944 | tf_op jit(solution)/shard_map/ppermute | solution.py:574
  61.4 1.3 %last_sum.1 = bf16[576,512]{1,0:T(8,128)(2,1)} custom-call(bf16[576,512]{1,0:T(8,128)(2,1)S(1)} %grads_for.10.a, bf16[576,512]{1,0:T(8,128)(2,1)S(1)} %collective-permute-done.20.b, bf16[576,256]{1,0:T(8,128)(2,1)S(1)} %collective-permute-done.21.c, bf16[576,256]{1,0:T(8,128)(2,1)S(1)} %collective-permute-done.22.d), custom_call_target="tpu_custom_call" | custom-call | tf_op jit(solution)/shard_map/last_sum/pallas_call | solution.py:563
  (51 shorter events, 3.3 us)
Async XLA Ops:
  0.6 19.5 %copy-start.2 = (f32[4,64]{1,0:T(4,128)S(1)}, f32[4,64]{1,0:T(4,128)}, u32[]{:S(2)}) copy-start(f32[4,64]{1,0:T(4,128)} %bias.1) | copy-start | bytes 3076
  9.2 9.0 %collective-permute-start.2 = (f16[304,128]{1,0:T(8,128)(2,1)S(1)}, f16[304,128]{1,0:T(8,128)(2,1)S(1)}, u32[]{:S(2)}, u32[]{:S(2)}) collective-permute-start(f16[304,128]{1,0:T(8,128)(2,1)S(1)} %convert_element_type.58), channel_id=1, source_target_pairs={{0,4},{4,0},{8,12},{12,8},{16,20},{20,16},{24,28},{28,24},{1,5},{5... | collective-permute-start | bytes 233480 | tf_op jit(solution)/shard_map/ppermute | solution.py:582
  12.2 9.7 %collective-permute-start.1 = (f16[304,128]{1,0:T(8,128)(2,1)S(1)}, f16[304,128]{1,0:T(8,128)(2,1)S(1)}, u32[]{:S(2)}, u32[]{:S(2)}) collective-permute-start(f16[304,128]{1,0:T(8,128)(2,1)S(1)} %convert_element_type.56), channel_id=1, source_target_pairs={{0,12},{4,8},{8,4},{12,0},{16,28},{20,24},{24,20},{28,16},{1,13},{... | collective-permute-start | bytes 233480 | tf_op jit(solution)/shard_map/ppermute | solution.py:582
  13.8 8.2 %collective-permute-start = (f16[304,128]{1,0:T(8,128)(2,1)S(1)}, f16[304,128]{1,0:T(8,128)(2,1)S(1)}, u32[]{:S(2)}, u32[]{:S(2)}) collective-permute-start(f16[304,128]{1,0:T(8,128)(2,1)S(1)} %convert_element_type.54), channel_id=1, source_target_pairs={{0,4},{4,0},{8,20},{12,16},{16,12},{20,8},{24,28},{28,24},{1,5},{5... | collective-permute-start | bytes 233480 | tf_op jit(solution)/shard_map/ppermute | solution.py:582
  15.4 8.4 %collective-permute-start.5 = (f16[304,128]{1,0:T(8,128)(2,1)S(1)}, f16[304,128]{1,0:T(8,128)(2,1)S(1)}, u32[]{:S(2)}, u32[]{:S(2)}) collective-permute-start(f16[304,128]{1,0:T(8,128)(2,1)S(1)} %convert_element_type.64), channel_id=1, source_target_pairs={{0,8},{4,16},{8,0},{12,24},{16,4},{20,28},{24,12},{28,20},{1,9},{5... | collective-permute-start | bytes 233480 | tf_op jit(solution)/shard_map/ppermute | solution.py:582
  18.1 5.7 %collective-permute-start.4 = (f16[304,128]{1,0:T(8,128)(2,1)S(1)}, f16[304,128]{1,0:T(8,128)(2,1)S(1)}, u32[]{:S(2)}, u32[]{:S(2)}) collective-permute-start(f16[304,128]{1,0:T(8,128)(2,1)S(1)} %convert_element_type.62), channel_id=1, source_target_pairs={{0,8},{4,12},{8,0},{12,4},{16,24},{20,28},{24,16},{28,20},{1,9},{5... | collective-permute-start | bytes 233480 | tf_op jit(solution)/shard_map/ppermute | solution.py:582
  18.2 5.6 %collective-permute-start.3 = (f16[304,128]{1,0:T(8,128)(2,1)S(1)}, f16[304,128]{1,0:T(8,128)(2,1)S(1)}, u32[]{:S(2)}, u32[]{:S(2)}) collective-permute-start(f16[304,128]{1,0:T(8,128)(2,1)S(1)} %convert_element_type.60), channel_id=1, source_target_pairs={{0,4},{4,0},{8,16},{12,20},{16,8},{20,12},{24,28},{28,24},{1,5},{5... | collective-permute-start | bytes 233480 | tf_op jit(solution)/shard_map/ppermute | solution.py:582
  21.9 7.6 %copy-start = (bf16[4,256,256]{2,1,0:T(8,128)(2,1)S(1)}, bf16[4,256,256]{2,1,0:T(8,128)(2,1)}, u32[]{:S(2)}) copy-start(bf16[4,256,256]{2,1,0:T(8,128)(2,1)} %project.3) | copy-start | bytes 1572868
  21.9 7.6 %copy-start.1 = (bf16[12,48,256]{2,1,0:T(8,128)(2,1)S(1)}, bf16[12,48,256]{2,1,0:T(8,128)(2,1)}, u32[]{:S(2)}) copy-start(bf16[12,48,256]{2,1,0:T(8,128)(2,1)} %param.13) | copy-start | bytes 884740
  21.9 7.6 %copy-start.3 = (f32[256]{0:T(256)S(1)}, f32[256]{0:T(256)}, u32[]{:S(2)}) copy-start(f32[256]{0:T(256)} %param.12) | copy-start | bytes 3076
  22.2 5.7 %collective-permute-start.6 = (bf16[576,128]{1,0:T(8,128)(2,1)S(1)}, bf16[576,128]{1,0:T(8,128)(2,1)S(1)}, u32[]{:S(2)}, u32[]{:S(2)}) collective-permute-start(bf16[576,128]{1,0:T(8,128)(2,1)S(1)} %activations.2.a0), channel_id=1, source_target_pairs={{0,2},{1,3},{2,0},{3,1},{4,6},{5,7},{6,4},{7,5},{8,10},{9,11},{10,... | collective-permute-start | bytes 442376 | tf_op jit(solution)/shard_map/ppermute | solution.py:574
  24.1 5.4 %collective-permute-start.7 = (bf16[576,128]{1,0:T(8,128)(2,1)S(1)}, bf16[576,128]{1,0:T(8,128)(2,1)S(1)}, u32[]{:S(2)}, u32[]{:S(2)}) collective-permute-start(bf16[576,128]{1,0:T(8,128)(2,1)S(1)} %activations.3.b0), channel_id=1, source_target_pairs={{0,2},{1,3},{2,0},{3,1},{4,6},{5,7},{6,4},{7,5},{8,10},{9,11},{10,... | collective-permute-start | bytes 442376 | tf_op jit(solution)/shard_map/ppermute | solution.py:574
  24.6 4.9 %collective-permute-start.10 = (bf16[576,128]{1,0:T(8,128)(2,1)S(1)}, bf16[576,128]{1,0:T(8,128)(2,1)S(1)}, u32[]{:S(2)}, u32[]{:S(2)}) collective-permute-start(bf16[576,128]{1,0:T(8,128)(2,1)S(1)} %activations.2.a0), channel_id=1, source_target_pairs={{0,1},{1,0},{2,3},{3,2},{4,5},{5,4},{6,7},{7,6},{8,9},{9,8},{10,11... | collective-permute-start | bytes 442376 | tf_op jit(solution)/shard_map/ppermute | solution.py:574
  24.6 4.9 %collective-permute-start.11 = (bf16[576,128]{1,0:T(8,128)(2,1)S(1)}, bf16[576,128]{1,0:T(8,128)(2,1)S(1)}, u32[]{:S(2)}, u32[]{:S(2)}) collective-permute-start(bf16[576,128]{1,0:T(8,128)(2,1)S(1)} %activations.3.b0), channel_id=1, source_target_pairs={{0,1},{1,0},{2,3},{3,2},{4,5},{5,4},{6,7},{7,6},{8,9},{9,8},{10,11... | collective-permute-start | bytes 442376 | tf_op jit(solution)/shard_map/ppermute | solution.py:574
  27.9 2.0 %collective-permute-start.8 = (bf16[576,128]{1,0:T(8,128)(2,1)S(1)}, bf16[576,128]{1,0:T(8,128)(2,1)S(1)}, u32[]{:S(2)}, u32[]{:S(2)}) collective-permute-start(bf16[576,128]{1,0:T(8,128)(2,1)S(1)} %collective-permute-done.6.a2), channel_id=1, source_target_pairs={{0,1},{1,0},{2,3},{3,2},{4,5},{5,4},{6,7},{7,6},{8,9},{9,8},{10,11... | collective-permute-start | bytes 442376 | tf_op jit(solution)/shard_map/ppermute | solution.py:574
  29.5 1.4 %collective-permute-start.9 = (bf16[576,128]{1,0:T(8,128)(2,1)S(1)}, bf16[576,128]{1,0:T(8,128)(2,1)S(1)}, u32[]{:S(2)}, u32[]{:S(2)}) collective-permute-start(bf16[576,128]{1,0:T(8,128)(2,1)S(1)} %collective-permute-done.7.b2), channel_id=1, source_target_pairs={{0,1},{1,0},{2,3},{3,2},{4,5},{5,4},{6,7},{7,6},{8,9},{9,8},{10,11... | collective-permute-start | bytes 442376 | tf_op jit(solution)/shard_map/ppermute | solution.py:574
  31.5 6.5 %collective-permute-start.12 = (bf16[288,128]{1,0:T(8,128)(2,1)S(1)}, bf16[288,128]{1,0:T(8,128)(2,1)S(1)}, u32[]{:S(2)}, u32[]{:S(2)}) collective-permute-start(bf16[288,128]{1,0:T(8,128)(2,1)S(1)} %get-tuple-element.38), channel_id=1, source_target_pairs={{0,4},{4,0},{8,20},{12,16},{16,12},{20,8},{24,28},{28,24},{1,5},{5... | collective-permute-start | bytes 221192 | tf_op jit(solution)/shard_map/ppermute | solution.py:582
  32.2 7.5 %collective-permute-start.13 = (bf16[288,128]{1,0:T(8,128)(2,1)S(1)}, bf16[288,128]{1,0:T(8,128)(2,1)S(1)}, u32[]{:S(2)}, u32[]{:S(2)}) collective-permute-start(bf16[288,128]{1,0:T(8,128)(2,1)S(1)} %get-tuple-element.39), channel_id=1, source_target_pairs={{0,8},{4,16},{8,0},{12,24},{16,4},{20,28},{24,12},{28,20},{1,9},{5... | collective-permute-start | bytes 221192 | tf_op jit(solution)/shard_map/ppermute | solution.py:582
  35.0 6.5 %collective-permute-start.14 = (bf16[288,128]{1,0:T(8,128)(2,1)S(1)}, bf16[288,128]{1,0:T(8,128)(2,1)S(1)}, u32[]{:S(2)}, u32[]{:S(2)}) collective-permute-start(bf16[288,128]{1,0:T(8,128)(2,1)S(1)} %get-tuple-element.40), channel_id=1, source_target_pairs={{0,4},{4,0},{8,16},{12,20},{16,8},{20,12},{24,28},{28,24},{1,5},{5... | collective-permute-start | bytes 221192 | tf_op jit(solution)/shard_map/ppermute | solution.py:582
  36.1 5.4 %collective-permute-start.15 = (bf16[288,128]{1,0:T(8,128)(2,1)S(1)}, bf16[288,128]{1,0:T(8,128)(2,1)S(1)}, u32[]{:S(2)}, u32[]{:S(2)}) collective-permute-start(bf16[288,128]{1,0:T(8,128)(2,1)S(1)} %get-tuple-element.41), channel_id=1, source_target_pairs={{0,12},{4,8},{8,4},{12,0},{16,28},{20,24},{24,20},{28,16},{1,13},{... | collective-permute-start | bytes 221192 | tf_op jit(solution)/shard_map/ppermute | solution.py:582
  36.7 5.6 %collective-permute-start.16 = (bf16[288,128]{1,0:T(8,128)(2,1)S(1)}, bf16[288,128]{1,0:T(8,128)(2,1)S(1)}, u32[]{:S(2)}, u32[]{:S(2)}) collective-permute-start(bf16[288,128]{1,0:T(8,128)(2,1)S(1)} %get-tuple-element.42), channel_id=1, source_target_pairs={{0,4},{4,0},{8,12},{12,8},{16,20},{20,16},{24,28},{28,24},{1,5},{5... | collective-permute-start | bytes 221192 | tf_op jit(solution)/shard_map/ppermute | solution.py:582
  38.0 4.6 %collective-permute-start.17 = (bf16[288,128]{1,0:T(8,128)(2,1)S(1)}, bf16[288,128]{1,0:T(8,128)(2,1)S(1)}, u32[]{:S(2)}, u32[]{:S(2)}) collective-permute-start(bf16[288,128]{1,0:T(8,128)(2,1)S(1)} %get-tuple-element.43), channel_id=1, source_target_pairs={{0,8},{4,12},{8,0},{12,4},{16,24},{20,28},{24,16},{28,20},{1,9},{5... | collective-permute-start | bytes 221192 | tf_op jit(solution)/shard_map/ppermute | solution.py:582
  43.9 2.1 %collective-permute-start.19 = (bf16[576,256]{1,0:T(8,128)(2,1)S(1)}, bf16[576,256]{1,0:T(8,128)(2,1)S(1)}, u32[]{:S(2)}, u32[]{:S(2)}) collective-permute-start(bf16[576,256]{1,0:T(8,128)(2,1)S(1)} %grads_for.7), channel_id=1, source_target_pairs={{0,1},{1,0},{2,3},{3,2},{4,5},{5,4},{6,7},{7,6},{8,9},{9,8},{10,11... | collective-permute-start | bytes 884744 | tf_op jit(solution)/shard_map/ppermute | solution.py:574
  44.7 3.6 %collective-permute-start.18 = (bf16[576,256]{1,0:T(8,128)(2,1)S(1)}, bf16[576,256]{1,0:T(8,128)(2,1)S(1)}, u32[]{:S(2)}, u32[]{:S(2)}) collective-permute-start(bf16[576,256]{1,0:T(8,128)(2,1)S(1)} %grads_for.6), channel_id=1, source_target_pairs={{0,1},{1,0},{2,3},{3,2},{4,5},{5,4},{6,7},{7,6},{8,9},{9,8},{10,11... | collective-permute-start | bytes 884744 | tf_op jit(solution)/shard_map/ppermute | solution.py:574
  46.1 15.3 %collective-permute-start.21 = (bf16[576,256]{1,0:T(8,128)(2,1)S(1)}, bf16[576,256]{1,0:T(8,128)(2,1)S(1)}, u32[]{:S(2)}, u32[]{:S(2)}) collective-permute-start(bf16[576,256]{1,0:T(8,128)(2,1)S(1)} %add_convert_fusion.1), channel_id=1, source_target_pairs={{0,2},{1,3},{2,0},{3,1},{4,6},{5,7},{6,4},{7,5},{8,10},{9,11},{10,... | collective-permute-start | bytes 884744 | tf_op jit(solution)/shard_map/ppermute | solution.py:574
  48.4 13.0 %collective-permute-start.22 = (bf16[576,256]{1,0:T(8,128)(2,1)S(1)}, bf16[576,256]{1,0:T(8,128)(2,1)S(1)}, u32[]{:S(2)}, u32[]{:S(2)}) collective-permute-start(bf16[576,256]{1,0:T(8,128)(2,1)S(1)} %add_convert_fusion), channel_id=1, source_target_pairs={{0,2},{1,3},{2,0},{3,1},{4,6},{5,7},{6,4},{7,5},{8,10},{9,11},{10,... | collective-permute-start | bytes 884744 | tf_op jit(solution)/shard_map/ppermute | solution.py:574
  50.3 11.1 %collective-permute-start.20 = (bf16[576,512]{1,0:T(8,128)(2,1)S(1)}, bf16[576,512]{1,0:T(8,128)(2,1)S(1)}, u32[]{:S(2)}, u32[]{:S(2)}) collective-permute-start(bf16[576,512]{1,0:T(8,128)(2,1)S(1)} %grads_for.11), channel_id=1, source_target_pairs={{0,1},{1,0},{2,3},{3,2},{4,5},{5,4},{6,7},{7,6},{8,9},{9,8},{10,11... | collective-permute-start | bytes 1769480 | tf_op jit(solution)/shard_map/ppermute | solution.py:574

commit v11 on v9

--- a/solution.py
+++ b/solution.py
@@ -550,13 +550,22 @@
     )(stack, weights)
 
 
-def last_kernel(a, b, c, d, out):
-    total = a[...].astype(F32) + b[...].astype(F32) + both(c, d).astype(F32)
-
-    def put(at, value):
-        out[at : at + 192, :] = value
-
-    from_blocks(order_matrix(True), total.astype(BF16), put)
+def last_kernel(a, b, c, d, out, done, sems):
+    order = order_matrix(True)
+    copies = []
+    for g in range(3):
+        parts = []
+        for m in range(4):
+            rows = slice(m * BLOCK + g * 48, m * BLOCK + g * 48 + 48)
+            crossed = jnp.concatenate([c[rows, :], d[rows, :]], 1)
+            total = a[rows, :].astype(F32) + b[rows, :].astype(F32) + crossed.astype(F32)
+            parts.append(total.astype(BF16))
+        rows = pl.ds(g * 192, 192)
+        done[g * 192 : (g + 1) * 192, :] = nn(order, jnp.concatenate(parts, 0)).astype(BF16)
+        copies.append(pltpu.make_async_copy(done.at[rows], out.at[rows], sems.at[g]))
+        copies[-1].start()
+    for copy in copies:
+        copy.wait()
 
 
 def last_sum(a, b, c, d):
@@ -564,7 +573,8 @@
         last_kernel,
         out_shape=jax.ShapeDtypeStruct((PIXELS, 512), BF16),
         in_specs=[pl.BlockSpec(memory_space=pltpu.VMEM)] * 4,
-        out_specs=pl.BlockSpec(memory_space=pltpu.VMEM),
+        out_specs=pl.BlockSpec(memory_space=pl.ANY),
+        scratch_shapes=[pltpu.VMEM((PIXELS, 512), BF16), pltpu.SemaphoreType.DMA((3,))],
         compiler_params=pltpu.CompilerParams(vmem_limit_bytes=10 * 2**20),
         name="last_sum",
     )(a, b, c, d)

time: 62.5 us -> 62.3 us (level)
  no operation moved by 1% of the time
where the time goes in v11:
time: 62.3 us; the launch traced here: 62.2 us
  starting transfers between devices  24.6 us (39%)
  Pallas kernels  19.6 us (31%)
  waiting for transfers between devices  16.7 us (27%)
  between operations  0.95 us (2%)
    ppermute x12, starting transfers between devices, swapped(): return lax.ppermute(x, 'rows', [(r, partner(r, bits)) for r in range(8)])  19 us
    ppermute x11, waiting for transfers between devices, flipped(): lax.ppermute(x, 'filt', [(i, i ^ bit) for i in range(lax.axis_size('filt'...  13.8 us
    pallas_call x1, Pallas kernels, outward_sums(): pl.pallas_call(outward_kernel, out_shape=[jax.ShapeDtypeStruct((SENT, 128...  8.22 us
    ppermute x11, starting transfers between devices, flipped(): lax.ppermute(x, 'filt', [(i, i ^ bit) for i in range(lax.axis_size('filt'...  5.56 us
    pallas_call x6, Pallas kernels, grads_for(): pl.pallas_call(functools.partial(grad_kernel, flip, first), out_shape=jax...  5.34 us
    ppermute x12, waiting for transfers between devices, swapped(): return lax.ppermute(x, 'rows', [(r, partner(r, bits)) for r in range(8)])  2.89 us
    pallas_call x1, Pallas kernels, own_sums(): pl.pallas_call(own_kernel, out_shape=[jax.ShapeDtypeStruct((PIXELS, 128),...  1.72 us
  transfers between devices with their start and end apart: 23, of which 7 were waited for; matrix products, arithmetic and copies ran while one was open for 0% of the time, Pallas kernels for 13%

profile of v11, /device:TPU:0, one launch (start us, length us, event | category | flops | bytes accessed | tf_op | source)
XLA Modules:
  0.0 62.2 jit_solution(12389747925075712012)
XLA Ops:
  0.6 8.2 %outward_sums.1 = (f32[304,128]{1,0:T(8,128)S(1)}, f32[304,128]{1,0:T(8,128)S(1)}, f32[304,128]{1,0:T(8,128)S(1)}, f32[304,128]{1,0:T(8,128)S(1)}, f32[304,128]{...) custom-call(bf16[576,2048]{1,0:T(8,128)(2,1)} %bitcast.12, ...), custom_call_target="tpu_custom_call" | custom-call | tf_op jit(solution)/shard_map/outward_sums/pallas_call | solution.py:297
  8.9 3.0 %collective-permute-start.2 = (f16[304,128]{1,0:T(8,128)(2,1)S(1)}, f16[304,128]{1,0:T(8,128)(2,1)S(1)}, u32[]{:S(2)}, u32[]{:S(2)}) collective-permute-start(f16[304,128]{1,0:T(8,128)(2,1)S(1)} %convert_element_type.58), channel_id=1, source_target_pairs={{0,4},{4,0},{8,12},{12,8},{16,20},{20,16},{24,28},{28,24},{1,5},{5... | collective-permute-start | bytes 233480 | tf_op jit(solution)/shard_map/ppermute | solution.py:592
  11.9 1.6 %collective-permute-start.1 = (f16[304,128]{1,0:T(8,128)(2,1)S(1)}, f16[304,128]{1,0:T(8,128)(2,1)S(1)}, u32[]{:S(2)}, u32[]{:S(2)}) collective-permute-start(f16[304,128]{1,0:T(8,128)(2,1)S(1)} %convert_element_type.56), channel_id=1, source_target_pairs={{0,12},{4,8},{8,4},{12,0},{16,28},{20,24},{24,20},{28,16},{1,13},{... | collective-permute-start | bytes 233480 | tf_op jit(solution)/shard_map/ppermute | solution.py:592
  13.6 1.5 %collective-permute-start = (f16[304,128]{1,0:T(8,128)(2,1)S(1)}, f16[304,128]{1,0:T(8,128)(2,1)S(1)}, u32[]{:S(2)}, u32[]{:S(2)}) collective-permute-start(f16[304,128]{1,0:T(8,128)(2,1)S(1)} %convert_element_type.54), channel_id=1, source_target_pairs={{0,4},{4,0},{8,20},{12,16},{16,12},{20,8},{24,28},{28,24},{1,5},{5... | collective-permute-start | bytes 233480 | tf_op jit(solution)/shard_map/ppermute | solution.py:592
  15.1 2.7 %collective-permute-start.5 = (f16[304,128]{1,0:T(8,128)(2,1)S(1)}, f16[304,128]{1,0:T(8,128)(2,1)S(1)}, u32[]{:S(2)}, u32[]{:S(2)}) collective-permute-start(f16[304,128]{1,0:T(8,128)(2,1)S(1)} %convert_element_type.64), channel_id=1, source_target_pairs={{0,8},{4,16},{8,0},{12,24},{16,4},{20,28},{24,12},{28,20},{1,9},{5... | collective-permute-start | bytes 233480 | tf_op jit(solution)/shard_map/ppermute | solution.py:592
  17.9 2.0 %collective-permute-start.3 = (f16[304,128]{1,0:T(8,128)(2,1)S(1)}, f16[304,128]{1,0:T(8,128)(2,1)S(1)}, u32[]{:S(2)}, u32[]{:S(2)}) collective-permute-start(f16[304,128]{1,0:T(8,128)(2,1)S(1)} %convert_element_type.60), channel_id=1, source_target_pairs={{0,4},{4,0},{8,16},{12,20},{16,8},{20,12},{24,28},{28,24},{1,5},{5... | collective-permute-start | bytes 233480 | tf_op jit(solution)/shard_map/ppermute | solution.py:592
  19.9 1.7 %own_sums.1 = (f32[576,128]{1,0:T(8,128)S(1)}, f32[576,128]{1,0:T(8,128)S(1)}) custom-call(bf16[576,2048]{1,0:T(8,128)(2,1)S(1)} %get-tuple-element.25.ordered, bf16[1792,2048]{1,0:T(8,128)(2,1)S(1)} %get-tuple-element.26.weights, f32[4,64]{1,0:T(4,128)S(1)} %copy-done.2), custom_call_target="tpu_custom_call" | custom-call | flops 1000000 | bytes 10000 | tf_op jit(solution)/shard_map/own_sums/pallas_call | solution.py:338
  21.9 1.6 %collective-permute-start.6 = (bf16[576,128]{1,0:T(8,128)(2,1)S(1)}, bf16[576,128]{1,0:T(8,128)(2,1)S(1)}, u32[]{:S(2)}, u32[]{:S(2)}) collective-permute-start(bf16[576,128]{1,0:T(8,128)(2,1)S(1)} %activations.2.a0), channel_id=1, source_target_pairs={{0,2},{1,3},{2,0},{3,1},{4,6},{5,7},{6,4},{7,5},{8,10},{9,11},{10,... | collective-permute-start | bytes 442376 | tf_op jit(solution)/shard_map/ppermute | solution.py:584
  23.8 0.6 collective-permute-start.7
  24.9 2.8 %collective-permute-done.6.a2 = bf16[576,128]{1,0:T(8,128)(2,1)S(1)} collective-permute-done((bf16[576,128]{1,0:T(8,128)(2,1)S(1)}, bf16[576,128]{1,0:T(8,128)(2,1)S(1)}, u32[]{:S(2)}, u32[]{:S(2)}) %collective-permute-start.6) | collective-permute-done | bytes 147488 | tf_op jit(solution)/shard_map/ppermute | solution.py:584
  27.6 1.6 %collective-permute-done.7.b2 = bf16[576,128]{1,0:T(8,128)(2,1)S(1)} collective-permute-done((bf16[576,128]{1,0:T(8,128)(2,1)S(1)}, bf16[576,128]{1,0:T(8,128)(2,1)S(1)}, u32[]{:S(2)}, u32[]{:S(2)}) %collective-permute-start.7) | collective-permute-done | bytes 147488 | tf_op jit(solution)/shard_map/ppermute | solution.py:584
  29.7 0.9 %collective-permute-done.9.b3 = bf16[576,128]{1,0:T(8,128)(2,1)S(1)} collective-permute-done((bf16[576,128]{1,0:T(8,128)(2,1)S(1)}, bf16[576,128]{1,0:T(8,128)(2,1)S(1)}, u32[]{:S(2)}, u32[]{:S(2)}) %collective-permute-start.9) | collective-permute-done | bytes 147488 | tf_op jit(solution)/shard_map/ppermute | solution.py:584
  30.6 0.6 %far_head.1 = (bf16[576,256]{1,0:T(8,128)(2,1)S(1)}, bf16[576,256]{1,0:T(8,128)(2,1)S(1)}, bf16[288,128]{1,0:T(8,128)(2,1)S(1)}, bf16[288,128]{1,0:T(8,128)(2,1)...) custom-call(bf16[576,128]{1,0:T(8,128)(2,1)S(1)} %activations.2.a0, ...), custom_call_target="tpu_custom_call" | custom-call | tf_op jit(solution)/shard_map/far_head/pallas_call | solution.py:444
  31.2 0.7 %collective-permute-start.12 = (bf16[288,128]{1,0:T(8,128)(2,1)S(1)}, bf16[288,128]{1,0:T(8,128)(2,1)S(1)}, u32[]{:S(2)}, u32[]{:S(2)}) collective-permute-start(bf16[288,128]{1,0:T(8,128)(2,1)S(1)} %get-tuple-element.38), channel_id=1, source_target_pairs={{0,4},{4,0},{8,20},{12,16},{16,12},{20,8},{24,28},{28,24},{1,5},{5... | collective-permute-start | bytes 221192 | tf_op jit(solution)/shard_map/ppermute | solution.py:592
  31.9 2.8 %collective-permute-start.13 = (bf16[288,128]{1,0:T(8,128)(2,1)S(1)}, bf16[288,128]{1,0:T(8,128)(2,1)S(1)}, u32[]{:S(2)}, u32[]{:S(2)}) collective-permute-start(bf16[288,128]{1,0:T(8,128)(2,1)S(1)} %get-tuple-element.39), channel_id=1, source_target_pairs={{0,8},{4,16},{8,0},{12,24},{16,4},{20,28},{24,12},{28,20},{1,9},{5... | collective-permute-start | bytes 221192 | tf_op jit(solution)/shard_map/ppermute | solution.py:592
  34.6 1.2 %collective-permute-start.14 = (bf16[288,128]{1,0:T(8,128)(2,1)S(1)}, bf16[288,128]{1,0:T(8,128)(2,1)S(1)}, u32[]{:S(2)}, u32[]{:S(2)}) collective-permute-start(bf16[288,128]{1,0:T(8,128)(2,1)S(1)} %get-tuple-element.40), channel_id=1, source_target_pairs={{0,4},{4,0},{8,16},{12,20},{16,8},{20,12},{24,28},{28,24},{1,5},{5... | collective-permute-start | bytes 221192 | tf_op jit(solution)/shard_map/ppermute | solution.py:592
  35.9 0.6 collective-permute-start.15
  36.5 1.2 %collective-permute-start.16 = (bf16[288,128]{1,0:T(8,128)(2,1)S(1)}, bf16[288,128]{1,0:T(8,128)(2,1)S(1)}, u32[]{:S(2)}, u32[]{:S(2)}) collective-permute-start(bf16[288,128]{1,0:T(8,128)(2,1)S(1)} %get-tuple-element.42), channel_id=1, source_target_pairs={{0,4},{4,0},{8,12},{12,8},{16,20},{20,16},{24,28},{28,24},{1,5},{5... | collective-permute-start | bytes 221192 | tf_op jit(solution)/shard_map/ppermute | solution.py:592
  37.7 1.7 %collective-permute-start.17 = (bf16[288,128]{1,0:T(8,128)(2,1)S(1)}, bf16[288,128]{1,0:T(8,128)(2,1)S(1)}, u32[]{:S(2)}, u32[]{:S(2)}) collective-permute-start(bf16[288,128]{1,0:T(8,128)(2,1)S(1)} %get-tuple-element.43), channel_id=1, source_target_pairs={{0,8},{4,12},{8,0},{12,4},{16,24},{20,28},{24,16},{28,20},{1,9},{5... | collective-permute-start | bytes 221192 | tf_op jit(solution)/shard_map/ppermute | solution.py:592
  39.4 1.9 %collective-permute-done.14.refs_2_ = bf16[288,128]{1,0:T(8,128)(2,1)S(1)} collective-permute-done((bf16[288,128]{1,0:T(8,128)(2,1)S(1)}, bf16[288,128]{1,0:T(8,128)(2,1)S(1)}, u32[]{:S(2)}, u32[]{:S(2)}) %collective-permute-start.14) | collective-permute-done | bytes 73760 | tf_op jit(solution)/shard_map/ppermute | solution.py:592
  41.2 0.8 %collective-permute-done.16.refs_4_ = bf16[288,128]{1,0:T(8,128)(2,1)S(1)} collective-permute-done((bf16[288,128]{1,0:T(8,128)(2,1)S(1)}, bf16[288,128]{1,0:T(8,128)(2,1)S(1)}, u32[]{:S(2)}, u32[]{:S(2)}) %collective-permute-start.16) | collective-permute-done | bytes 73760 | tf_op jit(solution)/shard_map/ppermute | solution.py:592
  42.2 0.6 spread.1.stack
  42.8 0.7 %grads_for.7 = bf16[576,256]{1,0:T(8,128)(2,1)S(1)} custom-call(bf16[576,1792]{1,0:T(8,128)(2,1)S(1)} %spread.1.stack, bf16[1792,2048]{1,0:T(8,128)(2,1)S(1)} %get-tuple-element.26.weights), custom_call_target="tpu_custom_call" | custom-call | flops 528482304 | bytes 1000000 | tf_op jit(solution)/shard_map/grads_for/pallas_call | solution.py:540
  43.6 0.7 %grads_for.6 = bf16[576,256]{1,0:T(8,128)(2,1)S(1)} custom-call(bf16[576,1792]{1,0:T(8,128)(2,1)S(1)} %spread.1.stack, bf16[1792,2048]{1,0:T(8,128)(2,1)S(1)} %get-tuple-element.26.weights), custom_call_target="tpu_custom_call" | custom-call | flops 528482304 | bytes 1000000 | tf_op jit(solution)/shard_map/grads_for/pallas_call | solution.py:540
  44.9 0.7 %grads_for.8 = bf16[576,256]{1,0:T(8,128)(2,1)S(1)} custom-call(bf16[576,1792]{1,0:T(8,128)(2,1)S(1)} %spread.1.stack, bf16[1792,2048]{1,0:T(8,128)(2,1)S(1)} %get-tuple-element.26.weights), custom_call_target="tpu_custom_call" | custom-call | flops 528482304 | bytes 1000000 | tf_op jit(solution)/shard_map/grads_for/pallas_call | solution.py:540
  45.7 1.6 %collective-permute-start.21 = (bf16[576,256]{1,0:T(8,128)(2,1)S(1)}, bf16[576,256]{1,0:T(8,128)(2,1)S(1)}, u32[]{:S(2)}, u32[]{:S(2)}) collective-permute-start(bf16[576,256]{1,0:T(8,128)(2,1)S(1)} %add_convert_fusion.1), channel_id=1, source_target_pairs={{0,2},{1,3},{2,0},{3,1},{4,6},{5,7},{6,4},{7,5},{8,10},{9,11},{10,... | collective-permute-start | bytes 884744 | tf_op jit(solution)/shard_map/ppermute | solution.py:584
  47.3 0.7 %grads_for.9 = bf16[576,256]{1,0:T(8,128)(2,1)S(1)} custom-call(bf16[576,1792]{1,0:T(8,128)(2,1)S(1)} %spread.1.stack, bf16[1792,2048]{1,0:T(8,128)(2,1)S(1)} %get-tuple-element.26.weights), custom_call_target="tpu_custom_call" | custom-call | flops 528482304 | bytes 1000000 | tf_op jit(solution)/shard_map/grads_for/pallas_call | solution.py:540
  48.7 1.2 %grads_for.11 = bf16[576,512]{1,0:T(8,128)(2,1)S(1)} custom-call(bf16[576,1792]{1,0:T(8,128)(2,1)S(1)} %spread.1.stack, bf16[1792,2048]{1,0:T(8,128)(2,1)S(1)} %get-tuple-element.26.weights), custom_call_target="tpu_custom_call" | custom-call | flops 1056964608 | bytes 1000000 | tf_op jit(solution)/shard_map/grads_for/pallas_call | solution.py:540
  50.0 1.2 %grads_for.10.a = bf16[576,512]{1,0:T(8,128)(2,1)S(1)} custom-call(bf16[576,1792]{1,0:T(8,128)(2,1)S(1)} %spread.1.stack, bf16[1792,2048]{1,0:T(8,128)(2,1)S(1)} %get-tuple-element.26.weights), custom_call_target="tpu_custom_call" | custom-call | flops 8455716864 | bytes 1000000 | tf_op jit(solution)/shard_map/grads_for/pallas_call | solution.py:540
  51.2 1.2 %own_output.1 = bf16[576,64]{1,0:T(8,128)(2,1)} custom-call(bf16[576,256]{1,0:T(8,128)(2,1)S(1)} %get-tuple-element.46.output), custom_call_target="tpu_custom_call" | custom-call | tf_op jit(solution)/shard_map/own_output/pallas_call | solution.py:469
  52.5 8.6 %collective-permute-done.22.d = bf16[576,256]{1,0:T(8,128)(2,1)S(1)} collective-permute-done((bf16[576,256]{1,0:T(8,128)(2,1)S(1)}, bf16[576,256]{1,0:T(8,128)(2,1)S(1)}, u32[]{:S(2)}, u32[]{:S(2)}) %collective-permute-start.22) | collective-permute-done | bytes 294944 | tf_op jit(solution)/shard_map/ppermute | solution.py:584
  61.0 1.1 %last_sum.1 = bf16[576,512]{1,0:T(8,128)(2,1)} custom-call(bf16[576,512]{1,0:T(8,128)(2,1)S(1)} %grads_for.10.a, bf16[576,512]{1,0:T(8,128)(2,1)S(1)} %collective-permute-done.20.b, bf16[576,256]{1,0:T(8,128)(2,1)S(1)} %collective-permute-done.21.c, bf16[576,256]{1,0:T(8,128)(2,1)S(1)} %collective-permute-done.22.d), custom_call_target="tpu_custom_call" | custom-call | tf_op jit(solution)/shard_map/last_sum/pallas_call | solution.py:572
  (51 shorter events, 3.2 us)
Async XLA Ops:
  0.6 19.2 %copy-start.2 = (f32[4,64]{1,0:T(4,128)S(1)}, f32[4,64]{1,0:T(4,128)}, u32[]{:S(2)}) copy-start(f32[4,64]{1,0:T(4,128)} %bias.1) | copy-start | bytes 3076
  8.9 9.0 %collective-permute-start.2 = (f16[304,128]{1,0:T(8,128)(2,1)S(1)}, f16[304,128]{1,0:T(8,128)(2,1)S(1)}, u32[]{:S(2)}, u32[]{:S(2)}) collective-permute-start(f16[304,128]{1,0:T(8,128)(2,1)S(1)} %convert_element_type.58), channel_id=1, source_target_pairs={{0,4},{4,0},{8,12},{12,8},{16,20},{20,16},{24,28},{28,24},{1,5},{5... | collective-permute-start | bytes 233480 | tf_op jit(solution)/shard_map/ppermute | solution.py:592
  11.9 9.7 %collective-permute-start.1 = (f16[304,128]{1,0:T(8,128)(2,1)S(1)}, f16[304,128]{1,0:T(8,128)(2,1)S(1)}, u32[]{:S(2)}, u32[]{:S(2)}) collective-permute-start(f16[304,128]{1,0:T(8,128)(2,1)S(1)} %convert_element_type.56), channel_id=1, source_target_pairs={{0,12},{4,8},{8,4},{12,0},{16,28},{20,24},{24,20},{28,16},{1,13},{... | collective-permute-start | bytes 233480 | tf_op jit(solution)/shard_map/ppermute | solution.py:592
  13.6 8.1 %collective-permute-start = (f16[304,128]{1,0:T(8,128)(2,1)S(1)}, f16[304,128]{1,0:T(8,128)(2,1)S(1)}, u32[]{:S(2)}, u32[]{:S(2)}) collective-permute-start(f16[304,128]{1,0:T(8,128)(2,1)S(1)} %convert_element_type.54), channel_id=1, source_target_pairs={{0,4},{4,0},{8,20},{12,16},{16,12},{20,8},{24,28},{28,24},{1,5},{5... | collective-permute-start | bytes 233480 | tf_op jit(solution)/shard_map/ppermute | solution.py:592
  15.1 8.4 %collective-permute-start.5 = (f16[304,128]{1,0:T(8,128)(2,1)S(1)}, f16[304,128]{1,0:T(8,128)(2,1)S(1)}, u32[]{:S(2)}, u32[]{:S(2)}) collective-permute-start(f16[304,128]{1,0:T(8,128)(2,1)S(1)} %convert_element_type.64), channel_id=1, source_target_pairs={{0,8},{4,16},{8,0},{12,24},{16,4},{20,28},{24,12},{28,20},{1,9},{5... | collective-permute-start | bytes 233480 | tf_op jit(solution)/shard_map/ppermute | solution.py:592
  17.8 5.7 %collective-permute-start.4 = (f16[304,128]{1,0:T(8,128)(2,1)S(1)}, f16[304,128]{1,0:T(8,128)(2,1)S(1)}, u32[]{:S(2)}, u32[]{:S(2)}) collective-permute-start(f16[304,128]{1,0:T(8,128)(2,1)S(1)} %convert_element_type.62), channel_id=1, source_target_pairs={{0,8},{4,12},{8,0},{12,4},{16,24},{20,28},{24,16},{28,20},{1,9},{5... | collective-permute-start | bytes 233480 | tf_op jit(solution)/shard_map/ppermute | solution.py:592
  17.9 5.6 %collective-permute-start.3 = (f16[304,128]{1,0:T(8,128)(2,1)S(1)}, f16[304,128]{1,0:T(8,128)(2,1)S(1)}, u32[]{:S(2)}, u32[]{:S(2)}) collective-permute-start(f16[304,128]{1,0:T(8,128)(2,1)S(1)} %convert_element_type.60), channel_id=1, source_target_pairs={{0,4},{4,0},{8,16},{12,20},{16,8},{20,12},{24,28},{28,24},{1,5},{5... | collective-permute-start | bytes 233480 | tf_op jit(solution)/shard_map/ppermute | solution.py:592
  21.6 7.6 %copy-start = (bf16[4,256,256]{2,1,0:T(8,128)(2,1)S(1)}, bf16[4,256,256]{2,1,0:T(8,128)(2,1)}, u32[]{:S(2)}) copy-start(bf16[4,256,256]{2,1,0:T(8,128)(2,1)} %project.3) | copy-start | bytes 1572868
  21.6 7.6 %copy-start.1 = (bf16[12,48,256]{2,1,0:T(8,128)(2,1)S(1)}, bf16[12,48,256]{2,1,0:T(8,128)(2,1)}, u32[]{:S(2)}) copy-start(bf16[12,48,256]{2,1,0:T(8,128)(2,1)} %param.13) | copy-start | bytes 884740
  21.6 7.6 %copy-start.3 = (f32[256]{0:T(256)S(1)}, f32[256]{0:T(256)}, u32[]{:S(2)}) copy-start(f32[256]{0:T(256)} %param.12) | copy-start | bytes 3076
  21.9 5.7 %collective-permute-start.6 = (bf16[576,128]{1,0:T(8,128)(2,1)S(1)}, bf16[576,128]{1,0:T(8,128)(2,1)S(1)}, u32[]{:S(2)}, u32[]{:S(2)}) collective-permute-start(bf16[576,128]{1,0:T(8,128)(2,1)S(1)} %activations.2.a0), channel_id=1, source_target_pairs={{0,2},{1,3},{2,0},{3,1},{4,6},{5,7},{6,4},{7,5},{8,10},{9,11},{10,... | collective-permute-start | bytes 442376 | tf_op jit(solution)/shard_map/ppermute | solution.py:584
  23.8 5.4 %collective-permute-start.7 = (bf16[576,128]{1,0:T(8,128)(2,1)S(1)}, bf16[576,128]{1,0:T(8,128)(2,1)S(1)}, u32[]{:S(2)}, u32[]{:S(2)}) collective-permute-start(bf16[576,128]{1,0:T(8,128)(2,1)S(1)} %activations.3.b0), channel_id=1, source_target_pairs={{0,2},{1,3},{2,0},{3,1},{4,6},{5,7},{6,4},{7,5},{8,10},{9,11},{10,... | collective-permute-start | bytes 442376 | tf_op jit(solution)/shard_map/ppermute | solution.py:584
  24.4 4.9 %collective-permute-start.10 = (bf16[576,128]{1,0:T(8,128)(2,1)S(1)}, bf16[576,128]{1,0:T(8,128)(2,1)S(1)}, u32[]{:S(2)}, u32[]{:S(2)}) collective-permute-start(bf16[576,128]{1,0:T(8,128)(2,1)S(1)} %activations.2.a0), channel_id=1, source_target_pairs={{0,1},{1,0},{2,3},{3,2},{4,5},{5,4},{6,7},{7,6},{8,9},{9,8},{10,11... | collective-permute-start | bytes 442376 | tf_op jit(solution)/shard_map/ppermute | solution.py:584
  24.4 4.9 %collective-permute-start.11 = (bf16[576,128]{1,0:T(8,128)(2,1)S(1)}, bf16[576,128]{1,0:T(8,128)(2,1)S(1)}, u32[]{:S(2)}, u32[]{:S(2)}) collective-permute-start(bf16[576,128]{1,0:T(8,128)(2,1)S(1)} %activations.3.b0), channel_id=1, source_target_pairs={{0,1},{1,0},{2,3},{3,2},{4,5},{5,4},{6,7},{7,6},{8,9},{9,8},{10,11... | collective-permute-start | bytes 442376 | tf_op jit(solution)/shard_map/ppermute | solution.py:584
  27.6 2.0 %collective-permute-start.8 = (bf16[576,128]{1,0:T(8,128)(2,1)S(1)}, bf16[576,128]{1,0:T(8,128)(2,1)S(1)}, u32[]{:S(2)}, u32[]{:S(2)}) collective-permute-start(bf16[576,128]{1,0:T(8,128)(2,1)S(1)} %collective-permute-done.6.a2), channel_id=1, source_target_pairs={{0,1},{1,0},{2,3},{3,2},{4,5},{5,4},{6,7},{7,6},{8,9},{9,8},{10,11... | collective-permute-start | bytes 442376 | tf_op jit(solution)/shard_map/ppermute | solution.py:584
  29.2 1.4 %collective-permute-start.9 = (bf16[576,128]{1,0:T(8,128)(2,1)S(1)}, bf16[576,128]{1,0:T(8,128)(2,1)S(1)}, u32[]{:S(2)}, u32[]{:S(2)}) collective-permute-start(bf16[576,128]{1,0:T(8,128)(2,1)S(1)} %collective-permute-done.7.b2), channel_id=1, source_target_pairs={{0,1},{1,0},{2,3},{3,2},{4,5},{5,4},{6,7},{7,6},{8,9},{9,8},{10,11... | collective-permute-start | bytes 442376 | tf_op jit(solution)/shard_map/ppermute | solution.py:584
  31.2 6.5 %collective-permute-start.12 = (bf16[288,128]{1,0:T(8,128)(2,1)S(1)}, bf16[288,128]{1,0:T(8,128)(2,1)S(1)}, u32[]{:S(2)}, u32[]{:S(2)}) collective-permute-start(bf16[288,128]{1,0:T(8,128)(2,1)S(1)} %get-tuple-element.38), channel_id=1, source_target_pairs={{0,4},{4,0},{8,20},{12,16},{16,12},{20,8},{24,28},{28,24},{1,5},{5... | collective-permute-start | bytes 221192 | tf_op jit(solution)/shard_map/ppermute | solution.py:592
  31.9 7.5 %collective-permute-start.13 = (bf16[288,128]{1,0:T(8,128)(2,1)S(1)}, bf16[288,128]{1,0:T(8,128)(2,1)S(1)}, u32[]{:S(2)}, u32[]{:S(2)}) collective-permute-start(bf16[288,128]{1,0:T(8,128)(2,1)S(1)} %get-tuple-element.39), channel_id=1, source_target_pairs={{0,8},{4,16},{8,0},{12,24},{16,4},{20,28},{24,12},{28,20},{1,9},{5... | collective-permute-start | bytes 221192 | tf_op jit(solution)/shard_map/ppermute | solution.py:592
  34.6 6.6 %collective-permute-start.14 = (bf16[288,128]{1,0:T(8,128)(2,1)S(1)}, bf16[288,128]{1,0:T(8,128)(2,1)S(1)}, u32[]{:S(2)}, u32[]{:S(2)}) collective-permute-start(bf16[288,128]{1,0:T(8,128)(2,1)S(1)} %get-tuple-element.40), channel_id=1, source_target_pairs={{0,4},{4,0},{8,16},{12,20},{16,8},{20,12},{24,28},{28,24},{1,5},{5... | collective-permute-start | bytes 221192 | tf_op jit(solution)/shard_map/ppermute | solution.py:592
  35.9 5.4 %collective-permute-start.15 = (bf16[288,128]{1,0:T(8,128)(2,1)S(1)}, bf16[288,128]{1,0:T(8,128)(2,1)S(1)}, u32[]{:S(2)}, u32[]{:S(2)}) collective-permute-start(bf16[288,128]{1,0:T(8,128)(2,1)S(1)} %get-tuple-element.41), channel_id=1, source_target_pairs={{0,12},{4,8},{8,4},{12,0},{16,28},{20,24},{24,20},{28,16},{1,13},{... | collective-permute-start | bytes 221192 | tf_op jit(solution)/shard_map/ppermute | solution.py:592
  36.5 5.6 %collective-permute-start.16 = (bf16[288,128]{1,0:T(8,128)(2,1)S(1)}, bf16[288,128]{1,0:T(8,128)(2,1)S(1)}, u32[]{:S(2)}, u32[]{:S(2)}) collective-permute-start(bf16[288,128]{1,0:T(8,128)(2,1)S(1)} %get-tuple-element.42), channel_id=1, source_target_pairs={{0,4},{4,0},{8,12},{12,8},{16,20},{20,16},{24,28},{28,24},{1,5},{5... | collective-permute-start | bytes 221192 | tf_op jit(solution)/shard_map/ppermute | solution.py:592
  37.7 4.5 %collective-permute-start.17 = (bf16[288,128]{1,0:T(8,128)(2,1)S(1)}, bf16[288,128]{1,0:T(8,128)(2,1)S(1)}, u32[]{:S(2)}, u32[]{:S(2)}) collective-permute-start(bf16[288,128]{1,0:T(8,128)(2,1)S(1)} %get-tuple-element.43), channel_id=1, source_target_pairs={{0,8},{4,12},{8,0},{12,4},{16,24},{20,28},{24,16},{28,20},{1,9},{5... | collective-permute-start | bytes 221192 | tf_op jit(solution)/shard_map/ppermute | solution.py:592
  43.5 2.1 %collective-permute-start.19 = (bf16[576,256]{1,0:T(8,128)(2,1)S(1)}, bf16[576,256]{1,0:T(8,128)(2,1)S(1)}, u32[]{:S(2)}, u32[]{:S(2)}) collective-permute-start(bf16[576,256]{1,0:T(8,128)(2,1)S(1)} %grads_for.7), channel_id=1, source_target_pairs={{0,1},{1,0},{2,3},{3,2},{4,5},{5,4},{6,7},{7,6},{8,9},{9,8},{10,11... | collective-permute-start | bytes 884744 | tf_op jit(solution)/shard_map/ppermute | solution.py:584
  44.4 3.7 %collective-permute-start.18 = (bf16[576,256]{1,0:T(8,128)(2,1)S(1)}, bf16[576,256]{1,0:T(8,128)(2,1)S(1)}, u32[]{:S(2)}, u32[]{:S(2)}) collective-permute-start(bf16[576,256]{1,0:T(8,128)(2,1)S(1)} %grads_for.6), channel_id=1, source_target_pairs={{0,1},{1,0},{2,3},{3,2},{4,5},{5,4},{6,7},{7,6},{8,9},{9,8},{10,11... | collective-permute-start | bytes 884744 | tf_op jit(solution)/shard_map/ppermute | solution.py:584
  45.7 15.3 %collective-permute-start.21 = (bf16[576,256]{1,0:T(8,128)(2,1)S(1)}, bf16[576,256]{1,0:T(8,128)(2,1)S(1)}, u32[]{:S(2)}, u32[]{:S(2)}) collective-permute-start(bf16[576,256]{1,0:T(8,128)(2,1)S(1)} %add_convert_fusion.1), channel_id=1, source_target_pairs={{0,2},{1,3},{2,0},{3,1},{4,6},{5,7},{6,4},{7,5},{8,10},{9,11},{10,... | collective-permute-start | bytes 884744 | tf_op jit(solution)/shard_map/ppermute | solution.py:584
  48.1 12.9 %collective-permute-start.22 = (bf16[576,256]{1,0:T(8,128)(2,1)S(1)}, bf16[576,256]{1,0:T(8,128)(2,1)S(1)}, u32[]{:S(2)}, u32[]{:S(2)}) collective-permute-start(bf16[576,256]{1,0:T(8,128)(2,1)S(1)} %add_convert_fusion), channel_id=1, source_target_pairs={{0,2},{1,3},{2,0},{3,1},{4,6},{5,7},{6,4},{7,5},{8,10},{9,11},{10,... | collective-permute-start | bytes 884744 | tf_op jit(solution)/shard_map/ppermute | solution.py:584
  49.9 11.1 %collective-permute-start.20 = (bf16[576,512]{1,0:T(8,128)(2,1)S(1)}, bf16[576,512]{1,0:T(8,128)(2,1)S(1)}, u32[]{:S(2)}, u32[]{:S(2)}) collective-permute-start(bf16[576,512]{1,0:T(8,128)(2,1)S(1)} %grads_for.11), channel_id=1, source_target_pairs={{0,1},{1,0},{2,3},{3,2},{4,5},{5,4},{6,7},{7,6},{8,9},{9,8},{10,11... | collective-permute-start | bytes 1769480 | tf_op jit(solution)/shard_map/ppermute | solution.py:584

commit v12 on v11

--- a/solution.py
+++ b/solution.py
@@ -156,7 +156,7 @@
 PARTS = ((0, 1), (2, 3))
 PART_SWAPS = ((7, 3, 1), (6, 2, 5, 7, 3))
 SWAPS = (1, 3, 7, 5, 2, 6)
-GRAD_SWAPS = (7, 5, 6, 3, 1, 2)
+GRAD_SWAPS = (5, 7, 6, 3, 2, 1)
 
 
 def fits(mesh):

time: 62.3 us -> 62.7 us (level)
  starting transfers between devices: 24.6 us -> 25.5 us
    ppermute x12, starting transfers between devices: 19 us -> 19.9 us  [swapped(): return lax.ppermute(x, 'rows', [(r, partner(r, bits)) for r in range(8)])]
where the time goes in v12:
time: 62.7 us; the launch traced here: 62.6 us
  starting transfers between devices  25.5 us (41%)
  Pallas kernels  19.6 us (31%)
  waiting for transfers between devices  16.2 us (26%)
  between operations  0.95 us (2%)
    ppermute x12, starting transfers between devices, swapped(): return lax.ppermute(x, 'rows', [(r, partner(r, bits)) for r in range(8)])  19.9 us
    ppermute x11, waiting for transfers between devices, flipped(): lax.ppermute(x, 'filt', [(i, i ^ bit) for i in range(lax.axis_size('filt'...  13.8 us
    pallas_call x1, Pallas kernels, outward_sums(): pl.pallas_call(outward_kernel, out_shape=[jax.ShapeDtypeStruct((SENT, 128...  8.22 us
    ppermute x11, starting transfers between devices, flipped(): lax.ppermute(x, 'filt', [(i, i ^ bit) for i in range(lax.axis_size('filt'...  5.57 us
    pallas_call x6, Pallas kernels, grads_for(): pl.pallas_call(functools.partial(grad_kernel, flip, first), out_shape=jax...  5.33 us
    ppermute x12, waiting for transfers between devices, swapped(): return lax.ppermute(x, 'rows', [(r, partner(r, bits)) for r in range(8)])  2.35 us
    pallas_call x1, Pallas kernels, own_sums(): pl.pallas_call(own_kernel, out_shape=[jax.ShapeDtypeStruct((PIXELS, 128),...  1.72 us
  transfers between devices with their start and end apart: 23, of which 7 were waited for; matrix products, arithmetic and copies ran while one was open for 0% of the time, Pallas kernels for 13%

profile of v12, /device:TPU:0, one launch (start us, length us, event | category | flops | bytes accessed | tf_op | source)
XLA Modules:
  0.0 62.6 jit_solution(2538862552433424713)
XLA Ops:
  0.6 8.2 %outward_sums.1 = (f32[304,128]{1,0:T(8,128)S(1)}, f32[304,128]{1,0:T(8,128)S(1)}, f32[304,128]{1,0:T(8,128)S(1)}, f32[304,128]{1,0:T(8,128)S(1)}, f32[304,128]{...) custom-call(bf16[576,2048]{1,0:T(8,128)(2,1)} %bitcast.12, ...), custom_call_target="tpu_custom_call" | custom-call | tf_op jit(solution)/shard_map/outward_sums/pallas_call | solution.py:297
  8.9 3.0 %collective-permute-start.2 = (f16[304,128]{1,0:T(8,128)(2,1)S(1)}, f16[304,128]{1,0:T(8,128)(2,1)S(1)}, u32[]{:S(2)}, u32[]{:S(2)}) collective-permute-start(f16[304,128]{1,0:T(8,128)(2,1)S(1)} %convert_element_type.58), channel_id=1, source_target_pairs={{0,4},{4,0},{8,12},{12,8},{16,20},{20,16},{24,28},{28,24},{1,5},{5... | collective-permute-start | bytes 233480 | tf_op jit(solution)/shard_map/ppermute | solution.py:592
  11.9 1.6 %collective-permute-start.1 = (f16[304,128]{1,0:T(8,128)(2,1)S(1)}, f16[304,128]{1,0:T(8,128)(2,1)S(1)}, u32[]{:S(2)}, u32[]{:S(2)}) collective-permute-start(f16[304,128]{1,0:T(8,128)(2,1)S(1)} %convert_element_type.56), channel_id=1, source_target_pairs={{0,12},{4,8},{8,4},{12,0},{16,28},{20,24},{24,20},{28,16},{1,13},{... | collective-permute-start | bytes 233480 | tf_op jit(solution)/shard_map/ppermute | solution.py:592
  13.6 1.5 %collective-permute-start = (f16[304,128]{1,0:T(8,128)(2,1)S(1)}, f16[304,128]{1,0:T(8,128)(2,1)S(1)}, u32[]{:S(2)}, u32[]{:S(2)}) collective-permute-start(f16[304,128]{1,0:T(8,128)(2,1)S(1)} %convert_element_type.54), channel_id=1, source_target_pairs={{0,4},{4,0},{8,20},{12,16},{16,12},{20,8},{24,28},{28,24},{1,5},{5... | collective-permute-start | bytes 233480 | tf_op jit(solution)/shard_map/ppermute | solution.py:592
  15.1 2.7 %collective-permute-start.5 = (f16[304,128]{1,0:T(8,128)(2,1)S(1)}, f16[304,128]{1,0:T(8,128)(2,1)S(1)}, u32[]{:S(2)}, u32[]{:S(2)}) collective-permute-start(f16[304,128]{1,0:T(8,128)(2,1)S(1)} %convert_element_type.64), channel_id=1, source_target_pairs={{0,8},{4,16},{8,0},{12,24},{16,4},{20,28},{24,12},{28,20},{1,9},{5... | collective-permute-start | bytes 233480 | tf_op jit(solution)/shard_map/ppermute | solution.py:592
  17.9 2.0 %collective-permute-start.3 = (f16[304,128]{1,0:T(8,128)(2,1)S(1)}, f16[304,128]{1,0:T(8,128)(2,1)S(1)}, u32[]{:S(2)}, u32[]{:S(2)}) collective-permute-start(f16[304,128]{1,0:T(8,128)(2,1)S(1)} %convert_element_type.60), channel_id=1, source_target_pairs={{0,4},{4,0},{8,16},{12,20},{16,8},{20,12},{24,28},{28,24},{1,5},{5... | collective-permute-start | bytes 233480 | tf_op jit(solution)/shard_map/ppermute | solution.py:592
  19.9 1.7 %own_sums.1 = (f32[576,128]{1,0:T(8,128)S(1)}, f32[576,128]{1,0:T(8,128)S(1)}) custom-call(bf16[576,2048]{1,0:T(8,128)(2,1)S(1)} %get-tuple-element.25.ordered, bf16[1792,2048]{1,0:T(8,128)(2,1)S(1)} %get-tuple-element.26.weights, f32[4,64]{1,0:T(4,128)S(1)} %copy-done.2), custom_call_target="tpu_custom_call" | custom-call | flops 1000000 | bytes 10000 | tf_op jit(solution)/shard_map/own_sums/pallas_call | solution.py:338
  21.9 1.6 %collective-permute-start.6 = (bf16[576,128]{1,0:T(8,128)(2,1)S(1)}, bf16[576,128]{1,0:T(8,128)(2,1)S(1)}, u32[]{:S(2)}, u32[]{:S(2)}) collective-permute-start(bf16[576,128]{1,0:T(8,128)(2,1)S(1)} %activations.2.a0), channel_id=1, source_target_pairs={{0,2},{1,3},{2,0},{3,1},{4,6},{5,7},{6,4},{7,5},{8,10},{9,11},{10,... | collective-permute-start | bytes 442376 | tf_op jit(solution)/shard_map/ppermute | solution.py:584
  23.8 0.6 collective-permute-start.7
  24.9 2.8 %collective-permute-done.6.a2 = bf16[576,128]{1,0:T(8,128)(2,1)S(1)} collective-permute-done((bf16[576,128]{1,0:T(8,128)(2,1)S(1)}, bf16[576,128]{1,0:T(8,128)(2,1)S(1)}, u32[]{:S(2)}, u32[]{:S(2)}) %collective-permute-start.6) | collective-permute-done | bytes 147488 | tf_op jit(solution)/shard_map/ppermute | solution.py:584
  27.6 1.6 %collective-permute-done.7.b2 = bf16[576,128]{1,0:T(8,128)(2,1)S(1)} collective-permute-done((bf16[576,128]{1,0:T(8,128)(2,1)S(1)}, bf16[576,128]{1,0:T(8,128)(2,1)S(1)}, u32[]{:S(2)}, u32[]{:S(2)}) %collective-permute-start.7) | collective-permute-done | bytes 147488 | tf_op jit(solution)/shard_map/ppermute | solution.py:584
  29.7 0.9 %collective-permute-done.9.b3 = bf16[576,128]{1,0:T(8,128)(2,1)S(1)} collective-permute-done((bf16[576,128]{1,0:T(8,128)(2,1)S(1)}, bf16[576,128]{1,0:T(8,128)(2,1)S(1)}, u32[]{:S(2)}, u32[]{:S(2)}) %collective-permute-start.9) | collective-permute-done | bytes 147488 | tf_op jit(solution)/shard_map/ppermute | solution.py:584
  30.6 0.6 %far_head.1 = (bf16[576,256]{1,0:T(8,128)(2,1)S(1)}, bf16[576,256]{1,0:T(8,128)(2,1)S(1)}, bf16[288,128]{1,0:T(8,128)(2,1)S(1)}, bf16[288,128]{1,0:T(8,128)(2,1)...) custom-call(bf16[576,128]{1,0:T(8,128)(2,1)S(1)} %activations.2.a0, ...), custom_call_target="tpu_custom_call" | custom-call | tf_op jit(solution)/shard_map/far_head/pallas_call | solution.py:444
  31.2 1.8 %collective-permute-start.12 = (bf16[288,128]{1,0:T(8,128)(2,1)S(1)}, bf16[288,128]{1,0:T(8,128)(2,1)S(1)}, u32[]{:S(2)}, u32[]{:S(2)}) collective-permute-start(bf16[288,128]{1,0:T(8,128)(2,1)S(1)} %get-tuple-element.38), channel_id=1, source_target_pairs={{0,8},{4,16},{8,0},{12,24},{16,4},{20,28},{24,12},{28,20},{1,9},{5... | collective-permute-start | bytes 221192 | tf_op jit(solution)/shard_map/ppermute | solution.py:592
  33.0 1.3 %collective-permute-start.13 = (bf16[288,128]{1,0:T(8,128)(2,1)S(1)}, bf16[288,128]{1,0:T(8,128)(2,1)S(1)}, u32[]{:S(2)}, u32[]{:S(2)}) collective-permute-start(bf16[288,128]{1,0:T(8,128)(2,1)S(1)} %get-tuple-element.39), channel_id=1, source_target_pairs={{0,4},{4,0},{8,20},{12,16},{16,12},{20,8},{24,28},{28,24},{1,5},{5... | collective-permute-start | bytes 221192 | tf_op jit(solution)/shard_map/ppermute | solution.py:592
  34.3 0.8 %collective-permute-start.14 = (bf16[288,128]{1,0:T(8,128)(2,1)S(1)}, bf16[288,128]{1,0:T(8,128)(2,1)S(1)}, u32[]{:S(2)}, u32[]{:S(2)}) collective-permute-start(bf16[288,128]{1,0:T(8,128)(2,1)S(1)} %get-tuple-element.40), channel_id=1, source_target_pairs={{0,4},{4,0},{8,16},{12,20},{16,8},{20,12},{24,28},{28,24},{1,5},{5... | collective-permute-start | bytes 221192 | tf_op jit(solution)/shard_map/ppermute | solution.py:592
  35.1 1.2 %collective-permute-start.15 = (bf16[288,128]{1,0:T(8,128)(2,1)S(1)}, bf16[288,128]{1,0:T(8,128)(2,1)S(1)}, u32[]{:S(2)}, u32[]{:S(2)}) collective-permute-start(bf16[288,128]{1,0:T(8,128)(2,1)S(1)} %get-tuple-element.41), channel_id=1, source_target_pairs={{0,12},{4,8},{8,4},{12,0},{16,28},{20,24},{24,20},{28,16},{1,13},{... | collective-permute-start | bytes 221192 | tf_op jit(solution)/shard_map/ppermute | solution.py:592
  36.2 1.6 %collective-permute-start.16 = (bf16[288,128]{1,0:T(8,128)(2,1)S(1)}, bf16[288,128]{1,0:T(8,128)(2,1)S(1)}, u32[]{:S(2)}, u32[]{:S(2)}) collective-permute-start(bf16[288,128]{1,0:T(8,128)(2,1)S(1)} %get-tuple-element.42), channel_id=1, source_target_pairs={{0,8},{4,12},{8,0},{12,4},{16,24},{20,28},{24,16},{28,20},{1,9},{5... | collective-permute-start | bytes 221192 | tf_op jit(solution)/shard_map/ppermute | solution.py:592
  37.8 2.5 %collective-permute-start.17 = (bf16[288,128]{1,0:T(8,128)(2,1)S(1)}, bf16[288,128]{1,0:T(8,128)(2,1)S(1)}, u32[]{:S(2)}, u32[]{:S(2)}) collective-permute-start(bf16[288,128]{1,0:T(8,128)(2,1)S(1)} %get-tuple-element.43), channel_id=1, source_target_pairs={{0,4},{4,0},{8,12},{12,8},{16,20},{20,16},{24,28},{28,24},{1,5},{5... | collective-permute-start | bytes 221192 | tf_op jit(solution)/shard_map/ppermute | solution.py:592
  41.3 1.3 %collective-permute-done.17.refs_5_ = bf16[288,128]{1,0:T(8,128)(2,1)S(1)} collective-permute-done((bf16[288,128]{1,0:T(8,128)(2,1)S(1)}, bf16[288,128]{1,0:T(8,128)(2,1)S(1)}, u32[]{:S(2)}, u32[]{:S(2)}) %collective-permute-start.17) | collective-permute-done | bytes 73760 | tf_op jit(solution)/shard_map/ppermute | solution.py:592
  42.6 0.6 spread.1.stack
  43.2 0.7 %grads_for.7 = bf16[576,256]{1,0:T(8,128)(2,1)S(1)} custom-call(bf16[576,1792]{1,0:T(8,128)(2,1)S(1)} %spread.1.stack, bf16[1792,2048]{1,0:T(8,128)(2,1)S(1)} %get-tuple-element.26.weights), custom_call_target="tpu_custom_call" | custom-call | flops 528482304 | bytes 1000000 | tf_op jit(solution)/shard_map/grads_for/pallas_call | solution.py:540
  44.0 0.7 %grads_for.6 = bf16[576,256]{1,0:T(8,128)(2,1)S(1)} custom-call(bf16[576,1792]{1,0:T(8,128)(2,1)S(1)} %spread.1.stack, bf16[1792,2048]{1,0:T(8,128)(2,1)S(1)} %get-tuple-element.26.weights), custom_call_target="tpu_custom_call" | custom-call | flops 528482304 | bytes 1000000 | tf_op jit(solution)/shard_map/grads_for/pallas_call | solution.py:540
  45.3 0.7 %grads_for.8 = bf16[576,256]{1,0:T(8,128)(2,1)S(1)} custom-call(bf16[576,1792]{1,0:T(8,128)(2,1)S(1)} %spread.1.stack, bf16[1792,2048]{1,0:T(8,128)(2,1)S(1)} %get-tuple-element.26.weights), custom_call_target="tpu_custom_call" | custom-call | flops 528482304 | bytes 1000000 | tf_op jit(solution)/shard_map/grads_for/pallas_call | solution.py:540
  46.1 1.6 %collective-permute-start.21 = (bf16[576,256]{1,0:T(8,128)(2,1)S(1)}, bf16[576,256]{1,0:T(8,128)(2,1)S(1)}, u32[]{:S(2)}, u32[]{:S(2)}) collective-permute-start(bf16[576,256]{1,0:T(8,128)(2,1)S(1)} %add_convert_fusion.1), channel_id=1, source_target_pairs={{0,2},{1,3},{2,0},{3,1},{4,6},{5,7},{6,4},{7,5},{8,10},{9,11},{10,... | collective-permute-start | bytes 884744 | tf_op jit(solution)/shard_map/ppermute | solution.py:584
  47.7 0.7 %grads_for.9 = bf16[576,256]{1,0:T(8,128)(2,1)S(1)} custom-call(bf16[576,1792]{1,0:T(8,128)(2,1)S(1)} %spread.1.stack, bf16[1792,2048]{1,0:T(8,128)(2,1)S(1)} %get-tuple-element.26.weights), custom_call_target="tpu_custom_call" | custom-call | flops 528482304 | bytes 1000000 | tf_op jit(solution)/shard_map/grads_for/pallas_call | solution.py:540
  48.5 0.6 collective-permute-start.22
  49.1 1.2 %grads_for.11 = bf16[576,512]{1,0:T(8,128)(2,1)S(1)} custom-call(bf16[576,1792]{1,0:T(8,128)(2,1)S(1)} %spread.1.stack, bf16[1792,2048]{1,0:T(8,128)(2,1)S(1)} %get-tuple-element.26.weights), custom_call_target="tpu_custom_call" | custom-call | flops 1056964608 | bytes 1000000 | tf_op jit(solution)/shard_map/grads_for/pallas_call | solution.py:540
  50.4 1.2 %grads_for.10.a = bf16[576,512]{1,0:T(8,128)(2,1)S(1)} custom-call(bf16[576,1792]{1,0:T(8,128)(2,1)S(1)} %spread.1.stack, bf16[1792,2048]{1,0:T(8,128)(2,1)S(1)} %get-tuple-element.26.weights), custom_call_target="tpu_custom_call" | custom-call | flops 8455716864 | bytes 1000000 | tf_op jit(solution)/shard_map/grads_for/pallas_call | solution.py:540
  51.6 1.2 %own_output.1 = bf16[576,64]{1,0:T(8,128)(2,1)} custom-call(bf16[576,256]{1,0:T(8,128)(2,1)S(1)} %get-tuple-element.46.output), custom_call_target="tpu_custom_call" | custom-call | tf_op jit(solution)/shard_map/own_output/pallas_call | solution.py:469
  52.8 8.6 %collective-permute-done.22.d = bf16[576,256]{1,0:T(8,128)(2,1)S(1)} collective-permute-done((bf16[576,256]{1,0:T(8,128)(2,1)S(1)}, bf16[576,256]{1,0:T(8,128)(2,1)S(1)}, u32[]{:S(2)}, u32[]{:S(2)}) %collective-permute-start.22) | collective-permute-done | bytes 294944 | tf_op jit(solution)/shard_map/ppermute | solution.py:584
  61.4 1.1 %last_sum.1 = bf16[576,512]{1,0:T(8,128)(2,1)} custom-call(bf16[576,512]{1,0:T(8,128)(2,1)S(1)} %grads_for.10.a, bf16[576,512]{1,0:T(8,128)(2,1)S(1)} %collective-permute-done.20.b, bf16[576,256]{1,0:T(8,128)(2,1)S(1)} %collective-permute-done.21.c, bf16[576,256]{1,0:T(8,128)(2,1)S(1)} %collective-permute-done.22.d), custom_call_target="tpu_custom_call" | custom-call | tf_op jit(solution)/shard_map/last_sum/pallas_call | solution.py:572
  (51 shorter events, 3.5 us)
Async XLA Ops:
  0.6 19.2 %copy-start.2 = (f32[4,64]{1,0:T(4,128)S(1)}, f32[4,64]{1,0:T(4,128)}, u32[]{:S(2)}) copy-start(f32[4,64]{1,0:T(4,128)} %bias.1) | copy-start | bytes 3076
  8.9 9.0 %collective-permute-start.2 = (f16[304,128]{1,0:T(8,128)(2,1)S(1)}, f16[304,128]{1,0:T(8,128)(2,1)S(1)}, u32[]{:S(2)}, u32[]{:S(2)}) collective-permute-start(f16[304,128]{1,0:T(8,128)(2,1)S(1)} %convert_element_type.58), channel_id=1, source_target_pairs={{0,4},{4,0},{8,12},{12,8},{16,20},{20,16},{24,28},{28,24},{1,5},{5... | collective-permute-start | bytes 233480 | tf_op jit(solution)/shard_map/ppermute | solution.py:592
  11.9 9.7 %collective-permute-start.1 = (f16[304,128]{1,0:T(8,128)(2,1)S(1)}, f16[304,128]{1,0:T(8,128)(2,1)S(1)}, u32[]{:S(2)}, u32[]{:S(2)}) collective-permute-start(f16[304,128]{1,0:T(8,128)(2,1)S(1)} %convert_element_type.56), channel_id=1, source_target_pairs={{0,12},{4,8},{8,4},{12,0},{16,28},{20,24},{24,20},{28,16},{1,13},{... | collective-permute-start | bytes 233480 | tf_op jit(solution)/shard_map/ppermute | solution.py:592
  13.6 8.1 %collective-permute-start = (f16[304,128]{1,0:T(8,128)(2,1)S(1)}, f16[304,128]{1,0:T(8,128)(2,1)S(1)}, u32[]{:S(2)}, u32[]{:S(2)}) collective-permute-start(f16[304,128]{1,0:T(8,128)(2,1)S(1)} %convert_element_type.54), channel_id=1, source_target_pairs={{0,4},{4,0},{8,20},{12,16},{16,12},{20,8},{24,28},{28,24},{1,5},{5... | collective-permute-start | bytes 233480 | tf_op jit(solution)/shard_map/ppermute | solution.py:592
  15.1 8.4 %collective-permute-start.5 = (f16[304,128]{1,0:T(8,128)(2,1)S(1)}, f16[304,128]{1,0:T(8,128)(2,1)S(1)}, u32[]{:S(2)}, u32[]{:S(2)}) collective-permute-start(f16[304,128]{1,0:T(8,128)(2,1)S(1)} %convert_element_type.64), channel_id=1, source_target_pairs={{0,8},{4,16},{8,0},{12,24},{16,4},{20,28},{24,12},{28,20},{1,9},{5... | collective-permute-start | bytes 233480 | tf_op jit(solution)/shard_map/ppermute | solution.py:592
  17.8 5.7 %collective-permute-start.4 = (f16[304,128]{1,0:T(8,128)(2,1)S(1)}, f16[304,128]{1,0:T(8,128)(2,1)S(1)}, u32[]{:S(2)}, u32[]{:S(2)}) collective-permute-start(f16[304,128]{1,0:T(8,128)(2,1)S(1)} %convert_element_type.62), channel_id=1, source_target_pairs={{0,8},{4,12},{8,0},{12,4},{16,24},{20,28},{24,16},{28,20},{1,9},{5... | collective-permute-start | bytes 233480 | tf_op jit(solution)/shard_map/ppermute | solution.py:592
  17.9 5.6 %collective-permute-start.3 = (f16[304,128]{1,0:T(8,128)(2,1)S(1)}, f16[304,128]{1,0:T(8,128)(2,1)S(1)}, u32[]{:S(2)}, u32[]{:S(2)}) collective-permute-start(f16[304,128]{1,0:T(8,128)(2,1)S(1)} %convert_element_type.60), channel_id=1, source_target_pairs={{0,4},{4,0},{8,16},{12,20},{16,8},{20,12},{24,28},{28,24},{1,5},{5... | collective-permute-start | bytes 233480 | tf_op jit(solution)/shard_map/ppermute | solution.py:592
  21.6 7.6 %copy-start = (bf16[4,256,256]{2,1,0:T(8,128)(2,1)S(1)}, bf16[4,256,256]{2,1,0:T(8,128)(2,1)}, u32[]{:S(2)}) copy-start(bf16[4,256,256]{2,1,0:T(8,128)(2,1)} %project.3) | copy-start | bytes 1572868
  21.6 7.6 %copy-start.1 = (bf16[12,48,256]{2,1,0:T(8,128)(2,1)S(1)}, bf16[12,48,256]{2,1,0:T(8,128)(2,1)}, u32[]{:S(2)}) copy-start(bf16[12,48,256]{2,1,0:T(8,128)(2,1)} %param.13) | copy-start | bytes 884740
  21.6 7.6 %copy-start.3 = (f32[256]{0:T(256)S(1)}, f32[256]{0:T(256)}, u32[]{:S(2)}) copy-start(f32[256]{0:T(256)} %param.12) | copy-start | bytes 3076
  21.9 5.7 %collective-permute-start.6 = (bf16[576,128]{1,0:T(8,128)(2,1)S(1)}, bf16[576,128]{1,0:T(8,128)(2,1)S(1)}, u32[]{:S(2)}, u32[]{:S(2)}) collective-permute-start(bf16[576,128]{1,0:T(8,128)(2,1)S(1)} %activations.2.a0), channel_id=1, source_target_pairs={{0,2},{1,3},{2,0},{3,1},{4,6},{5,7},{6,4},{7,5},{8,10},{9,11},{10,... | collective-permute-start | bytes 442376 | tf_op jit(solution)/shard_map/ppermute | solution.py:584
  23.8 5.4 %collective-permute-start.7 = (bf16[576,128]{1,0:T(8,128)(2,1)S(1)}, bf16[576,128]{1,0:T(8,128)(2,1)S(1)}, u32[]{:S(2)}, u32[]{:S(2)}) collective-permute-start(bf16[576,128]{1,0:T(8,128)(2,1)S(1)} %activations.3.b0), channel_id=1, source_target_pairs={{0,2},{1,3},{2,0},{3,1},{4,6},{5,7},{6,4},{7,5},{8,10},{9,11},{10,... | collective-permute-start | bytes 442376 | tf_op jit(solution)/shard_map/ppermute | solution.py:584
  24.4 4.9 %collective-permute-start.10 = (bf16[576,128]{1,0:T(8,128)(2,1)S(1)}, bf16[576,128]{1,0:T(8,128)(2,1)S(1)}, u32[]{:S(2)}, u32[]{:S(2)}) collective-permute-start(bf16[576,128]{1,0:T(8,128)(2,1)S(1)} %activations.2.a0), channel_id=1, source_target_pairs={{0,1},{1,0},{2,3},{3,2},{4,5},{5,4},{6,7},{7,6},{8,9},{9,8},{10,11... | collective-permute-start | bytes 442376 | tf_op jit(solution)/shard_map/ppermute | solution.py:584
  24.4 4.9 %collective-permute-start.11 = (bf16[576,128]{1,0:T(8,128)(2,1)S(1)}, bf16[576,128]{1,0:T(8,128)(2,1)S(1)}, u32[]{:S(2)}, u32[]{:S(2)}) collective-permute-start(bf16[576,128]{1,0:T(8,128)(2,1)S(1)} %activations.3.b0), channel_id=1, source_target_pairs={{0,1},{1,0},{2,3},{3,2},{4,5},{5,4},{6,7},{7,6},{8,9},{9,8},{10,11... | collective-permute-start | bytes 442376 | tf_op jit(solution)/shard_map/ppermute | solution.py:584
  27.6 2.0 %collective-permute-start.8 = (bf16[576,128]{1,0:T(8,128)(2,1)S(1)}, bf16[576,128]{1,0:T(8,128)(2,1)S(1)}, u32[]{:S(2)}, u32[]{:S(2)}) collective-permute-start(bf16[576,128]{1,0:T(8,128)(2,1)S(1)} %collective-permute-done.6.a2), channel_id=1, source_target_pairs={{0,1},{1,0},{2,3},{3,2},{4,5},{5,4},{6,7},{7,6},{8,9},{9,8},{10,11... | collective-permute-start | bytes 442376 | tf_op jit(solution)/shard_map/ppermute | solution.py:584
  29.2 1.4 %collective-permute-start.9 = (bf16[576,128]{1,0:T(8,128)(2,1)S(1)}, bf16[576,128]{1,0:T(8,128)(2,1)S(1)}, u32[]{:S(2)}, u32[]{:S(2)}) collective-permute-start(bf16[576,128]{1,0:T(8,128)(2,1)S(1)} %collective-permute-done.7.b2), channel_id=1, source_target_pairs={{0,1},{1,0},{2,3},{3,2},{4,5},{5,4},{6,7},{7,6},{8,9},{9,8},{10,11... | collective-permute-start | bytes 442376 | tf_op jit(solution)/shard_map/ppermute | solution.py:584
  31.2 6.6 %collective-permute-start.12 = (bf16[288,128]{1,0:T(8,128)(2,1)S(1)}, bf16[288,128]{1,0:T(8,128)(2,1)S(1)}, u32[]{:S(2)}, u32[]{:S(2)}) collective-permute-start(bf16[288,128]{1,0:T(8,128)(2,1)S(1)} %get-tuple-element.38), channel_id=1, source_target_pairs={{0,8},{4,16},{8,0},{12,24},{16,4},{20,28},{24,12},{28,20},{1,9},{5... | collective-permute-start | bytes 221192 | tf_op jit(solution)/shard_map/ppermute | solution.py:592
  33.0 7.2 %collective-permute-start.13 = (bf16[288,128]{1,0:T(8,128)(2,1)S(1)}, bf16[288,128]{1,0:T(8,128)(2,1)S(1)}, u32[]{:S(2)}, u32[]{:S(2)}) collective-permute-start(bf16[288,128]{1,0:T(8,128)(2,1)S(1)} %get-tuple-element.39), channel_id=1, source_target_pairs={{0,4},{4,0},{8,20},{12,16},{16,12},{20,8},{24,28},{28,24},{1,5},{5... | collective-permute-start | bytes 221192 | tf_op jit(solution)/shard_map/ppermute | solution.py:592
  34.3 6.5 %collective-permute-start.14 = (bf16[288,128]{1,0:T(8,128)(2,1)S(1)}, bf16[288,128]{1,0:T(8,128)(2,1)S(1)}, u32[]{:S(2)}, u32[]{:S(2)}) collective-permute-start(bf16[288,128]{1,0:T(8,128)(2,1)S(1)} %get-tuple-element.40), channel_id=1, source_target_pairs={{0,4},{4,0},{8,16},{12,20},{16,8},{20,12},{24,28},{28,24},{1,5},{5... | collective-permute-start | bytes 221192 | tf_op jit(solution)/shard_map/ppermute | solution.py:592
  35.1 5.8 %collective-permute-start.15 = (bf16[288,128]{1,0:T(8,128)(2,1)S(1)}, bf16[288,128]{1,0:T(8,128)(2,1)S(1)}, u32[]{:S(2)}, u32[]{:S(2)}) collective-permute-start(bf16[288,128]{1,0:T(8,128)(2,1)S(1)} %get-tuple-element.41), channel_id=1, source_target_pairs={{0,12},{4,8},{8,4},{12,0},{16,28},{20,24},{24,20},{28,16},{1,13},{... | collective-permute-start | bytes 221192 | tf_op jit(solution)/shard_map/ppermute | solution.py:592
  36.2 5.1 %collective-permute-start.16 = (bf16[288,128]{1,0:T(8,128)(2,1)S(1)}, bf16[288,128]{1,0:T(8,128)(2,1)S(1)}, u32[]{:S(2)}, u32[]{:S(2)}) collective-permute-start(bf16[288,128]{1,0:T(8,128)(2,1)S(1)} %get-tuple-element.42), channel_id=1, source_target_pairs={{0,8},{4,12},{8,0},{12,4},{16,24},{20,28},{24,16},{28,20},{1,9},{5... | collective-permute-start | bytes 221192 | tf_op jit(solution)/shard_map/ppermute | solution.py:592
  37.8 4.8 %collective-permute-start.17 = (bf16[288,128]{1,0:T(8,128)(2,1)S(1)}, bf16[288,128]{1,0:T(8,128)(2,1)S(1)}, u32[]{:S(2)}, u32[]{:S(2)}) collective-permute-start(bf16[288,128]{1,0:T(8,128)(2,1)S(1)} %get-tuple-element.43), channel_id=1, source_target_pairs={{0,4},{4,0},{8,12},{12,8},{16,20},{20,16},{24,28},{28,24},{1,5},{5... | collective-permute-start | bytes 221192 | tf_op jit(solution)/shard_map/ppermute | solution.py:592
  43.9 2.1 %collective-permute-start.19 = (bf16[576,256]{1,0:T(8,128)(2,1)S(1)}, bf16[576,256]{1,0:T(8,128)(2,1)S(1)}, u32[]{:S(2)}, u32[]{:S(2)}) collective-permute-start(bf16[576,256]{1,0:T(8,128)(2,1)S(1)} %grads_for.7), channel_id=1, source_target_pairs={{0,1},{1,0},{2,3},{3,2},{4,5},{5,4},{6,7},{7,6},{8,9},{9,8},{10,11... | collective-permute-start | bytes 884744 | tf_op jit(solution)/shard_map/ppermute | solution.py:584
  44.7 3.6 %collective-permute-start.18 = (bf16[576,256]{1,0:T(8,128)(2,1)S(1)}, bf16[576,256]{1,0:T(8,128)(2,1)S(1)}, u32[]{:S(2)}, u32[]{:S(2)}) collective-permute-start(bf16[576,256]{1,0:T(8,128)(2,1)S(1)} %grads_for.6), channel_id=1, source_target_pairs={{0,1},{1,0},{2,3},{3,2},{4,5},{5,4},{6,7},{7,6},{8,9},{9,8},{10,11... | collective-permute-start | bytes 884744 | tf_op jit(solution)/shard_map/ppermute | solution.py:584
  46.1 15.3 %collective-permute-start.21 = (bf16[576,256]{1,0:T(8,128)(2,1)S(1)}, bf16[576,256]{1,0:T(8,128)(2,1)S(1)}, u32[]{:S(2)}, u32[]{:S(2)}) collective-permute-start(bf16[576,256]{1,0:T(8,128)(2,1)S(1)} %add_convert_fusion.1), channel_id=1, source_target_pairs={{0,2},{1,3},{2,0},{3,1},{4,6},{5,7},{6,4},{7,5},{8,10},{9,11},{10,... | collective-permute-start | bytes 884744 | tf_op jit(solution)/shard_map/ppermute | solution.py:584
  48.5 13.0 %collective-permute-start.22 = (bf16[576,256]{1,0:T(8,128)(2,1)S(1)}, bf16[576,256]{1,0:T(8,128)(2,1)S(1)}, u32[]{:S(2)}, u32[]{:S(2)}) collective-permute-start(bf16[576,256]{1,0:T(8,128)(2,1)S(1)} %add_convert_fusion), channel_id=1, source_target_pairs={{0,2},{1,3},{2,0},{3,1},{4,6},{5,7},{6,4},{7,5},{8,10},{9,11},{10,... | collective-permute-start | bytes 884744 | tf_op jit(solution)/shard_map/ppermute | solution.py:584
  50.3 11.1 %collective-permute-start.20 = (bf16[576,512]{1,0:T(8,128)(2,1)S(1)}, bf16[576,512]{1,0:T(8,128)(2,1)S(1)}, u32[]{:S(2)}, u32[]{:S(2)}) collective-permute-start(bf16[576,512]{1,0:T(8,128)(2,1)S(1)} %grads_for.11), channel_id=1, source_target_pairs={{0,1},{1,0},{2,3},{3,2},{4,5},{5,4},{6,7},{7,6},{8,9},{9,8},{10,11... | collective-permute-start | bytes 1769480 | tf_op jit(solution)/shard_map/ppermute | solution.py:584
